TPU v7x, 32 devices: a whole 2x2x4 slice. The times are simulated.
32 devices in a mesh: rows: 8 (over z, y), seq: 4 (over x, core).
Axes of the slice: x: 2, y: 2, z: 4, core: 2. Of those that a mesh axis runs over, the one named last changes fastest.
Arguments:
- noisy_mel: bfloat16 [8, 3328, 100], P('rows', 'seq'), may hold values from -6 to 6
- cond_mel: bfloat16 [8, 3328, 100], P('rows', 'seq'), may hold values from -6 to 6
- text_feat: bfloat16 [8, 3328, 512], P('rows', 'seq'), may hold values from -6 to 6
- time_embed: bfloat16 [8, 1024], P('rows'), may hold values from -6 to 6
- seg_lengths: int32 [8, 8], P('rows'), may hold values from 1 to 3224, as said below
- audio_drop: int32 [8, 8], P('rows'), may hold values 0 or 1
- text_drop: int32 [8, 8], P('rows'), may hold values 0 or 1
- w_in: bfloat16 [712, 1024], replicated, may hold values from -0.21875 to 0.21875
- b_in: bfloat16 [1024], replicated, may hold values from -1 to 1
- ada_w: bfloat16 [1024, 6144], replicated, may hold values from -0.1875 to 0.1875
- ada_b: bfloat16 [6144], replicated, may hold values from -1 to 1
- w_qkv: bfloat16 [1024, 3072], replicated, may hold values from -0.1875 to 0.1875
- b_qkv: bfloat16 [3072], replicated, may hold values from -1 to 1
- w_out: bfloat16 [1024, 1024], replicated, may hold values from -3 to 3
- b_out: bfloat16 [1024], replicated, may hold values from -1 to 1
- w_up: bfloat16 [1024, 2048], replicated, may hold values from -0.1875 to 0.1875
- b_up: bfloat16 [2048], replicated, may hold values from -1 to 1
- w_down: bfloat16 [2048, 1024], replicated, may hold values from -0.125 to 0.125
- b_down: bfloat16 [1024], replicated, may hold values from -1 to 1
- cotangent: bfloat16 [8, 3328, 1024], P('rows', 'seq'), may hold values from -6 to 6
Outputs:
- out: bfloat16 [8, 3328, 1024], P('rows', 'seq')
- noisy_grad: float32 [8, 3328, 100], P('rows', 'seq')
- cond_grad: float32 [8, 3328, 100], P('rows', 'seq')
- text_grad: float32 [8, 3328, 512], P('rows', 'seq')
- time_grad: float32 [8, 1024], P('rows')
- w_in_grad: float32 [712, 1024], P(None, 'seq')
- b_in_grad: float32 [1024], P('seq')
- ada_w_grad: float32 [1024, 6144], P('seq')
- ada_b_grad: float32 [6144], P('seq')
- w_qkv_grad: float32 [1024, 3072], P('seq')
- b_qkv_grad: float32 [3072], P('seq')
- w_out_grad: float32 [1024, 1024], P('seq')
- b_out_grad: float32 [1024], P('seq')
- w_up_grad: float32 [1024, 2048], P('seq')
- b_up_grad: float32 [2048], P('seq')
- w_down_grad: float32 [2048, 1024], P('seq')
- b_down_grad: float32 [1024], P('seq')
Inputs may be any that keep to these rules, and one draw needn't show every extreme that they name: `seg_lengths`: each row's 8 lengths are positive and sum to 3328; in one row of each group of 1 row one segment other than the last has exactly 3224 frames.
All inputs are finite; a program needn't handle non-finite values. No bound on the sum of `audio_drop` or of `text_drop` on one device may be relied on, other than what follows from the above.
Results may differ from a plain program's by a relative error of at most 0.02.
Values may be sent and summed in bfloat16 or wider, within the bound.
No kernel may reach another device: no remote copies, remote signals or barrier semaphores. Data moves between devices by JAX's collectives and lax.ppermute only.
A program may use at most 448 MiB of HBM per device.

v0:
```python
import math

import jax
import jax.numpy as jnp
from jax import lax
from jax.sharding import PartitionSpec as P

HEADS = 16


EPS = 1e-06
THETA = 10000.0
MASKED = -1e30


def frame_table(row_lengths, first_frame, frame_count):
    seg_ends = jnp.cumsum(row_lengths)
    starts = seg_ends - row_lengths
    frames = first_frame + jnp.arange(frame_count, dtype=jnp.int32)
    inside = ((frames[:, None] >= starts[None, :]) & (frames[:, None] < seg_ends[None, :])).astype(
        jnp.int32
    )
    numbers = jnp.arange(row_lengths.shape[0], dtype=jnp.int32)
    labels = jnp.sum(inside * numbers[None, :], axis=1)
    offsets = frames - jnp.sum(inside * starts[None, :], axis=1)
    return (inside.astype(jnp.float32), labels, offsets)


def rotary_tables(offsets, head_dim):
    halves = head_dim // 2
    frequency = jnp.exp(-math.log(THETA) * 2.0 * jnp.arange(halves, dtype=jnp.float32) / head_dim)
    angles = offsets.astype(jnp.float32)[..., None] * frequency
    return (jnp.cos(angles), jnp.sin(angles))


def rotate(values, cos_table, sin_table, head_count):
    full_shape = values.shape
    split_parts = values.reshape(
        full_shape[:-1] + (head_count, 2, full_shape[-1] // (2 * head_count))
    )
    first_half = split_parts[..., 0, :]
    second_half = split_parts[..., 1, :]
    cos_part = cos_table[..., None, :]
    sin_part = sin_table[..., None, :]
    turned = jnp.stack(
        [
            first_half * cos_part - second_half * sin_part,
            second_half * cos_part + first_half * sin_part,
        ],
        axis=-2,
    )
    return turned.reshape(full_shape)


def normalize(stream):
    center = stream - jnp.mean(stream, axis=-1, keepdims=True)
    inv_std = lax.rsqrt(jnp.mean(center * center, axis=-1, keepdims=True) + EPS)
    return (center * inv_std, inv_std)


def normalize_back(normed, inv_std, upstream):
    return inv_std * (
        upstream
        - jnp.mean(upstream, axis=-1, keepdims=True)
        - normed * jnp.mean(upstream * normed, axis=-1, keepdims=True)
    )


def outer_grad(left_rows, right_rows):
    return lax.dot_general(
        left_rows, right_rows, (((0,), (0,)), ((), ())), preferred_element_type=jnp.float32
    )


def back_grad(upstream, weight):
    return lax.dot_general(
        upstream, weight, (((1,), (1,)), ((), ())), preferred_element_type=jnp.float32
    )


def shards(
    noisy_mel,
    cond_mel,
    text_feat,
    time_embed,
    seg_lengths,
    audio_drop,
    text_drop,
    w_in,
    b_in,
    ada_w,
    ada_b,
    w_qkv,
    b_qkv,
    w_out,
    b_out,
    w_up,
    b_up,
    w_down,
    b_down,
    cotangent,
):
    row_count, span_len, mel_width = noisy_mel.shape
    model_width = w_qkv.shape[0]
    head_dim = model_width // HEADS
    frame_count = row_count * span_len
    seq_count = lax.axis_size("seq")
    seq_index = lax.axis_index("seq")
    first_frame = seq_index * span_len
    score_scale = head_dim ** (-0.5)
    member, labels, offsets = jax.vmap(
        lambda row_lengths: frame_table(row_lengths, first_frame, span_len)
    )(seg_lengths)
    keep_audio = 1.0 - jnp.einsum("rcs,rs->rc", member, audio_drop.astype(jnp.float32))
    keep_text = 1.0 - jnp.einsum("rcs,rs->rc", member, text_drop.astype(jnp.float32))
    frame_valid = 1.0 - member[:, :, -1]
    inputs = jnp.concatenate(
        [
            noisy_mel,
            cond_mel * keep_audio[..., None].astype(jnp.bfloat16),
            text_feat * keep_text[..., None].astype(jnp.bfloat16),
        ],
        axis=2,
    ).reshape(frame_count, -1)
    cos_table, sin_table = rotary_tables(offsets, head_dim)
    time_float = time_embed.astype(jnp.float32)
    time_act = jax.nn.silu(time_float).astype(jnp.bfloat16)
    embedding = jnp.dot(time_act, ada_w, preferred_element_type=jnp.float32) + ada_b.astype(
        jnp.float32
    )
    shift_one, scale_one, gate_one, shift_two, scale_two, gate_two = [
        emb_part[:, None, :] for emb_part in jnp.split(embedding, 6, axis=1)
    ]
    resid_zero = (
        jnp.dot(inputs, w_in, preferred_element_type=jnp.float32) + b_in.astype(jnp.float32)
    ).reshape(row_count, span_len, model_width)
    normed_one, inv_one = normalize(resid_zero)
    mod_one = (
        (normed_one * (1.0 + scale_one) + shift_one)
        .astype(jnp.bfloat16)
        .reshape(frame_count, model_width)
    )
    projected = (
        jnp.dot(mod_one, w_qkv, preferred_element_type=jnp.float32) + b_qkv.astype(jnp.float32)
    ).reshape(row_count, span_len, 3 * model_width)
    queries = rotate(projected[..., :model_width], cos_table, sin_table, HEADS).astype(jnp.bfloat16)
    key_rows = rotate(
        projected[..., model_width : 2 * model_width], cos_table, sin_table, HEADS
    ).astype(jnp.bfloat16)
    value_rows = projected[..., 2 * model_width :].astype(jnp.bfloat16)
    query_heads = queries.reshape(row_count, span_len, HEADS, head_dim)

    def key_labels(start_frame, length):
        return jax.vmap(lambda row_lengths: frame_table(row_lengths, start_frame, length)[1])(
            seg_lengths
        )

    start_state = (
        jnp.full((row_count, HEADS, span_len), MASKED, jnp.float32),
        jnp.zeros((row_count, HEADS, span_len), jnp.float32),
        jnp.zeros((row_count, HEADS, span_len, head_dim), jnp.float32),
    )
    key_piece = lax.all_gather(key_rows, "seq", axis=1, tiled=True)
    value_piece = lax.all_gather(value_rows, "seq", axis=1, tiled=True)
    block_len = math.gcd(key_piece.shape[1], span_len)

    def one_block(block_index, running):
        running_max, row_total, accumulated = running
        key_block = lax.dynamic_slice_in_dim(
            key_piece, block_index * block_len, block_len, 1
        ).reshape(row_count, block_len, HEADS, head_dim)
        value_block = lax.dynamic_slice_in_dim(
            value_piece, block_index * block_len, block_len, 1
        ).reshape(row_count, block_len, HEADS, head_dim)
        scores = (
            jnp.einsum(
                "rqhd,rkhd->rhqk", query_heads, key_block, preferred_element_type=jnp.float32
            )
            * score_scale
        )
        matches = (
            labels[:, None, :, None]
            == key_labels(block_index * block_len, block_len)[:, None, None, :]
        )
        masked = jnp.where(matches, scores, MASKED)
        new_max = jnp.maximum(running_max, jnp.max(masked, axis=3))
        weights = jnp.where(matches, jnp.exp(masked - new_max[..., None]), 0.0)
        rescale = jnp.exp(running_max - new_max)
        row_total = row_total * rescale + jnp.sum(weights, axis=3)
        mixed_block = jnp.einsum(
            "rhqk,rkhd->rhqd",
            weights.astype(jnp.bfloat16),
            value_block,
            preferred_element_type=jnp.float32,
        )
        accumulated = accumulated * rescale[..., None] + mixed_block
        return (new_max, row_total, accumulated)

    running_max, row_total, accumulated = lax.fori_loop(
        0, key_piece.shape[1] // block_len, one_block, start_state
    )
    log_total = running_max + jnp.log(row_total)
    attn_full = accumulated / row_total[..., None]
    mixed_rows = (
        jnp.transpose(attn_full, (0, 2, 1, 3))
        .reshape(frame_count, model_width)
        .astype(jnp.bfloat16)
    )
    branch = (
        jnp.dot(mixed_rows, w_out, preferred_element_type=jnp.float32) + b_out.astype(jnp.float32)
    ).reshape(row_count, span_len, model_width)
    resid_one = resid_zero + gate_one * branch * frame_valid[..., None]
    normed_two, inv_two = normalize(resid_one)
    mod_two = (
        (normed_two * (1.0 + scale_two) + shift_two)
        .astype(jnp.bfloat16)
        .reshape(frame_count, model_width)
    )
    hidden = jnp.dot(mod_two, w_up, preferred_element_type=jnp.float32) + b_up.astype(jnp.float32)
    activated = jax.nn.gelu(hidden, approximate=True).astype(jnp.bfloat16)
    ff_out = (
        jnp.dot(activated, w_down, preferred_element_type=jnp.float32) + b_down.astype(jnp.float32)
    ).reshape(row_count, span_len, model_width)
    result = (resid_one + gate_two * ff_out).astype(jnp.bfloat16)
    grad_out = cotangent.astype(jnp.float32)
    d_gate_two = jnp.sum(grad_out * ff_out, axis=1)
    d_ff = (grad_out * gate_two).astype(jnp.bfloat16).reshape(frame_count, model_width)
    w_down_grad = outer_grad(activated, d_ff)
    b_down_grad = jnp.sum(d_ff.astype(jnp.float32), axis=0)
    grad_act = back_grad(d_ff, w_down)
    gelu_out, gelu_pull = jax.vjp(lambda pre_act: jax.nn.gelu(pre_act, approximate=True), hidden)
    d_hidden = gelu_pull(grad_act)[0].astype(jnp.bfloat16)
    w_up_grad = outer_grad(mod_two, d_hidden)
    b_up_grad = jnp.sum(d_hidden.astype(jnp.float32), axis=0)
    d_mod_two = back_grad(d_hidden, w_up).reshape(row_count, span_len, model_width)
    d_shift_two = jnp.sum(d_mod_two, axis=1)
    d_scale_two = jnp.sum(d_mod_two * normed_two, axis=1)
    d_resid_one = grad_out + normalize_back(normed_two, inv_two, d_mod_two * (1.0 + scale_two))
    d_gate_one = jnp.sum(d_resid_one * branch * frame_valid[..., None], axis=1)
    d_branch = (
        (d_resid_one * gate_one * frame_valid[..., None])
        .astype(jnp.bfloat16)
        .reshape(frame_count, model_width)
    )
    w_out_grad = outer_grad(mixed_rows, d_branch)
    b_out_grad = jnp.sum(d_branch.astype(jnp.float32), axis=0)
    d_mixed = (
        back_grad(d_branch, w_out).astype(jnp.bfloat16).reshape(row_count, span_len, model_width)
    )
    d_mixed_heads = d_mixed.reshape(row_count, span_len, HEADS, head_dim)
    delta = jnp.einsum("rqhd,rhqd->rhq", d_mixed_heads.astype(jnp.float32), attn_full)

    def pair_grads(
        query_block,
        dout_block,
        lse_block,
        delta_block,
        query_labels,
        key_block,
        value_block,
        key_start,
    ):
        key_len = key_block.shape[1]
        key_split = key_block.reshape(row_count, key_len, HEADS, head_dim)
        value_split = value_block.reshape(row_count, key_len, HEADS, head_dim)
        scores = (
            jnp.einsum(
                "rqhd,rkhd->rhqk", query_block, key_split, preferred_element_type=jnp.float32
            )
            * score_scale
        )
        matches = query_labels[:, None, :, None] == key_labels(key_start, key_len)[:, None, None, :]
        probs = jnp.where(matches, jnp.exp(scores - lse_block[..., None]), 0.0)
        d_probs = jnp.einsum(
            "rqhd,rkhd->rhqk", dout_block, value_split, preferred_element_type=jnp.float32
        )
        d_scores = (probs * (d_probs - delta_block[..., None])).astype(jnp.bfloat16)
        return (d_scores, probs.astype(jnp.bfloat16), key_split)

    full_keys, full_values = (
        lax.all_gather(key_rows, "seq", axis=1, tiled=True),
        lax.all_gather(value_rows, "seq", axis=1, tiled=True),
    )
    zero_heads = jnp.zeros((row_count, span_len, HEADS, head_dim), jnp.float32)

    def both_pass(dq_total, shard_index):
        key_block = lax.dynamic_slice_in_dim(full_keys, shard_index * span_len, span_len, 1)
        value_block = lax.dynamic_slice_in_dim(full_values, shard_index * span_len, span_len, 1)
        d_scores, probs, key_split = pair_grads(
            query_heads,
            d_mixed_heads,
            log_total,
            delta,
            labels,
            key_block,
            value_block,
            shard_index * span_len,
        )
        dq_total = dq_total + jnp.einsum(
            "rhqk,rkhd->rqhd", d_scores, key_split, preferred_element_type=jnp.float32
        )
        dk_term = (
            jnp.einsum("rhqk,rqhd->rkhd", d_scores, query_heads, preferred_element_type=jnp.float32)
            * score_scale
        )
        dv_term = jnp.einsum(
            "rhqk,rqhd->rkhd", probs, d_mixed_heads, preferred_element_type=jnp.float32
        )
        term = jnp.concatenate(
            [
                dk_term.reshape(row_count, span_len, model_width),
                dv_term.reshape(row_count, span_len, model_width),
            ],
            axis=2,
        )
        return (dq_total, term)

    dq_total, key_terms = lax.scan(both_pass, zero_heads, jnp.arange(seq_count))
    summed = lax.psum_scatter(
        key_terms.astype(jnp.bfloat16), "seq", scatter_dimension=0, tiled=True
    ).astype(jnp.float32)[0]
    dk_rot = summed[..., :model_width]
    dv_rows = summed[..., model_width:]
    dq_rot = (dq_total * score_scale).reshape(row_count, span_len, model_width)
    d_proj = (
        jnp.concatenate(
            [
                rotate(dq_rot, cos_table, -sin_table, HEADS),
                rotate(dk_rot, cos_table, -sin_table, HEADS),
                dv_rows,
            ],
            axis=2,
        )
        .astype(jnp.bfloat16)
        .reshape(frame_count, 3 * model_width)
    )
    w_qkv_grad = outer_grad(mod_one, d_proj)
    b_qkv_grad = jnp.sum(d_proj.astype(jnp.float32), axis=0)
    d_mod_one = back_grad(d_proj, w_qkv).reshape(row_count, span_len, model_width)
    d_shift_one = jnp.sum(d_mod_one, axis=1)
    d_scale_one = jnp.sum(d_mod_one * normed_one, axis=1)
    d_resid_zero = (
        (d_resid_one + normalize_back(normed_one, inv_one, d_mod_one * (1.0 + scale_one)))
        .astype(jnp.bfloat16)
        .reshape(frame_count, model_width)
    )
    w_in_grad = outer_grad(inputs, d_resid_zero)
    b_in_grad = jnp.sum(d_resid_zero.astype(jnp.float32), axis=0)
    d_inputs = back_grad(d_resid_zero, w_in).reshape(row_count, span_len, -1)
    noisy_grad = d_inputs[..., :mel_width]
    cond_grad = d_inputs[..., mel_width : 2 * mel_width] * keep_audio[..., None]
    text_grad = d_inputs[..., 2 * mel_width :] * keep_text[..., None]
    emb_partial = jnp.concatenate(
        [d_shift_one, d_scale_one, d_gate_one, d_shift_two, d_scale_two, d_gate_two], axis=1
    )
    d_embedding = lax.psum(emb_partial.astype(jnp.bfloat16), "seq")
    silu_out, silu_pull = jax.vjp(jax.nn.silu, time_float)
    time_grad = silu_pull(back_grad(d_embedding, ada_w))[0]
    width_share = model_width // seq_count
    emb_share = 6 * model_width // seq_count
    ada_w_grad = outer_grad(
        lax.dynamic_slice_in_dim(time_act, seq_index * width_share, width_share, 1), d_embedding
    )
    ada_b_grad = lax.dynamic_slice_in_dim(
        jnp.sum(d_embedding.astype(jnp.float32), axis=0), seq_index * emb_share, emb_share, 0
    )
    seq_parts = (
        lax.psum_scatter(
            w_in_grad.astype(jnp.bfloat16), "seq", scatter_dimension=1, tiled=True
        ).astype(jnp.float32),
        lax.psum_scatter(
            b_in_grad.astype(jnp.bfloat16), "seq", scatter_dimension=0, tiled=True
        ).astype(jnp.float32),
        lax.psum_scatter(
            w_qkv_grad.astype(jnp.bfloat16), "seq", scatter_dimension=0, tiled=True
        ).astype(jnp.float32),
        lax.psum_scatter(
            b_qkv_grad.astype(jnp.bfloat16), "seq", scatter_dimension=0, tiled=True
        ).astype(jnp.float32),
        lax.psum_scatter(
            w_out_grad.astype(jnp.bfloat16), "seq", scatter_dimension=0, tiled=True
        ).astype(jnp.float32),
        lax.psum_scatter(
            b_out_grad.astype(jnp.bfloat16), "seq", scatter_dimension=0, tiled=True
        ).astype(jnp.float32),
        lax.psum_scatter(
            w_up_grad.astype(jnp.bfloat16), "seq", scatter_dimension=0, tiled=True
        ).astype(jnp.float32),
        lax.psum_scatter(
            b_up_grad.astype(jnp.bfloat16), "seq", scatter_dimension=0, tiled=True
        ).astype(jnp.float32),
        lax.psum_scatter(
            w_down_grad.astype(jnp.bfloat16), "seq", scatter_dimension=0, tiled=True
        ).astype(jnp.float32),
        lax.psum_scatter(
            b_down_grad.astype(jnp.bfloat16), "seq", scatter_dimension=0, tiled=True
        ).astype(jnp.float32),
    )
    totals = (
        lax.psum(seq_parts[0].astype(jnp.bfloat16), "rows").astype(jnp.float32),
        lax.psum(seq_parts[1].astype(jnp.bfloat16), "rows").astype(jnp.float32),
        lax.psum(seq_parts[2].astype(jnp.bfloat16), "rows").astype(jnp.float32),
        lax.psum(seq_parts[3].astype(jnp.bfloat16), "rows").astype(jnp.float32),
        lax.psum(seq_parts[4].astype(jnp.bfloat16), "rows").astype(jnp.float32),
        lax.psum(seq_parts[5].astype(jnp.bfloat16), "rows").astype(jnp.float32),
        lax.psum(seq_parts[6].astype(jnp.bfloat16), "rows").astype(jnp.float32),
        lax.psum(seq_parts[7].astype(jnp.bfloat16), "rows").astype(jnp.float32),
        lax.psum(seq_parts[8].astype(jnp.bfloat16), "rows").astype(jnp.float32),
        lax.psum(seq_parts[9].astype(jnp.bfloat16), "rows").astype(jnp.float32),
        lax.psum(ada_w_grad.astype(jnp.bfloat16), "rows").astype(jnp.float32),
        lax.psum(ada_b_grad.astype(jnp.bfloat16), "rows").astype(jnp.float32),
    )
    grad_list = (
        totals[0],
        totals[1],
        totals[10],
        totals[11],
        totals[2],
        totals[3],
        totals[4],
        totals[5],
        totals[6],
        totals[7],
        totals[8],
        totals[9],
    )
    return (
        result,
        noisy_grad,
        cond_grad,
        text_grad,
        time_grad,
        grad_list[0],
        grad_list[1],
        grad_list[2],
        grad_list[3],
        grad_list[4],
        grad_list[5],
        grad_list[6],
        grad_list[7],
        grad_list[8],
        grad_list[9],
        grad_list[10],
        grad_list[11],
    )


def solution(mesh):
    in_specs = (
        P("rows", "seq", None),
        P("rows", "seq", None),
        P("rows", "seq", None),
        P("rows", None),
        P("rows", None),
        P("rows", None),
        P("rows", None),
        P(),
        P(),
        P(),
        P(),
        P(),
        P(),
        P(),
        P(),
        P(),
        P(),
        P(),
        P(),
        P("rows", "seq", None),
    )
    out_specs = (
        P("rows", "seq", None),
        P("rows", "seq", None),
        P("rows", "seq", None),
        P("rows", "seq", None),
        P("rows", None),
        P(None, "seq"),
        P("seq"),
        P("seq", None),
        P("seq"),
        P("seq", None),
        P("seq"),
        P("seq", None),
        P("seq"),
        P("seq", None),
        P("seq"),
        P("seq", None),
        P("seq"),
    )
    return jax.shard_map(shards, mesh=mesh, in_specs=in_specs, out_specs=out_specs, check_vma=False)
```

profile of v0, /device:TPU:0, one launch (start us, length us, event | category | flops | bytes accessed | tf_op | source)
XLA Modules:
  0.0 1542.6 jit_solution(4551961169523036025)
XLA Ops:
  100.8 41.6 %all-gather.3.cloned.1.call-done = bf16[1,3328,1024]{2,1,0:T(8,128)(2,1)} async-done(((bf16[1,832,1024]{2,1,0:T(8,128)(2,1)}), bf16[1,3328,1024]{2,1,0:T(8,128)(2,1)}) %all-gather.3.cloned.1.call-update) | async-done | bytes 6815760 | tf_op jit(solution)/shard_map/all_gather | solution.py:163
  152.3 291.2 %while.35 = (s32[]{:T(128)}, f32[1,16,832]{2,1,0:T(8,128)S(1)}, f32[1,16,832]{2,1,0:T(8,128)S(1)}, f32[1,16,832,64]{2,3,1,0:T(8,128)}, s32[1,832]{1,0:T(1,128)S(...) while((s32[]{:T(128)}, f32[1,16,832]{2,1,0:T(8,128)S(1)}, ...), condition=%wide.region_9.10_spmd.clone, body=%wide.region_5.9_spmd.clone.sunk | while | flops 2982693376 | bytes 189373568 | solution.py:199
  159.1 20.4 %fusion.155 = (f32[16,832]{1,0:T(8,128)S(1)}, f32[16,832,832]{2,1,0:T(8,128)}) fusion(pred[832,832]{0,1:T(8,128)(4,1)S(1)} %broadcast_compare_fusion.4, bf16[832,16,64]{0,2,1:T(8,128)(2,1)} %bitcast.298, bf16[1,832,16,64]{1,3,2,0:T(8,128)(2,1)} %get-tuple-element.986), kind=kOutput, calls=%fused_computation.2.clone.1 | convolution fusion | flops 1450888192 | bytes 48455680 | tf_op jit(solution)/shard_map/while/body/eval_jaxpr/rqhd,rkhd->rhqk/dot_general | solution.py:176
  179.6 22.1 %fusion.157 = f32[16,832]{1,0:T(8,128)S(1)} fusion(f32[16,832,832]{2,1,0:T(8,128)} %get-tuple-element.932, f32[16,832]{1,0:T(8,128)S(1)} %bitcast.303, pred[832,832]{0,1:T(8,128)(4,1)S(1)} %broadcast_compare_fusion.4), kind=kLoop, calls=%fused_computation.4.clone.1 | loop fusion | flops 55364608 | bytes 45101056 | tf_op jit(solution)/shard_map/while/body/eval_jaxpr/reduce_sum | solution.py:189
  201.7 19.6 %bitcast_add_fusion.8 = f32[1,16,832,64]{2,3,1,0:T(8,128)S(1)} fusion(f32[1,16,832,64]{2,3,1,0:T(8,128)S(1)} %copy-done.7, bf16[832,16,64]{0,2,1:T(8,128)(2,1)S(1)} %bitcast.299, f32[16,832,832]{2,1,0:T(8,128)} %get-tuple-element.932, f32[16,832]{1,0:T(8,128)S(1)} %bitcast.304, pred[832,832]{0,1:T(8,128)(4,1)S(1)} %broadcast_compare_fusion.4, ...), kind=kOutput, calls=%fused_computation.7.clone.1 | convolution fusion | flops 1475608576 | bytes 53620736 | tf_op jit(solution)/shard_map/while/body/eval_jaxpr/rhqk,rkhd->rhqd/dot_general | solution.py:190
  229.9 20.4 %fusion.155 = (f32[16,832]{1,0:T(8,128)S(1)}, f32[16,832,832]{2,1,0:T(8,128)}) fusion(pred[832,832]{0,1:T(8,128)(4,1)S(1)} %broadcast_compare_fusion.4, bf16[832,16,64]{0,2,1:T(8,128)(2,1)} %bitcast.298, bf16[1,832,16,64]{1,3,2,0:T(8,128)(2,1)} %get-tuple-element.986), kind=kOutput, calls=%fused_computation.2.clone.1 | convolution fusion | flops 1450888192 | bytes 48455680 | tf_op jit(solution)/shard_map/while/body/eval_jaxpr/rqhd,rkhd->rhqk/dot_general | solution.py:176
  250.4 22.1 %fusion.157 = f32[16,832]{1,0:T(8,128)S(1)} fusion(f32[16,832,832]{2,1,0:T(8,128)} %get-tuple-element.932, f32[16,832]{1,0:T(8,128)S(1)} %bitcast.303, pred[832,832]{0,1:T(8,128)(4,1)S(1)} %broadcast_compare_fusion.4), kind=kLoop, calls=%fused_computation.4.clone.1 | loop fusion | flops 55364608 | bytes 45101056 | tf_op jit(solution)/shard_map/while/body/eval_jaxpr/reduce_sum | solution.py:189
  272.5 19.6 %bitcast_add_fusion.8 = f32[1,16,832,64]{2,3,1,0:T(8,128)S(1)} fusion(f32[1,16,832,64]{2,3,1,0:T(8,128)S(1)} %copy-done.7, bf16[832,16,64]{0,2,1:T(8,128)(2,1)S(1)} %bitcast.299, f32[16,832,832]{2,1,0:T(8,128)} %get-tuple-element.932, f32[16,832]{1,0:T(8,128)S(1)} %bitcast.304, pred[832,832]{0,1:T(8,128)(4,1)S(1)} %broadcast_compare_fusion.4, ...), kind=kOutput, calls=%fused_computation.7.clone.1 | convolution fusion | flops 1475608576 | bytes 53620736 | tf_op jit(solution)/shard_map/while/body/eval_jaxpr/rhqk,rkhd->rhqd/dot_general | solution.py:190
  300.7 20.4 %fusion.155 = (f32[16,832]{1,0:T(8,128)S(1)}, f32[16,832,832]{2,1,0:T(8,128)}) fusion(pred[832,832]{0,1:T(8,128)(4,1)S(1)} %broadcast_compare_fusion.4, bf16[832,16,64]{0,2,1:T(8,128)(2,1)} %bitcast.298, bf16[1,832,16,64]{1,3,2,0:T(8,128)(2,1)} %get-tuple-element.986), kind=kOutput, calls=%fused_computation.2.clone.1 | convolution fusion | flops 1450888192 | bytes 48455680 | tf_op jit(solution)/shard_map/while/body/eval_jaxpr/rqhd,rkhd->rhqk/dot_general | solution.py:176
  321.2 22.1 %fusion.157 = f32[16,832]{1,0:T(8,128)S(1)} fusion(f32[16,832,832]{2,1,0:T(8,128)} %get-tuple-element.932, f32[16,832]{1,0:T(8,128)S(1)} %bitcast.303, pred[832,832]{0,1:T(8,128)(4,1)S(1)} %broadcast_compare_fusion.4), kind=kLoop, calls=%fused_computation.4.clone.1 | loop fusion | flops 55364608 | bytes 45101056 | tf_op jit(solution)/shard_map/while/body/eval_jaxpr/reduce_sum | solution.py:189
  343.3 19.6 %bitcast_add_fusion.8 = f32[1,16,832,64]{2,3,1,0:T(8,128)S(1)} fusion(f32[1,16,832,64]{2,3,1,0:T(8,128)S(1)} %copy-done.7, bf16[832,16,64]{0,2,1:T(8,128)(2,1)S(1)} %bitcast.299, f32[16,832,832]{2,1,0:T(8,128)} %get-tuple-element.932, f32[16,832]{1,0:T(8,128)S(1)} %bitcast.304, pred[832,832]{0,1:T(8,128)(4,1)S(1)} %broadcast_compare_fusion.4, ...), kind=kOutput, calls=%fused_computation.7.clone.1 | convolution fusion | flops 1475608576 | bytes 53620736 | tf_op jit(solution)/shard_map/while/body/eval_jaxpr/rhqk,rkhd->rhqd/dot_general | solution.py:190
  371.3 20.4 %fusion.155 = (f32[16,832]{1,0:T(8,128)S(1)}, f32[16,832,832]{2,1,0:T(8,128)}) fusion(pred[832,832]{0,1:T(8,128)(4,1)S(1)} %broadcast_compare_fusion.4, bf16[832,16,64]{0,2,1:T(8,128)(2,1)} %bitcast.298, bf16[1,832,16,64]{1,3,2,0:T(8,128)(2,1)} %get-tuple-element.986), kind=kOutput, calls=%fused_computation.2.clone.1 | convolution fusion | flops 1450888192 | bytes 48455680 | tf_op jit(solution)/shard_map/while/body/eval_jaxpr/rqhd,rkhd->rhqk/dot_general | solution.py:176
  391.8 22.1 %fusion.157 = f32[16,832]{1,0:T(8,128)S(1)} fusion(f32[16,832,832]{2,1,0:T(8,128)} %get-tuple-element.932, f32[16,832]{1,0:T(8,128)S(1)} %bitcast.303, pred[832,832]{0,1:T(8,128)(4,1)S(1)} %broadcast_compare_fusion.4), kind=kLoop, calls=%fused_computation.4.clone.1 | loop fusion | flops 55364608 | bytes 45101056 | tf_op jit(solution)/shard_map/while/body/eval_jaxpr/reduce_sum | solution.py:189
  413.9 19.6 %bitcast_add_fusion.8 = f32[1,16,832,64]{2,3,1,0:T(8,128)S(1)} fusion(f32[1,16,832,64]{2,3,1,0:T(8,128)S(1)} %copy-done.7, bf16[832,16,64]{0,2,1:T(8,128)(2,1)S(1)} %bitcast.299, f32[16,832,832]{2,1,0:T(8,128)} %get-tuple-element.932, f32[16,832]{1,0:T(8,128)S(1)} %bitcast.304, pred[832,832]{0,1:T(8,128)(4,1)S(1)} %broadcast_compare_fusion.4, ...), kind=kOutput, calls=%fused_computation.7.clone.1 | convolution fusion | flops 1475608576 | bytes 53620736 | tf_op jit(solution)/shard_map/while/body/eval_jaxpr/rhqk,rkhd->rhqd/dot_general | solution.py:190
  492.5 432.6 %while.36 = (s32[]{:T(128)}, f32[1,832,16,64]{1,3,2,0:T(8,128)}, bf16[4,1,832,2048]{2,3,1,0:T(8,128)(2,1)}, s32[4]{0:T(128)S(1)}, bf16[1,3328,1024]{1,2,0:T(8,12...) while((s32[]{:T(128)}, f32[1,832,16,64]{1,3,2,0:T(8,128)}, ...), condition=%wide.region_16.17_spmd.clone, body=%wide.region_14.16_spmd.clone.sunk | while | flops 7210078720 | bytes 244612176 | solution.py:318
  519.6 22.1 %fusion.170 = bf16[16,832,64]{1,2,0:T(8,128)(2,1)} fusion(f32[16,832,832]{2,1,0:T(8,128)} %fusion.168, f32[16,832]{1,0:T(8,128)S(1)} %bitcast.333, pred[832,832]{0,1:T(8,128)(4,1)S(1)} %broadcast_compare_fusion.5, bf16[1,832,16,64]{1,3,2,0:T(8,128)(2,1)} %get-tuple-element.1037), kind=kOutput, calls=%fused_computation.28.clone.1 | convolution fusion | flops 1461977088 | bytes 48455680 | tf_op jit(solution)/shard_map/while/body/eval_jaxpr/rhqk,rqhd->rkhd/dot_general | solution.py:306
  541.7 28.0 %fusion.169 = bf16[16,832,832]{1,2,0:T(8,128)(2,1)} fusion(f32[16,832,832]{2,1,0:T(8,128)} %fusion.168, f32[16,832]{1,0:T(8,128)S(1)} %bitcast.332, f32[16,832]{1,0:T(8,128)S(1)} %bitcast.334, pred[832,832]{0,1:T(8,128)(4,1)S(1)} %broadcast_compare_fusion.5, bf16[832,16,64]{0,2,1:T(8,128)(2,1)} %bitcast.301, ...), kind=kOutput, calls=%fused_computation.25.clone.1 | convolution fusion | flops 1484128256 | bytes 70660096 | tf_op jit(solution)/shard_map/while/body/eval_jaxpr/rqhd,rkhd->rhqk/dot_general | solution.py:274
  607.3 19.5 %fusion.168 = f32[16,832,832]{2,1,0:T(8,128)} fusion(bf16[832,16,64]{0,2,1:T(8,128)(2,1)S(1)} %bitcast.295, bf16[1,832,16,64]{1,3,2,0:T(8,128)(2,1)} %get-tuple-element.1034), kind=kOutput, calls=%fused_computation.37.clone.1 | convolution fusion | flops 1417674752 | bytes 47710208 | tf_op jit(solution)/shard_map/while/body/eval_jaxpr/rqhd,rkhd->rhqk/dot_general | solution.py:267
  626.8 22.1 %fusion.170 = bf16[16,832,64]{1,2,0:T(8,128)(2,1)} fusion(f32[16,832,832]{2,1,0:T(8,128)} %fusion.168, f32[16,832]{1,0:T(8,128)S(1)} %bitcast.333, pred[832,832]{0,1:T(8,128)(4,1)S(1)} %broadcast_compare_fusion.5, bf16[1,832,16,64]{1,3,2,0:T(8,128)(2,1)} %get-tuple-element.1037), kind=kOutput, calls=%fused_computation.28.clone.1 | convolution fusion | flops 1461977088 | bytes 48455680 | tf_op jit(solution)/shard_map/while/body/eval_jaxpr/rhqk,rqhd->rkhd/dot_general | solution.py:306
  648.9 28.0 %fusion.169 = bf16[16,832,832]{1,2,0:T(8,128)(2,1)} fusion(f32[16,832,832]{2,1,0:T(8,128)} %fusion.168, f32[16,832]{1,0:T(8,128)S(1)} %bitcast.332, f32[16,832]{1,0:T(8,128)S(1)} %bitcast.334, pred[832,832]{0,1:T(8,128)(4,1)S(1)} %broadcast_compare_fusion.5, bf16[832,16,64]{0,2,1:T(8,128)(2,1)} %bitcast.301, ...), kind=kOutput, calls=%fused_computation.25.clone.1 | convolution fusion | flops 1484128256 | bytes 70660096 | tf_op jit(solution)/shard_map/while/body/eval_jaxpr/rqhd,rkhd->rhqk/dot_general | solution.py:274
  715.5 19.5 %fusion.168 = f32[16,832,832]{2,1,0:T(8,128)} fusion(bf16[832,16,64]{0,2,1:T(8,128)(2,1)S(1)} %bitcast.295, bf16[1,832,16,64]{1,3,2,0:T(8,128)(2,1)} %get-tuple-element.1034), kind=kOutput, calls=%fused_computation.37.clone.1 | convolution fusion | flops 1417674752 | bytes 47710208 | tf_op jit(solution)/shard_map/while/body/eval_jaxpr/rqhd,rkhd->rhqk/dot_general | solution.py:267
  735.1 22.1 %fusion.170 = bf16[16,832,64]{1,2,0:T(8,128)(2,1)} fusion(f32[16,832,832]{2,1,0:T(8,128)} %fusion.168, f32[16,832]{1,0:T(8,128)S(1)} %bitcast.333, pred[832,832]{0,1:T(8,128)(4,1)S(1)} %broadcast_compare_fusion.5, bf16[1,832,16,64]{1,3,2,0:T(8,128)(2,1)} %get-tuple-element.1037), kind=kOutput, calls=%fused_computation.28.clone.1 | convolution fusion | flops 1461977088 | bytes 48455680 | tf_op jit(solution)/shard_map/while/body/eval_jaxpr/rhqk,rqhd->rkhd/dot_general | solution.py:306
  757.1 28.0 %fusion.169 = bf16[16,832,832]{1,2,0:T(8,128)(2,1)} fusion(f32[16,832,832]{2,1,0:T(8,128)} %fusion.168, f32[16,832]{1,0:T(8,128)S(1)} %bitcast.332, f32[16,832]{1,0:T(8,128)S(1)} %bitcast.334, pred[832,832]{0,1:T(8,128)(4,1)S(1)} %broadcast_compare_fusion.5, bf16[832,16,64]{0,2,1:T(8,128)(2,1)} %bitcast.301, ...), kind=kOutput, calls=%fused_computation.25.clone.1 | convolution fusion | flops 1484128256 | bytes 70660096 | tf_op jit(solution)/shard_map/while/body/eval_jaxpr/rqhd,rkhd->rhqk/dot_general | solution.py:274
  823.7 19.5 %fusion.168 = f32[16,832,832]{2,1,0:T(8,128)} fusion(bf16[832,16,64]{0,2,1:T(8,128)(2,1)S(1)} %bitcast.295, bf16[1,832,16,64]{1,3,2,0:T(8,128)(2,1)} %get-tuple-element.1034), kind=kOutput, calls=%fused_computation.37.clone.1 | convolution fusion | flops 1417674752 | bytes 47710208 | tf_op jit(solution)/shard_map/while/body/eval_jaxpr/rqhd,rkhd->rhqk/dot_general | solution.py:267
  843.3 22.1 %fusion.170 = bf16[16,832,64]{1,2,0:T(8,128)(2,1)} fusion(f32[16,832,832]{2,1,0:T(8,128)} %fusion.168, f32[16,832]{1,0:T(8,128)S(1)} %bitcast.333, pred[832,832]{0,1:T(8,128)(4,1)S(1)} %broadcast_compare_fusion.5, bf16[1,832,16,64]{1,3,2,0:T(8,128)(2,1)} %get-tuple-element.1037), kind=kOutput, calls=%fused_computation.28.clone.1 | convolution fusion | flops 1461977088 | bytes 48455680 | tf_op jit(solution)/shard_map/while/body/eval_jaxpr/rhqk,rqhd->rkhd/dot_general | solution.py:306
  865.3 28.0 %fusion.169 = bf16[16,832,832]{1,2,0:T(8,128)(2,1)} fusion(f32[16,832,832]{2,1,0:T(8,128)} %fusion.168, f32[16,832]{1,0:T(8,128)S(1)} %bitcast.332, f32[16,832]{1,0:T(8,128)S(1)} %bitcast.334, pred[832,832]{0,1:T(8,128)(4,1)S(1)} %broadcast_compare_fusion.5, bf16[832,16,64]{0,2,1:T(8,128)(2,1)} %bitcast.301, ...), kind=kOutput, calls=%fused_computation.25.clone.1 | convolution fusion | flops 1484128256 | bytes 70660096 | tf_op jit(solution)/shard_map/while/body/eval_jaxpr/rqhd,rkhd->rhqk/dot_general | solution.py:274
  961.1 77.1 %reduce-scatter.7.cloned.1.call-done = bf16[1,1,832,2048]{2,3,1,0:T(8,128)(2,1)} async-done(((bf16[4,1,832,2048]{2,3,1,0:T(8,128)(2,1)}), bf16[1,1,832,2048]{2,3,1,0:T(8,128)(2,1)}) %reduce-scatter.7.cloned.1.call-update) | async-done | bytes 3407888 | tf_op jit(solution)/shard_map/reduce_scatter | solution.py:319
  1120.3 46.9 %reduce-scatter.15.cloned.1.call-done = bf16[256,2048]{1,0:T(8,128)(2,1)} async-done(((bf16[1024,2048]{1,0:T(8,128)(2,1)}), bf16[256,2048]{1,0:T(8,128)(2,1)}) %reduce-scatter.15.cloned.1.call-update) | async-done | bytes 1048592 | tf_op jit(solution)/shard_map/reduce_scatter | solution.py:386
  1167.2 30.2 %reduce-scatter.9.cloned.1.call-done = bf16[712,256]{1,0:T(8,128)(2,1)} async-done(((bf16[712,1024]{1,0:T(8,128)(2,1)}), bf16[712,256]{1,0:T(8,128)(2,1)}) %reduce-scatter.9.cloned.1.call-update) | async-done | bytes 364560 | tf_op jit(solution)/shard_map/reduce_scatter | solution.py:368
  1197.4 61.5 %reduce-scatter.11.cloned.1.call-done = bf16[256,3072]{1,0:T(8,128)(2,1)} async-done(((bf16[1024,3072]{1,0:T(8,128)(2,1)}), bf16[256,3072]{1,0:T(8,128)(2,1)}) %reduce-scatter.11.cloned.1.call-update) | async-done | bytes 1572880 | tf_op jit(solution)/shard_map/reduce_scatter | solution.py:374
  1262.5 22.5 %all-reduce.5 = (bf16[256]{0:T(256)(128)(2,1)S(1)}, bf16[1536]{0:T(1024)(128)(2,1)S(1)}, bf16[768]{0:T(1024)(128)(2,1)S(1)}, bf16[256]{0:T(256)(128)(2,1)S(1)}, ...) all-reduce(bf16[256]{0:T(256)(128)(2,1)S(1)} %dynamic-slice.2, ...), channel_id=1, replica_groups=mesh['rows'=8,'seq'=4] {'rows'}, use_global_device_ids=true, to_apply=%region_31.32 | all-reduce | flops 3584 | bytes 14336 | tf_op jit(solution)/shard_map/psum | solution.py:401
  1305.5 216.0 %all-reduce.10.cloned.1.call-done = (bf16[712,256]{1,0:T(8,128)(2,1)}, bf16[256,6144]{1,0:T(8,128)(2,1)}, bf16[256,3072]{1,0:T(8,128)(2,1)}, bf16[256,1024]{1,0:...) async-done(((bf16[712,256]{1,0:T(8,128)(2,1)}, bf16[256,6144]{1,0:T(8,128)(2,1)}, bf16[256,3072]{1,0:T(8,128)(2,1)}, bf16[256,1024]{1,0:T(8,128)(2,1)}, ...) | async-done | bytes 7704592 | tf_op jit(solution)/shard_map/psum | solution.py:400
  (415 shorter events, 510.1 us)
Async XLA Ops:
  7.2 439.0 %copy-start = (bf16[1024,1024]{1,0:T(8,128)(2,1)S(1)}, bf16[1024,1024]{1,0:T(8,128)(2,1)}, u32[]{:S(2)}) copy-start(bf16[1024,1024]{1,0:T(8,128)(2,1)} %param.37) | copy-start | bytes 6291460
  7.2 83.6 %all-gather.5.cloned.1.call-start = ((), (), s32[]{:S(2)}) async-start(), calls=%async_computation.7 | async-start | bytes 8519680 | tf_op jit(solution)/shard_map/all_gather | solution.py:164
  9.6 17.8 %copy-start.49 = (f32[1024]{0:T(1024)}, f32[1024]{0:T(1024)S(1)}, u32[]{:S(2)}) copy-start(f32[1024]{0:T(1024)S(1)} %convert_element_type.333) | copy-start | bytes 12292
  13.8 8.2 copy-start.29
  38.6 103.8 %all-gather.3.cloned.1.call-start = ((), (), s32[]{:S(2)}) async-start(), calls=%async_computation.6 | async-start | bytes 8519680 | tf_op jit(solution)/shard_map/all_gather | solution.py:163
  68.4 969.8 %reduce-scatter.7.cloned.1.call-start = ((), (), s32[]{:S(2)}) async-start(), calls=%async_computation.8 | async-start | bytes 18350080 | tf_op jit(solution)/shard_map/reduce_scatter | solution.py:319
  179.5 22.2 %copy-start.2 = (bf16[1,832,1024]{1,2,0:T(8,128)(2,1)S(1)}, bf16[1,832,1024]{1,2,0:T(8,128)(2,1)}, u32[]{:S(2)}) copy-start(bf16[1,832,1024]{1,2,0:T(8,128)(2,1)} %get-tuple-element.933) | copy-start | bytes 5111812 | tf_op jit(solution)/shard_map/while
  179.6 22.2 %copy-start.7 = (f32[1,16,832,64]{2,3,1,0:T(8,128)S(1)}, f32[1,16,832,64]{2,3,1,0:T(8,128)}, u32[]{:S(2)}) copy-start(f32[1,16,832,64]{2,3,1,0:T(8,128)} %get-tuple-element.967) | copy-start | bytes 10223620 | tf_op jit(solution)/shard_map/while
  250.3 22.2 %copy-start.2 = (bf16[1,832,1024]{1,2,0:T(8,128)(2,1)S(1)}, bf16[1,832,1024]{1,2,0:T(8,128)(2,1)}, u32[]{:S(2)}) copy-start(bf16[1,832,1024]{1,2,0:T(8,128)(2,1)} %get-tuple-element.933) | copy-start | bytes 5111812 | tf_op jit(solution)/shard_map/while
  250.3 22.2 %copy-start.7 = (f32[1,16,832,64]{2,3,1,0:T(8,128)S(1)}, f32[1,16,832,64]{2,3,1,0:T(8,128)}, u32[]{:S(2)}) copy-start(f32[1,16,832,64]{2,3,1,0:T(8,128)} %get-tuple-element.967) | copy-start | bytes 10223620 | tf_op jit(solution)/shard_map/while
  321.1 22.2 %copy-start.2 = (bf16[1,832,1024]{1,2,0:T(8,128)(2,1)S(1)}, bf16[1,832,1024]{1,2,0:T(8,128)(2,1)}, u32[]{:S(2)}) copy-start(bf16[1,832,1024]{1,2,0:T(8,128)(2,1)} %get-tuple-element.933) | copy-start | bytes 5111812 | tf_op jit(solution)/shard_map/while
  321.1 22.2 %copy-start.7 = (f32[1,16,832,64]{2,3,1,0:T(8,128)S(1)}, f32[1,16,832,64]{2,3,1,0:T(8,128)}, u32[]{:S(2)}) copy-start(f32[1,16,832,64]{2,3,1,0:T(8,128)} %get-tuple-element.967) | copy-start | bytes 10223620 | tf_op jit(solution)/shard_map/while
  391.8 22.2 %copy-start.2 = (bf16[1,832,1024]{1,2,0:T(8,128)(2,1)S(1)}, bf16[1,832,1024]{1,2,0:T(8,128)(2,1)}, u32[]{:S(2)}) copy-start(bf16[1,832,1024]{1,2,0:T(8,128)(2,1)} %get-tuple-element.933) | copy-start | bytes 5111812 | tf_op jit(solution)/shard_map/while
  391.8 22.2 %copy-start.7 = (f32[1,16,832,64]{2,3,1,0:T(8,128)S(1)}, f32[1,16,832,64]{2,3,1,0:T(8,128)}, u32[]{:S(2)}) copy-start(f32[1,16,832,64]{2,3,1,0:T(8,128)} %get-tuple-element.967) | copy-start | bytes 10223620 | tf_op jit(solution)/shard_map/while
  450.9 26.4 %copy-start.5 = (f32[832,1024]{1,0:T(8,128)}, f32[832,1024]{1,0:T(8,128)S(1)}, u32[]{:S(2)}) copy-start(f32[832,1024]{1,0:T(8,128)S(1)} %get-tuple-element.742) | copy-start | bytes 10223620
  450.9 26.4 %copy-start.38 = (f32[832]{0:T(1024)}, f32[832]{0:T(1024)S(1)}, u32[]{:S(2)}) copy-start(f32[832]{0:T(1024)S(1)} %broadcast_multiply_fusion.8) | copy-start | bytes 9988
  451.4 25.9 %copy-start.45 = (f32[832]{0:T(1024)}, f32[832]{0:T(1024)S(1)}, u32[]{:S(2)}) copy-start(f32[832]{0:T(1024)S(1)} %add_rsqrt_fusion) | copy-start | bytes 9988
  583.4 12.9 copy-start.3
  691.6 12.9 copy-start.3
  799.9 12.9 copy-start.3
  908.1 12.9 copy-start.3
  925.2 179.3 %reduce-scatter.13.cloned.1.call-start = ((), (), s32[]{:S(2)}) async-start(), calls=%async_computation.11 | async-start | bytes 2621440 | tf_op jit(solution)/shard_map/reduce_scatter | solution.py:380
  931.7 188.5 %reduce-scatter.17.cloned.1.call-start = ((), (), s32[]{:S(2)}) async-start(), calls=%async_computation.13 | async-start | bytes 5242880 | tf_op jit(solution)/shard_map/reduce_scatter | solution.py:392
  945.2 222.0 %reduce-scatter.15.cloned.1.call-start = ((), (), s32[]{:S(2)}) async-start(), calls=%async_computation.12 | async-start | bytes 5242880 | tf_op jit(solution)/shard_map/reduce_scatter | solution.py:386
  956.4 241.0 %reduce-scatter.9.cloned.1.call-start = ((), (), s32[]{:S(2)}) async-start(), calls=%async_computation.9 | async-start | bytes 1822720 | tf_op jit(solution)/shard_map/reduce_scatter | solution.py:368
  1044.1 15.1 copy-start.12
  1044.3 14.9 copy-start.14
  1047.3 11.9 copy-start.4
  1066.9 192.0 %reduce-scatter.11.cloned.1.call-start = ((), (), s32[]{:S(2)}) async-start(), calls=%async_computation.10 | async-start | bytes 7864320 | tf_op jit(solution)/shard_map/reduce_scatter | solution.py:374
  1080.0 441.6 %all-reduce.10.cloned.1.call-start = ((), (), s32[]{:S(2)}) async-start(), calls=%async_computation.14 | async-start | bytes 15409152 | tf_op jit(solution)/shard_map/psum | solution.py:400
  1258.9 29.6 %copy-start.24 = (bf16[1,832,1024]{2,1,0:T(8,128)(2,1)S(1)}, bf16[1,832,1024]{2,1,0:T(8,128)(2,1)}, u32[]{:S(2)}) copy-start(bf16[1,832,1024]{2,1,0:T(8,128)(2,1)} %copy-done.23) | copy-start | bytes 5111812
  1258.9 29.6 %copy-start.85 = (bf16[712,1024]{1,0:T(8,128)(2,1)S(1)}, bf16[712,1024]{1,0:T(8,128)(2,1)}, u32[]{:S(2)}) copy-start(bf16[712,1024]{1,0:T(8,128)(2,1)} %param.31) | copy-start | bytes 4374532
  (80 other events, 283.9 us)
Sparse Core Ops, SparseCore 0:
  38.7 52.0 all-gather.4
  93.0 49.3 all-gather.2
  925.3 112.9 reduce-scatter.6
  1041.2 31.4 reduce-scatter.12
  1075.2 45.0 reduce-scatter.16
  1122.6 44.5 reduce-scatter.14
  1170.0 27.4 reduce-scatter.8
  1200.5 58.3 reduce-scatter.10
  1265.5 255.9 all-reduce.9
where the time goes:
time: 1550 us; the launch traced here: 1540 us
  matrix products  663 us (43%)
  waiting for transfers between devices  506 us (33%)
  other arithmetic  182 us (12%)
  local copies, waits for them, and re-layouts  127 us (8%)
  blocking collectives  34.1 us (2%)
  between operations  17.3 us (1%)
    psum x1, waiting for transfers between devices, shards(): lax.psum(seq_parts[0].astype(jnp.bfloat16), 'rows').astype(jnp.float32)  216 us
    dot_general x4, matrix products, pair_grads(): jnp.einsum('rqhd,rkhd->rhqk', dout_block, value_split, preferred_element_...  112 us
    reduce_sum x4, other arithmetic, one_block(): row_total = row_total * rescale + jnp.sum(weights, axis=3)  88.5 us
    dot_general x4, matrix products, both_pass(): jnp.einsum('rhqk,rqhd->rkhd', probs, d_mixed_heads, preferred_element_typ...  88.2 us
    dot_general x4, matrix products, one_block(): jnp.einsum('rqhd,rkhd->rhqk', query_heads, key_block, preferred_element_t...  81.8 us
    dot_general x4, matrix products, one_block(): jnp.einsum('rhqk,rkhd->rhqd', weights.astype(jnp.bfloat16), value_block,...  78.3 us
    dot_general x4, matrix products, pair_grads(): jnp.einsum('rqhd,rkhd->rhqk', query_block, key_split, preferred_element_t...  78.2 us
    reduce_scatter x1, waiting for transfers between devices, shards(): lax.psum_scatter(key_terms.astype(jnp.bfloat16), 'seq', scatter_dimension...  77.1 us
  transfers between devices with their start and end apart: 9, of which 8 were waited for; matrix products, arithmetic and copies ran while one was open for 9% of the time, Pallas kernels for 0%

commit v1 on v0

v1 whole, which is shorter than its diff:
```python
import functools
import math

import jax
import jax.numpy as jnp
from jax import lax
from jax.experimental import pallas as pl
from jax.experimental.pallas import tpu as pltpu
from jax.sharding import Mesh, PartitionSpec as P

HEADS = 16
EPS = 1e-06
THETA = 10000.0
MASKED = -1e30
F32 = jnp.float32
BF = jnp.bfloat16
MIB = 2**20


def dot_nn(a, b):
    return jnp.dot(a, b, preferred_element_type=F32)


def dot_tn(a, b):
    return lax.dot_general(a, b, (((0,), (0,)), ((), ())), preferred_element_type=F32)


def dot_nt(a, b):
    return lax.dot_general(a, b, (((1,), (1,)), ((), ())), preferred_element_type=F32)


def shift(v, axis, step):
    size = lax.axis_size(axis)
    return lax.ppermute(v, axis, [(i, (i + step) % size) for i in range(size)])


def flip(v, axis, bit):
    size = lax.axis_size(axis)
    return lax.ppermute(v, axis, [(i, i ^ bit) for i in range(size)])


def bits(axis):
    size = lax.axis_size(axis)
    assert size & (size - 1) == 0
    return [1 << b for b in range(size.bit_length() - 1)]


def sum_small(v, axis):
    for bit in bits(axis):
        v = v + flip(v, axis, bit)
    return v


def gather_small(v, axis):
    for bit in bits(axis):
        v = jnp.concatenate([v, flip(v, axis, bit)], axis=0)
    return v


def pick(v, index):
    return lax.dynamic_index_in_dim(v, index, 0, keepdims=False)


def add_bf16(a, b):
    return (a.astype(F32) + b.astype(F32)).astype(BF)


def scatter_seq(g):
    core, sx = lax.axis_index("core"), lax.axis_index("sx")
    chips = lax.axis_size("sx")
    g = g.reshape((chips, 2) + g.shape[1:])
    recv = flip(lax.dynamic_index_in_dim(g, 1 - core, 1, keepdims=False), "core", 1)
    part = add_bf16(lax.dynamic_index_in_dim(g, core, 1, keepdims=False), recv)
    total = pick(part, sx)
    for t in range(1, chips):
        total = add_bf16(total, shift(pick(part, (sx + t) % chips), "sx", t))
    return total


def sum_rows(v):
    sent = []
    for axis in ("ry", "rz"):
        for bit in reversed(bits(axis)):
            half = v.shape[0] // 2
            upper = (lax.axis_index(axis) // bit) % 2
            two = v.reshape((2, half) + v.shape[1:])
            recv = flip(pick(two, 1 - upper), axis, bit)
            v = add_bf16(pick(two, upper), recv)
            sent.append((axis, bit, upper))
    for axis, bit, upper in reversed(sent):
        recv = flip(v, axis, bit)
        low = upper == 0
        v = jnp.concatenate([jnp.where(low, v, recv), jnp.where(low, recv, v)], axis=0)
    return v


def total_grad(g):
    seq = lax.axis_size("sx") * 2
    return sum_rows(scatter_seq(g.reshape((seq, g.shape[0] // seq) + g.shape[1:])))


def turn(x, cos, sin, lane):
    partner = jnp.where(lane % 64 < 32, pltpu.roll(x, 96, 1), pltpu.roll(x, 32, 1))
    return x * cos + partner * sin


def front_kernel(core, x_ref, win_ref, bin_ref, shift_ref, scale_ref, *rest, parts):
    weights = rest[: 2 * len(parts)]
    cos_ref, sin_ref = rest[2 * len(parts) : 2 * len(parts) + 2]
    mod_ref = rest[2 * len(parts) + 2]
    outs = rest[2 * len(parts) + 3 :]
    resid = dot_nn(x_ref[...], win_ref[...]) + bin_ref[...]
    center = resid - jnp.mean(resid, axis=1, keepdims=True)
    inv = lax.rsqrt(jnp.mean(center * center, axis=1, keepdims=True) + EPS)
    mod = (center * inv * (1.0 + scale_ref[...]) + shift_ref[...]).astype(BF)
    mod_ref[...] = mod
    lane = lax.broadcasted_iota(jnp.int32, (1, 128), 1)
    for n, part in enumerate(parts):
        y = dot_nn(mod, weights[2 * n][...]) + weights[2 * n + 1][...]
        if part == "v":
            outs[n][...] = y.astype(BF)
            continue
        scale = 0.125 if part == "q" else 1.0
        for t in range(0, y.shape[1], 128):
            z = turn(y[:, t : t + 128], cos_ref[...], sin_ref[...], lane)
            outs[n][:, t : t + 128] = (z * scale).astype(BF)


def front(core, x, w_in, b_in, shift_one, scale_one, w_qkv, b_qkv, cos, sin, parts):
    rows, n, width = x.shape
    model = w_in.shape[1]
    half = model // 2
    block = 416 if n % 416 == 0 else n
    place = {"q": 0, "k": 1, "v": 2}
    frame = lambda w: pl.BlockSpec((None, block, w), lambda r, i, c: (r, i, 0))
    row = lambda w: pl.BlockSpec((None, 1, w), lambda r, i, c: (r, 0, 0))
    whole = lambda a, b: pl.BlockSpec((a, b), lambda r, i, c: (0, 0))
    w_specs, w_args = [], []
    for part in parts:
        j = place[part]
        w_specs.append(pl.BlockSpec((model, half), lambda r, i, c, j=j: (0, 2 * j + c[0])))
        w_specs.append(pl.BlockSpec((1, half), lambda r, i, c, j=j: (0, 2 * j + c[0])))
        w_args += [w_qkv, b_qkv]
    return pl.pallas_call(
        functools.partial(front_kernel, parts=parts),
        grid_spec=pltpu.PrefetchScalarGridSpec(
            num_scalar_prefetch=1,
            grid=(rows, n // block),
            in_specs=[frame(width), whole(width, model), whole(1, model), row(model), row(model)]
            + w_specs
            + [frame(128), frame(128)],
            out_specs=[frame(model)] + [frame(half)] * len(parts),
        ),
        out_shape=[jax.ShapeDtypeStruct((rows, n, model), BF)]
        + [jax.ShapeDtypeStruct((rows, n, half), BF)] * len(parts),
        compiler_params=pltpu.CompilerParams(vmem_limit_bytes=48 * MIB),
        cost_estimate=pl.CostEstimate(
            flops=2 * rows * n * model * (width + half * len(parts)),
            bytes_accessed=rows * n * 2 * (width + model + half * len(parts)) + 8 * MIB,
            transcendentals=0,
        ),
        name="front",
    )(core, x, w_in, b_in, shift_one, scale_one, *w_args, cos, sin)


def attend_kernel(q_ref, qx_ref, k_ref, kx_ref, v_ref, o_ref, l_ref, s_ref, m_ref, acc_ref):
    frames = k_ref.shape[0]
    h, phase = pl.program_id(2), pl.program_id(3)
    lane = lax.broadcasted_iota(jnp.int32, (1, 128), 1)
    mine = (lane // 64) == h
    zero = jnp.zeros((), BF)
    step = 256 if frames % 256 == 0 else frames

    @pl.when(phase == 0)
    def _():
        q2 = jnp.concatenate([q_ref[...], qx_ref[...]], axis=1)
        top = None
        for c in range(0, frames, step):
            keys = jnp.where(mine, k_ref[c : c + step, :], zero)
            s = dot_nt(q2, jnp.concatenate([keys, kx_ref[c : c + step, :]], axis=1))
            s_ref[:, c : c + step] = s
            for t in range(0, step, 128):
                part = s[:, t : t + 128]
                top = part if top is None else jnp.maximum(top, part)
        m_ref[...] = jnp.broadcast_to(jnp.max(top, axis=1, keepdims=True), m_ref.shape)

    @pl.when(phase == 1)
    def _():
        top = m_ref[:, :1]
        ones = jnp.broadcast_to(jnp.where(mine, 1.0, 0.0).astype(BF), (step, 128))
        acc = None
        for c in range(0, frames, step):
            p = jnp.exp(s_ref[:, c : c + step] - top).astype(BF)
            values = jnp.where(mine, v_ref[c : c + step, :], zero)
            d = dot_nn(p, jnp.concatenate([values, ones], axis=1))
            acc = d if acc is None else acc + d

        @pl.when(h == 0)
        def _():
            acc_ref[...] = acc
            l_ref[...] = m_ref[...]

        @pl.when(h == 1)
        def _():
            both = acc + acc_ref[...]
            total = both[:, 128:]
            o_ref[...] = (both[:, :128] / total).astype(BF)
            l_ref[...] = jnp.where(mine, m_ref[...], l_ref[...]) + jnp.log(total)


def attend(q, qx, k, kx, v):
    rows, m, width = q.shape
    n = k.shape[1]
    pairs = width // 128
    qs = pl.BlockSpec((None, m, 128), lambda r, p, h, f: (r, 0, p))
    q0 = pl.BlockSpec((None, m, 128), lambda r, p, h, f: (r, 0, 0))
    ks = pl.BlockSpec((None, n, 128), lambda r, p, h, f: (r, 0, p))
    k0 = pl.BlockSpec((None, n, 128), lambda r, p, h, f: (r, 0, 0))
    return pl.pallas_call(
        attend_kernel,
        grid=(rows, pairs, 2, 2),
        in_specs=[qs, q0, ks, k0, ks],
        out_specs=[qs, qs],
        out_shape=[
            jax.ShapeDtypeStruct((rows, m, width), BF),
            jax.ShapeDtypeStruct((rows, m, width), F32),
        ],
        scratch_shapes=[
            pltpu.VMEM((m, n), F32),
            pltpu.VMEM((m, 128), F32),
            pltpu.VMEM((m, 256), F32),
        ],
        compiler_params=pltpu.CompilerParams(vmem_limit_bytes=56 * MIB),
        cost_estimate=pl.CostEstimate(
            flops=16 * rows * pairs * m * n * 256,
            bytes_accessed=rows * width * (m * 8 + n * 4),
            transcendentals=rows * pairs * 2 * m * n,
        ),
        name="attend",
    )(q, qx, k, kx, v)


def split3(x, lane, rest):
    hi = x.astype(BF).astype(F32)
    mid = (x - hi).astype(BF).astype(F32)
    low = x - hi - mid
    place = lane % 64
    return jnp.where(
        place == 8, hi, jnp.where(place == 9, mid, jnp.where(place == 10, low, rest))
    ).astype(BF)


def attend_back_kernel(
    q_ref, qx_ref, k_ref, kx_ref, v_ref, o_ref, do_ref, l_ref, cq_ref, sq_ref, ck_ref, sk_ref,
    dq_ref, dk_ref, dv_ref,
    q2, d2, k2, v2, kk, qt, dt, p_s, s_s, dq_s, dk_s, dv_s,
):
    m, n = q_ref.shape[0], k_ref.shape[0]
    h, phase = pl.program_id(2), pl.program_id(3)
    lane = lax.broadcasted_iota(jnp.int32, (1, 128), 1)
    mine = (lane // 64) == h
    zero = jnp.zeros((), BF)
    step = 256 if n % 256 == 0 else n
    half = pl.ds(pl.multiple_of(h * 64, 64), 64)

    @pl.when((phase == 0) & (h == 0))
    def _():
        q2[:, :128] = q_ref[...]
        q2[:, 128:] = split3(l_ref[...], lane, qx_ref[...].astype(F32))
        prod = do_ref[...].astype(F32) * o_ref[...].astype(F32)
        same = (
            lax.broadcasted_iota(jnp.int32, (128, 128), 0) // 64
            == lax.broadcasted_iota(jnp.int32, (128, 128), 1) // 64
        )
        same = jnp.where(same, 1.0, 0.0).astype(BF)
        hi = prod.astype(BF)
        low = (prod - hi.astype(F32)).astype(BF)
        delta = dot_nn(
            jnp.concatenate([hi, low], axis=1), jnp.concatenate([same, same], axis=0)
        )
        d2[:, :128] = do_ref[...]
        d2[:, 128:] = split3(delta, lane, jnp.zeros((m, 128), F32))
        qt[...] = q_ref[...].T
        dt[...] = do_ref[...].T

    @pl.when(phase == 0)
    def _():
        keys = jnp.where(mine, k_ref[...], zero)
        kk[...] = keys
        k2[:128, :] = keys.T
        less = (lane - 64 * h >= 8) & (lane - 64 * h < 11)
        k2[128:, :] = jnp.where(less, -1.0, kx_ref[...].astype(F32)).astype(BF).T
        v2[:128, :] = jnp.where(mine, v_ref[...], zero).T
        v2[128:, :] = jnp.broadcast_to(jnp.where(less, -1.0, 0.0), (n, 128)).astype(BF).T

    @pl.when(phase == 1)
    def _():
        for c in range(0, n, step):
            s = dot_nn(q2[...], k2[:, c : c + step])
            d = dot_nn(d2[...], v2[:, c : c + step])
            p = jnp.exp(s)
            p_s[:, c : c + step] = p.astype(BF)
            s_s[:, c : c + step] = (p * d).astype(BF)

    @pl.when(phase == 2)
    def _():
        acc = dot_nn(s_s[...], kk[...])

        @pl.when(h == 0)
        def _():
            dq_s[...] = acc

        @pl.when(h == 1)
        def _():
            total = (dq_s[...] + acc) * 0.125
            dq_ref[...] = turn(total, cq_ref[...], -sq_ref[...], lane).astype(BF)

    @pl.when(phase == 3)
    def _():
        for c in range(0, n, step):
            dk_s[half, c : c + step] = dot_nn(qt[half, :], s_s[:, c : c + step])
            dv_s[half, c : c + step] = dot_nn(dt[half, :], p_s[:, c : c + step])

        @pl.when(h == 1)
        def _():
            dk_ref[...] = turn(dk_s[...].T, ck_ref[...], -sk_ref[...], lane).astype(BF)
            dv_ref[...] = dv_s[...].astype(BF).T


def attend_back(q, qx, k, kx, v, o, do, l, cos_q, sin_q, cos_k, sin_k):
    rows, m, width = q.shape
    n = k.shape[1]
    pairs = width // 128
    qs = pl.BlockSpec((None, m, 128), lambda r, p, h, f: (r, 0, p))
    q0 = pl.BlockSpec((None, m, 128), lambda r, p, h, f: (r, 0, 0))
    ks = pl.BlockSpec((None, n, 128), lambda r, p, h, f: (r, 0, p))
    k0 = pl.BlockSpec((None, n, 128), lambda r, p, h, f: (r, 0, 0))
    return pl.pallas_call(
        attend_back_kernel,
        grid=(rows, pairs, 2, 4),
        in_specs=[qs, q0, ks, k0, ks, qs, qs, qs, q0, q0, k0, k0],
        out_specs=[qs, ks, ks],
        out_shape=[
            jax.ShapeDtypeStruct((rows, m, width), BF),
            jax.ShapeDtypeStruct((rows, n, width), BF),
            jax.ShapeDtypeStruct((rows, n, width), BF),
        ],
        scratch_shapes=[
            pltpu.VMEM((m, 256), BF),
            pltpu.VMEM((m, 256), BF),
            pltpu.VMEM((256, n), BF),
            pltpu.VMEM((256, n), BF),
            pltpu.VMEM((n, 128), BF),
            pltpu.VMEM((128, m), BF),
            pltpu.VMEM((128, m), BF),
            pltpu.VMEM((m, n), BF),
            pltpu.VMEM((m, n), BF),
            pltpu.VMEM((m, 128), F32),
            pltpu.VMEM((128, n), F32),
            pltpu.VMEM((128, n), F32),
        ],
        compiler_params=pltpu.CompilerParams(vmem_limit_bytes=60 * MIB),
        cost_estimate=pl.CostEstimate(
            flops=40 * rows * pairs * m * n * 256,
            bytes_accessed=rows * width * (m * 12 + n * 8),
            transcendentals=rows * pairs * 2 * m * n,
        ),
        name="attend_back",
    )(q, qx, k, kx, v, o, do, l, cos_q, sin_q, cos_k, sin_k)


def frame_table(seg_lengths, frames):
    ends = jnp.cumsum(seg_lengths, axis=1)
    starts = ends - seg_lengths
    at = frames[None, :, None]
    inside = (at >= starts[:, None, :]) & (at < ends[:, None, :])
    offsets = frames[None, :] - jnp.sum(jnp.where(inside, starts[:, None, :], 0), axis=2)
    return inside.astype(F32), offsets


def rotary_tables(offsets, head_dim):
    halves = head_dim // 2
    place = jnp.arange(128, dtype=jnp.int32)
    index = (place % halves).astype(F32)
    frequency = jnp.exp(-math.log(THETA) * 2.0 * index / head_dim)
    angles = offsets.astype(F32)[..., None] * frequency
    sign = jnp.where(place % head_dim < halves, -1.0, 1.0)
    return jnp.cos(angles), jnp.sin(angles) * sign


def normalize(stream):
    center = stream - jnp.mean(stream, axis=-1, keepdims=True)
    inv_std = lax.rsqrt(jnp.mean(center * center, axis=-1, keepdims=True) + EPS)
    return (center * inv_std, inv_std)


def normalize_back(normed, inv_std, upstream):
    return inv_std * (
        upstream
        - jnp.mean(upstream, axis=-1, keepdims=True)
        - normed * jnp.mean(upstream * normed, axis=-1, keepdims=True)
    )


def shards(
    noisy_mel, cond_mel, text_feat, time_embed, seg_lengths, audio_drop, text_drop, w_in, b_in,
    ada_w, ada_b, w_qkv, b_qkv, w_out, b_out, w_up, b_up, w_down, b_down, cotangent,
):
    rows, span, mel = noisy_mel.shape
    model = w_qkv.shape[0]
    half = model // 2
    head_dim = model // HEADS
    frames = rows * span
    core, sx = lax.axis_index("core"), lax.axis_index("sx")
    chips = lax.axis_size("sx")
    seq = chips * 2
    seq_index = sx * 2 + core
    core_arg = core.astype(jnp.int32).reshape(1)
    as_row = lambda v: v.astype(F32).reshape(1, -1)

    ramp = jnp.arange(span, dtype=jnp.int32)

    def chip_frames(chip):
        return jnp.concatenate([(chip * 2 + core) * span + ramp, (chip * 2 + 1 - core) * span + ramp])

    member, _ = frame_table(seg_lengths, seq_index * span + ramp)
    keep_audio = 1.0 - jnp.einsum("rcs,rs->rc", member, audio_drop.astype(F32))
    keep_text = 1.0 - jnp.einsum("rcs,rs->rc", member, text_drop.astype(F32))
    frame_valid = 1.0 - member[:, :, -1]
    inputs = jnp.concatenate(
        [
            noisy_mel,
            cond_mel * keep_audio[..., None].astype(BF),
            text_feat * keep_text[..., None].astype(BF),
        ],
        axis=2,
    )
    inputs_local = jnp.concatenate([inputs, flip(inputs, "core", 1)], axis=1)
    far = []
    for t in range(1, chips):
        block = shift(inputs, "sx", -t)
        far += [block, flip(block, "core", 1)]
    inputs_far = jnp.concatenate(far, axis=1)

    time_float = time_embed.astype(F32)
    time_act = jax.nn.silu(time_float).astype(BF)
    embedding = dot_nn(time_act, ada_w) + ada_b.astype(F32)
    shift_one, scale_one, gate_one, shift_two, scale_two, gate_two = [
        part[:, None, :] for part in jnp.split(embedding, 6, axis=1)
    ]

    def tables(frame_ids):
        inside, offsets = frame_table(seg_lengths, frame_ids)
        cos, sin = rotary_tables(offsets, head_dim)
        pad = jnp.zeros(inside.shape[:2] + (128 - inside.shape[2],), F32)
        return jnp.concatenate([inside, pad], axis=2), cos, sin

    inside_near, cos_near, sin_near = tables(chip_frames(sx))
    inside_far, cos_far, sin_far = tables(
        jnp.concatenate([chip_frames((sx + t) % chips) for t in range(1, chips)])
    )
    segs = seg_lengths.shape[1]
    lanes = jnp.arange(128)
    qx = jnp.where(lanes < segs, 1.0 - inside_near, 0.0).astype(BF)
    kx = (MASKED * jnp.concatenate([inside_far, inside_near], axis=1)).astype(BF)
    cos_all = jnp.concatenate([cos_far, cos_near], axis=1)
    sin_all = jnp.concatenate([sin_far, sin_near], axis=1)

    bq = as_row(b_qkv)
    mod_near, q, k_near, v_near = front(
        core_arg, inputs_local, w_in, as_row(b_in), shift_one, scale_one, w_qkv, bq,
        cos_near, sin_near, ("q", "k", "v"),
    )
    mod_far, k_far, v_far = front(
        core_arg, inputs_far, w_in, as_row(b_in), shift_one, scale_one, w_qkv, bq,
        cos_far, sin_far, ("k", "v"),
    )
    k = jnp.concatenate([k_far, k_near], axis=1)
    v = jnp.concatenate([v_far, v_near], axis=1)
    o, lse = attend(q, qx, k, kx, v)

    o_other = flip(o[:, span:], "core", 1)
    mixed = jnp.concatenate([o[:, :span], o_other], axis=2).reshape(frames, model)
    own = lax.dynamic_slice_in_dim
    w_out_two = w_out.reshape(2, half, model)
    w_out_turned = jnp.concatenate([pick(w_out_two, core), pick(w_out_two, 1 - core)], axis=0)
    resid_zero = (
        dot_nn(inputs.reshape(frames, -1), w_in) + b_in.astype(F32)
    ).reshape(rows, span, model)
    branch = (dot_nn(mixed, w_out_turned) + b_out.astype(F32)).reshape(rows, span, model)
    resid_one = resid_zero + gate_one * branch * frame_valid[..., None]
    normed_two, inv_two = normalize(resid_one)
    mod_two = (normed_two * (1.0 + scale_two) + shift_two).astype(BF).reshape(frames, model)
    hidden = dot_nn(mod_two, w_up) + b_up.astype(F32)
    activated = jax.nn.gelu(hidden, approximate=True).astype(BF)
    ff_out = (dot_nn(activated, w_down) + b_down.astype(F32)).reshape(rows, span, model)
    result = (resid_one + gate_two * ff_out).astype(BF)

    grad_out = cotangent.astype(F32)
    d_gate_two = jnp.sum(grad_out * ff_out, axis=1)
    d_ff = (grad_out * gate_two).astype(BF).reshape(frames, model)
    w_down_grad = total_grad(dot_tn(activated, d_ff).astype(BF))
    b_down_grad = jnp.sum(d_ff.astype(F32), axis=0)
    grad_act = dot_nt(d_ff, w_down)
    _, gelu_pull = jax.vjp(lambda pre: jax.nn.gelu(pre, approximate=True), hidden)
    d_hidden = gelu_pull(grad_act)[0].astype(BF)
    w_up_grad = total_grad(dot_tn(mod_two, d_hidden).astype(BF))
    b_up_grad = jnp.sum(d_hidden.astype(F32), axis=0)
    d_mod_two = dot_nt(d_hidden, w_up).reshape(rows, span, model)
    d_shift_two = jnp.sum(d_mod_two, axis=1)
    d_scale_two = jnp.sum(d_mod_two * normed_two, axis=1)
    d_resid_one = grad_out + normalize_back(normed_two, inv_two, d_mod_two * (1.0 + scale_two))
    d_gate_one = jnp.sum(d_resid_one * branch * frame_valid[..., None], axis=1)
    d_branch = (
        (d_resid_one * gate_one * frame_valid[..., None]).astype(BF).reshape(frames, model)
    )
    w_out_turned_grad = dot_tn(mixed, d_branch).astype(BF).reshape(2, half, model)
    w_out_grad = total_grad(
        jnp.concatenate([pick(w_out_turned_grad, core), pick(w_out_turned_grad, 1 - core)], axis=0)
    )
    b_out_grad = jnp.sum(d_branch.astype(F32), axis=0)
    d_mixed = dot_nt(d_branch, w_out_turned).astype(BF).reshape(rows, span, model)
    d_o = jnp.concatenate([d_mixed[..., :half], flip(d_mixed[..., half:], "core", 1)], axis=1)

    dq, dk, dv = attend_back(
        q, qx, k, kx, v, o, d_o, lse, cos_near, sin_near, cos_all, sin_all
    )

    chip_span = 2 * span
    far_span = k_far.shape[1]
    w_parts = w_qkv.reshape(model, 3, 2, half)
    w_mine = lax.dynamic_index_in_dim(w_parts, core, 2, keepdims=False)
    mod_all = jnp.concatenate([mod_far, mod_near], axis=1).reshape(-1, model)
    flat = lambda a: a.reshape(-1, a.shape[-1])
    w_q_grad = dot_tn(flat(mod_near), flat(dq)).astype(BF)
    w_k_grad = dot_tn(mod_all, flat(dk)).astype(BF)
    w_v_grad = dot_tn(mod_all, flat(dv)).astype(BF)
    near = jnp.concatenate([dq, dk[:, far_span:], dv[:, far_span:]], axis=2)
    d_mod_near = dot_nt(flat(near), w_mine.reshape(model, 3 * half)).astype(BF)
    far_grads = jnp.concatenate([dk[:, :far_span], dv[:, :far_span]], axis=2)
    d_mod_far = dot_nt(flat(far_grads), w_mine[:, 1:].reshape(model, 2 * half)).astype(BF)
    d_mod_near = d_mod_near.reshape(rows, 2, span, model)
    d_mod_far = d_mod_far.reshape(rows, chips - 1, 2, span, model)
    far_sum = add_bf16(d_mod_far[:, :, 0], flip(d_mod_far[:, :, 1], "core", 1))
    d_mod_one = d_mod_near[:, 0].astype(F32) + flip(d_mod_near[:, 1], "core", 1).astype(F32)
    for t in range(1, chips):
        d_mod_one = d_mod_one + shift(far_sum[:, t - 1], "sx", t).astype(F32)

    stacked = jnp.stack([w_q_grad, w_k_grad, w_v_grad], axis=0)
    stacked = stacked.reshape(3, chips, 2, model // seq, half)
    to_other = flip(lax.dynamic_index_in_dim(stacked, 1 - core, 2, keepdims=False), "core", 1)
    to_own = lax.dynamic_index_in_dim(stacked, core, 2, keepdims=False)
    low = core == 0
    both = jnp.stack([jnp.where(low, to_own, to_other), jnp.where(low, to_other, to_own)], axis=3)
    part = jnp.transpose(both, (1, 2, 0, 3, 4)).reshape(chips, model // seq, 3 * model)
    w_qkv_grad = pick(part, sx)
    for t in range(1, chips):
        w_qkv_grad = add_bf16(w_qkv_grad, shift(pick(part, (sx + t) % chips), "sx", t))
    w_qkv_grad = sum_rows(w_qkv_grad)
    b_mine = jnp.stack(
        [jnp.sum(flat(a).astype(F32), axis=0) for a in (dq, dk, dv)], axis=0
    )
    gap = jnp.zeros_like(b_mine)
    b_qkv_grad = jnp.stack([jnp.where(low, b_mine, gap), jnp.where(low, gap, b_mine)], axis=1)

    normed_one, inv_one = normalize(resid_zero)
    d_shift_one = jnp.sum(d_mod_one, axis=1)
    d_scale_one = jnp.sum(d_mod_one * normed_one, axis=1)
    d_resid_zero = (
        (d_resid_one + normalize_back(normed_one, inv_one, d_mod_one * (1.0 + scale_one)))
        .astype(BF)
        .reshape(frames, model)
    )
    w_in_grad = total_grad(dot_tn(d_resid_zero, inputs.reshape(frames, -1)).astype(BF)).T
    b_in_grad = jnp.sum(d_resid_zero.astype(F32), axis=0)
    d_inputs = dot_nt(d_resid_zero, w_in).reshape(rows, span, -1)
    noisy_grad = d_inputs[..., :mel]
    cond_grad = d_inputs[..., mel : 2 * mel] * keep_audio[..., None]
    text_grad = d_inputs[..., 2 * mel :] * keep_text[..., None]

    emb_partial = jnp.concatenate(
        [d_shift_one, d_scale_one, d_gate_one, d_shift_two, d_scale_two, d_gate_two], axis=1
    )
    bias_sizes = [model, 3 * model, model, w_up.shape[1], model]
    biases = jnp.concatenate(
        [b_in_grad, b_qkv_grad.reshape(-1), b_out_grad, b_up_grad, b_down_grad]
    )
    vector = jnp.concatenate([emb_partial.reshape(-1), biases])
    for axis in ("core", "sx"):
        vector = sum_small(vector, axis)
    emb_size = rows * 6 * model
    d_embedding = vector[:emb_size].reshape(rows, 6 * model).astype(BF)
    biases = vector[emb_size:]
    for axis in ("ry", "rz"):
        biases = sum_small(biases, axis)
    pieces, at = [], 0
    for size in bias_sizes:
        share = size // seq
        pieces.append(lax.dynamic_slice_in_dim(biases, at + seq_index * share, share, 0))
        at += size
    b_in_grad, b_qkv_grad, b_out_grad, b_up_grad, b_down_grad = pieces

    _, silu_pull = jax.vjp(jax.nn.silu, time_float)
    time_grad = silu_pull(dot_nt(d_embedding, ada_w))[0]
    width_share = model // seq
    emb_share = 6 * model // seq
    act_share = lax.dynamic_slice_in_dim(time_act, seq_index * width_share, width_share, 1)
    joined = jnp.concatenate([act_share, d_embedding], axis=1)
    for axis in ("ry", "rz"):
        joined = gather_small(joined, axis)
    all_act, all_emb = joined[:, :width_share], joined[:, width_share:]
    ada_w_grad = dot_tn(all_act, all_emb)
    ada_b_grad = lax.dynamic_slice_in_dim(
        jnp.sum(all_emb.astype(F32), axis=0), seq_index * emb_share, emb_share, 0
    )
    return (
        result,
        noisy_grad,
        cond_grad,
        text_grad,
        time_grad,
        w_in_grad.astype(F32),
        b_in_grad,
        ada_w_grad,
        ada_b_grad,
        w_qkv_grad.astype(F32),
        b_qkv_grad,
        w_out_grad.astype(F32),
        b_out_grad,
        w_up_grad.astype(F32),
        b_up_grad,
        w_down_grad.astype(F32),
        b_down_grad,
    )


def solution(mesh):
    rows, seq = mesh.shape["rows"], mesh.shape["seq"]
    mesh = Mesh(mesh.devices.reshape(rows // 2, 2, seq // 2, 2), ("rz", "ry", "sx", "core"))
    r, s = ("rz", "ry"), ("sx", "core")
    in_specs = (
        (P(r, s, None),) * 3 + (P(r, None),) * 4 + (P(),) * 12 + (P(r, s, None),)
    )
    out_specs = (
        (P(r, s, None),) * 4
        + (P(r, None), P(None, s), P(s))
        + (P(s, None), P(s)) * 5
    )
    return jax.shard_map(shards, mesh=mesh, in_specs=in_specs, out_specs=out_specs, check_vma=False)
```

time: 1550 us -> 735 us (0.47)
  matrix products: 663 us -> 110 us
  waiting for transfers between devices: 506 us -> 154 us
  Pallas kernels: 0 us -> 216 us
  other arithmetic: 182 us -> 85 us
  starting transfers between devices: 0.8 us -> 63.3 us
  blocking collectives: 34.1 us -> 0 us
  local copies, waits for them, and re-layouts: 127 us -> 98.4 us
    dot_general x47 -> x22, matrix products: 663 us -> 110 us  [the longest x7 43.1 us: dot_nt(): lax.dot_general(a, b, (((1,), (1,)), ((), ())), preferred_element_type=F32)]
    reduce_scatter x6 -> x0, waiting for transfers between devices: 232 us -> none  [the longest x1 77.1 us: shards(): lax.psum_scatter(key_terms.astype(jnp.bfloat16), 'seq', scatter_dimension...]
    pallas_call x0 -> x4, Pallas kernels: none -> 216 us  [the longest x1 133 us: attend_back(): pl.pallas_call(attend_back_kernel, grid=(rows, pairs, 2, 4), in_specs=[qs...]
    psum x1 -> x0, waiting for transfers between devices: 216 us -> none  [shards(): lax.psum(seq_parts[0].astype(jnp.bfloat16), 'rows').astype(jnp.float32)]
    ppermute x0 -> x56, waiting for transfers between devices: none -> 154 us  [the longest x49 93.4 us: flip(): return lax.ppermute(v, axis, [(i, i ^ bit) for i in range(size)])]
    reduce_sum x17 -> x8, other arithmetic: 104 us -> 14.3 us  [the longest x1 4.29 us: shards(): d_scale_one = jnp.sum(d_mod_one * normed_one, axis=1)]
    ppermute x0 -> x56, starting transfers between devices: none -> 63.3 us  [the longest x49 55.5 us: flip(): return lax.ppermute(v, axis, [(i, i ^ bit) for i in range(size)])]
    all_gather x2 -> x0, waiting for transfers between devices: 58.5 us -> none  [the longest x1 41.6 us: shards(): key_piece = lax.all_gather(key_rows, 'seq', axis=1, tiled=True)]
  transfers between devices with their start and end apart: 9 -> 56, of which waited for: 8 -> 29; matrix products, arithmetic and copies ran while one was open for 9% -> 29% of each run, Pallas kernels for 0% -> 20%
where the time goes in v1:
time: 735 us; the launch traced here: 729 us
  Pallas kernels  216 us (29%)
  waiting for transfers between devices  154 us (21%)
  matrix products  110 us (15%)
  local copies, waits for them, and re-layouts  98.4 us (13%)
  other arithmetic  85 us (12%)
  starting transfers between devices  63.3 us (9%)
    pallas_call x1, Pallas kernels, attend_back(): pl.pallas_call(attend_back_kernel, grid=(rows, pairs, 2, 4), in_specs=[qs...  133 us
    ppermute x49, waiting for transfers between devices, flip(): return lax.ppermute(v, axis, [(i, i ^ bit) for i in range(size)])  93.4 us
    ppermute x7, waiting for transfers between devices, shift(): return lax.ppermute(v, axis, [(i, (i + step) % size) for i in range(size)])  60.4 us
    pallas_call x1, Pallas kernels, attend(): pl.pallas_call(attend_kernel, grid=(rows, pairs, 2, 2), in_specs=[qs, q0,...  57.9 us
    ppermute x49, starting transfers between devices, flip(): return lax.ppermute(v, axis, [(i, i ^ bit) for i in range(size)])  55.5 us
    dot_general x7, matrix products, dot_nt(): lax.dot_general(a, b, (((1,), (1,)), ((), ())), preferred_element_type=F32)  43.1 us
    dot_general x8, matrix products, dot_tn(): lax.dot_general(a, b, (((0,), (0,)), ((), ())), preferred_element_type=F32)  36 us
    unnamed x200, local copies, waits for them, and re-layouts  34.6 us
  transfers between devices with their start and end apart: 56, of which 29 were waited for; matrix products, arithmetic and copies ran while one was open for 29% of the time, Pallas kernels for 20%

profile of v1, /device:TPU:0, one launch (start us, length us, event | category | flops | bytes accessed | tf_op | source)
XLA Modules:
  0.0 729.4 jit_solution(3307953381052655109)
XLA Ops:
  17.6 6.3 fusion.111
  26.6 8.9 %copy.134 = bf16[1024,3072]{0,1:T(8,128)(2,1)} copy(bf16[1024,3072]{1,0:T(8,128)(2,1)} %rest_2_.3) | data formatting | bytes 12582912 | tf_op args[11]
  37.7 4.2 add_reduce_fusion
  45.9 6.0 fusion.79
  64.2 14.1 %front.2 = (bf16[1,1664,1024]{2,1,0:T(8,128)(2,1)}, bf16[1,1664,512]{2,1,0:T(8,128)(2,1)S(1)}, bf16[1,1664,512]{2,1,0:T(8,128)(2,1)}, bf16[1,1664,512]{2,1,0:T(8,128)(2,1)}) custom-call(s32[1]{0:T(128)} %bitcast.11.core, bf16[1,1664,712]{2,1,0:T(8,128)(2,1)} %pad_maximum_fusion.2.x_ref, bf16[712,1024]{1,0:T(8,128)(2,1)S(1)} %copy-done.5, ...), custom_call_target="tpu_custom_call" | custom-call | flops 7660896256 | bytes 19277824 | tf_op jit(solution)/shard_map/front/pallas_call | solution.py:144
  85.5 11.2 %front.3 = (bf16[1,1664,1024]{2,1,0:T(8,128)(2,1)}, bf16[1,1664,512]{2,1,0:T(8,128)(2,1)S(1)}, bf16[1,1664,512]{2,1,0:T(8,128)(2,1)}) custom-call(s32[1]{0:T(128)} %bitcast.11.core, bf16[1,1664,712]{2,1,0:T(8,128)(2,1)} %pad_maximum_fusion.3.x_ref, bf16[712,1024]{1,0:T(8,128)(2,1)S(1)} %copy-done.6, f32[1,1024]{1,0:T(1,128)S(1)} %bitcast.380, ...), custom_call_target="tpu_custom_call" | custom-call | flops 5916065792 | bytes 17573888 | tf_op jit(solution)/shard_map/front/pallas_call | solution.py:144
  102.3 57.9 %attend.1 = (bf16[1,1664,512]{2,1,0:T(8,128)(2,1)}, f32[1,1664,512]{2,1,0:T(8,128)}) custom-call(bf16[1,1664,512]{2,1,0:T(8,128)(2,1)} %copy-done.8, bf16[1,1664,128]{2,1,0:T(8,128)(2,1)} %select_convert_fusion.qx_ref, bf16[1,3328,512]{2,1,0:T(8,128)(2,1)} %copy-done.56, bf16[1,3328,128]{2,1,0:T(8,128)(2,1)} %fusion.42.kx_ref, bf16[1,3328,512]{2,1,0:T(8,128)(2,1)} %copy-done.57), custom_call_target="tpu_custom_call" | custom-call | flops 90731184128 | bytes 13631488 | tf_op jit(solution)/shard_map/attend/pallas_call | solution.py:219
  164.8 4.6 copy.135
  179.5 4.6 fusion.133
  184.7 6.2 fusion.128
  190.9 9.3 %convolution_convert_fusion = bf16[2048,1024]{1,0:T(8,128)(2,1)S(1)} fusion(bf16[1,832,1024]{2,1,0:T(8,128)(2,1)S(1)} %copy-done.45, f32[1024]{0:T(1024)S(1)} %bitcast.443, f32[832,2048]{1,0:T(8,128)} %fusion.128, f32[2048]{0:T(1024)S(1)} %convert_element_type.550), kind=kOutput, calls=%fused_computation.30 | convolution fusion | flops 3511353344 | bytes 12726272 | tf_op jit(solution)/shard_map/dot_general | solution.py:25
  200.2 12.1 %convert_reduce_fusion = (f32[2048]{0:T(1024)}, bf16[832,2048]{1,0:T(8,128)(2,1)S(1)}) fusion(f32[832,2048]{1,0:T(8,128)} %fusion.128, f32[2048]{0:T(1024)S(1)} %convert_element_type.550, bf16[2048,1024]{1,0:T(8,128)(2,1)S(1)} %copy-done.85, bf16[1,832,1024]{2,1,0:T(8,128)(2,1)S(1)} %copy-done.45, f32[1024]{0:T(1024)S(1)} %bitcast.444), kind=kOutput, calls=%fused_computation.10 | convolution fusion | flops 3531405312 | bytes 16142336 | tf_op jit(solution)/shard_map/dot_general | solution.py:29
  212.3 5.6 convolution_convert_fusion.1
  217.9 4.9 multiply_reduce_fusion
  226.4 7.4 %fusion.18 = (f32[1024]{0:T(1024)}, f32[832,1024]{1,0:T(8,128)S(1)}) fusion(bf16[1,832,1024]{2,1,0:T(8,128)(2,1)S(1)} %copy-done.45, f32[1024]{0:T(1024)S(1)} %convert_element_type.552, bf16[2048,1024]{1,0:T(8,128)(2,1)S(1)} %copy-done.86, f32[832,2048]{1,0:T(8,128)} %fusion.128, f32[2048]{0:T(1024)S(1)} %convert_element_type.550), kind=kOutput, calls=%fused_computation.34 | convolution fusion | flops 3510107136 | bytes 16138240 | tf_op jit(solution)/shard_map/dot_general | solution.py:21
  249.9 133.2 %attend_back.1 = (bf16[1,1664,512]{2,1,0:T(8,128)(2,1)}, bf16[1,3328,512]{2,1,0:T(8,128)(2,1)}, bf16[1,3328,512]{2,1,0:T(8,128)(2,1)}) custom-call(bf16[1,1664,512]{2,1,0:T(8,128)(2,1)} %copy-done.8, bf16[1,1664,128]{2,1,0:T(8,128)(2,1)} %select_convert_fusion.qx_ref, bf16[1,3328,512]{2,1,0:T(8,128)(2,1)} %copy-done.56, ...), custom_call_target="tpu_custom_call" | custom-call | flops 226827960320 | bytes 23855104 | tf_op jit(solution)/shard_map/attend_back/pallas_call | solution.py:338
  388.3 5.8 fusion.54
  407.4 8.4 %fusion.16 = bf16[1664,1024]{1,0:T(8,128)(2,1)S(1)} fusion(bf16[1024,1536]{0,1:T(8,128)(2,1)} %bitcast.387, bf16[1,1664,512]{2,1,0:T(8,128)(2,1)} %get-tuple-element.167, bf16[1,1664,512]{2,1,0:T(8,128)(2,1)} %get-tuple-element.165, bf16[1,1664,512]{2,1,0:T(8,128)(2,1)} %get-tuple-element.36), kind=kOutput, calls=%fused_computation.29 | convolution fusion | flops 5251530752 | bytes 11665408 | tf_op jit(solution)/shard_map/dot_general | solution.py:29
  429.4 12.8 %collective-permute-done.33 = bf16[256,1024]{1,0:T(8,128)(2,1)S(1)} collective-permute-done((bf16[256,1024]{1,0:T(8,128)(2,1)S(1)}, bf16[256,1024]{1,0:T(8,128)(2,1)S(1)}, u32[]{:S(2)}, u32[]{:S(2)}) %collective-permute-start.33) | collective-permute-done | bytes 524320 | tf_op jit(solution)/shard_map/ppermute | solution.py:34
  445.9 4.9 collective-permute-done.34
  454.6 4.8 collective-permute-done.35
  489.4 5.1 collective-permute-done.49
  496.6 20.3 %collective-permute-done.41 = bf16[256,2048]{1,0:T(8,128)(2,1)S(1)} collective-permute-done((bf16[256,2048]{1,0:T(8,128)(2,1)S(1)}, bf16[256,2048]{1,0:T(8,128)(2,1)S(1)}, u32[]{:S(2)}, u32[]{:S(2)}) %collective-permute-start.41) | collective-permute-done | bytes 1048608 | tf_op jit(solution)/shard_map/ppermute | solution.py:34
  524.6 4.8 collective-permute-done.42
  533.1 7.8 %collective-permute-done.51 = bf16[128,1024]{1,0:T(8,128)(2,1)S(1)} collective-permute-done((bf16[128,1024]{1,0:T(8,128)(2,1)S(1)}, bf16[128,1024]{1,0:T(8,128)(2,1)S(1)}, u32[]{:S(2)}, u32[]{:S(2)}) %collective-permute-start.51) | collective-permute-done | bytes 262176 | tf_op jit(solution)/shard_map/ppermute | solution.py:39
  571.9 14.3 %collective-permute-done.7 = bf16[1,832,1024]{2,1,0:T(8,128)(2,1)} collective-permute-done((bf16[1,832,1024]{2,1,0:T(8,128)(2,1)}, bf16[1,832,1024]{2,1,0:T(8,128)(2,1)}, u32[]{:S(2)}, u32[]{:S(2)}) %collective-permute-start.7) | collective-permute-done | bytes 1703968 | tf_op jit(solution)/shard_map/ppermute | solution.py:34
  586.3 4.3 fusion.33
  615.9 8.6 %fusion.100 = f32[1,1024]{1,0:T(1,128)} fusion(f32[1,1024]{1,0:T(1,128)S(1)} %copy-done.68, bf16[1,1024]{1,0:T(2,128)(2,1)S(1)} %copy-done.67, bf16[6144,1]{0,1:T(2,128)(2,1)S(1)} %reshape.1677, bf16[1024,6144]{1,0:T(8,128)(2,1)} %param.29), kind=kOutput, calls=%fused_computation.301 | convolution fusion | flops 12590080 | bytes 12605440 | tf_op jit(solution)/shard_map/dot_general | solution.py:29
  655.6 7.1 collective-permute-done.47
  668.5 4.3 collective-permute-done.11
  699.4 8.5 %collective-permute-done.16 = bf16[64,712]{1,0:T(8,128)(2,1)S(1)} collective-permute-done((bf16[64,712]{1,0:T(8,128)(2,1)S(1)}, bf16[64,712]{1,0:T(8,128)(2,1)S(1)}, u32[]{:S(2)}, u32[]{:S(2)}) %collective-permute-start.16) | collective-permute-done | bytes 91168 | tf_op jit(solution)/shard_map/ppermute | solution.py:39
  717.1 9.5 %collective-permute-done.31 = bf16[128,3072]{1,0:T(8,128)(2,1)S(1)} collective-permute-done((bf16[128,3072]{1,0:T(8,128)(2,1)S(1)}, bf16[128,3072]{1,0:T(8,128)(2,1)S(1)}, u32[]{:S(2)}, u32[]{:S(2)}) %collective-permute-start.31) | collective-permute-done | bytes 786464 | tf_op jit(solution)/shard_map/ppermute | solution.py:39
  (494 shorter events, 298.7 us)
Async XLA Ops:
  11.8 41.5 %collective-permute-start.1 = (bf16[1,832,712]{1,2,0:T(8,128)(2,1)}, bf16[1,832,712]{1,2,0:T(8,128)(2,1)}, u32[]{:S(2)}, u32[]{:S(2)}) collective-permute-start(bf16[1,832,712]{1,2,0:T(8,128)(2,1)} %copy.129), channel_id=1, source_target_pairs={{0,2},{2,0},{1,3},{3,1},{4,6},{6,4},{5,7},{7,5},{8,10},{10,8},{9,1... | collective-permute-start | bytes 3554312 | tf_op jit(solution)/shard_map/ppermute | solution.py:34
  14.8 43.0 %collective-permute-start = (bf16[1,832,712]{1,2,0:T(8,128)(2,1)}, bf16[1,832,712]{1,2,0:T(8,128)(2,1)}, u32[]{:S(2)}, u32[]{:S(2)}) collective-permute-start(bf16[1,832,712]{1,2,0:T(8,128)(2,1)} %copy.129), channel_id=1, source_target_pairs={{0,1},{1,0},{2,3},{3,2},{4,5},{5,4},{6,7},{7,6},{8,9},{9,8},{10,11... | collective-permute-start | bytes 3554312 | tf_op jit(solution)/shard_map/ppermute | solution.py:39
  53.3 26.2 %collective-permute-start.2 = (bf16[1,832,712]{1,2,0:T(8,128)(2,1)}, bf16[1,832,712]{1,2,0:T(8,128)(2,1)}, u32[]{:S(2)}, u32[]{:S(2)}) collective-permute-start(bf16[1,832,712]{1,2,0:T(8,128)(2,1)} %collective-permute-done.1), channel_id=1, source_target_pairs={{0,1},{1,0},{2,3},{3,2},{4,5},{5,4},{6,7},{7,6},{8,9},{9,8},{10,11... | collective-permute-start | bytes 3554312 | tf_op jit(solution)/shard_map/ppermute | solution.py:39
  163.0 16.5 %collective-permute-start.3 = (bf16[1,832,512]{2,1,0:T(8,128)(2,1)}, bf16[1,832,512]{2,1,0:T(8,128)(2,1)}, u32[]{:S(2)}, u32[]{:S(2)}) collective-permute-start(bf16[1,832,512]{2,1,0:T(8,128)(2,1)} %get-tuple-element.184), channel_id=1, source_target_pairs={{0,1},{1,0},{2,3},{3,2},{4,5},{5,4},{6,7},{7,6},{8,9},{9,8},{10,11... | collective-permute-start | bytes 2555912 | tf_op jit(solution)/shard_map/ppermute | solution.py:39
  224.3 239.5 %collective-permute-start.48 = (bf16[2,512,1024]{2,1,0:T(8,128)(2,1)}, bf16[2,512,1024]{2,1,0:T(8,128)(2,1)}, u32[]{:S(2)}, u32[]{:S(2)}) collective-permute-start(bf16[2,512,1024]{2,1,0:T(8,128)(2,1)} %dynamic-slice_bitcast_fusion), channel_id=1, source_target_pairs={{0,1},{1,0},{2,3},{3,2},{4,5},{5,4},{6,7},{7,6},{8,9},{9,8},{10,11... | collective-permute-start | bytes 6291464 | tf_op jit(solution)/shard_map/ppermute | solution.py:39
  226.4 243.0 %collective-permute-start.40 = (bf16[2,256,2048]{2,1,0:T(8,128)(2,1)}, bf16[2,256,2048]{2,1,0:T(8,128)(2,1)}, u32[]{:S(2)}, u32[]{:S(2)}) collective-permute-start(bf16[2,256,2048]{2,1,0:T(8,128)(2,1)} %dynamic-slice_bitcast_fusion.1), channel_id=1, source_target_pairs={{0,1},{1,0},{2,3},{3,2},{4,5},{5,4},{6,7},{7,6},{8,9},{9,8},{10,11... | collective-permute-start | bytes 6291464 | tf_op jit(solution)/shard_map/ppermute | solution.py:39
  246.8 177.7 %collective-permute-start.32 = (bf16[2,256,1024]{2,1,0:T(8,128)(2,1)}, bf16[2,256,1024]{2,1,0:T(8,128)(2,1)}, u32[]{:S(2)}, u32[]{:S(2)}) collective-permute-start(bf16[2,256,1024]{2,1,0:T(8,128)(2,1)} %dynamic-slice_bitcast_fusion.5), channel_id=1, source_target_pairs={{0,1},{1,0},{2,3},{3,2},{4,5},{5,4},{6,7},{7,6},{8,9},{9,8},{10,11... | collective-permute-start | bytes 3145736 | tf_op jit(solution)/shard_map/ppermute | solution.py:39
  407.0 73.0 %collective-permute-start.24 = (bf16[3,2,256,512]{2,3,0,1:T(8,128)(2,1)}, bf16[3,2,256,512]{2,3,0,1:T(8,128)(2,1)}, u32[]{:S(2)}, u32[]{:S(2)}) collective-permute-start(bf16[3,2,256,512]{2,3,0,1:T(8,128)(2,1)} %bitcast.419), channel_id=1, source_target_pairs={{0,1},{1,0},{2,3},{3,2},{4,5},{5,4},{6,7},{7,6},{8,9},{9,8},{10,11... | collective-permute-start | bytes 4718600 | tf_op jit(solution)/shard_map/ppermute | solution.py:39
  428.3 13.9 %collective-permute-start.33 = (bf16[256,1024]{1,0:T(8,128)(2,1)S(1)}, bf16[256,1024]{1,0:T(8,128)(2,1)S(1)}, u32[]{:S(2)}, u32[]{:S(2)}) collective-permute-start(bf16[256,1024]{1,0:T(8,128)(2,1)S(1)} %dynamic-slice_bitcast_fusion.13), channel_id=1, source_target_pairs={{0,2},{2,0},{1,3},{3,1},{4,6},{6,4},{5,7},{7,5},{8,10},{10,8},{9,1... | collective-permute-start | bytes 1572872 | tf_op jit(solution)/shard_map/ppermute | solution.py:34
  460.8 111.1 %collective-permute-start.5 = (bf16[1,832,1024]{2,1,0:T(8,128)(2,1)}, bf16[1,832,1024]{2,1,0:T(8,128)(2,1)}, u32[]{:S(2)}, u32[]{:S(2)}) collective-permute-start(bf16[1,832,1024]{2,1,0:T(8,128)(2,1)} %slice_bitcast_fusion.2), channel_id=1, source_target_pairs={{0,1},{1,0},{2,3},{3,2},{4,5},{5,4},{6,7},{7,6},{8,9},{9,8},{10,11... | collective-permute-start | bytes 5111816 | tf_op jit(solution)/shard_map/ppermute | solution.py:39
  463.8 55.2 %collective-permute-start.6 = (bf16[1,1,832,1024]{3,2,1,0:T(8,128)(2,1)}, bf16[1,1,832,1024]{3,2,1,0:T(8,128)(2,1)S(1)}, u32[]{:S(2)}, u32[]{:S(2)}) collective-permute-start(bf16[1,1,832,1024]{3,2,1,0:T(8,128)(2,1)} %slice_bitcast_fusion), channel_id=1, source_target_pairs={{0,1},{1,0},{2,3},{3,2},{4,5},{5,4},{6,7},{7,6},{8,9},{9,8},{10,11... | collective-permute-start | bytes 5111816 | tf_op jit(solution)/shard_map/ppermute | solution.py:39
  468.4 26.0 %collective-permute-start.49 = (bf16[512,1024]{1,0:T(8,128)(2,1)S(1)}, bf16[512,1024]{1,0:T(8,128)(2,1)S(1)}, u32[]{:S(2)}, u32[]{:S(2)}) collective-permute-start(bf16[512,1024]{1,0:T(8,128)(2,1)S(1)} %dynamic-slice_bitcast_fusion.3), channel_id=1, source_target_pairs={{0,2},{2,0},{1,3},{3,1},{4,6},{6,4},{5,7},{7,5},{8,10},{10,8},{9,1... | collective-permute-start | bytes 3145736 | tf_op jit(solution)/shard_map/ppermute | solution.py:34
  478.4 38.5 %collective-permute-start.41 = (bf16[256,2048]{1,0:T(8,128)(2,1)S(1)}, bf16[256,2048]{1,0:T(8,128)(2,1)S(1)}, u32[]{:S(2)}, u32[]{:S(2)}) collective-permute-start(bf16[256,2048]{1,0:T(8,128)(2,1)S(1)} %dynamic-slice_bitcast_fusion.4), channel_id=1, source_target_pairs={{0,2},{2,0},{1,3},{3,1},{4,6},{6,4},{5,7},{7,5},{8,10},{10,8},{9,1... | collective-permute-start | bytes 3145736 | tf_op jit(solution)/shard_map/ppermute | solution.py:34
  487.8 62.8 %collective-permute-start.25 = (bf16[256,3072]{0,1:T(8,128)(2,1)S(1)}, bf16[256,3072]{0,1:T(8,128)(2,1)S(1)}, u32[]{:S(2)}, u32[]{:S(2)}) collective-permute-start(bf16[256,3072]{0,1:T(8,128)(2,1)S(1)} %dynamic-slice_bitcast_fusion.2), channel_id=1, source_target_pairs={{0,2},{2,0},{1,3},{3,1},{4,6},{6,4},{5,7},{7,5},{8,10},{10,8},{9,1... | collective-permute-start | bytes 4718600 | tf_op jit(solution)/shard_map/ppermute | solution.py:34
  494.9 26.5 %collective-permute-start.50 = (bf16[256,1024]{1,0:T(8,128)(2,1)S(1)}, bf16[256,1024]{1,0:T(8,128)(2,1)S(1)}, u32[]{:S(2)}, u32[]{:S(2)}) collective-permute-start(bf16[256,1024]{1,0:T(8,128)(2,1)S(1)} %dynamic-slice_bitcast_fusion.11), channel_id=1, source_target_pairs={{0,4},{4,0},{1,5},{5,1},{2,6},{6,2},{3,7},{7,3},{8,12},{12,8},{9,1... | collective-permute-start | bytes 1572872 | tf_op jit(solution)/shard_map/ppermute | solution.py:39
  517.4 12.1 %collective-permute-start.42 = (bf16[128,2048]{1,0:T(8,128)(2,1)S(1)}, bf16[128,2048]{1,0:T(8,128)(2,1)S(1)}, u32[]{:S(2)}, u32[]{:S(2)}) collective-permute-start(bf16[128,2048]{1,0:T(8,128)(2,1)S(1)} %dynamic-slice_bitcast_fusion.12), channel_id=1, source_target_pairs={{0,4},{4,0},{1,5},{5,1},{2,6},{6,2},{3,7},{7,3},{8,12},{12,8},{9,1... | collective-permute-start | bytes 1572872 | tf_op jit(solution)/shard_map/ppermute | solution.py:39
  521.0 65.3 %collective-permute-start.7 = (bf16[1,832,1024]{2,1,0:T(8,128)(2,1)}, bf16[1,832,1024]{2,1,0:T(8,128)(2,1)}, u32[]{:S(2)}, u32[]{:S(2)}) collective-permute-start(bf16[1,832,1024]{2,1,0:T(8,128)(2,1)} %fusion.40), channel_id=1, source_target_pairs={{0,2},{2,0},{1,3},{3,1},{4,6},{6,4},{5,7},{7,5},{8,10},{10,8},{9,1... | collective-permute-start | bytes 5111816 | tf_op jit(solution)/shard_map/ppermute | solution.py:34
  521.7 19.2 %collective-permute-start.51 = (bf16[128,1024]{1,0:T(8,128)(2,1)S(1)}, bf16[128,1024]{1,0:T(8,128)(2,1)S(1)}, u32[]{:S(2)}, u32[]{:S(2)}) collective-permute-start(bf16[128,1024]{1,0:T(8,128)(2,1)S(1)} %dynamic-slice_bitcast_fusion.16), channel_id=1, source_target_pairs={{0,16},{8,24},{16,0},{24,8},{1,17},{9,25},{17,1},{25,9},{2,18},{10... | collective-permute-start | bytes 786440 | tf_op jit(solution)/shard_map/ppermute | solution.py:39
  529.6 16.6 %collective-permute-start.43 = (bf16[64,2048]{1,0:T(8,128)(2,1)S(1)}, bf16[64,2048]{1,0:T(8,128)(2,1)S(1)}, u32[]{:S(2)}, u32[]{:S(2)}) collective-permute-start(bf16[64,2048]{1,0:T(8,128)(2,1)S(1)} %dynamic-slice_bitcast_fusion.17), channel_id=1, source_target_pairs={{0,16},{8,24},{16,0},{24,8},{1,17},{9,25},{17,1},{25,9},{2,18},{10... | collective-permute-start | bytes 786440 | tf_op jit(solution)/shard_map/ppermute | solution.py:39
  541.7 17.0 %collective-permute-start.52 = (bf16[64,1024]{1,0:T(8,128)(2,1)}, bf16[64,1024]{1,0:T(8,128)(2,1)S(1)}, u32[]{:S(2)}, u32[]{:S(2)}) collective-permute-start(bf16[64,1024]{1,0:T(8,128)(2,1)} %dynamic-slice_bitcast_fusion.20), channel_id=1, source_target_pairs={{0,8},{8,0},{16,24},{24,16},{1,9},{9,1},{17,25},{25,17},{2,10},{10... | collective-permute-start | bytes 393224 | tf_op jit(solution)/shard_map/ppermute | solution.py:39
  547.0 13.6 %collective-permute-start.44 = (bf16[32,2048]{1,0:T(8,128)(2,1)}, bf16[32,2048]{1,0:T(8,128)(2,1)}, u32[]{:S(2)}, u32[]{:S(2)}) collective-permute-start(bf16[32,2048]{1,0:T(8,128)(2,1)} %dynamic-slice_bitcast_fusion.21), channel_id=1, source_target_pairs={{0,8},{8,0},{16,24},{24,16},{1,9},{9,1},{17,25},{25,17},{2,10},{10... | collective-permute-start | bytes 393224 | tf_op jit(solution)/shard_map/ppermute | solution.py:39
  557.1 94.2 %collective-permute-start.26 = (bf16[128,3072]{1,0:T(8,128)(2,1)}, bf16[128,3072]{1,0:T(8,128)(2,1)}, u32[]{:S(2)}, u32[]{:S(2)}) collective-permute-start(bf16[128,3072]{1,0:T(8,128)(2,1)} %dynamic-slice_bitcast_fusion.10), channel_id=1, source_target_pairs={{0,4},{4,0},{1,5},{5,1},{2,6},{6,2},{3,7},{7,3},{8,12},{12,8},{9,1... | collective-permute-start | bytes 2359304 | tf_op jit(solution)/shard_map/ppermute | solution.py:39
  566.3 73.3 %collective-permute-start.54 = (bf16[128,1024]{1,0:T(8,128)(2,1)}, bf16[128,1024]{1,0:T(8,128)(2,1)}, u32[]{:S(2)}, u32[]{:S(2)}) collective-permute-start(bf16[128,1024]{1,0:T(8,128)(2,1)} %pad_maximum_fusion.18), channel_id=1, source_target_pairs={{0,16},{8,24},{16,0},{24,8},{1,17},{9,25},{17,1},{25,9},{2,18},{10... | collective-permute-start | bytes 786440 | tf_op jit(solution)/shard_map/ppermute | solution.py:39
  569.4 72.1 %collective-permute-start.46 = (bf16[64,2048]{1,0:T(8,128)(2,1)}, bf16[64,2048]{1,0:T(8,128)(2,1)}, u32[]{:S(2)}, u32[]{:S(2)}) collective-permute-start(bf16[64,2048]{1,0:T(8,128)(2,1)} %pad_maximum_fusion.17), channel_id=1, source_target_pairs={{0,16},{8,24},{16,0},{24,8},{1,17},{9,25},{17,1},{25,9},{2,18},{10... | collective-permute-start | bytes 786440 | tf_op jit(solution)/shard_map/ppermute | solution.py:39
  605.1 58.8 %collective-permute-start.10 = (bf16[2,256,712]{1,2,0:T(8,128)(2,1)}, bf16[2,256,712]{1,2,0:T(8,128)(2,1)}, u32[]{:S(2)}, u32[]{:S(2)}) collective-permute-start(bf16[2,256,712]{1,2,0:T(8,128)(2,1)} %bitcast.377), channel_id=1, source_target_pairs={{0,1},{1,0},{2,3},{3,2},{4,5},{5,4},{6,7},{7,6},{8,9},{9,8},{10,11... | collective-permute-start | bytes 2187272 | tf_op jit(solution)/shard_map/ppermute | solution.py:39
  614.4 10.1 %collective-permute-start.21 = (bf16[1,6400]{1,0:T(2,128)(2,1)S(1)}, bf16[1,6400]{1,0:T(2,128)(2,1)S(1)}, u32[]{:S(2)}, u32[]{:S(2)}) collective-permute-start(bf16[1,6400]{1,0:T(2,128)(2,1)S(1)} %pad_maximum_fusion.27), channel_id=1, source_target_pairs={{0,4},{4,0},{1,5},{5,1},{2,6},{6,2},{3,7},{7,3},{8,12},{12,8},{9,1... | collective-permute-start | bytes 38408 | tf_op jit(solution)/shard_map/ppermute | solution.py:39
  641.5 68.8 %collective-permute-start.55 = (bf16[256,1024]{1,0:T(8,128)(2,1)}, bf16[256,1024]{1,0:T(8,128)(2,1)}, u32[]{:S(2)}, u32[]{:S(2)}) collective-permute-start(bf16[256,1024]{1,0:T(8,128)(2,1)} %pad_maximum_fusion.14), channel_id=1, source_target_pairs={{0,4},{4,0},{1,5},{5,1},{2,6},{6,2},{3,7},{7,3},{8,12},{12,8},{9,1... | collective-permute-start | bytes 1572872 | tf_op jit(solution)/shard_map/ppermute | solution.py:39
  643.2 19.6 %collective-permute-start.47 = (bf16[128,2048]{1,0:T(8,128)(2,1)S(1)}, bf16[128,2048]{1,0:T(8,128)(2,1)S(1)}, u32[]{:S(2)}, u32[]{:S(2)}) collective-permute-start(bf16[128,2048]{1,0:T(8,128)(2,1)S(1)} %pad_maximum_fusion.13), channel_id=1, source_target_pairs={{0,4},{4,0},{1,5},{5,1},{2,6},{6,2},{3,7},{7,3},{8,12},{12,8},{9,1... | collective-permute-start | bytes 1572872 | tf_op jit(solution)/shard_map/ppermute | solution.py:39
  652.7 15.8 %collective-permute-start.27 = (bf16[64,3072]{1,0:T(8,128)(2,1)S(1)}, bf16[64,3072]{1,0:T(8,128)(2,1)S(1)}, u32[]{:S(2)}, u32[]{:S(2)}) collective-permute-start(bf16[64,3072]{1,0:T(8,128)(2,1)S(1)} %dynamic-slice_bitcast_fusion.14), channel_id=1, source_target_pairs={{0,16},{8,24},{16,0},{24,8},{1,17},{9,25},{17,1},{25,9},{2,18},{10... | collective-permute-start | bytes 1179656 | tf_op jit(solution)/shard_map/ppermute | solution.py:39
  693.2 15.9 %collective-permute-start.30 = (bf16[64,3072]{1,0:T(8,128)(2,1)S(1)}, bf16[64,3072]{1,0:T(8,128)(2,1)S(1)}, u32[]{:S(2)}, u32[]{:S(2)}) collective-permute-start(bf16[64,3072]{1,0:T(8,128)(2,1)S(1)} %pad_maximum_fusion.15), channel_id=1, source_target_pairs={{0,16},{8,24},{16,0},{24,8},{1,17},{9,25},{17,1},{25,9},{2,18},{10... | collective-permute-start | bytes 1179656 | tf_op jit(solution)/shard_map/ppermute | solution.py:39
  697.8 10.1 %collective-permute-start.16 = (bf16[64,712]{1,0:T(8,128)(2,1)S(1)}, bf16[64,712]{1,0:T(8,128)(2,1)S(1)}, u32[]{:S(2)}, u32[]{:S(2)}) collective-permute-start(bf16[64,712]{1,0:T(8,128)(2,1)S(1)} %pad_maximum_fusion.25), channel_id=1, source_target_pairs={{0,16},{8,24},{16,0},{24,8},{1,17},{9,25},{17,1},{25,9},{2,18},{10... | collective-permute-start | bytes 273416 | tf_op jit(solution)/shard_map/ppermute | solution.py:39
  709.3 17.3 %collective-permute-start.31 = (bf16[128,3072]{1,0:T(8,128)(2,1)S(1)}, bf16[128,3072]{1,0:T(8,128)(2,1)S(1)}, u32[]{:S(2)}, u32[]{:S(2)}) collective-permute-start(bf16[128,3072]{1,0:T(8,128)(2,1)S(1)} %pad_maximum_fusion.12), channel_id=1, source_target_pairs={{0,4},{4,0},{1,5},{5,1},{2,6},{6,2},{3,7},{7,3},{8,12},{12,8},{9,1... | collective-permute-start | bytes 2359304 | tf_op jit(solution)/shard_map/ppermute | solution.py:39
  (113 other events, 1277.6 us)

commit v2 on v1

v2 whole, which is shorter than its diff:
```python
import functools
import math

import jax
import jax.numpy as jnp
from jax import lax
from jax.experimental import pallas as pl
from jax.experimental.pallas import tpu as pltpu
from jax.sharding import Mesh, PartitionSpec as P

HEADS = 16
EPS = 1e-06
THETA = 10000.0
MASKED = -1e30
F32 = jnp.float32
BF = jnp.bfloat16
MIB = 2**20
QUICK = pl.CostEstimate(flops=10**8, bytes_accessed=10**5, transcendentals=0)


def dot_nn(a, b):
    return jnp.dot(a, b, preferred_element_type=F32)


def dot_tn(a, b):
    return lax.dot_general(a, b, (((0,), (0,)), ((), ())), preferred_element_type=F32)


def dot_nt(a, b):
    return lax.dot_general(a, b, (((1,), (1,)), ((), ())), preferred_element_type=F32)


def shift(v, axis, step):
    size = lax.axis_size(axis)
    return lax.ppermute(v, axis, [(i, (i + step) % size) for i in range(size)])


def flip(v, axis, bit):
    size = lax.axis_size(axis)
    return lax.ppermute(v, axis, [(i, i ^ bit) for i in range(size)])


def bits(axis):
    size = lax.axis_size(axis)
    assert size & (size - 1) == 0
    return [1 << b for b in range(size.bit_length() - 1)]


def sum_small(v, axis):
    for bit in bits(axis):
        v = v + flip(v, axis, bit)
    return v


def gather_small(v, axis):
    for bit in bits(axis):
        v = jnp.concatenate([v, flip(v, axis, bit)], axis=0)
    return v


def pick(v, index):
    return lax.dynamic_index_in_dim(v, index, 0, keepdims=False)


def part_of(v, index, count):
    size = v.shape[0] // count
    return lax.dynamic_slice_in_dim(v, index * size, size, 0)


def total(terms):
    acc = terms[0].astype(F32)
    for term in terms[1:]:
        acc = acc + term.astype(F32)
    return acc.astype(BF)


def rows_give(terms):
    return total([part_of(t, 1 - lax.axis_index("ry"), 2) for t in terms])


def rows_mine(terms, recv):
    return total([part_of(t, lax.axis_index("ry"), 2) for t in terms] + [recv])


def rows_turn(mine):
    z, deep = lax.axis_index("rz"), lax.axis_size("rz")
    got = [shift(part_of(mine, (z + t) % deep, deep), "rz", t) for t in range(1, deep)]
    return [part_of(mine, z, deep)] + got


def rows_spread(block):
    return [shift(block, "rz", t) for t in range(lax.axis_size("rz") - 1, 0, -1)] + [block]


def rows_half(ring):
    z, deep = lax.axis_index("rz"), lax.axis_size("rz")
    ring = jnp.concatenate(ring + ring[:-1], axis=0)
    size = ring.shape[0] // (2 * deep - 1)
    return lax.dynamic_slice_in_dim(ring, (deep - 1 - z) * size, deep * size, 0)


def rows_join(mine):
    y = lax.axis_index("ry")
    recv = flip(mine, "ry", 1)
    return jnp.where(y == 0, mine, recv), jnp.where(y == 0, recv, mine)


def sum_rows(terms):
    recv = flip(rows_give(terms), "ry", 1)
    return rows_join(rows_half(rows_spread(total(rows_turn(rows_mine(terms, recv))))))


def sum_chips(blocks):
    return list(blocks[0]) + [shift(total(blocks[t]), "sx", t) for t in range(1, len(blocks))]


def turn(x, cos, sin, lane):
    partner = jnp.where(lane % 64 < 32, pltpu.roll(x, 96, 1), pltpu.roll(x, 32, 1))
    return x * cos + partner * sin


def wide_tables(angles):
    cos, sin = angles[0], angles[1]
    return (
        jnp.concatenate([cos, cos, cos, cos], axis=0).T,
        jnp.concatenate([-sin, sin, -sin, sin], axis=0).T,
    )


def front_kernel(core, x0_ref, x1_ref, win_ref, bin_ref, emb_ref, *rest, parts):
    weights = rest[: 2 * len(parts)]
    angle_ref, mod_ref = rest[2 * len(parts) : 2 * len(parts) + 2]
    outs = rest[2 * len(parts) + 2 :]
    x = jnp.where(pl.program_id(1) == 0, x0_ref[...], x1_ref[...])[:, : win_ref.shape[0]]
    cos, sin = wide_tables(angle_ref)
    resid = dot_nn(x, win_ref[...]) + bin_ref[...]
    center = resid - jnp.mean(resid, axis=1, keepdims=True)
    inv = lax.rsqrt(jnp.mean(center * center, axis=1, keepdims=True) + EPS)
    mod = (center * inv * (1.0 + emb_ref[1:2, :]) + emb_ref[0:1, :]).astype(BF)
    mod_ref[...] = mod.T
    lane = lax.broadcasted_iota(jnp.int32, (1, 128), 1)
    for n, part in enumerate(parts):
        y = dot_nn(mod, weights[2 * n][...]) + weights[2 * n + 1][...]
        if part == "v":
            outs[n][...] = y.astype(BF)
            continue
        scale = 0.125 if part == "q" else 1.0
        for t in range(0, y.shape[1], 128):
            z = turn(y[:, t : t + 128], cos, sin, lane)
            outs[n][:, t : t + 128] = (z * scale).astype(BF)


def front(core, x0, x1, w_in, b_in, emb, w_qkv, b_qkv, angles, parts):
    rows, span, width = x0.shape
    n = 2 * span
    model = w_in.shape[1]
    half = model // 2
    place = {"q": 0, "k": 1, "v": 2}
    one = pl.BlockSpec((None, span, width), lambda r, i, c: (r, 0, 0))
    frame = lambda w: pl.BlockSpec((None, span, w), lambda r, i, c: (r, i, 0))
    whole = lambda a, b: pl.BlockSpec((a, b), lambda r, i, c: (0, 0))
    w_specs, w_args = [], []
    for part in parts:
        j = place[part]
        w_specs.append(pl.BlockSpec((model, half), lambda r, i, c, j=j: (0, 2 * j + c[0])))
        w_specs.append(pl.BlockSpec((1, half), lambda r, i, c, j=j: (0, 2 * j + c[0])))
        w_args += [w_qkv, b_qkv]
    return pl.pallas_call(
        functools.partial(front_kernel, parts=parts),
        grid_spec=pltpu.PrefetchScalarGridSpec(
            num_scalar_prefetch=1,
            grid=(rows, 2),
            in_specs=[one, one, whole(*w_in.shape), whole(1, model)]
            + [pl.BlockSpec((None, 6, model), lambda r, i, c: (r, 0, 0))]
            + w_specs
            + [pl.BlockSpec((None, None, 2, 32, span), lambda r, i, c: (r, i, 0, 0, 0))],
            out_specs=[pl.BlockSpec((None, None, model, span), lambda r, i, c: (r, i, 0, 0))]
            + [frame(half)] * len(parts),
        ),
        out_shape=[jax.ShapeDtypeStruct((rows, 2, model, span), BF)]
        + [jax.ShapeDtypeStruct((rows, n, half), BF)] * len(parts),
        compiler_params=pltpu.CompilerParams(vmem_limit_bytes=56 * MIB),
        cost_estimate=QUICK,
        name="front",
    )(core, x0, x1, w_in, b_in, emb, *w_args, angles)


def mid_kernel(
    core, x_ref, om_ref, oo_ref, g_ref, valid_ref, emb_ref,
    win_ref, bin_ref, wom_ref, woo_ref, bout_ref, wup_ref, bup_ref, wdn_ref, bdn_ref,
    out_ref, dres_ref, dom_ref, doo_ref, mod_ref, act_ref, dhid_ref, dff_ref, dbr_ref,
    sums_ref, bupg_ref, slope_ref,
):
    hidden_width = wup_ref.shape[1]
    step = 512
    gate_one, shift_two = emb_ref[2:3, :], emb_ref[3:4, :]
    scale_two, gate_two = emb_ref[4:5, :], emb_ref[5:6, :]
    total = lambda v: jnp.sum(v, axis=0, keepdims=True)
    mean = lambda v: jnp.mean(v, axis=1, keepdims=True)
    resid = dot_nn(x_ref[:, : win_ref.shape[0]], win_ref[...]) + bin_ref[...]
    branch = dot_nn(om_ref[...], wom_ref[...]) + dot_nn(oo_ref[...], woo_ref[...]) + bout_ref[...]
    branch = branch * valid_ref[...]
    resid = resid + gate_one * branch
    center = resid - mean(resid)
    inv = lax.rsqrt(mean(center * center) + EPS)
    normed = center * inv
    mod = (normed * (1.0 + scale_two) + shift_two).astype(BF)
    mod_ref[...] = mod
    ff = None
    for j in range(0, hidden_width, step):
        h = dot_nn(mod, wup_ref[:, j : j + step]) + bup_ref[:, j : j + step]
        square = h * h
        t = jnp.tanh(h * (0.7978845608028654 + 0.035677408136300125 * square))
        up = 0.5 + 0.5 * t
        act = (h * up).astype(BF)
        act_ref[:, j : j + step] = act
        slope = up + h * (0.5 - 0.5 * t * t) * (0.7978845608028654 + 0.10703222440890037 * square)
        slope_ref[:, j : j + step] = slope.astype(BF)
        part = dot_nn(act, wdn_ref[j : j + step, :])
        ff = part if ff is None else ff + part
    ff = ff + bdn_ref[...]
    out_ref[...] = (resid + gate_two * ff).astype(BF)
    g = g_ref[...].astype(F32)
    sums_ref[0:1, :] = total(g * ff)
    d_ff = (g * gate_two).astype(BF)
    dff_ref[...] = d_ff
    sums_ref[1:2, :] = total(d_ff.astype(F32))
    d_mod = None
    for j in range(0, hidden_width, step):
        d_act = dot_nt(d_ff, wdn_ref[j : j + step, :])
        d_hid = (d_act * slope_ref[:, j : j + step].astype(F32)).astype(BF)
        dhid_ref[:, j : j + step] = d_hid
        bupg_ref[:, j : j + step] = total(d_hid.astype(F32))
        part = dot_nt(d_hid, wup_ref[:, j : j + step])
        d_mod = part if d_mod is None else d_mod + part
    sums_ref[2:3, :] = total(d_mod)
    sums_ref[3:4, :] = total(d_mod * normed)
    u = d_mod * (1.0 + scale_two)
    d_res = g + inv * (u - mean(u) - normed * mean(u * normed))
    dres_ref[...] = d_res
    sums_ref[4:5, :] = total(d_res * branch)
    d_branch = (d_res * gate_one * valid_ref[...]).astype(BF)
    dbr_ref[...] = d_branch
    sums_ref[5:6, :] = total(d_branch.astype(F32))
    dom_ref[...] = dot_nt(d_branch, wom_ref[...]).astype(BF)
    doo_ref[...] = dot_nt(d_branch, woo_ref[...]).astype(BF)


def mid(core, x, o_mine, o_other, g, valid, emb, w_in, b_in, w_out, b_out, w_up, b_up, w_down, b_down):
    rows, span, width = x.shape
    model, hidden = w_up.shape
    half = model // 2
    frame = lambda w: pl.BlockSpec((None, span, w), lambda r, c: (r, 0, 0))
    whole = lambda a, b: pl.BlockSpec(
        (a, b), lambda r, c: (0, 0), pipeline_mode=pl.Buffered(buffer_count=1)
    )
    out_half = lambda f: pl.BlockSpec(
        (half, model), lambda r, c: (f(c[0]), 0), pipeline_mode=pl.Buffered(buffer_count=1)
    )
    shape = lambda w, t: jax.ShapeDtypeStruct((rows, span, w), t)
    return pl.pallas_call(
        mid_kernel,
        grid_spec=pltpu.PrefetchScalarGridSpec(
            num_scalar_prefetch=1,
            grid=(rows,),
            in_specs=[
                frame(width), frame(half), frame(half), frame(model), frame(1),
                pl.BlockSpec((None, 6, model), lambda r, c: (r, 0, 0)),
                whole(*w_in.shape), whole(1, model),
                out_half(lambda c: c), out_half(lambda c: 1 - c), whole(1, model),
                whole(model, hidden), whole(1, hidden), whole(hidden, model), whole(1, model),
            ],
            out_specs=[
                frame(model), frame(model), frame(half), frame(half), frame(model),
                frame(hidden), frame(hidden), frame(model), frame(model),
                pl.BlockSpec((None, 8, model), lambda r, c: (r, 0, 0)),
                pl.BlockSpec((None, 1, hidden), lambda r, c: (r, 0, 0)),
            ],
            scratch_shapes=[pltpu.VMEM((span, hidden), BF)],
        ),
        out_shape=[
            shape(model, BF), shape(model, F32), shape(half, BF), shape(half, BF), shape(model, BF),
            shape(hidden, BF), shape(hidden, BF), shape(model, BF), shape(model, BF),
            jax.ShapeDtypeStruct((rows, 8, model), F32),
            jax.ShapeDtypeStruct((rows, 1, hidden), F32),
        ],
        compiler_params=pltpu.CompilerParams(vmem_limit_bytes=62 * MIB),
        cost_estimate=QUICK,
        name="mid",
    )(core, x, o_mine, o_other, g, valid, emb, w_in, b_in, w_out, w_out, b_out, w_up, b_up, w_down, b_down)


def outer_kernel(core, mod_ref, act_ref, om_ref, oo_ref, dhid_ref, dff_ref, dbr_ref, out_ref):
    step = pl.program_id(0)
    seq, model = out_ref.shape[0], out_ref.shape[2]
    r = model // seq

    def put(left, right, size, first, at):
        product = dot_nn(left.T, right).astype(BF)
        for n in range(model // size):
            out_ref[first + n, at : at + size, :] = product[n * size : (n + 1) * size]

    @pl.when(step < 2)
    def _():
        product = dot_nn(mod_ref[...].T, dhid_ref[...]).astype(BF)
        for j in range(2):
            @pl.when(step == j)
            def _():
                for n in range(seq):
                    out_ref[n, j * r : (j + 1) * r, :] = product[n * r : (n + 1) * r]

    @pl.when((step >= 2) & (step < 4))
    def _():
        product = dot_nn(act_ref[...].T, dff_ref[...]).astype(BF)
        for j in range(2):
            @pl.when(step == 2 + j)
            def _():
                for n in range(seq // 2):
                    out_ref[j * (seq // 2) + n, 2 * r : 4 * r, :] = product[
                        n * 2 * r : (n + 1) * 2 * r
                    ]

    @pl.when(step == 4)
    def _():
        mine, other = om_ref[...], oo_ref[...]
        low = core[0] == 0
        mixed = jnp.concatenate([jnp.where(low, mine, other), jnp.where(low, other, mine)], axis=1)
        product = dot_nn(mixed.T, dbr_ref[...]).astype(BF)
        for n in range(seq):
            out_ref[n, 4 * r :, :] = product[n * r : (n + 1) * r]


def outer(core, mod, act, o_mine, o_other, d_hid, d_ff, d_br):
    n, model = mod.shape
    seq = lax.axis_size("sx") * 2
    low = lambda i: jnp.minimum(i, 1)
    high = lambda i: jnp.clip(i - 2, 0, 1)
    once = lambda w: pl.BlockSpec((n, w), lambda i, c: (0, 0))
    shape = (seq, 5 * model // seq, model)
    return pl.pallas_call(
        outer_kernel,
        grid_spec=pltpu.PrefetchScalarGridSpec(
            num_scalar_prefetch=1,
            grid=(5,),
            in_specs=[
                once(model), pl.BlockSpec((n, model), lambda i, c: (0, high(i))),
                once(model // 2), once(model // 2),
                pl.BlockSpec((n, model), lambda i, c: (0, low(i))), once(model), once(model),
            ],
            out_specs=pl.BlockSpec(shape, lambda i, c: (0, 0, 0)),
        ),
        out_shape=jax.ShapeDtypeStruct(shape, BF),
        compiler_params=pltpu.CompilerParams(vmem_limit_bytes=60 * MIB),
        cost_estimate=QUICK,
        name="outer",
    )(core, mod, act, o_mine, o_other, d_hid, d_ff, d_br)


def qkv_outer_kernel(place, *refs, far):
    near_ref, dq_ref, dk_ref, dv_ref = refs[:4]
    far_refs = refs[4 : 4 + 3 * far]
    keep_ref, give_ref = refs[-2:]
    chips, _, rows, width = keep_ref.shape
    span = near_ref.shape[2]
    acc_q, acc = None, None
    add = lambda a, b: b if a is None else a + b
    for i in range(2):
        cut = slice(i * span, (i + 1) * span)
        both = jnp.concatenate([dk_ref[cut, :], dv_ref[cut, :]], axis=1)
        acc_q = add(acc_q, dot_nn(near_ref[i], dq_ref[cut, :]))
        acc = add(acc, dot_nn(near_ref[i], both))
    for f in range(far):
        mod_ref, dkf_ref, dvf_ref = far_refs[3 * f : 3 * f + 3]
        for i in range(2):
            cut = slice(i * span, (i + 1) * span)
            both = jnp.concatenate([dkf_ref[cut, :], dvf_ref[cut, :]], axis=1)
            acc = add(acc, dot_nn(mod_ref[i], both))
    parts = [acc_q.astype(BF), acc[:, :width].astype(BF), acc[:, width:].astype(BF)]
    for side in range(2):
        for out_ref, core in ((keep_ref, side), (give_ref, 1 - side)):
            @pl.when(place[1] == core)
            def _():
                for n in range(side, 2 * chips, 2):
                    chip = (n // 2 + chips - place[0]) % chips
                    for j, part in enumerate(parts):
                        out_ref[chip, j] = part[n * rows : (n + 1) * rows]


def qkv_outer(place, mod_near, dq, dk, dv, far):
    model = mod_near.shape[1]
    width = dq.shape[1]
    chips = lax.axis_size("sx")
    shape = (chips, 3, model // (2 * chips), width)
    args = [mod_near, dq, dk, dv]
    for item in far:
        args += list(item)
    return pl.pallas_call(
        functools.partial(qkv_outer_kernel, far=len(far)),
        grid_spec=pltpu.PrefetchScalarGridSpec(
            num_scalar_prefetch=1,
            grid=(1,),
            in_specs=[
                pl.BlockSpec(a.shape, lambda i, c, n=a.ndim: (0,) * n) for a in args
            ],
            out_specs=[pl.BlockSpec(shape, lambda i, c: (0,) * 4)] * 2,
        ),
        out_shape=[jax.ShapeDtypeStruct(shape, BF)] * 2,
        compiler_params=pltpu.CompilerParams(vmem_limit_bytes=60 * MIB),
        cost_estimate=QUICK,
        name="qkv_outer",
    )(place, *args)


def d_mod_kernel(core, *refs, parts):
    acc, at = None, 0
    for n, count in enumerate(parts):
        left = jnp.concatenate([ref[...] for ref in refs[at : at + count]], axis=1)
        part = dot_nt(left, refs[sum(parts) + n][...])
        acc = part if acc is None else acc + part
        at += count
    mine_ref, other_ref = refs[-2:]

    @pl.when(pl.program_id(1) % 2 == 0)
    def _():
        mine_ref[...] = acc.astype(BF)

    @pl.when(pl.program_id(1) % 2 == 1)
    def _():
        other_ref[...] = acc.astype(BF)


def d_mod(core, grads, w_qkv, span):
    arrays = [a for _, g in grads for a in g]
    rows, n = arrays[0].shape[:2]
    model = w_qkv.shape[0]
    half = model // 2
    specs = [pl.BlockSpec((None, span, a.shape[2]), lambda r, i, c: (r, i, 0)) for a in arrays]
    specs += [
        pl.BlockSpec((model, half), lambda r, i, c, j=j: (0, 2 * j + c[0])) for j, _ in grads
    ]
    out = pl.BlockSpec((None, span, model), lambda r, i, c: (r, 0, 0))
    return pl.pallas_call(
        functools.partial(d_mod_kernel, parts=tuple(len(g) for _, g in grads)),
        grid_spec=pltpu.PrefetchScalarGridSpec(
            num_scalar_prefetch=1,
            grid=(rows, n // span),
            in_specs=specs,
            out_specs=[out, out],
        ),
        out_shape=[jax.ShapeDtypeStruct((rows, span, model), BF)] * 2,
        compiler_params=pltpu.CompilerParams(vmem_limit_bytes=48 * MIB),
        cost_estimate=QUICK,
        name="d_mod",
    )(core, *arrays, *[w_qkv] * len(grads))


def tail_kernel(place, *refs, far, mel):
    x_ref, dres_ref, emb_ref, keep_ref, win_ref, bin_ref, near_ref, recv_ref = refs[:8]
    far_refs = refs[8 : 8 + far]
    noisy_ref, cond_ref, text_ref, keep_out, send_out, sums_ref, turned = refs[8 + far :]
    total = lambda v: jnp.sum(v, axis=0, keepdims=True)
    mean = lambda v: jnp.mean(v, axis=1, keepdims=True)
    width = win_ref.shape[0]
    resid = dot_nn(x_ref[:, :width], win_ref[...]) + bin_ref[...]
    center = resid - mean(resid)
    inv = lax.rsqrt(mean(center * center) + EPS)
    normed = center * inv
    d = near_ref[...].astype(F32) + recv_ref[...].astype(F32)
    for ref in far_refs:
        d = d + ref[...].astype(F32)
    sums_ref[0:1, :] = total(d)
    sums_ref[1:2, :] = total(d * normed)
    u = d * (1.0 + emb_ref[1:2, :])
    d_res = (dres_ref[...] + inv * (u - mean(u) - normed * mean(u * normed))).astype(BF)
    sums_ref[2:3, :] = total(d_res.astype(F32))
    turned[...] = d_res.T
    chips, rows = keep_out.shape[0], keep_out.shape[1]
    for t in range(chips):
        block = ((place[0] + t) % chips) * 2
        for out, core in ((send_out, 1 - place[1]), (keep_out, place[1])):
            at = pl.ds(pl.multiple_of((block + core) * rows, rows), rows)
            out[t] = dot_nn(turned[at, :], x_ref[...]).astype(BF)
    d_in = dot_nt(d_res, win_ref[...])
    noisy_ref[...] = d_in[:, :mel]
    cond_ref[...] = d_in[:, mel : 2 * mel] * keep_ref[:, 0:1]
    text_ref[...] = d_in[:, 2 * mel : width] * keep_ref[:, 1:2]


def tail(place, x, d_res, emb, keep, w_in, b_in, near, recv, far, mel):
    rows, span, width = x.shape
    model = w_in.shape[1]
    chips = lax.axis_size("sx")
    block = model // (2 * chips)
    frame = lambda w: pl.BlockSpec((None, span, w), lambda r, c: (r, 0, 0))
    whole = lambda a, b: pl.BlockSpec((a, b), lambda r, c: (0, 0))
    blocks = pl.BlockSpec((None, chips, block, width), lambda r, c: (r, 0, 0, 0))
    shape = lambda w: jax.ShapeDtypeStruct((rows, span, w), F32)
    return pl.pallas_call(
        functools.partial(tail_kernel, far=len(far), mel=mel),
        grid_spec=pltpu.PrefetchScalarGridSpec(
            num_scalar_prefetch=1,
            grid=(rows,),
            in_specs=[
                frame(width), frame(model), pl.BlockSpec((None, 6, model), lambda r, c: (r, 0, 0)),
                frame(2), whole(*w_in.shape), whole(1, model), frame(model), frame(model),
            ] + [frame(model)] * len(far),
            out_specs=[
                frame(mel), frame(mel), frame(w_in.shape[0] - 2 * mel), blocks, blocks,
                pl.BlockSpec((None, 8, model), lambda r, c: (r, 0, 0)),
            ],
            scratch_shapes=[pltpu.VMEM((model, span), BF)],
        ),
        out_shape=[
            shape(mel), shape(mel), shape(w_in.shape[0] - 2 * mel),
            jax.ShapeDtypeStruct((rows, chips, block, width), BF),
            jax.ShapeDtypeStruct((rows, chips, block, width), BF),
            jax.ShapeDtypeStruct((rows, 8, model), F32),
        ],
        compiler_params=pltpu.CompilerParams(vmem_limit_bytes=60 * MIB),
        cost_estimate=QUICK,
        name="tail",
    )(place, x, d_res, emb, keep, w_in, b_in, near, recv, *far)


def rows_of(refs, start, stop):
    parts, at = [], 0
    for ref in refs:
        size = ref.shape[0]
        lo, hi = max(start - at, 0), min(stop - at, size)
        if lo < hi:
            parts.append(ref[lo:hi, :])
        at += size
    return parts[0] if len(parts) == 1 else jnp.concatenate(parts, axis=0)


def attend_kernel(
    flag, q_ref, qx_ref, kf_ref, kn_ref, kxf_ref, kxn_ref, vf_ref, vn_ref,
    o_mine_ref, o_other_ref, l_ref, s_ref, m_ref, acc_ref,
):
    frames = s_ref.shape[1]
    span = o_mine_ref.shape[0]
    lane = lax.broadcasted_iota(jnp.int32, (1, 128), 1)
    zero = jnp.zeros((), BF)
    step = 256 if frames % 256 == 0 else frames
    apart = lambda n: pl.when(flag[0] >= -n)
    for h in range(2):
        mine = (lane // 64) == h

        @apart(2 * h)
        def _():
            q2 = jnp.concatenate([q_ref[...], qx_ref[...]], axis=1)
            top = None
            for c in range(0, frames, step):
                keys = jnp.where(mine, rows_of((kf_ref, kn_ref), c, c + step), zero)
                labels = rows_of((kxf_ref, kxn_ref), c, c + step)
                s = dot_nt(q2, jnp.concatenate([keys, labels], axis=1))
                s_ref[:, c : c + step] = s
                for t in range(0, step, 128):
                    part = s[:, t : t + 128]
                    top = part if top is None else jnp.maximum(top, part)
            m_ref[...] = jnp.broadcast_to(jnp.max(top, axis=1, keepdims=True), m_ref.shape)

        @apart(2 * h + 1)
        def _():
            top = m_ref[:, :1]
            ones = jnp.broadcast_to(jnp.where(mine, 1.0, 0.0).astype(BF), (step, 128))
            acc = None
            for c in range(0, frames, step):
                p = jnp.exp(s_ref[:, c : c + step] - top).astype(BF)
                values = jnp.where(mine, rows_of((vf_ref, vn_ref), c, c + step), zero)
                d = dot_nn(p, jnp.concatenate([values, ones], axis=1))
                acc = d if acc is None else acc + d
            if h == 0:
                acc_ref[...] = acc
                l_ref[...] = m_ref[...]
            if h == 1:
                both = acc + acc_ref[...]
                total = both[:, 128:]
                o = (both[:, :128] / total).astype(BF)
                o_mine_ref[...] = o[:span]
                o_other_ref[...] = o[span:]
                l_ref[...] = jnp.where(mine, m_ref[...], l_ref[...]) + jnp.log(total)


def attend(core, q, qx, k_far, k_near, kx_far, kx_near, v_far, v_near):
    rows, m, width = q.shape
    span = m // 2
    far, near = k_far.shape[1], k_near.shape[1]
    n = far + near
    pairs = width // 128
    at = lambda size: pl.BlockSpec((None, size, 128), lambda r, p, c: (r, 0, p))
    once = lambda size: pl.BlockSpec((None, size, 128), lambda r, p, c: (r, 0, 0))
    return pl.pallas_call(
        attend_kernel,
        grid_spec=pltpu.PrefetchScalarGridSpec(
            num_scalar_prefetch=1,
            grid=(rows, pairs),
            in_specs=[at(m), once(m), at(far), at(near), once(far), once(near), at(far), at(near)],
            out_specs=[at(span), at(span), at(m)],
            scratch_shapes=[
                pltpu.VMEM((m, n), F32),
                pltpu.VMEM((m, 128), F32),
                pltpu.VMEM((m, 256), F32),
            ],
        ),
        out_shape=[
            jax.ShapeDtypeStruct((rows, span, width), BF),
            jax.ShapeDtypeStruct((rows, span, width), BF),
            jax.ShapeDtypeStruct((rows, m, width), F32),
        ],
        compiler_params=pltpu.CompilerParams(vmem_limit_bytes=60 * MIB),
        cost_estimate=QUICK,
        name="attend",
    )(core, q, qx, k_far, k_near, kx_far, kx_near, v_far, v_near)


def split3(x, lane, rest):
    hi = x.astype(BF).astype(F32)
    mid = (x - hi).astype(BF).astype(F32)
    low = x - hi - mid
    place = lane % 64
    return jnp.where(
        place == 8, hi, jnp.where(place == 9, mid, jnp.where(place == 10, low, rest))
    ).astype(BF)


def attend_back_kernel(
    flag, q_ref, qx_ref, kf_ref, kn_ref, kxf_ref, kxn_ref, vf_ref, vn_ref,
    om_ref, oo_ref, dom_ref, doo_ref, l_ref, angf_ref, angn_ref,
    dq_ref, dkf_ref, dkn_ref, dvf_ref, dvn_ref,
    q2, d2, k2, v2, kk, qt, dt, p_s, s_s, dq_s, dk_s, dv_s,
):
    m, n = q_ref.shape[0], kk.shape[0]
    far = kf_ref.shape[0]
    span = om_ref.shape[0]
    lane = lax.broadcasted_iota(jnp.int32, (1, 128), 1)
    zero = jnp.zeros((), BF)
    steps = [(c, min(c + 256, n)) for c in range(0, n, 256)] if n % 128 == 0 else [(0, n)]
    apart = pl.when(flag[0] >= 0)

    @apart
    def _():
        q2[:, :128] = q_ref[...]
        q2[:, 128:] = split3(l_ref[...], lane, qx_ref[...].astype(F32))
        same = (
            lax.broadcasted_iota(jnp.int32, (128, 128), 0) // 64
            == lax.broadcasted_iota(jnp.int32, (128, 128), 1) // 64
        )
        same = jnp.where(same, 1.0, 0.0).astype(BF)
        same = jnp.concatenate([same, same], axis=0)
        for at, do_ref, o_ref in ((0, dom_ref, om_ref), (span, doo_ref, oo_ref)):
            cut = slice(at, at + span)
            prod = do_ref[...].astype(F32) * o_ref[...].astype(F32)
            hi = prod.astype(BF)
            low = (prod - hi.astype(F32)).astype(BF)
            delta = dot_nn(jnp.concatenate([hi, low], axis=1), same)
            d2[cut, :128] = do_ref[...]
            d2[cut, 128:] = split3(delta, lane, jnp.zeros((span, 128), F32))
        qt[...] = q_ref[...].T
        dt[...] = d2[:, :128].T

    for h in range(2):
        mine = (lane // 64) == h
        half = slice(h * 64, (h + 1) * 64)

        @apart
        def _():
            less = (lane - 64 * h >= 8) & (lane - 64 * h < 11)
            for at, k_ref, kx_ref, v_ref in (
                (0, kf_ref, kxf_ref, vf_ref), (far, kn_ref, kxn_ref, vn_ref)
            ):
                cut = slice(at, at + k_ref.shape[0])
                keys = jnp.where(mine, k_ref[...], zero)
                kk[cut, :] = keys
                k2[:128, cut] = keys.T
                k2[128:, cut] = jnp.where(less, -1.0, kx_ref[...].astype(F32)).astype(BF).T
                v2[:128, cut] = jnp.where(mine, v_ref[...], zero).T
            v2[128:, :] = jnp.broadcast_to(jnp.where(less, -1.0, 0.0), (n, 128)).astype(BF).T

        @apart
        def _():
            for c, e in steps:
                s = dot_nn(q2[...], k2[:, c:e])
                d = dot_nn(d2[...], v2[:, c:e])
                p = jnp.exp(s)
                p_s[:, c:e] = p.astype(BF)
                s_s[:, c:e] = (p * d).astype(BF)

        @apart
        def _():
            acc = dot_nn(s_s[...], kk[...])
            if h == 0:
                dq_s[...] = acc
            if h == 1:
                cos, sin = wide_tables(angn_ref)
                dq_ref[...] = turn((dq_s[...] + acc) * 0.125, cos, -sin, lane).astype(BF)

        @apart
        def _():
            for c, e in steps:
                dk_s[half, c:e] = dot_nn(qt[half, :], s_s[:, c:e])
                dv_s[half, c:e] = dot_nn(dt[half, :], p_s[:, c:e])

    @apart
    def _():
        for at, ang_ref, dk_ref, dv_ref in (
            (0, angf_ref, dkf_ref, dvf_ref), (far, angn_ref, dkn_ref, dvn_ref)
        ):
            cut = slice(at, at + dk_ref.shape[0])
            cos, sin = ang_ref[0], ang_ref[1]
            turned = []
            for h in range(2):
                a, b = dk_s[64 * h : 64 * h + 32, cut], dk_s[64 * h + 32 : 64 * h + 64, cut]
                turned += [a * cos + b * sin, b * cos - a * sin]
            dk_ref[...] = jnp.concatenate(turned, axis=0).astype(BF).T
            dv_ref[...] = dv_s[:, cut].astype(BF).T


def attend_back(
    core, q, qx, k_far, k_near, kx_far, kx_near, v_far, v_near, o_mine, o_other, d_mine, d_other,
    lse, ang_far, ang_near, first, pairs,
):
    rows, m, width = q.shape
    span = m // 2
    far, near = k_far.shape[1], k_near.shape[1]
    n = far + near
    at = lambda size: pl.BlockSpec((None, size, 128), lambda r, p, c: (r, 0, first + p))
    out = lambda size: pl.BlockSpec((None, size, 128), lambda r, p, c: (r, 0, p))
    once = lambda size: pl.BlockSpec((None, size, 128), lambda r, p, c: (r, 0, 0))
    angle = lambda size: pl.BlockSpec((None, 2, 32, size), lambda r, p, c: (r, 0, 0, 0))
    shape = lambda size: jax.ShapeDtypeStruct((rows, size, pairs * 128), BF)
    return pl.pallas_call(
        attend_back_kernel,
        grid_spec=pltpu.PrefetchScalarGridSpec(
            num_scalar_prefetch=1,
            grid=(rows, pairs),
            in_specs=[
                at(m), once(m), at(far), at(near), once(far), once(near), at(far), at(near),
                at(span), at(span), at(span), at(span), at(m), angle(far), angle(near),
            ],
            out_specs=[out(m), out(far), out(near), out(far), out(near)],
            scratch_shapes=[
                pltpu.VMEM((m, 256), BF),
                pltpu.VMEM((m, 256), BF),
                pltpu.VMEM((256, n), BF),
                pltpu.VMEM((256, n), BF),
                pltpu.VMEM((n, 128), BF),
                pltpu.VMEM((128, m), BF),
                pltpu.VMEM((128, m), BF),
                pltpu.VMEM((m, n), BF),
                pltpu.VMEM((m, n), BF),
                pltpu.VMEM((m, 128), F32),
                pltpu.VMEM((128, n), F32),
                pltpu.VMEM((128, n), F32),
            ],
        ),
        out_shape=[shape(m), shape(far), shape(near), shape(far), shape(near)],
        compiler_params=pltpu.CompilerParams(vmem_limit_bytes=60 * MIB),
        cost_estimate=QUICK,
        name="attend_back",
    )(
        core, q, qx, k_far, k_near, kx_far, kx_near, v_far, v_near, o_mine, o_other, d_mine,
        d_other, lse, ang_far, ang_near,
    )


def frame_table(seg_lengths, frames):
    ends = jnp.cumsum(seg_lengths, axis=1)
    starts = ends - seg_lengths
    at = frames[None, :, None]
    inside = (at >= starts[:, None, :]) & (at < ends[:, None, :])
    offsets = frames[None, :] - jnp.sum(jnp.where(inside, starts[:, None, :], 0), axis=2)
    return inside.astype(F32), offsets


def rotary_angles(offsets, head_dim):
    halves = head_dim // 2
    frequency = jnp.exp(-math.log(THETA) * 2.0 * jnp.arange(halves, dtype=F32) / head_dim)
    angles = offsets.astype(F32)[:, None, :] * frequency[:, None]
    return jnp.stack([jnp.cos(angles), jnp.sin(angles)], axis=1)


def shards(
    noisy_mel, cond_mel, text_feat, time_embed, seg_lengths, audio_drop, text_drop, w_in, b_in,
    ada_w, ada_b, w_qkv, b_qkv, w_out, b_out, w_up, b_up, w_down, b_down, cotangent,
):
    rows, span, mel = noisy_mel.shape
    model = w_qkv.shape[0]
    half = model // 2
    head_dim = model // HEADS
    core, sx = lax.axis_index("core"), lax.axis_index("sx")
    chips = lax.axis_size("sx")
    seq = chips * 2
    seq_index = sx * 2 + core
    place = jnp.stack([sx, core]).astype(jnp.int32)
    core_arg = place[1:]
    as_row = lambda v: v.astype(F32).reshape(1, -1)
    flat = lambda a: a.reshape(-1, a.shape[-1])

    ramp = jnp.arange(span, dtype=jnp.int32)

    def chip_frames(chip):
        return jnp.concatenate([(chip * 2 + core) * span + ramp, (chip * 2 + 1 - core) * span + ramp])

    member, _ = frame_table(seg_lengths, seq_index * span + ramp)
    keep_audio = 1.0 - jnp.einsum("rcs,rs->rc", member, audio_drop.astype(F32))
    keep_text = 1.0 - jnp.einsum("rcs,rs->rc", member, text_drop.astype(F32))
    keep = jnp.stack([keep_audio, keep_text], axis=2)
    frame_valid = 1.0 - member[:, :, -1:]
    width = w_in.shape[0]
    inputs = jnp.concatenate(
        [
            noisy_mel,
            cond_mel * keep_audio[..., None].astype(BF),
            text_feat * keep_text[..., None].astype(BF),
            jnp.zeros((rows, span, -width % 128), BF),
        ],
        axis=2,
    )
    inputs_other = flip(inputs, "core", 1)
    far_blocks = [shift(inputs, "sx", -t) for t in range(1, chips)]

    time_float = time_embed.astype(F32)
    time_act = jax.nn.silu(time_float).astype(BF)
    embedding = (dot_nn(time_act, ada_w) + ada_b.astype(F32)).reshape(rows, 6, model)

    def tables(frame_ids):
        inside, offsets = frame_table(seg_lengths, frame_ids)
        pad = jnp.zeros(inside.shape[:2] + (128 - inside.shape[2],), F32)
        angles = rotary_angles(offsets, head_dim)
        return jnp.concatenate([inside, pad], axis=2), angles

    def two_blocks(angles):
        return jnp.moveaxis(angles.reshape(rows, 2, 32, 2, span), 3, 1)

    inside_near, ang_near = tables(chip_frames(sx))
    qx = jnp.where(jnp.arange(128) < seg_lengths.shape[1], 1.0 - inside_near, 0.0).astype(BF)
    kx_near = (MASKED * inside_near).astype(BF)
    bq, bi = as_row(b_qkv), as_row(b_in)
    mod_near, q, k_near, v_near = front(
        core_arg, inputs, inputs_other, w_in, bi, embedding, w_qkv, bq, two_blocks(ang_near),
        ("q", "k", "v"),
    )
    q, far_blocks = lax.optimization_barrier((q, far_blocks))
    far = []
    for t in range(1, chips):
        block = far_blocks[t - 1]
        inside, angles = tables(chip_frames((sx + t) % chips))
        made = front(
            core_arg, block, flip(block, "core", 1), w_in, bi, embedding, w_qkv, bq,
            two_blocks(angles), ("k", "v"),
        )
        far.append((*made, (MASKED * inside).astype(BF), angles))
    join = lambda n, axis: far[0][n] if chips == 2 else jnp.concatenate([f[n] for f in far], axis=axis)
    k_far, v_far, kx_far, ang_far = join(1, 1), join(2, 1), join(3, 1), join(4, 3)
    o_mine, o_give, lse = attend(
        core_arg, q, qx, k_far, k_near, kx_far, kx_near, v_far, v_near
    )

    o_other = flip(o_give, "core", 1)
    result, d_resid, d_o_mine, d_o_give, mod_two, act, d_hid, d_ff, d_br, sums, up_sums = mid(
        core_arg, inputs, o_mine, o_other, cotangent, frame_valid, embedding, w_in, bi,
        w_out, as_row(b_out), w_up, as_row(b_up), w_down, as_row(b_down),
    )
    d_o_other = flip(d_o_give, "core", 1)

    early = outer(
        core_arg, *[flat(a) for a in (mod_two, act, o_mine, o_other, d_hid, d_ff, d_br)]
    )
    early = lax.psum_scatter(early, ("sx", "core"), scatter_dimension=0, tiled=False)

    pairs = half // 128
    shared = [q, qx, k_far, k_near, kx_far, kx_near, v_far, v_near, o_mine, o_give, d_o_mine]
    shared += [d_o_other, lse, ang_far, ang_near]
    def far_part(far_grads):
        made = []
        for t in range(chips - 1):
            cut = slice(2 * span * t, 2 * span * (t + 1))
            grads = [(j, [a[:, cut] if chips > 2 else a for a in g]) for j, g in far_grads]
            mine, other = d_mod(core_arg, grads, w_qkv, span)
            made.append((mine, flip(other, "core", 1)))
        return made

    def outers(dq, dk_far, dk, dv_far, dv):
        pieces = []
        for r in range(rows):
            block = lambda a, t: a[r, 2 * span * t : 2 * span * (t + 1)]
            pieces.append(
                qkv_outer(
                    place, mod_near[r], dq[r], dk[r], dv[r],
                    [(far[t][0][r], block(dk_far, t), block(dv_far, t)) for t in range(chips - 1)],
                )
            )
        return pieces[0] if rows == 1 else [total(p) for p in zip(*pieces)]

    def by_chip(kept, given):
        return [
            jnp.stack([kept[t], given[t]], axis=0).reshape(-1, kept.shape[-1]) for t in range(chips)
        ]

    def send(blocks):
        return [blocks[0]] + [shift(b, "sx", t + 1) for t, b in enumerate(blocks[1:])]

    tie = lambda *trees: lax.optimization_barrier(trees)

    first_made = attend_back(core_arg, *shared, 0, pairs - 1)
    first_kept, first_given = outers(*first_made)
    first_blocks = by_chip(first_kept, flip(first_given, "core", 1))
    give = rows_give([early])
    shared, give, first_blocks = tie(shared, give, first_blocks)
    early_recv = flip(give, "ry", 1)
    first_late = send(first_blocks)
    last_made = attend_back(core_arg, *shared, pairs - 1, 1)
    last_made, early_recv, first_late = tie(last_made, early_recv, first_late)

    near_grads = [(0, [m[0] for m in (first_made, last_made)])]
    near_grads += [(j, [m[2 * j] for m in (first_made, last_made)]) for j in (1, 2)]
    far_grads = [(j, [m[2 * j - 1] for m in (first_made, last_made)]) for j in (1, 2)]
    far_parts = far_part(far_grads)
    first_late = total(first_late)
    late_give = rows_give([first_late])
    far_parts, late_give = tie(far_parts, late_give)
    far_parts = [total(p) for p in far_parts]
    early_mine = rows_mine([early], early_recv)
    last_made, far_parts, late_give, early_mine = tie(last_made, far_parts, late_give, early_mine)
    far_got = [shift(p, "sx", t + 1) for t, p in enumerate(far_parts)]
    late_recv = flip(late_give, "ry", 1)
    early = rows_turn(early_mine)
    last_kept, last_given = outers(*last_made)
    near_mine, near_give = d_mod(core_arg, near_grads, w_qkv, span)
    last_kept, last_given, near_give, far_got, early, late_recv = tie(
        last_kept, last_given, near_give, far_got, early, late_recv
    )
    near_recv = flip(near_give, "core", 1)
    last_given = flip(last_given, "core", 1)
    early = total(early)
    first_late = rows_turn(rows_mine([first_late], late_recv))
    last_blocks = by_chip(last_kept, last_given)
    near_recv, early, first_late, last_blocks = tie(near_recv, early, first_late, last_blocks)
    early = rows_spread(early)
    last_late = send(last_blocks)
    noisy_grad, cond_grad, text_grad, in_kept, in_given, in_sums = tail(
        place, inputs, d_resid, embedding, keep, w_in, bi, near_mine, near_recv, far_got, mel
    )
    in_kept, in_given, in_sums, early, first_late, last_late = tie(
        in_kept, in_given, in_sums, early, first_late, last_late
    )
    if rows > 1:
        in_kept, in_given = [jnp.sum(a.astype(F32), axis=0).astype(BF) for a in (in_kept, in_given)]
    else:
        in_kept, in_given = in_kept[0], in_given[0]

    emb_partial = jnp.stack(
        [in_sums[:, 0], in_sums[:, 1], sums[:, 4], sums[:, 2], sums[:, 3], sums[:, 0]], axis=1
    )
    over = lambda a: jnp.sum(a, axis=0)
    columns = lambda *a: sum(jnp.sum(flat(b).astype(F32), axis=0) for b in a)
    bias_mine = jnp.stack(
        [
            jnp.concatenate([columns(m[0]) for m in (first_made, last_made)]),
            jnp.concatenate([columns(m[1], m[2]) for m in (first_made, last_made)]),
            jnp.concatenate([columns(m[3], m[4]) for m in (first_made, last_made)]),
        ]
    )
    gap = jnp.zeros_like(bias_mine)
    b_qkv_grad = jnp.stack(
        [jnp.where(core == 0, bias_mine, gap), jnp.where(core == 0, gap, bias_mine)], axis=1
    )
    bias_sizes = [model, 3 * model, model, w_up.shape[1], model]
    biases = jnp.concatenate(
        [over(in_sums[:, 2]), b_qkv_grad.reshape(-1), over(sums[:, 5]), over(up_sums[:, 0]), over(sums[:, 1])]
    )
    vector = jnp.concatenate([emb_partial.reshape(-1), biases])

    in_given = flip(in_given, "core", 1)
    other = flip(vector, "core", 1)
    early = rows_half(early)
    early_other = flip(early, "ry", 1)
    first_late = rows_spread(total(first_late))
    last_late = total(last_late)
    last_give = rows_give([last_late])
    in_given, other, early, first_late[-1], last_give = tie(
        in_given, other, early, first_late[-1], last_give
    )
    in_late = sum_chips([(in_kept[t], in_given[t]) for t in range(chips)])
    vector = sum_small(vector + other, "sx")
    last_recv = flip(last_give, "ry", 1)
    first_late, last_recv = tie(first_late, last_recv)
    last_mine = rows_mine([last_late], last_recv)
    first_late = rows_half(first_late)
    in_late, vector, last_mine, first_late = tie(in_late, vector, last_mine, first_late)
    last_late = rows_turn(last_mine)
    first_other = flip(first_late, "ry", 1)
    in_late = total(in_late)
    in_recv = flip(rows_give([in_late]), "ry", 1)
    emb_size = rows * 6 * model
    d_embedding = vector[:emb_size].reshape(rows, 6 * model).astype(BF)
    biases = vector[emb_size:]
    shares, at = [], 0
    for size in bias_sizes:
        share = size // seq
        shares.append(lax.dynamic_slice_in_dim(biases, at + seq_index * share, share, 0))
        at += size
    width_share = model // seq
    act_share = lax.dynamic_slice_in_dim(time_act, seq_index * width_share, width_share, 1)
    shares = jnp.concatenate(shares)
    bias_share = shares.shape[0]
    shares = jnp.concatenate([shares[None], jnp.zeros((rows - 1, bias_share), F32)], axis=0)
    joined = jnp.concatenate([shares, act_share.astype(F32), d_embedding.astype(F32)], axis=1)
    joined = gather_small(joined, "ry")
    _, silu_pull = jax.vjp(jax.nn.silu, time_float)
    time_grad = silu_pull(dot_nt(d_embedding, ada_w))[0]
    in_recv, joined, last_late, time_grad = tie(in_recv, joined, last_late, time_grad)
    in_late = rows_turn(rows_mine([in_late], in_recv))
    joined = gather_small(joined, "rz")
    last_late = rows_spread(total(last_late))
    in_late, joined, last_late, early_other, first_other = tie(
        in_late, joined, last_late, early_other, first_other
    )
    in_late = rows_spread(total(in_late))
    last_late = rows_half(last_late)
    last_other = flip(last_late, "ry", 1)
    by_row = lambda a, b: jnp.concatenate(
        [jnp.where(lax.axis_index("ry") == 0, a, b), jnp.where(lax.axis_index("ry") == 0, b, a)],
        axis=0,
    )
    early = by_row(early, early_other)
    in_late, last_other, early = tie(in_late, last_other, early)
    late = jnp.concatenate([by_row(first_late, first_other), by_row(last_late, last_other)], axis=1)
    late = late.reshape(2, 3, model // seq, half)
    in_low, in_high = rows_join(rows_half(in_late))
    w_in_grad = jnp.concatenate([in_low, in_high], axis=0)[:, :width].astype(F32).T

    block = model // seq
    early = early.astype(F32)
    w_up_grad = jnp.concatenate([early[:block], early[block : 2 * block]], axis=1)
    w_down_grad = early[2 * block : 4 * block]
    w_out_grad = early[4 * block :]
    late = [jnp.where(core == 0, late[0], late[1]), jnp.where(core == 0, late[1], late[0])]
    w_qkv_grad = jnp.concatenate(
        [late[c][j].astype(F32) for j in range(3) for c in range(2)], axis=1
    )
    shares = jnp.sum(joined[:, :bias_share], axis=0)
    all_act = joined[:, bias_share : bias_share + width_share].astype(BF)
    all_emb = joined[:, bias_share + width_share :]
    b_in_grad, b_qkv_grad, b_out_grad, b_up_grad, b_down_grad = jnp.split(
        shares, [sum(bias_sizes[:n]) // seq for n in range(1, 5)]
    )
    ada_w_grad = dot_tn(all_act, all_emb.astype(BF))
    emb_share = 6 * model // seq
    ada_b_grad = lax.dynamic_slice_in_dim(
        jnp.sum(all_emb, axis=0), seq_index * emb_share, emb_share, 0
    )
    return (
        result,
        noisy_grad,
        cond_grad,
        text_grad,
        time_grad,
        w_in_grad,
        b_in_grad,
        ada_w_grad,
        ada_b_grad,
        w_qkv_grad,
        b_qkv_grad,
        w_out_grad,
        b_out_grad,
        w_up_grad,
        b_up_grad,
        w_down_grad,
        b_down_grad,
    )


def solution(mesh):
    rows, seq = mesh.shape["rows"], mesh.shape["seq"]
    mesh = Mesh(mesh.devices.reshape(rows // 2, 2, seq // 2, 2), ("rz", "ry", "sx", "core"))
    r, s = ("rz", "ry"), ("sx", "core")
    in_specs = (
        (P(r, s, None),) * 3 + (P(r, None),) * 4 + (P(),) * 12 + (P(r, s, None),)
    )
    out_specs = (
        (P(r, s, None),) * 4
        + (P(r, None), P(None, s), P(s))
        + (P(s, None), P(s)) * 5
    )
    return jax.shard_map(shards, mesh=mesh, in_specs=in_specs, out_specs=out_specs, check_vma=False)
```

time: 735 us -> 566 us (0.77)
  Pallas kernels: 216 us -> 311 us
  waiting for transfers between devices: 154 us -> 59.6 us
  matrix products: 110 us -> 20.3 us
  local copies, waits for them, and re-layouts: 98.4 us -> 44.2 us
  other arithmetic: 85 us -> 44.9 us
  between operations: 2.9 us -> 15.4 us
    pallas_call x2 -> x10, Pallas kernels: 191 us -> 285 us  [the longest x2 115 us: attend_back(): pl.pallas_call(attend_back_kernel, grid_spec=pltpu.PrefetchScalarGridSpec...]
    ppermute x49 -> x22, waiting for transfers between devices: 93.4 us -> 26.6 us  [flip(): return lax.ppermute(v, axis, [(i, i ^ bit) for i in range(size)])]
    ppermute x7 -> x29, starting transfers between devices: 7.79 us -> 51.4 us  [shift(): return lax.ppermute(v, axis, [(i, (i + step) % size) for i in range(size)])]
    ppermute x49 -> x22, starting transfers between devices: 55.5 us -> 12.8 us  [flip(): return lax.ppermute(v, axis, [(i, i ^ bit) for i in range(size)])]
    dot_general x7 -> x1, matrix products: 43.1 us -> 8.53 us  [dot_nt(): lax.dot_general(a, b, (((1,), (1,)), ((), ())), preferred_element_type=F32)]
    dot_general x8 -> x1, matrix products: 36 us -> 3.72 us  [dot_tn(): lax.dot_general(a, b, (((0,), (0,)), ((), ())), preferred_element_type=F32)]
    ppermute x7 -> x29, waiting for transfers between devices: 60.4 us -> 33 us  [shift(): return lax.ppermute(v, axis, [(i, (i + step) % size) for i in range(size)])]
    dot_general x5 -> x1, matrix products: 28.7 us -> 6.35 us  [dot_nn(): return jnp.dot(a, b, preferred_element_type=F32)]
  transfers between devices with their start and end apart: 56 -> 52, of which waited for: 29 -> 18; matrix products, arithmetic and copies ran while one was open for 29% -> 14% of each run, Pallas kernels for 20% -> 32%
where the time goes in v2:
time: 566 us; the launch traced here: 560 us
  Pallas kernels  311 us (55%)
  starting transfers between devices  64.2 us (11%)
  waiting for transfers between devices  59.6 us (11%)
  other arithmetic  44.9 us (8%)
  local copies, waits for them, and re-layouts  44.2 us (8%)
  matrix products  20.3 us (4%)
  between operations  15.4 us (3%)
    pallas_call x2, Pallas kernels, attend_back(): pl.pallas_call(attend_back_kernel, grid_spec=pltpu.PrefetchScalarGridSpec...  115 us
    pallas_call x1, Pallas kernels, attend(): pl.pallas_call(attend_kernel, grid_spec=pltpu.PrefetchScalarGridSpec(num_...  57.5 us
    ppermute x29, starting transfers between devices, shift(): return lax.ppermute(v, axis, [(i, (i + step) % size) for i in range(size)])  51.4 us
    pallas_call x1, Pallas kernels, mid(): pl.pallas_call(mid_kernel, grid_spec=pltpu.PrefetchScalarGridSpec(num_sca...  35.4 us
    ppermute x29, waiting for transfers between devices, shift(): return lax.ppermute(v, axis, [(i, (i + step) % size) for i in range(size)])  33 us
    ppermute x22, waiting for transfers between devices, flip(): return lax.ppermute(v, axis, [(i, i ^ bit) for i in range(size)])  26.6 us
    pallas_call x2, Pallas kernels, front(): pl.pallas_call(functools.partial(front_kernel, parts=parts), grid_spec=pl...  26.4 us
    pallas_call x2, Pallas kernels, qkv_outer(): pl.pallas_call(functools.partial(qkv_outer_kernel, far=len(far)), grid_sp...  24.8 us
  transfers between devices with their start and end apart: 52, of which 18 were waited for; matrix products, arithmetic and copies ran while one was open for 14% of the time, Pallas kernels for 32%

profile of v2, /device:TPU:0, one launch (start us, length us, event | category | flops | bytes accessed | tf_op | source)
XLA Modules:
  0.0 559.6 jit_solution(5745355740829208233)
XLA Ops:
  15.6 2.6 collective-permute-start.1
  18.9 6.4 %fusion.11 = f32[1,6144]{1,0:T(1,128)S(1)} fusion(bf16[1024,6144]{1,0:T(8,128)(2,1)} %param.29, bf16[1,1024]{1,0:T(2,128)(2,1)S(1)} %get-tuple-element.416), kind=kOutput, calls=%fused_computation.176 | convolution fusion | flops 12582912 | bytes 12609536 | tf_op jit(solution)/shard_map/dot_general | solution.py:22
  31.9 14.6 %front.2 = (bf16[1,2,1024,832]{3,2,1,0:T(8,128)(2,1)}, bf16[1,1664,512]{2,1,0:T(8,128)(2,1)}, bf16[1,1664,512]{2,1,0:T(8,128)(2,1)}, bf16[1,1664,512]{2,1,0:T(8,128)(2,1)}) custom-call(s32[1]{0:T(128)} %bitcast.core.flag, bf16[1,832,768]{2,1,0:T(8,128)(2,1)} %copy-done.15, bf16[1,832,768]{2,1,0:T(8,128)(2,1)} %collective-permute-done.x1_ref, ...), custom_call_target="tpu_custom_call" | custom-call | flops 100000000 | bytes 100000 | tf_op jit(solution)/shard_map/front/pallas_call | solution.py:168
  50.9 11.8 %front.3 = (bf16[1,2,1024,832]{3,2,1,0:T(8,128)(2,1)}, bf16[1,1664,512]{2,1,0:T(8,128)(2,1)}, bf16[1,1664,512]{2,1,0:T(8,128)(2,1)}) custom-call(s32[1]{0:T(128)} %bitcast.core.flag, bf16[1,832,768]{2,1,0:T(8,128)(2,1)} %copy-done.24, bf16[1,832,768]{2,1,0:T(8,128)(2,1)} %copy-done.25, bf16[712,1024]{1,0:T(8,128)(2,1)} %refs_4_.3, f32[1,1024]{1,0:T(1,128)} %bitcast.128, ...), custom_call_target="tpu_custom_call" | custom-call | flops 100000000 | bytes 100000 | tf_op jit(solution)/shard_map/front/pallas_call | solution.py:168
  62.7 57.5 %attend.1 = (bf16[1,832,512]{2,1,0:T(8,128)(2,1)}, bf16[1,832,512]{2,1,0:T(8,128)(2,1)}, f32[1,1664,512]{2,1,0:T(8,128)}) custom-call(s32[1]{0:T(128)} %bitcast.core.flag, bf16[1,1664,512]{2,1,0:T(8,128)(2,1)} %get-tuple-element.199.q_ref, bf16[1,1664,128]{2,1,0:T(8,128)(2,1)} %get-tuple-element.200.qx_ref, bf16[1,1664,512]{2,1,0:T(8,128)(2,1)} %get-tuple-element.201.kf_ref, ...), custom_call_target="tpu_custom_call" | custom-call | flops 100000000 | bytes 100000 | tf_op jit(solution)/shard_map/attend/pallas_call | solution.py:593
  126.9 35.4 %mid.1 = (bf16[1,832,1024]{2,1,0:T(8,128)(2,1)}, f32[1,832,1024]{2,1,0:T(8,128)}, bf16[1,832,512]{2,1,0:T(8,128)(2,1)}, bf16[1,832,512]{2,1,0:T(8,128)(2,1)}, bf...) custom-call(s32[1]{0:T(128)} %bitcast.core.flag, ...), custom_call_target="tpu_custom_call" | custom-call | flops 100000000 | bytes 100000 | tf_op jit(solution)/shard_map/mid/pallas_call | solution.py:261
  162.2 21.2 %outer.1 = bf16[4,1280,1024]{2,1,0:T(8,128)(2,1)} custom-call(s32[1]{0:T(128)} %bitcast.core.flag, bf16[832,1024]{1,0:T(8,128)(2,1)} %bitcast.116, bf16[832,2048]{1,0:T(8,128)(2,1)} %bitcast.113, bf16[832,512]{1,0:T(8,128)(2,1)} %bitcast.111, bf16[832,512]{1,0:T(8,128)(2,1)} %bitcast.115, bf16[832,2048]{1,0:T(8,128)(2,1)} %bitcast.114, ...), custom_call_target="tpu_custom_call" | custom-call | flops 100000000 | bytes 100000 | tf_op jit(solution)/shard_map/outer/pallas_call | solution.py:340
  188.7 83.9 %attend_back.2 = (bf16[1,1664,384]{2,1,0:T(8,128)(2,1)}, bf16[1,1664,384]{2,1,0:T(8,128)(2,1)}, bf16[1,1664,384]{2,1,0:T(8,128)(2,1)}, bf16[1,1664,384]{2,1,0:T(8,128)(2,1)}, bf16[1,1664,384]{2,1,0:T(8,128)(2,1)}) custom-call(s32[1]{0:T(128)} %bitcast.core.flag, bf16[1,1664,512]{2,1,0:T(8,128)(2,1)} %get-tuple-element.199.q_ref, ...), custom_call_target="tpu_custom_call" | custom-call | flops 100000000 | bytes 100000 | tf_op jit(solution)/shard_map/attend_back/pallas_call | solution.py:732
  272.7 15.9 %qkv_outer.2 = (bf16[2,3,256,384]{3,2,1,0:T(8,128)(2,1)}, bf16[2,3,256,384]{3,2,1,0:T(8,128)(2,1)}) custom-call(s32[2]{0:T(128)} %pad_add_fusion.2.place, bf16[2,1024,832]{2,1,0:T(8,128)(2,1)} %bitcast.107, bf16[1664,384]{1,0:T(8,128)(2,1)} %bitcast.99, bf16[1664,384]{1,0:T(8,128)(2,1)} %bitcast.100, bf16[1664,384]{1,0:T(8,128)(2,1)} %bitcast.101, ...), custom_call_target="tpu_custom_call" | custom-call | flops 100000000 | bytes 100000 | tf_op jit(solution)/shard_map/qkv_outer/pallas_call | solution.py:397
  300.1 30.8 %attend_back.3 = (bf16[1,1664,128]{2,1,0:T(8,128)(2,1)}, bf16[1,1664,128]{2,1,0:T(8,128)(2,1)}, bf16[1,1664,128]{2,1,0:T(8,128)(2,1)}, bf16[1,1664,128]{2,1,0:T(8,128)(2,1)}, bf16[1,1664,128]{2,1,0:T(8,128)(2,1)}) custom-call(s32[1]{0:T(128)} %bitcast.core.flag, bf16[1,1664,512]{2,1,0:T(8,128)(2,1)} %get-tuple-element.199.q_ref, ...), custom_call_target="tpu_custom_call" | custom-call | flops 100000000 | bytes 100000 | tf_op jit(solution)/shard_map/attend_back/pallas_call | solution.py:732
  333.0 7.0 %d_mod.3 = (bf16[1,832,1024]{2,1,0:T(8,128)(2,1)S(1)}, bf16[1,832,1024]{2,1,0:T(8,128)(2,1)}) custom-call(s32[1]{0:T(128)} %bitcast.core.flag, bf16[1,1664,384]{2,1,0:T(8,128)(2,1)S(1)} %copy-done, bf16[1,1664,128]{2,1,0:T(8,128)(2,1)S(1)} %copy-done.5, bf16[1,1664,384]{2,1,0:T(8,128)(2,1)S(1)} %copy-done.1, bf16[1,1664,128]{2,1,0:T(8,128)(2,1)S(1)} %copy-done.7, ...), custom_call_target="tpu_custom_call" | custom-call | flops 100000000 | bytes 100000 | tf_op jit(solution)/shard_map/d_mod/pallas_call | solution.py:442
  348.7 3.4 add_convert_fusion
  356.0 9.7 %d_mod.2 = (bf16[1,832,1024]{2,1,0:T(8,128)(2,1)}, bf16[1,832,1024]{2,1,0:T(8,128)(2,1)}) custom-call(s32[1]{0:T(128)} %bitcast.core.flag, bf16[1,1664,384]{2,1,0:T(8,128)(2,1)S(1)} %copy-done.2, bf16[1,1664,128]{2,1,0:T(8,128)(2,1)S(1)} %copy-done.9, bf16[1,1664,384]{2,1,0:T(8,128)(2,1)S(1)} %copy-done.3, bf16[1,1664,128]{2,1,0:T(8,128)(2,1)S(1)} %copy-done.11, ...), custom_call_target="tpu_custom_call" | custom-call | flops 100000000 | bytes 100000 | tf_op jit(solution)/shard_map/d_mod/pallas_call | solution.py:442
  367.5 2.7 collective-permute-start.11
  373.0 8.9 %qkv_outer.3 = (bf16[2,3,256,128]{3,2,1,0:T(8,128)(2,1)}, bf16[2,3,256,128]{3,2,1,0:T(8,128)(2,1)}) custom-call(s32[2]{0:T(128)} %pad_add_fusion.2.place, bf16[2,1024,832]{2,1,0:T(8,128)(2,1)} %bitcast.108, bf16[1664,128]{1,0:T(8,128)(2,1)} %bitcast.104, bf16[1664,128]{1,0:T(8,128)(2,1)} %bitcast.105, bf16[1664,128]{1,0:T(8,128)(2,1)} %bitcast.106, ...), custom_call_target="tpu_custom_call" | custom-call | flops 100000000 | bytes 100000 | tf_op jit(solution)/shard_map/qkv_outer/pallas_call | solution.py:397
  382.0 10.0 %collective-permute-done.11 = bf16[160,1024]{1,0:T(8,128)(2,1)S(1)} collective-permute-done((bf16[160,1024]{1,0:T(8,128)(2,1)S(1)}, bf16[160,1024]{1,0:T(8,128)(2,1)S(1)}, u32[]{:S(2)}, u32[]{:S(2)}) %collective-permute-start.11) | collective-permute-done | bytes 327712 | tf_op jit(solution)/shard_map/ppermute | solution.py:35
  394.4 7.5 %collective-permute-start.15 = (bf16[192,384]{1,0:T(8,128)(2,1)S(1)}, bf16[192,384]{1,0:T(8,128)(2,1)S(1)}, u32[]{:S(2)}, u32[]{:S(2)}) collective-permute-start(bf16[192,384]{1,0:T(8,128)(2,1)S(1)} %get-tuple-element.437), channel_id=1, source_target_pairs={{0,8},{8,16},{16,24},{24,0},{1,9},{9,17},{17,25},{25,1},{2,10},{10... | collective-permute-start | bytes 442376 | tf_op jit(solution)/shard_map/ppermute | solution.py:35
  407.8 6.1 %collective-permute-done.16 = bf16[192,384]{1,0:T(8,128)(2,1)S(1)} collective-permute-done((bf16[192,384]{1,0:T(8,128)(2,1)S(1)}, bf16[192,384]{1,0:T(8,128)(2,1)S(1)}, u32[]{:S(2)}, u32[]{:S(2)}) %collective-permute-start.16) | collective-permute-done | bytes 147488 | tf_op jit(solution)/shard_map/ppermute | solution.py:35
  415.5 4.4 collective-permute-start.19
  420.7 14.4 %tail.1 = (f32[1,832,100]{2,1,0:T(8,128)}, f32[1,832,100]{2,1,0:T(8,128)}, f32[1,832,512]{2,1,0:T(8,128)}, bf16[1,2,256,768]{3,2,1,0:T(8,128)(2,1)}, bf16[1,2,25...) custom-call(s32[2]{0:T(128)} %pad_add_fusion.2.place, bf16[1,832,768]{2,1,0:T(8,128)(2,1)} %copy-done.15, ...), custom_call_target="tpu_custom_call" | custom-call | flops 100000000 | bytes 100000 | tf_op jit(solution)/shard_map/tail/pallas_call | solution.py:498
  439.1 10.2 %collective-permute-done.20 = bf16[160,1024]{1,0:T(8,128)(2,1)S(1)} collective-permute-done((bf16[160,1024]{1,0:T(8,128)(2,1)}, bf16[160,1024]{1,0:T(8,128)(2,1)S(1)}, u32[]{:S(2)}, u32[]{:S(2)}) %collective-permute-start.20) | collective-permute-done | bytes 327712 | tf_op jit(solution)/shard_map/ppermute | solution.py:35
  464.6 3.1 collective-permute-done.26
  468.8 3.0 collective-permute-done.30
  483.3 8.5 %fusion.10 = f32[1,1024]{1,0:T(1,128)} fusion(f32[1,1024]{1,0:T(1,128)S(1)} %copy-done.42, bf16[1,1024]{1,0:T(2,128)(2,1)S(1)} %copy-done.41, bf16[6144,1]{0,1:T(2,128)(2,1)S(1)} %reshape.1406, bf16[1024,6144]{1,0:T(8,128)(2,1)} %param.29), kind=kOutput, calls=%fused_computation.167 | convolution fusion | flops 12590080 | bytes 12605440 | tf_op jit(solution)/shard_map/dot_general | solution.py:30
  491.9 11.7 %collective-permute-done.32 = f32[1,8448]{1,0:T(1,128)S(1)} collective-permute-done((f32[1,8448]{1,0:T(1,128)S(1)}, f32[1,8448]{1,0:T(1,128)S(1)}, u32[]{:S(2)}, u32[]{:S(2)}) %collective-permute-start.32) | collective-permute-done | bytes 33824 | tf_op jit(solution)/shard_map/ppermute | solution.py:40
  509.9 2.5 collective-permute-start.37
  512.4 2.6 collective-permute-start.40
  516.1 2.9 collective-permute-start.42
  520.0 3.3 collective-permute-done.40
  523.4 3.0 collective-permute-start.38
  528.1 4.2 collective-permute-start.46
  533.0 3.7 fusion.2
  (389 shorter events, 131.3 us)
Async XLA Ops:
  7.2 287.2 %reduce-scatter.2.cloned.1.call-start = ((), (), s32[]{:S(2)}) async-start(), calls=%async_computation.1 | async-start | bytes 13107200 | tf_op jit(solution)/shard_map/reduce_scatter | solution.py:870
  15.1 16.8 %collective-permute-start = (bf16[1,832,768]{2,1,0:T(8,128)(2,1)S(1)}, bf16[1,832,768]{2,1,0:T(8,128)(2,1)}, u32[]{:S(2)}, u32[]{:S(2)}) collective-permute-start(bf16[1,832,768]{2,1,0:T(8,128)(2,1)S(1)} %maximum_maximum_fusion.1.x0_ref.x_ref.refs_0_), channel_id=1, source_target_pairs={{0,1},{1,0},{2,3},{3,2},{4,5},{5,4},{6,7},{7,6},{8,9},{9,8},{10,11... | collective-permute-start | bytes 3833864 | tf_op jit(solution)/shard_map/ppermute | solution.py:40
  15.6 31.2 %collective-permute-start.1 = (bf16[1,832,768]{2,1,0:T(8,128)(2,1)S(1)}, bf16[1,832,768]{2,1,0:T(8,128)(2,1)S(1)}, u32[]{:S(2)}, u32[]{:S(2)}) collective-permute-start(bf16[1,832,768]{2,1,0:T(8,128)(2,1)S(1)} %maximum_maximum_fusion.1.x0_ref.x_ref.refs_0_), channel_id=1, source_target_pairs={{0,2},{2,0},{1,3},{3,1},{4,6},{6,4},{5,7},{7,5},{8,10},{10,8},{9,1... | collective-permute-start | bytes 3833864 | tf_op jit(solution)/shard_map/ppermute | solution.py:35
  296.9 34.1 %collective-permute-start.6 = (bf16[640,1024]{1,0:T(8,128)(2,1)}, bf16[640,1024]{1,0:T(8,128)(2,1)}, u32[]{:S(2)}, u32[]{:S(2)}) collective-permute-start(bf16[640,1024]{1,0:T(8,128)(2,1)} %dynamic-slice_bitcast_fusion), channel_id=1, source_target_pairs={{0,4},{4,0},{1,5},{5,1},{2,6},{6,2},{3,7},{7,3},{8,12},{12,8},{9,1... | collective-permute-start | bytes 3932168 | tf_op jit(solution)/shard_map/ppermute | solution.py:40
  298.6 32.3 %collective-permute-start.7 = (bf16[1536,384]{1,0:T(8,128)(2,1)}, bf16[1536,384]{1,0:T(8,128)(2,1)}, u32[]{:S(2)}, u32[]{:S(2)}) collective-permute-start(bf16[1536,384]{1,0:T(8,128)(2,1)} %bitcast.33), channel_id=1, source_target_pairs={{0,2},{2,0},{1,3},{3,1},{4,6},{6,4},{5,7},{7,5},{8,10},{10,8},{9,1... | collective-permute-start | bytes 3538952 | tf_op jit(solution)/shard_map/ppermute | solution.py:35
  352.1 39.9 %collective-permute-start.9 = (bf16[1,832,1024]{2,1,0:T(8,128)(2,1)}, bf16[1,832,1024]{2,1,0:T(8,128)(2,1)}, u32[]{:S(2)}, u32[]{:S(2)}) collective-permute-start(bf16[1,832,1024]{2,1,0:T(8,128)(2,1)} %add_convert_fusion), channel_id=1, source_target_pairs={{0,2},{2,0},{1,3},{3,1},{4,6},{6,4},{5,7},{7,5},{8,10},{10,8},{9,1... | collective-permute-start | bytes 5111816 | tf_op jit(solution)/shard_map/ppermute | solution.py:35
  365.8 16.2 %collective-permute-start.10 = (bf16[160,1024]{1,0:T(8,128)(2,1)S(1)}, bf16[160,1024]{1,0:T(8,128)(2,1)S(1)}, u32[]{:S(2)}, u32[]{:S(2)}) collective-permute-start(bf16[160,1024]{1,0:T(8,128)(2,1)S(1)} %get-tuple-element.427), channel_id=1, source_target_pairs={{0,8},{8,16},{16,24},{24,0},{1,9},{9,17},{17,25},{25,1},{2,10},{10... | collective-permute-start | bytes 983048 | tf_op jit(solution)/shard_map/ppermute | solution.py:35
  367.5 24.4 %collective-permute-start.11 = (bf16[160,1024]{1,0:T(8,128)(2,1)S(1)}, bf16[160,1024]{1,0:T(8,128)(2,1)S(1)}, u32[]{:S(2)}, u32[]{:S(2)}) collective-permute-start(bf16[160,1024]{1,0:T(8,128)(2,1)S(1)} %get-tuple-element.426), channel_id=1, source_target_pairs={{0,16},{8,24},{16,0},{24,8},{1,17},{9,25},{17,1},{25,9},{2,18},{10... | collective-permute-start | bytes 983048 | tf_op jit(solution)/shard_map/ppermute | solution.py:35
  370.2 21.7 %collective-permute-start.12 = (bf16[160,1024]{1,0:T(8,128)(2,1)S(1)}, bf16[160,1024]{1,0:T(8,128)(2,1)S(1)}, u32[]{:S(2)}, u32[]{:S(2)}) collective-permute-start(bf16[160,1024]{1,0:T(8,128)(2,1)S(1)} %get-tuple-element.425), channel_id=1, source_target_pairs={{0,24},{8,0},{16,8},{24,16},{1,25},{9,1},{17,9},{25,17},{2,26},{10... | collective-permute-start | bytes 983048 | tf_op jit(solution)/shard_map/ppermute | solution.py:35
  371.6 20.4 %collective-permute-start.13 = (bf16[768,384]{1,0:T(8,128)(2,1)}, bf16[768,384]{1,0:T(8,128)(2,1)}, u32[]{:S(2)}, u32[]{:S(2)}) collective-permute-start(bf16[768,384]{1,0:T(8,128)(2,1)} %constant_dynamic-slice_fusion.23), channel_id=1, source_target_pairs={{0,4},{4,0},{1,5},{5,1},{2,6},{6,2},{3,7},{7,3},{8,12},{12,8},{9,1... | collective-permute-start | bytes 1769480 | tf_op jit(solution)/shard_map/ppermute | solution.py:40
  392.8 21.2 %collective-permute-start.14 = (bf16[1,832,1024]{2,1,0:T(8,128)(2,1)}, bf16[1,832,1024]{2,1,0:T(8,128)(2,1)S(1)}, u32[]{:S(2)}, u32[]{:S(2)}) collective-permute-start(bf16[1,832,1024]{2,1,0:T(8,128)(2,1)} %get-tuple-element.247), channel_id=1, source_target_pairs={{0,1},{1,0},{2,3},{3,2},{4,5},{5,4},{6,7},{7,6},{8,9},{9,8},{10,11... | collective-permute-start | bytes 5111816 | tf_op jit(solution)/shard_map/ppermute | solution.py:40
  394.4 13.4 %collective-permute-start.15 = (bf16[192,384]{1,0:T(8,128)(2,1)S(1)}, bf16[192,384]{1,0:T(8,128)(2,1)S(1)}, u32[]{:S(2)}, u32[]{:S(2)}) collective-permute-start(bf16[192,384]{1,0:T(8,128)(2,1)S(1)} %get-tuple-element.437), channel_id=1, source_target_pairs={{0,8},{8,16},{16,24},{24,0},{1,9},{9,17},{17,25},{25,1},{2,10},{10... | collective-permute-start | bytes 442376 | tf_op jit(solution)/shard_map/ppermute | solution.py:35
  401.9 12.0 %collective-permute-start.16 = (bf16[192,384]{1,0:T(8,128)(2,1)S(1)}, bf16[192,384]{1,0:T(8,128)(2,1)S(1)}, u32[]{:S(2)}, u32[]{:S(2)}) collective-permute-start(bf16[192,384]{1,0:T(8,128)(2,1)S(1)} %get-tuple-element.436), channel_id=1, source_target_pairs={{0,16},{8,24},{16,0},{24,8},{1,17},{9,25},{17,1},{25,9},{2,18},{10... | collective-permute-start | bytes 442376 | tf_op jit(solution)/shard_map/ppermute | solution.py:35
  403.6 10.3 %collective-permute-start.17 = (bf16[192,384]{1,0:T(8,128)(2,1)S(1)}, bf16[192,384]{1,0:T(8,128)(2,1)S(1)}, u32[]{:S(2)}, u32[]{:S(2)}) collective-permute-start(bf16[192,384]{1,0:T(8,128)(2,1)S(1)} %get-tuple-element.435), channel_id=1, source_target_pairs={{0,24},{8,0},{16,8},{24,16},{1,25},{9,1},{17,9},{25,17},{2,26},{10... | collective-permute-start | bytes 442376 | tf_op jit(solution)/shard_map/ppermute | solution.py:35
  413.9 35.3 %collective-permute-start.22 = (bf16[1536,128]{1,0:T(8,128)(2,1)}, bf16[1536,128]{1,0:T(8,128)(2,1)}, u32[]{:S(2)}, u32[]{:S(2)}) collective-permute-start(bf16[1536,128]{1,0:T(8,128)(2,1)} %bitcast.41), channel_id=1, source_target_pairs={{0,2},{2,0},{1,3},{3,1},{4,6},{6,4},{5,7},{7,5},{8,10},{10,8},{9,1... | collective-permute-start | bytes 1179656 | tf_op jit(solution)/shard_map/ppermute | solution.py:35
  415.5 23.6 %collective-permute-start.19 = (bf16[160,1024]{1,0:T(8,128)(2,1)}, bf16[160,1024]{1,0:T(8,128)(2,1)S(1)}, u32[]{:S(2)}, u32[]{:S(2)}) collective-permute-start(bf16[160,1024]{1,0:T(8,128)(2,1)} %add_convert_fusion.5), channel_id=1, source_target_pairs={{0,24},{8,0},{16,8},{24,16},{1,25},{9,1},{17,9},{25,17},{2,26},{10... | collective-permute-start | bytes 983048 | tf_op jit(solution)/shard_map/ppermute | solution.py:35
  419.9 29.4 %collective-permute-start.20 = (bf16[160,1024]{1,0:T(8,128)(2,1)}, bf16[160,1024]{1,0:T(8,128)(2,1)S(1)}, u32[]{:S(2)}, u32[]{:S(2)}) collective-permute-start(bf16[160,1024]{1,0:T(8,128)(2,1)} %add_convert_fusion.5), channel_id=1, source_target_pairs={{0,16},{8,24},{16,0},{24,8},{1,17},{9,25},{17,1},{25,9},{2,18},{10... | collective-permute-start | bytes 983048 | tf_op jit(solution)/shard_map/ppermute | solution.py:35
  420.6 28.6 %collective-permute-start.21 = (bf16[160,1024]{1,0:T(8,128)(2,1)}, bf16[160,1024]{1,0:T(8,128)(2,1)S(1)}, u32[]{:S(2)}, u32[]{:S(2)}) collective-permute-start(bf16[160,1024]{1,0:T(8,128)(2,1)} %add_convert_fusion.5), channel_id=1, source_target_pairs={{0,8},{8,16},{16,24},{24,0},{1,9},{9,17},{17,25},{25,1},{2,10},{10... | collective-permute-start | bytes 983048 | tf_op jit(solution)/shard_map/ppermute | solution.py:35
  452.2 16.0 %collective-permute-start.27 = (bf16[192,384]{1,0:T(8,128)(2,1)}, bf16[192,384]{1,0:T(8,128)(2,1)S(1)}, u32[]{:S(2)}, u32[]{:S(2)}) collective-permute-start(bf16[192,384]{1,0:T(8,128)(2,1)} %add_convert_fusion.8), channel_id=1, source_target_pairs={{0,24},{8,0},{16,8},{24,16},{1,25},{9,1},{17,9},{25,17},{2,26},{10... | collective-permute-start | bytes 442376 | tf_op jit(solution)/shard_map/ppermute | solution.py:35
  452.2 16.6 %collective-permute-start.28 = (bf16[192,384]{1,0:T(8,128)(2,1)}, bf16[192,384]{1,0:T(8,128)(2,1)}, u32[]{:S(2)}, u32[]{:S(2)}) collective-permute-start(bf16[192,384]{1,0:T(8,128)(2,1)} %add_convert_fusion.8), channel_id=1, source_target_pairs={{0,16},{8,24},{16,0},{24,8},{1,17},{9,25},{17,1},{25,9},{2,18},{10... | collective-permute-start | bytes 442376 | tf_op jit(solution)/shard_map/ppermute | solution.py:35
  453.4 15.4 %collective-permute-start.29 = (bf16[192,384]{1,0:T(8,128)(2,1)}, bf16[192,384]{1,0:T(8,128)(2,1)}, u32[]{:S(2)}, u32[]{:S(2)}) collective-permute-start(bf16[192,384]{1,0:T(8,128)(2,1)} %add_convert_fusion.8), channel_id=1, source_target_pairs={{0,8},{8,16},{16,24},{24,0},{1,9},{9,17},{17,25},{25,1},{2,10},{10... | collective-permute-start | bytes 442376 | tf_op jit(solution)/shard_map/ppermute | solution.py:35
  467.7 47.4 %collective-permute-start.44 = (bf16[640,1024]{1,0:T(8,128)(2,1)S(1)}, bf16[640,1024]{1,0:T(8,128)(2,1)S(1)}, u32[]{:S(2)}, u32[]{:S(2)}) collective-permute-start(bf16[640,1024]{1,0:T(8,128)(2,1)S(1)} %constant_dynamic-slice_fusion.14), channel_id=1, source_target_pairs={{0,4},{4,0},{1,5},{5,1},{2,6},{6,2},{3,7},{7,3},{8,12},{12,8},{9,1... | collective-permute-start | bytes 3932168 | tf_op jit(solution)/shard_map/ppermute | solution.py:40
  478.1 29.6 %collective-permute-start.31 = (bf16[128,768]{1,0:T(8,128)(2,1)S(1)}, bf16[128,768]{1,0:T(8,128)(2,1)S(1)}, u32[]{:S(2)}, u32[]{:S(2)}) collective-permute-start(bf16[128,768]{1,0:T(8,128)(2,1)S(1)} %constant_dynamic-slice_fusion.11), channel_id=1, source_target_pairs={{0,4},{4,0},{1,5},{5,1},{2,6},{6,2},{3,7},{7,3},{8,12},{12,8},{9,1... | collective-permute-start | bytes 589832 | tf_op jit(solution)/shard_map/ppermute | solution.py:40
  480.1 23.5 %collective-permute-start.32 = (f32[1,8448]{1,0:T(1,128)S(1)}, f32[1,8448]{1,0:T(1,128)S(1)}, u32[]{:S(2)}, u32[]{:S(2)}) collective-permute-start(f32[1,8448]{1,0:T(1,128)S(1)} %pad_maximum_fusion.12), channel_id=1, source_target_pairs={{0,4},{4,0},{1,5},{5,1},{2,6},{6,2},{3,7},{7,3},{8,12},{12,8},{9,1... | collective-permute-start | bytes 101384 | tf_op jit(solution)/shard_map/ppermute | solution.py:40
  480.7 24.8 %collective-permute-start.33 = (bf16[192,128]{1,0:T(8,128)(2,1)S(1)}, bf16[192,128]{1,0:T(8,128)(2,1)S(1)}, u32[]{:S(2)}, u32[]{:S(2)}) collective-permute-start(bf16[192,128]{1,0:T(8,128)(2,1)S(1)} %get-tuple-element.455), channel_id=1, source_target_pairs={{0,8},{8,16},{16,24},{24,0},{1,9},{9,17},{17,25},{25,1},{2,10},{10... | collective-permute-start | bytes 147464 | tf_op jit(solution)/shard_map/ppermute | solution.py:35
  481.2 24.9 %collective-permute-start.34 = (bf16[192,128]{1,0:T(8,128)(2,1)S(1)}, bf16[192,128]{1,0:T(8,128)(2,1)S(1)}, u32[]{:S(2)}, u32[]{:S(2)}) collective-permute-start(bf16[192,128]{1,0:T(8,128)(2,1)S(1)} %get-tuple-element.454), channel_id=1, source_target_pairs={{0,16},{8,24},{16,0},{24,8},{1,17},{9,25},{17,1},{25,9},{2,18},{10... | collective-permute-start | bytes 147464 | tf_op jit(solution)/shard_map/ppermute | solution.py:35
  505.5 22.6 %collective-permute-start.45 = (bf16[768,384]{1,0:T(8,128)(2,1)S(1)}, bf16[768,384]{1,0:T(8,128)(2,1)S(1)}, u32[]{:S(2)}, u32[]{:S(2)}) collective-permute-start(bf16[768,384]{1,0:T(8,128)(2,1)S(1)} %constant_dynamic-slice_fusion.12), channel_id=1, source_target_pairs={{0,4},{4,0},{1,5},{5,1},{2,6},{6,2},{3,7},{7,3},{8,12},{12,8},{9,1... | collective-permute-start | bytes 1769480 | tf_op jit(solution)/shard_map/ppermute | solution.py:40
  509.9 10.1 %collective-permute-start.37 = (bf16[32,768]{1,0:T(8,128)(2,1)S(1)}, bf16[32,768]{1,0:T(8,128)(2,1)S(1)}, u32[]{:S(2)}, u32[]{:S(2)}) collective-permute-start(bf16[32,768]{1,0:T(8,128)(2,1)S(1)} %get-tuple-element.450), channel_id=1, source_target_pairs={{0,16},{8,24},{16,0},{24,8},{1,17},{9,25},{17,1},{25,9},{2,18},{10... | collective-permute-start | bytes 147464 | tf_op jit(solution)/shard_map/ppermute | solution.py:35
  512.4 10.9 %collective-permute-start.40 = (f32[4,8448]{1,0:T(4,128)S(1)}, f32[4,8448]{1,0:T(4,128)S(1)}, u32[]{:S(2)}, u32[]{:S(2)}) collective-permute-start(f32[4,8448]{1,0:T(4,128)S(1)} %pad_maximum_fusion.10), channel_id=1, source_target_pairs={{0,16},{8,24},{16,0},{24,8},{1,17},{9,25},{17,1},{25,9},{2,18},{10... | collective-permute-start | bytes 405512 | tf_op jit(solution)/shard_map/ppermute | solution.py:40
  515.1 13.0 %collective-permute-start.41 = (bf16[192,128]{1,0:T(8,128)(2,1)S(1)}, bf16[192,128]{1,0:T(8,128)(2,1)S(1)}, u32[]{:S(2)}, u32[]{:S(2)}) collective-permute-start(bf16[192,128]{1,0:T(8,128)(2,1)S(1)} %add_convert_fusion.10), channel_id=1, source_target_pairs={{0,24},{8,0},{16,8},{24,16},{1,25},{9,1},{17,9},{25,17},{2,26},{10... | collective-permute-start | bytes 147464 | tf_op jit(solution)/shard_map/ppermute | solution.py:35
  516.1 12.0 %collective-permute-start.42 = (bf16[192,128]{1,0:T(8,128)(2,1)S(1)}, bf16[192,128]{1,0:T(8,128)(2,1)S(1)}, u32[]{:S(2)}, u32[]{:S(2)}) collective-permute-start(bf16[192,128]{1,0:T(8,128)(2,1)S(1)} %add_convert_fusion.10), channel_id=1, source_target_pairs={{0,16},{8,24},{16,0},{24,8},{1,17},{9,25},{17,1},{25,9},{2,18},{10... | collective-permute-start | bytes 147464 | tf_op jit(solution)/shard_map/ppermute | solution.py:35
  528.1 12.3 %collective-permute-start.46 = (bf16[32,768]{1,0:T(8,128)(2,1)S(1)}, bf16[32,768]{1,0:T(8,128)(2,1)S(1)}, u32[]{:S(2)}, u32[]{:S(2)}) collective-permute-start(bf16[32,768]{1,0:T(8,128)(2,1)S(1)} %add_convert_fusion.9), channel_id=1, source_target_pairs={{0,24},{8,0},{16,8},{24,16},{1,25},{9,1},{17,9},{25,17},{2,26},{10... | collective-permute-start | bytes 147464 | tf_op jit(solution)/shard_map/ppermute | solution.py:35
  (72 other events, 694.4 us)
Sparse Core Ops, SparseCore 0:
  183.5 86.8 reduce-scatter.1

commit v3 on v2

--- a/solution.py
+++ b/solution.py
@@ -15,7 +15,7 @@
 F32 = jnp.float32
 BF = jnp.bfloat16
 MIB = 2**20
-QUICK = pl.CostEstimate(flops=10**8, bytes_accessed=10**5, transcendentals=0)
+QUICK = pl.CostEstimate(flops=1, bytes_accessed=1, transcendentals=0)
 
 
 def dot_nn(a, b):
@@ -38,6 +38,16 @@
 def flip(v, axis, bit):
     size = lax.axis_size(axis)
     return lax.ppermute(v, axis, [(i, i ^ bit) for i in range(size)])
+
+
+def gray(i):
+    return i ^ (i >> 1)
+
+
+def near_flip(v, axis, bit):
+    size = lax.axis_size(axis)
+    place = {gray(i): i for i in range(size)}
+    return lax.ppermute(v, axis, [(i, place[gray(i) ^ bit]) for i in range(size)])
 
 
 def bits(axis):
@@ -82,32 +92,26 @@
     return total([part_of(t, lax.axis_index("ry"), 2) for t in terms] + [recv])
 
 
-def rows_turn(mine):
-    z, deep = lax.axis_index("rz"), lax.axis_size("rz")
-    got = [shift(part_of(mine, (z + t) % deep, deep), "rz", t) for t in range(1, deep)]
-    return [part_of(mine, z, deep)] + got
-
-
-def rows_spread(block):
-    return [shift(block, "rz", t) for t in range(lax.axis_size("rz") - 1, 0, -1)] + [block]
-
-
-def rows_half(ring):
-    z, deep = lax.axis_index("rz"), lax.axis_size("rz")
-    ring = jnp.concatenate(ring + ring[:-1], axis=0)
-    size = ring.shape[0] // (2 * deep - 1)
-    return lax.dynamic_slice_in_dim(ring, (deep - 1 - z) * size, deep * size, 0)
-
-
-def rows_join(mine):
-    y = lax.axis_index("ry")
-    recv = flip(mine, "ry", 1)
-    return jnp.where(y == 0, mine, recv), jnp.where(y == 0, recv, mine)
-
-
-def sum_rows(terms):
-    recv = flip(rows_give(terms), "ry", 1)
-    return rows_join(rows_half(rows_spread(total(rows_turn(rows_mine(terms, recv))))))
+def side(axis, bit):
+    return (gray(lax.axis_index(axis)) // bit) % 2
+
+
+def give_half(v, axis, bit):
+    return part_of(v, 1 - side(axis, bit), 2)
+
+
+def keep_half(v, recv, axis, bit):
+    return total([part_of(v, side(axis, bit), 2), recv])
+
+
+def join_halves(mine, recv, axis, bit):
+    low = side(axis, bit) == 0
+    return jnp.concatenate([jnp.where(low, mine, recv), jnp.where(low, recv, mine)], axis=0)
+
+
+def by_row(mine, recv):
+    low = lax.axis_index("ry") == 0
+    return jnp.concatenate([jnp.where(low, mine, recv), jnp.where(low, recv, mine)], axis=0)
 
 
 def sum_chips(blocks):
@@ -179,10 +183,34 @@
         ),
         out_shape=[jax.ShapeDtypeStruct((rows, 2, model, span), BF)]
         + [jax.ShapeDtypeStruct((rows, n, half), BF)] * len(parts),
-        compiler_params=pltpu.CompilerParams(vmem_limit_bytes=56 * MIB),
+        compiler_params=pltpu.CompilerParams(vmem_limit_bytes=60 * MIB),
         cost_estimate=QUICK,
         name="front",
     )(core, x0, x1, w_in, b_in, emb, *w_args, angles)
+
+
+def ada_kernel(t_ref, w_ref, out_ref, *, turned):
+    out_ref[...] = (dot_nt if turned else dot_nn)(t_ref[...], w_ref[...])
+
+
+def ada(t, w, turned):
+    rows = t.shape[0]
+    n = w.shape[0] if turned else w.shape[1]
+    step = 256 if turned else 1024
+    block = (step, w.shape[1]) if turned else (w.shape[0], step)
+    return pl.pallas_call(
+        functools.partial(ada_kernel, turned=turned),
+        grid=(n // step,),
+        in_specs=[
+            pl.BlockSpec(t.shape, lambda i: (0, 0)),
+            pl.BlockSpec(block, lambda i: (i, 0) if turned else (0, i)),
+        ],
+        out_specs=pl.BlockSpec((rows, step), lambda i: (0, i)),
+        out_shape=jax.ShapeDtypeStruct((rows, n), F32),
+        compiler_params=pltpu.CompilerParams(vmem_limit_bytes=60 * MIB),
+        cost_estimate=QUICK,
+        name="ada",
+    )(t, w)
 
 
 def mid_kernel(
@@ -284,7 +312,7 @@
             jax.ShapeDtypeStruct((rows, 8, model), F32),
             jax.ShapeDtypeStruct((rows, 1, hidden), F32),
         ],
-        compiler_params=pltpu.CompilerParams(vmem_limit_bytes=62 * MIB),
+        compiler_params=pltpu.CompilerParams(vmem_limit_bytes=60 * MIB),
         cost_estimate=QUICK,
         name="mid",
     )(core, x, o_mine, o_other, g, valid, emb, w_in, b_in, w_out, w_out, b_out, w_up, b_up, w_down, b_down)
@@ -359,8 +387,9 @@
 def qkv_outer_kernel(place, *refs, far):
     near_ref, dq_ref, dk_ref, dv_ref = refs[:4]
     far_refs = refs[4 : 4 + 3 * far]
-    keep_ref, give_ref = refs[-2:]
-    chips, _, rows, width = keep_ref.shape
+    keep_ref, give_ref, sums_ref = refs[-3:]
+    chips, rows, width = keep_ref.shape
+    width //= 3
     span = near_ref.shape[2]
     acc_q, acc = None, None
     add = lambda a, b: b if a is None else a + b
@@ -376,6 +405,13 @@
             both = jnp.concatenate([dkf_ref[cut, :], dvf_ref[cut, :]], axis=1)
             acc = add(acc, dot_nn(mod_ref[i], both))
     parts = [acc_q.astype(BF), acc[:, :width].astype(BF), acc[:, width:].astype(BF)]
+    column = lambda ref: jnp.sum(ref[...].astype(F32), axis=0, keepdims=True)
+    sums = [column(dq_ref), column(dk_ref), column(dv_ref)]
+    for f in range(far):
+        for j in (1, 2):
+            sums[j] = sums[j] + column(far_refs[3 * f + j])
+    for j in range(3):
+        sums_ref[:, j * width : (j + 1) * width] = jnp.broadcast_to(sums[j], (8, width))
     for side in range(2):
         for out_ref, core in ((keep_ref, side), (give_ref, 1 - side)):
             @pl.when(place[1] == core)
@@ -383,28 +419,32 @@
                 for n in range(side, 2 * chips, 2):
                     chip = (n // 2 + chips - place[0]) % chips
                     for j, part in enumerate(parts):
-                        out_ref[chip, j] = part[n * rows : (n + 1) * rows]
+                        out_ref[chip, :, j * width : (j + 1) * width] = part[
+                            n * rows : (n + 1) * rows
+                        ]
 
 
 def qkv_outer(place, mod_near, dq, dk, dv, far):
     model = mod_near.shape[1]
     width = dq.shape[1]
     chips = lax.axis_size("sx")
-    shape = (chips, 3, model // (2 * chips), width)
+    shape = (chips, model // (2 * chips), 3 * width)
     args = [mod_near, dq, dk, dv]
+    whole = lambda a: pl.BlockSpec(a.shape, lambda i, c: (0,) * a.ndim)
     for item in far:
         args += list(item)
+    specs = [whole(a) for a in args]
     return pl.pallas_call(
         functools.partial(qkv_outer_kernel, far=len(far)),
         grid_spec=pltpu.PrefetchScalarGridSpec(
             num_scalar_prefetch=1,
             grid=(1,),
-            in_specs=[
-                pl.BlockSpec(a.shape, lambda i, c, n=a.ndim: (0,) * n) for a in args
-            ],
-            out_specs=[pl.BlockSpec(shape, lambda i, c: (0,) * 4)] * 2,
+            in_specs=specs,
+            out_specs=[pl.BlockSpec(shape, lambda i, c: (0,) * 3)] * 2
+            + [pl.BlockSpec((8, 3 * width), lambda i, c: (0, 0))],
         ),
-        out_shape=[jax.ShapeDtypeStruct(shape, BF)] * 2,
+        out_shape=[jax.ShapeDtypeStruct(shape, BF)] * 2
+        + [jax.ShapeDtypeStruct((8, 3 * width), F32)],
         compiler_params=pltpu.CompilerParams(vmem_limit_bytes=60 * MIB),
         cost_estimate=QUICK,
         name="qkv_outer",
@@ -448,78 +488,121 @@
             out_specs=[out, out],
         ),
         out_shape=[jax.ShapeDtypeStruct((rows, span, model), BF)] * 2,
-        compiler_params=pltpu.CompilerParams(vmem_limit_bytes=48 * MIB),
+        compiler_params=pltpu.CompilerParams(vmem_limit_bytes=60 * MIB),
         cost_estimate=QUICK,
         name="d_mod",
     )(core, *arrays, *[w_qkv] * len(grads))
 
 
-def tail_kernel(place, *refs, far, mel):
-    x_ref, dres_ref, emb_ref, keep_ref, win_ref, bin_ref, near_ref, recv_ref = refs[:8]
-    far_refs = refs[8 : 8 + far]
-    noisy_ref, cond_ref, text_ref, keep_out, send_out, sums_ref, turned = refs[8 + far :]
+def norm_back(normed, inv, upstream):
+    mean = lambda v: jnp.mean(v, axis=1, keepdims=True)
+    return inv * (upstream - mean(upstream) - normed * mean(upstream * normed))
+
+
+def first_norm(x_ref, win_ref, bin_ref):
+    resid = dot_nn(x_ref[:, : win_ref.shape[0]], win_ref[...]) + bin_ref[...]
+    center = resid - jnp.mean(resid, axis=1, keepdims=True)
+    inv = lax.rsqrt(jnp.mean(center * center, axis=1, keepdims=True) + EPS)
+    return center * inv, inv
+
+
+def in_outer_kernel(place, dres_ref, emb_ref, win_ref, bin_ref, *refs, blocks):
+    ins, refs = [refs[3 * n : 3 * n + 3] for n in range(blocks)], refs[3 * blocks :]
+    keep_out, give_out, sums_ref = refs[:3]
+    far_out, turned, joined = refs[3:-2], refs[-2], refs[-1]
+    span = dres_ref.shape[0]
     total = lambda v: jnp.sum(v, axis=0, keepdims=True)
-    mean = lambda v: jnp.mean(v, axis=1, keepdims=True)
-    width = win_ref.shape[0]
-    resid = dot_nn(x_ref[:, :width], win_ref[...]) + bin_ref[...]
-    center = resid - mean(resid)
-    inv = lax.rsqrt(mean(center * center) + EPS)
-    normed = center * inv
-    d = near_ref[...].astype(F32) + recv_ref[...].astype(F32)
-    for ref in far_refs:
-        d = d + ref[...].astype(F32)
-    sums_ref[0:1, :] = total(d)
-    sums_ref[1:2, :] = total(d * normed)
-    u = d * (1.0 + emb_ref[1:2, :])
-    d_res = (dres_ref[...] + inv * (u - mean(u) - normed * mean(u * normed))).astype(BF)
-    sums_ref[2:3, :] = total(d_res.astype(F32))
-    turned[...] = d_res.T
+    sums_ref[...] = jnp.zeros(sums_ref.shape, F32)
+    for n, (x_ref, mine_ref, recv_ref) in enumerate(ins):
+        cut = slice(n * span, (n + 1) * span)
+        normed, inv = first_norm(x_ref, win_ref, bin_ref)
+        d = mine_ref[...].astype(F32) + recv_ref[...].astype(F32)
+        if n:
+            far_out[n - 1][...] = d.astype(BF)
+        sums_ref[0:1, :] += total(d)
+        sums_ref[1:2, :] += total(d * normed)
+        d = norm_back(normed, inv, d * (1.0 + emb_ref[1:2, :]))
+        d = (d if n else d + dres_ref[...]).astype(BF)
+        sums_ref[2:3, :] += total(d.astype(F32))
+        turned[:, cut] = d.T
+        joined[cut, :] = x_ref[...]
     chips, rows = keep_out.shape[0], keep_out.shape[1]
     for t in range(chips):
         block = ((place[0] + t) % chips) * 2
-        for out, core in ((send_out, 1 - place[1]), (keep_out, place[1])):
+        for out, core in ((give_out, 1 - place[1]), (keep_out, place[1])):
             at = pl.ds(pl.multiple_of((block + core) * rows, rows), rows)
-            out[t] = dot_nn(turned[at, :], x_ref[...]).astype(BF)
-    d_in = dot_nt(d_res, win_ref[...])
-    noisy_ref[...] = d_in[:, :mel]
-    cond_ref[...] = d_in[:, mel : 2 * mel] * keep_ref[:, 0:1]
-    text_ref[...] = d_in[:, 2 * mel : width] * keep_ref[:, 1:2]
-
-
-def tail(place, x, d_res, emb, keep, w_in, b_in, near, recv, far, mel):
+            out[t] = dot_nn(turned[at, :], joined[...]).astype(BF)
+
+
+def in_outer(place, blocks, d_res, emb, w_in, b_in):
+    x = blocks[0][0]
     rows, span, width = x.shape
     model = w_in.shape[1]
     chips = lax.axis_size("sx")
     block = model // (2 * chips)
     frame = lambda w: pl.BlockSpec((None, span, w), lambda r, c: (r, 0, 0))
     whole = lambda a, b: pl.BlockSpec((a, b), lambda r, c: (0, 0))
-    blocks = pl.BlockSpec((None, chips, block, width), lambda r, c: (r, 0, 0, 0))
-    shape = lambda w: jax.ShapeDtypeStruct((rows, span, w), F32)
+    out = pl.BlockSpec((None, chips, block, width), lambda r, c: (r, 0, 0, 0))
     return pl.pallas_call(
-        functools.partial(tail_kernel, far=len(far), mel=mel),
+        functools.partial(in_outer_kernel, blocks=len(blocks)),
         grid_spec=pltpu.PrefetchScalarGridSpec(
             num_scalar_prefetch=1,
             grid=(rows,),
             in_specs=[
-                frame(width), frame(model), pl.BlockSpec((None, 6, model), lambda r, c: (r, 0, 0)),
-                frame(2), whole(*w_in.shape), whole(1, model), frame(model), frame(model),
-            ] + [frame(model)] * len(far),
-            out_specs=[
-                frame(mel), frame(mel), frame(w_in.shape[0] - 2 * mel), blocks, blocks,
-                pl.BlockSpec((None, 8, model), lambda r, c: (r, 0, 0)),
+                frame(model), pl.BlockSpec((None, 6, model), lambda r, c: (r, 0, 0)),
+                whole(*w_in.shape), whole(1, model),
+            ] + [frame(width), frame(model), frame(model)] * len(blocks),
+            out_specs=[out, out, pl.BlockSpec((None, 8, model), lambda r, c: (r, 0, 0))]
+            + [frame(model)] * (len(blocks) - 1),
+            scratch_shapes=[
+                pltpu.VMEM((model, len(blocks) * span), BF),
+                pltpu.VMEM((len(blocks) * span, width), BF),
             ],
-            scratch_shapes=[pltpu.VMEM((model, span), BF)],
         ),
         out_shape=[
-            shape(mel), shape(mel), shape(w_in.shape[0] - 2 * mel),
             jax.ShapeDtypeStruct((rows, chips, block, width), BF),
             jax.ShapeDtypeStruct((rows, chips, block, width), BF),
             jax.ShapeDtypeStruct((rows, 8, model), F32),
-        ],
+        ] + [jax.ShapeDtypeStruct((rows, span, model), BF)] * (len(blocks) - 1),
         compiler_params=pltpu.CompilerParams(vmem_limit_bytes=60 * MIB),
         cost_estimate=QUICK,
-        name="tail",
-    )(place, x, d_res, emb, keep, w_in, b_in, near, recv, *far)
+        name="in_outer",
+    )(place, d_res, emb, w_in, b_in, *[a for b in blocks for a in b])
+
+
+def d_in_kernel(*refs, parts, mel):
+    x_ref, dres_ref, emb_ref, keep_ref, win_ref, bin_ref = refs[:6]
+    noisy_ref, cond_ref, text_ref = refs[6 + parts :]
+    normed, inv = first_norm(x_ref, win_ref, bin_ref)
+    d = refs[6][...].astype(F32)
+    for ref in refs[7 : 6 + parts]:
+        d = d + ref[...].astype(F32)
+    d = norm_back(normed, inv, d * (1.0 + emb_ref[1:2, :]))
+    d_in = dot_nt((dres_ref[...] + d).astype(BF), win_ref[...])
+    noisy_ref[...] = d_in[:, :mel]
+    cond_ref[...] = d_in[:, mel : 2 * mel] * keep_ref[:, 0:1]
+    text_ref[...] = d_in[:, 2 * mel :] * keep_ref[:, 1:2]
+
+
+def d_in(x, d_res, emb, keep, w_in, b_in, parts, mel):
+    rows, span, width = x.shape
+    model = w_in.shape[1]
+    frame = lambda w: pl.BlockSpec((None, span, w), lambda r: (r, 0, 0))
+    whole = lambda a, b: pl.BlockSpec((a, b), lambda r: (0, 0))
+    sizes = [mel, mel, w_in.shape[0] - 2 * mel]
+    return pl.pallas_call(
+        functools.partial(d_in_kernel, parts=len(parts), mel=mel),
+        grid=(rows,),
+        in_specs=[
+            frame(width), frame(model), pl.BlockSpec((None, 6, model), lambda r: (r, 0, 0)),
+            frame(2), whole(*w_in.shape), whole(1, model),
+        ] + [frame(model)] * len(parts),
+        out_specs=[frame(w) for w in sizes],
+        out_shape=[jax.ShapeDtypeStruct((rows, span, w), F32) for w in sizes],
+        compiler_params=pltpu.CompilerParams(vmem_limit_bytes=60 * MIB),
+        cost_estimate=QUICK,
+        name="d_in",
+    )(x, d_res, emb, keep, w_in, b_in, *parts)
 
 
 def rows_of(refs, start, stop):
@@ -624,18 +707,26 @@
     ).astype(BF)
 
 
-def attend_back_kernel(
-    flag, q_ref, qx_ref, kf_ref, kn_ref, kxf_ref, kxn_ref, vf_ref, vn_ref,
-    om_ref, oo_ref, dom_ref, doo_ref, l_ref, angf_ref, angn_ref,
-    dq_ref, dkf_ref, dkn_ref, dvf_ref, dvn_ref,
-    q2, d2, k2, v2, kk, qt, dt, p_s, s_s, dq_s, dk_s, dv_s,
-):
+def attend_back_kernel(flag, *refs, blocks, start, finish):
+    q_ref, qx_ref, om_ref, oo_ref, dom_ref, doo_ref, l_ref = refs[:7]
+    refs = refs[7:]
+    keys_in, refs = [refs[4 * n : 4 * n + 4] for n in range(blocks)], refs[4 * blocks :]
+    if finish:
+        angle_ref, refs = refs[0], refs[1:]
+    if not start:
+        before_ref, refs = refs[0], refs[1:]
+    dq_ref, refs = refs[0], refs[1:]
+    keys_out, refs = [refs[2 * n : 2 * n + 2] for n in range(blocks)], refs[2 * blocks :]
+    q2, d2, k2, v2, kk, qt, dt, p_s, s_s, dq_s, dk_s, dv_s = refs
     m, n = q_ref.shape[0], kk.shape[0]
-    far = kf_ref.shape[0]
     span = om_ref.shape[0]
     lane = lax.broadcasted_iota(jnp.int32, (1, 128), 1)
     zero = jnp.zeros((), BF)
     steps = [(c, min(c + 256, n)) for c in range(0, n, 256)] if n % 128 == 0 else [(0, n)]
+    cuts, at = [], 0
+    for k_ref, _, _, _ in keys_in:
+        cuts.append(slice(at, at + k_ref.shape[0]))
+        at += k_ref.shape[0]
     apart = pl.when(flag[0] >= 0)
 
     @apart
@@ -666,10 +757,7 @@
         @apart
         def _():
             less = (lane - 64 * h >= 8) & (lane - 64 * h < 11)
-            for at, k_ref, kx_ref, v_ref in (
-                (0, kf_ref, kxf_ref, vf_ref), (far, kn_ref, kxn_ref, vn_ref)
-            ):
-                cut = slice(at, at + k_ref.shape[0])
+            for cut, (k_ref, kx_ref, v_ref, _) in zip(cuts, keys_in):
                 keys = jnp.where(mine, k_ref[...], zero)
                 kk[cut, :] = keys
                 k2[:128, cut] = keys.T
@@ -690,10 +778,13 @@
         def _():
             acc = dot_nn(s_s[...], kk[...])
             if h == 0:
-                dq_s[...] = acc
+                dq_s[...] = acc if start else acc + before_ref[...]
             if h == 1:
-                cos, sin = wide_tables(angn_ref)
-                dq_ref[...] = turn((dq_s[...] + acc) * 0.125, cos, -sin, lane).astype(BF)
+                acc = dq_s[...] + acc
+                if finish:
+                    cos, sin = wide_tables(angle_ref)
+                    acc = turn(acc * 0.125, cos, -sin, lane)
+                dq_ref[...] = acc.astype(dq_ref.dtype)
 
         @apart
         def _():
@@ -703,10 +794,7 @@
 
     @apart
     def _():
-        for at, ang_ref, dk_ref, dv_ref in (
-            (0, angf_ref, dkf_ref, dvf_ref), (far, angn_ref, dkn_ref, dvn_ref)
-        ):
-            cut = slice(at, at + dk_ref.shape[0])
+        for cut, (_, _, _, ang_ref), (dk_ref, dv_ref) in zip(cuts, keys_in, keys_out):
             cos, sin = ang_ref[0], ang_ref[1]
             turned = []
             for h in range(2):
@@ -716,29 +804,38 @@
             dv_ref[...] = dv_s[:, cut].astype(BF).T
 
 
-def attend_back(
-    core, q, qx, k_far, k_near, kx_far, kx_near, v_far, v_near, o_mine, o_other, d_mine, d_other,
-    lse, ang_far, ang_near, first, pairs,
-):
+def attend_back(core, queries, blocks, first, pairs, angles=None, before=None):
+    q, qx, o_mine, o_other, d_mine, d_other, lse = queries
     rows, m, width = q.shape
     span = m // 2
-    far, near = k_far.shape[1], k_near.shape[1]
-    n = far + near
+    sizes = [k.shape[1] for k, _, _, _ in blocks]
+    n = sum(sizes)
     at = lambda size: pl.BlockSpec((None, size, 128), lambda r, p, c: (r, 0, first + p))
     out = lambda size: pl.BlockSpec((None, size, 128), lambda r, p, c: (r, 0, p))
     once = lambda size: pl.BlockSpec((None, size, 128), lambda r, p, c: (r, 0, 0))
     angle = lambda size: pl.BlockSpec((None, 2, 32, size), lambda r, p, c: (r, 0, 0, 0))
-    shape = lambda size: jax.ShapeDtypeStruct((rows, size, pairs * 128), BF)
+    shape = lambda size, t: jax.ShapeDtypeStruct((rows, size, pairs * 128), t)
+    in_specs = [at(m), once(m), at(span), at(span), at(span), at(span), at(m)]
+    args = [q, qx, o_mine, o_other, d_mine, d_other, lse]
+    for size, block in zip(sizes, blocks):
+        in_specs += [at(size), once(size), at(size), angle(size)]
+        args += list(block)
+    if angles is not None:
+        in_specs.append(angle(m))
+        args.append(angles)
+    if before is not None:
+        in_specs.append(at(m))
+        args.append(before)
+    twice = [size for size in sizes for _ in range(2)]
     return pl.pallas_call(
-        attend_back_kernel,
+        functools.partial(
+            attend_back_kernel, blocks=len(blocks), start=before is None, finish=angles is not None
+        ),
         grid_spec=pltpu.PrefetchScalarGridSpec(
             num_scalar_prefetch=1,
             grid=(rows, pairs),
-            in_specs=[
-                at(m), once(m), at(far), at(near), once(far), once(near), at(far), at(near),
-                at(span), at(span), at(span), at(span), at(m), angle(far), angle(near),
-            ],
-            out_specs=[out(m), out(far), out(near), out(far), out(near)],
+            in_specs=in_specs,
+            out_specs=[out(m)] + [out(size) for size in twice],
             scratch_shapes=[
                 pltpu.VMEM((m, 256), BF),
                 pltpu.VMEM((m, 256), BF),
@@ -754,14 +851,11 @@
                 pltpu.VMEM((128, n), F32),
             ],
         ),
-        out_shape=[shape(m), shape(far), shape(near), shape(far), shape(near)],
+        out_shape=[shape(m, F32 if angles is None else BF)] + [shape(size, BF) for size in twice],
         compiler_params=pltpu.CompilerParams(vmem_limit_bytes=60 * MIB),
         cost_estimate=QUICK,
         name="attend_back",
-    )(
-        core, q, qx, k_far, k_near, kx_far, kx_near, v_far, v_near, o_mine, o_other, d_mine,
-        d_other, lse, ang_far, ang_near,
-    )
+    )(core, *args)
 
 
 def frame_table(seg_lengths, frames):
@@ -822,7 +916,7 @@
 
     time_float = time_embed.astype(F32)
     time_act = jax.nn.silu(time_float).astype(BF)
-    embedding = (dot_nn(time_act, ada_w) + ada_b.astype(F32)).reshape(rows, 6, model)
+    embedding = (ada(time_act, ada_w, False) + ada_b.astype(F32)).reshape(rows, 6, model)
 
     def tables(frame_ids):
         inside, offsets = frame_table(seg_lengths, frame_ids)
@@ -870,80 +964,98 @@
     early = lax.psum_scatter(early, ("sx", "core"), scatter_dimension=0, tiled=False)
 
     pairs = half // 128
-    shared = [q, qx, k_far, k_near, kx_far, kx_near, v_far, v_near, o_mine, o_give, d_o_mine]
-    shared += [d_o_other, lse, ang_far, ang_near]
+    queries = (q, qx, o_mine, o_give, d_o_mine, d_o_other, lse)
+    keys_far = (k_far, kx_far, v_far, ang_far)
+    keys_near = (k_near, kx_near, v_near, ang_near)
+
     def far_part(far_grads):
         made = []
         for t in range(chips - 1):
             cut = slice(2 * span * t, 2 * span * (t + 1))
             grads = [(j, [a[:, cut] if chips > 2 else a for a in g]) for j, g in far_grads]
-            mine, other = d_mod(core_arg, grads, w_qkv, span)
-            made.append((mine, flip(other, "core", 1)))
+            made.append(d_mod(core_arg, grads, w_qkv, span))
         return made
 
     def outers(dq, dk_far, dk, dv_far, dv):
         pieces = []
         for r in range(rows):
             block = lambda a, t: a[r, 2 * span * t : 2 * span * (t + 1)]
-            pieces.append(
-                qkv_outer(
-                    place, mod_near[r], dq[r], dk[r], dv[r],
-                    [(far[t][0][r], block(dk_far, t), block(dv_far, t)) for t in range(chips - 1)],
-                )
-            )
-        return pieces[0] if rows == 1 else [total(p) for p in zip(*pieces)]
-
-    def by_chip(kept, given):
-        return [
-            jnp.stack([kept[t], given[t]], axis=0).reshape(-1, kept.shape[-1]) for t in range(chips)
-        ]
+            others = [
+                (far[t][0][r], block(dk_far, t), block(dv_far, t)) for t in range(chips - 1)
+            ]
+            pieces.append(qkv_outer(place, mod_near[r], dq[r], dk[r], dv[r], others))
+        if rows == 1:
+            return pieces[0]
+        kept, given, sums = zip(*pieces)
+        return total(kept), total(given), sum(sums)
 
     def send(blocks):
-        return [blocks[0]] + [shift(b, "sx", t + 1) for t, b in enumerate(blocks[1:])]
+        return [shift(b, "sx", t + 1) for t, b in enumerate(blocks)]
 
     tie = lambda *trees: lax.optimization_barrier(trees)
 
-    first_made = attend_back(core_arg, *shared, 0, pairs - 1)
-    first_kept, first_given = outers(*first_made)
-    first_blocks = by_chip(first_kept, flip(first_given, "core", 1))
-    give = rows_give([early])
-    shared, give, first_blocks = tie(shared, give, first_blocks)
-    early_recv = flip(give, "ry", 1)
-    first_late = send(first_blocks)
-    last_made = attend_back(core_arg, *shared, pairs - 1, 1)
-    last_made, early_recv, first_late = tie(last_made, early_recv, first_late)
-
+    order = (0, 1, 3, 2, 4)
+    cut = 128 * (pairs - 1)
+    made = attend_back(core_arg, queries, (keys_far, keys_near), 0, pairs - 1, angles=ang_near)
+    first_made = [made[n] for n in order]
+    first_made, early = tie(first_made, early)
+    early_give = rows_give([early])
+    first_made, early_give = tie(first_made, early_give)
+    early_recv = flip(early_give, "ry", 1)
+    first_kept, first_given, first_sums = outers(*first_made)
+    first_given = flip(first_given, "core", 1)
+    first_blocks = [
+        jnp.concatenate([first_kept[t], first_given[t]], axis=0) for t in range(1, chips)
+    ]
+    queries, first_blocks = tie(queries, first_blocks)
+    first_got = send(first_blocks)
+    made = attend_back(core_arg, queries, (keys_far, keys_near), pairs - 1, 1, angles=ang_near)
+    last_made = [made[n] for n in order]
+    last_made, early_recv, first_got = tie(last_made, early_recv, first_got)
+
+    def first_half(i):
+        return total(
+            [jnp.where(i == 0, first_kept[0], first_given[0])] + [part_of(g, i, 2) for g in first_got]
+        )
+
+    y = lax.axis_index("ry")
+    zbits = bits("rz")
+    early = rows_mine([early], early_recv)
+    early_give = give_half(early, "rz", zbits[0])
+    first_give = first_half(1 - y)
+    last_made, early_give, first_give = tie(last_made, early_give, first_give)
+    early_got = near_flip(early_give, "rz", zbits[0])
+    first_recv = flip(first_give, "ry", 1)
+    last_kept, last_given, last_sums = outers(*last_made)
+    last_made, last_given = tie(last_made, last_given)
+    far_parts = far_part([(j, [m[2 * j - 1] for m in (first_made, last_made)]) for j in (1, 2)])
     near_grads = [(0, [m[0] for m in (first_made, last_made)])]
     near_grads += [(j, [m[2 * j] for m in (first_made, last_made)]) for j in (1, 2)]
-    far_grads = [(j, [m[2 * j - 1] for m in (first_made, last_made)]) for j in (1, 2)]
-    far_parts = far_part(far_grads)
-    first_late = total(first_late)
-    late_give = rows_give([first_late])
-    far_parts, late_give = tie(far_parts, late_give)
-    far_parts = [total(p) for p in far_parts]
-    early_mine = rows_mine([early], early_recv)
-    last_made, far_parts, late_give, early_mine = tie(last_made, far_parts, late_give, early_mine)
-    far_got = [shift(p, "sx", t + 1) for t, p in enumerate(far_parts)]
-    late_recv = flip(late_give, "ry", 1)
-    early = rows_turn(early_mine)
-    last_kept, last_given = outers(*last_made)
     near_mine, near_give = d_mod(core_arg, near_grads, w_qkv, span)
-    last_kept, last_given, near_give, far_got, early, late_recv = tie(
-        last_kept, last_given, near_give, far_got, early, late_recv
+    far_parts, near_mine, near_give, last_given, early_got, first_recv = tie(
+        far_parts, near_mine, near_give, last_given, early_got, first_recv
     )
     near_recv = flip(near_give, "core", 1)
+    far_parts = [(mine, flip(give, "core", 1)) for mine, give in far_parts]
     last_given = flip(last_given, "core", 1)
-    early = total(early)
-    first_late = rows_turn(rows_mine([first_late], late_recv))
-    last_blocks = by_chip(last_kept, last_given)
-    near_recv, early, first_late, last_blocks = tie(near_recv, early, first_late, last_blocks)
-    early = rows_spread(early)
-    last_late = send(last_blocks)
-    noisy_grad, cond_grad, text_grad, in_kept, in_given, in_sums = tail(
-        place, inputs, d_resid, embedding, keep, w_in, bi, near_mine, near_recv, far_got, mel
-    )
-    in_kept, in_given, in_sums, early, first_late, last_late = tie(
-        in_kept, in_given, in_sums, early, first_late, last_late
+    early = keep_half(early, early_got, "rz", zbits[0])
+    for bit in zbits[1:-1]:
+        early = keep_half(early, near_flip(give_half(early, "rz", bit), "rz", bit), "rz", bit)
+    early_give = give_half(early, "rz", zbits[-1])
+    first_late = total([first_half(y), first_recv])
+    first_give = give_half(first_late, "rz", zbits[0])
+    last_blocks = [jnp.concatenate([last_kept[t], last_given[t]], axis=1) for t in range(1, chips)]
+    far_parts, near_recv, early_give, last_blocks, first_give = tie(
+        far_parts, near_recv, early_give, last_blocks, first_give
+    )
+    early_got = near_flip(early_give, "rz", zbits[-1])
+    first_recv = near_flip(first_give, "rz", zbits[0])
+    last_got = send(last_blocks)
+    d_blocks = [(inputs, near_mine, near_recv)]
+    d_blocks += [(far_blocks[t], *far_parts[t]) for t in range(chips - 1)]
+    in_kept, in_given, in_sums, *far_sums = in_outer(place, d_blocks, d_resid, embedding, w_in, bi)
+    in_kept, in_given, in_sums, far_sums, last_got, early_got, first_recv = tie(
+        in_kept, in_given, in_sums, far_sums, last_got, early_got, first_recv
     )
     if rows > 1:
         in_kept, in_given = [jnp.sum(a.astype(F32), axis=0).astype(BF) for a in (in_kept, in_given)]
@@ -954,13 +1066,8 @@
         [in_sums[:, 0], in_sums[:, 1], sums[:, 4], sums[:, 2], sums[:, 3], sums[:, 0]], axis=1
     )
     over = lambda a: jnp.sum(a, axis=0)
-    columns = lambda *a: sum(jnp.sum(flat(b).astype(F32), axis=0) for b in a)
-    bias_mine = jnp.stack(
-        [
-            jnp.concatenate([columns(m[0]) for m in (first_made, last_made)]),
-            jnp.concatenate([columns(m[1], m[2]) for m in (first_made, last_made)]),
-            jnp.concatenate([columns(m[3], m[4]) for m in (first_made, last_made)]),
-        ]
+    bias_mine = jnp.concatenate(
+        [first_sums[0].reshape(3, -1), last_sums[0].reshape(3, -1)], axis=1
     )
     gap = jnp.zeros_like(bias_mine)
     b_qkv_grad = jnp.stack(
@@ -974,25 +1081,30 @@
 
     in_given = flip(in_given, "core", 1)
     other = flip(vector, "core", 1)
-    early = rows_half(early)
-    early_other = flip(early, "ry", 1)
-    first_late = rows_spread(total(first_late))
-    last_late = total(last_late)
-    last_give = rows_give([last_late])
-    in_given, other, early, first_late[-1], last_give = tie(
-        in_given, other, early, first_late[-1], last_give
-    )
-    in_late = sum_chips([(in_kept[t], in_given[t]) for t in range(chips)])
-    vector = sum_small(vector + other, "sx")
-    last_recv = flip(last_give, "ry", 1)
-    first_late, last_recv = tie(first_late, last_recv)
-    last_mine = rows_mine([last_late], last_recv)
-    first_late = rows_half(first_late)
-    in_late, vector, last_mine, first_late = tie(in_late, vector, last_mine, first_late)
-    last_late = rows_turn(last_mine)
-    first_other = flip(first_late, "ry", 1)
-    in_late = total(in_late)
-    in_recv = flip(rows_give([in_late]), "ry", 1)
+    first_late = keep_half(first_late, first_recv, "rz", zbits[0])
+    for bit in zbits[1:-1]:
+        first_give = give_half(first_late, "rz", bit)
+        first_late = keep_half(first_late, near_flip(first_give, "rz", bit), "rz", bit)
+    early = keep_half(early, early_got, "rz", zbits[-1])
+    early_got = near_flip(early, "rz", zbits[-1])
+    in_given, other, first_late, early_got = tie(in_given, other, first_late, early_got)
+    in_blocks = [total([in_kept[t], in_given[t]]) for t in range(1, chips)]
+    vector = vector + other
+    early = join_halves(early, early_got, "rz", zbits[-1])
+    for bit in zbits[-2:0:-1]:
+        early = join_halves(early, near_flip(early, "rz", bit), "rz", bit)
+    in_blocks, vector, far_sums, first_late, early = tie(
+        in_blocks, vector, far_sums, first_late, early
+    )
+    in_got = send(in_blocks)
+    vector = sum_small(vector, "sx")
+    early_got = near_flip(early, "rz", zbits[0])
+    first_got = near_flip(give_half(first_late, "rz", zbits[-1]), "rz", zbits[-1])
+    in_got, vector, first_got = tie(in_got, vector, first_got)
+    far_got = [shift(p, "sx", t + 1) for t, p in enumerate(far_sums)]
+    in_terms = [in_kept[0], in_given[0]] + in_got
+    last_terms = [jnp.concatenate([last_kept[0], last_given[0]], axis=1)] + last_got
+    in_give = jnp.concatenate([rows_give(in_terms), rows_give(last_terms)], axis=0)
     emb_size = rows * 6 * model
     d_embedding = vector[:emb_size].reshape(rows, 6 * model).astype(BF)
     biases = vector[emb_size:]
@@ -1007,46 +1119,75 @@
     bias_share = shares.shape[0]
     shares = jnp.concatenate([shares[None], jnp.zeros((rows - 1, bias_share), F32)], axis=0)
     joined = jnp.concatenate([shares, act_share.astype(F32), d_embedding.astype(F32)], axis=1)
+    first_late = keep_half(first_late, first_got, "rz", zbits[-1])
+    time_float, in_give, joined, first_late = tie(time_float, in_give, joined, first_late)
+    in_recv = flip(in_give, "ry", 1)
     joined = gather_small(joined, "ry")
+    for bit in zbits[:0:-1]:
+        first_late = join_halves(first_late, near_flip(first_late, "rz", bit), "rz", bit)
     _, silu_pull = jax.vjp(jax.nn.silu, time_float)
-    time_grad = silu_pull(dot_nt(d_embedding, ada_w))[0]
-    in_recv, joined, last_late, time_grad = tie(in_recv, joined, last_late, time_grad)
-    in_late = rows_turn(rows_mine([in_late], in_recv))
-    joined = gather_small(joined, "rz")
-    last_late = rows_spread(total(last_late))
-    in_late, joined, last_late, early_other, first_other = tie(
-        in_late, joined, last_late, early_other, first_other
-    )
-    in_late = rows_spread(total(in_late))
-    last_late = rows_half(last_late)
-    last_other = flip(last_late, "ry", 1)
-    by_row = lambda a, b: jnp.concatenate(
-        [jnp.where(lax.axis_index("ry") == 0, a, b), jnp.where(lax.axis_index("ry") == 0, b, a)],
-        axis=0,
-    )
-    early = by_row(early, early_other)
-    in_late, last_other, early = tie(in_late, last_other, early)
-    late = jnp.concatenate([by_row(first_late, first_other), by_row(last_late, last_other)], axis=1)
-    late = late.reshape(2, 3, model // seq, half)
-    in_low, in_high = rows_join(rows_half(in_late))
-    w_in_grad = jnp.concatenate([in_low, in_high], axis=0)[:, :width].astype(F32).T
-
+    time_grad = ada(d_embedding, ada_w, True)
+    in_mine = [total([part_of(t, y, 2) for t in terms]) for terms in (in_terms, last_terms)]
+    in_mine = jnp.concatenate(in_mine, axis=0)
+    joined, in_recv, time_grad, in_mine, early_got, first_late = tie(
+        joined, in_recv, time_grad, in_mine, early_got, first_late
+    )
+    time_grad = silu_pull(time_grad)[0]
+    in_mine = total([in_mine, in_recv])
+    early = join_halves(early, early_got, "rz", zbits[0])
+    in_mine, first_late, early = tie(in_mine, first_late, early)
+    early_other = flip(early, "ry", 1)
+    for n, bit in enumerate(bits("rz")):
+        in_got = near_flip(in_mine, "rz", bit)
+        far_bit = bits("rz")[::-1][n]
+        joined = jnp.concatenate([joined, near_flip(joined, "rz", far_bit)], axis=0)
+        if n == 1:
+            noisy_grad, cond_grad, text_grad = d_in(
+                inputs, d_resid, embedding, keep, w_in, bi, [near_mine, near_recv] + far_got, mel
+            )
+            in_got, joined, noisy_grad = tie(in_got, joined, noisy_grad)
+        in_mine = total([in_mine, in_got])
+        if n == 0:
+            first_got = near_flip(first_late, "rz", zbits[0])
+            in_mine, joined, first_got = tie(in_mine, joined, first_got)
+            first_late = join_halves(first_late, first_got, "rz", zbits[0])
+            first_other = flip(first_late, "ry", 1)
+        else:
+            in_mine, joined = tie(in_mine, joined)
+    in_mine, noisy_grad = tie(in_mine, noisy_grad)
+    in_recv = flip(in_mine, "ry", 1)
+    all_act = joined[:, bias_share : bias_share + width_share].astype(BF)
+    all_emb = joined[:, bias_share + width_share :]
+    ada_w_grad = dot_tn(all_act, all_emb.astype(BF))
+    early = by_row(early, early_other).astype(F32)
     block = model // seq
-    early = early.astype(F32)
     w_up_grad = jnp.concatenate([early[:block], early[block : 2 * block]], axis=1)
     w_down_grad = early[2 * block : 4 * block]
     w_out_grad = early[4 * block :]
-    late = [jnp.where(core == 0, late[0], late[1]), jnp.where(core == 0, late[1], late[0])]
+    in_recv, ada_w_grad, first_other, w_up_grad, w_down_grad, w_out_grad = tie(
+        in_recv, ada_w_grad, first_other, w_up_grad, w_down_grad, w_out_grad
+    )
+    share = in_mine.shape[0] // 2
+    w_in_grad = by_row(in_mine[:share], in_recv[:share])[:, :width].astype(F32).T
+    last_late = by_row(in_mine[share:], in_recv[share:])
+
+    low, high = jnp.where(y == 0, first_late, first_other), jnp.where(y == 0, first_other, first_late)
+    first_late = [jnp.where(core == 0, low, high), jnp.where(core == 0, high, low)]
+    low, high = last_late[:, : 3 * 128], last_late[:, 3 * 128 :]
+    last_late = [jnp.where(core == 0, low, high), jnp.where(core == 0, high, low)]
     w_qkv_grad = jnp.concatenate(
-        [late[c][j].astype(F32) for j in range(3) for c in range(2)], axis=1
+        [
+            part[c][:, j * size : (j + 1) * size].astype(F32)
+            for j in range(3)
+            for c in range(2)
+            for part, size in ((first_late, cut), (last_late, 128))
+        ],
+        axis=1,
     )
     shares = jnp.sum(joined[:, :bias_share], axis=0)
-    all_act = joined[:, bias_share : bias_share + width_share].astype(BF)
-    all_emb = joined[:, bias_share + width_share :]
     b_in_grad, b_qkv_grad, b_out_grad, b_up_grad, b_down_grad = jnp.split(
         shares, [sum(bias_sizes[:n]) // seq for n in range(1, 5)]
     )
-    ada_w_grad = dot_tn(all_act, all_emb.astype(BF))
     emb_share = 6 * model // seq
     ada_b_grad = lax.dynamic_slice_in_dim(
         jnp.sum(all_emb, axis=0), seq_index * emb_share, emb_share, 0

time: 566 us -> 516 us (0.912)
  Pallas kernels: 311 us -> 344 us
  waiting for transfers between devices: 59.6 us -> 27.1 us
  starting transfers between devices: 64.2 us -> 41.6 us
  matrix products: 20.3 us -> 5.43 us
  local copies, waits for them, and re-layouts: 44.2 us -> 32 us
    ppermute x29 -> x5, starting transfers between devices: 51.4 us -> 7.13 us  [shift(): return lax.ppermute(v, axis, [(i, (i + step) % size) for i in range(size)])]
    ppermute x29 -> x5, waiting for transfers between devices: 33 us -> 0.01 us  [shift(): return lax.ppermute(v, axis, [(i, (i + step) % size) for i in range(size)])]
    pallas_call x3 -> x6, Pallas kernels: 129 us -> 160 us  [the longest x2 116 us: attend_back(): pl.pallas_call(functools.partial(attend_back_kernel, blocks=len(blocks),...]
    ppermute x0 -> x12, waiting for transfers between devices: none -> 24.6 us  [near_flip(): lax.ppermute(v, axis, [(i, place[gray(i) ^ bit]) for i in range(size)])]
    ppermute x22 -> x18, waiting for transfers between devices: 26.6 us -> 2.54 us  [flip(): return lax.ppermute(v, axis, [(i, i ^ bit) for i in range(size)])]
    ppermute x0 -> x12, starting transfers between devices: none -> 21.6 us  [near_flip(): lax.ppermute(v, axis, [(i, place[gray(i) ^ bit]) for i in range(size)])]
    dot_general x2 -> x0, matrix products: 14.9 us -> none  [the longest x1 8.53 us: dot_nt(): lax.dot_general(a, b, (((1,), (1,)), ((), ())), preferred_element_type=F32)]
    unnamed x148 -> x92, local copies, waits for them, and re-layouts: 24.6 us -> 14.9 us
  transfers between devices with their start and end apart: 52 -> 36, of which waited for: 18 -> 8; matrix products, arithmetic and copies ran while one was open for 14% -> 11% of each run, Pallas kernels for 32% -> 39%
where the time goes in v3:
time: 516 us; the launch traced here: 512 us
  Pallas kernels  344 us (67%)
  other arithmetic  46.6 us (9%)
  starting transfers between devices  41.6 us (8%)
  local copies, waits for them, and re-layouts  32 us (6%)
  waiting for transfers between devices  27.1 us (5%)
  between operations  15.3 us (3%)
  matrix products  5.43 us (1%)
    pallas_call x2, Pallas kernels, attend_back(): pl.pallas_call(functools.partial(attend_back_kernel, blocks=len(blocks),...  116 us
    pallas_call x1, Pallas kernels, attend(): pl.pallas_call(attend_kernel, grid_spec=pltpu.PrefetchScalarGridSpec(num_...  57.4 us
    pallas_call x1, Pallas kernels, mid(): pl.pallas_call(mid_kernel, grid_spec=pltpu.PrefetchScalarGridSpec(num_sca...  35.3 us
    pallas_call x2, Pallas kernels, front(): pl.pallas_call(functools.partial(front_kernel, parts=parts), grid_spec=pl...  26.3 us
    pallas_call x2, Pallas kernels, qkv_outer(): pl.pallas_call(functools.partial(qkv_outer_kernel, far=len(far)), grid_sp...  24.6 us
    ppermute x12, waiting for transfers between devices, near_flip(): lax.ppermute(v, axis, [(i, place[gray(i) ^ bit]) for i in range(size)])  24.6 us
    ppermute x12, starting transfers between devices, near_flip(): lax.ppermute(v, axis, [(i, place[gray(i) ^ bit]) for i in range(size)])  21.6 us
    pallas_call x1, Pallas kernels, outer(): pl.pallas_call(outer_kernel, grid_spec=pltpu.PrefetchScalarGridSpec(num_s...  21.4 us
  transfers between devices with their start and end apart: 36, of which 8 were waited for; matrix products, arithmetic and copies ran while one was open for 11% of the time, Pallas kernels for 39%

profile of v3, /device:TPU:0, one launch (start us, length us, event | category | flops | bytes accessed | tf_op | source)
XLA Modules:
  0.0 511.7 jit_solution(17495035975949249654)
XLA Ops:
  14.5 2.6 collective-permute-start.1
  19.2 7.7 %ada.2 = f32[1,6144]{1,0:T(1,128)} custom-call(bf16[1,1024]{1,0:T(2,128)(2,1)} %fusion.22.t_ref, bf16[1024,6144]{1,0:T(8,128)(2,1)} %w_ref.3), custom_call_target="tpu_custom_call" | custom-call | flops 1 | bytes 1 | tf_op jit(solution)/shard_map/ada/pallas_call | solution.py:201
  33.0 14.4 %front.2 = (bf16[1,2,1024,832]{3,2,1,0:T(8,128)(2,1)}, bf16[1,1664,512]{2,1,0:T(8,128)(2,1)}, bf16[1,1664,512]{2,1,0:T(8,128)(2,1)}, bf16[1,1664,512]{2,1,0:T(8,128)(2,1)}) custom-call(s32[1]{0:T(128)} %bitcast.core.flag, bf16[1,832,768]{2,1,0:T(8,128)(2,1)} %copy-done, bf16[1,832,768]{2,1,0:T(8,128)(2,1)} %collective-permute-done.x1_ref, ...), custom_call_target="tpu_custom_call" | custom-call | flops 1 | bytes 1 | tf_op jit(solution)/shard_map/front/pallas_call | solution.py:172
  51.8 11.8 %front.3 = (bf16[1,2,1024,832]{3,2,1,0:T(8,128)(2,1)}, bf16[1,1664,512]{2,1,0:T(8,128)(2,1)}, bf16[1,1664,512]{2,1,0:T(8,128)(2,1)}) custom-call(s32[1]{0:T(128)} %bitcast.core.flag, bf16[1,832,768]{2,1,0:T(8,128)(2,1)} %copy-done.2, bf16[1,832,768]{2,1,0:T(8,128)(2,1)} %copy-done.13, bf16[712,1024]{1,0:T(8,128)(2,1)} %refs_4_.3, f32[1,1024]{1,0:T(1,128)} %bitcast.125, ...), custom_call_target="tpu_custom_call" | custom-call | flops 1 | bytes 1 | tf_op jit(solution)/shard_map/front/pallas_call | solution.py:172
  63.6 57.4 %attend.1 = (bf16[1,832,512]{2,1,0:T(8,128)(2,1)}, bf16[1,832,512]{2,1,0:T(8,128)(2,1)}, f32[1,1664,512]{2,1,0:T(8,128)}) custom-call(s32[1]{0:T(128)} %bitcast.core.flag, bf16[1,1664,512]{2,1,0:T(8,128)(2,1)} %get-tuple-element.207.q_ref.refs_0_, bf16[1,1664,128]{2,1,0:T(8,128)(2,1)} %get-tuple-element.208.qx_ref.refs_1_, ...), custom_call_target="tpu_custom_call" | custom-call | flops 1 | bytes 1 | tf_op jit(solution)/shard_map/attend/pallas_call | solution.py:676
  124.4 2.2 convert_subtract_fusion.valid_ref
  127.6 35.3 %mid.1 = (bf16[1,832,1024]{2,1,0:T(8,128)(2,1)}, f32[1,832,1024]{2,1,0:T(8,128)}, bf16[1,832,512]{2,1,0:T(8,128)(2,1)}, bf16[1,832,512]{2,1,0:T(8,128)(2,1)}, bf...) custom-call(s32[1]{0:T(128)} %bitcast.core.flag, ...), custom_call_target="tpu_custom_call" | custom-call | flops 1 | bytes 1 | tf_op jit(solution)/shard_map/mid/pallas_call | solution.py:289
  162.9 21.4 %outer.1 = bf16[4,1280,1024]{2,1,0:T(8,128)(2,1)} custom-call(s32[1]{0:T(128)} %bitcast.core.flag, bf16[832,1024]{1,0:T(8,128)(2,1)} %bitcast.111, bf16[832,2048]{1,0:T(8,128)(2,1)} %bitcast.106, bf16[832,512]{1,0:T(8,128)(2,1)} %bitcast.100, bf16[832,512]{1,0:T(8,128)(2,1)} %bitcast.108, bf16[832,2048]{1,0:T(8,128)(2,1)} %bitcast.107, ...), custom_call_target="tpu_custom_call" | custom-call | flops 1 | bytes 1 | tf_op jit(solution)/shard_map/outer/pallas_call | solution.py:368
  189.7 84.6 %attend_back.2 = (bf16[1,1664,384]{2,1,0:T(8,128)(2,1)}, bf16[1,1664,384]{2,1,0:T(8,128)(2,1)}, bf16[1,1664,384]{2,1,0:T(8,128)(2,1)}, bf16[1,1664,384]{2,1,0:T(8,128)(2,1)}, bf16[1,1664,384]{2,1,0:T(8,128)(2,1)}) custom-call(s32[1]{0:T(128)} %bitcast.core.flag, bf16[1,1664,512]{2,1,0:T(8,128)(2,1)} %get-tuple-element.207.q_ref.refs_0_, ...), custom_call_target="tpu_custom_call" | custom-call | flops 1 | bytes 1 | tf_op jit(solution)/shard_map/attend_back/pallas_call | solution.py:830
  274.3 2.6 constant_dynamic-slice_fusion.5
  276.8 16.0 %qkv_outer.2 = (bf16[2,256,1152]{2,1,0:T(8,128)(2,1)}, bf16[2,256,1152]{2,1,0:T(8,128)(2,1)}, f32[8,1152]{1,0:T(8,128)}) custom-call(s32[2]{0:T(128)} %pad_add_fusion.2.place, bf16[2,1024,832]{2,1,0:T(8,128)(2,1)} %bitcast.96, bf16[1664,384]{1,0:T(8,128)(2,1)} %bitcast.103, bf16[1664,384]{1,0:T(8,128)(2,1)} %bitcast.104, bf16[1664,384]{1,0:T(8,128)(2,1)} %bitcast.105, ...), custom_call_target="tpu_custom_call" | custom-call | flops 1 | bytes 1 | tf_op jit(solution)/shard_map/qkv_outer/pallas_call | solution.py:437
  297.8 31.0 %attend_back.3 = (bf16[1,1664,128]{2,1,0:T(8,128)(2,1)}, bf16[1,1664,128]{2,1,0:T(8,128)(2,1)}, bf16[1,1664,128]{2,1,0:T(8,128)(2,1)}, bf16[1,1664,128]{2,1,0:T(8,128)(2,1)}, bf16[1,1664,128]{2,1,0:T(8,128)(2,1)}) custom-call(s32[1]{0:T(128)} %bitcast.core.flag, bf16[1,1664,512]{2,1,0:T(8,128)(2,1)} %get-tuple-element.207.q_ref.refs_0_, ...), custom_call_target="tpu_custom_call" | custom-call | flops 1 | bytes 1 | tf_op jit(solution)/shard_map/attend_back/pallas_call | solution.py:830
  329.9 2.2 add_convert_fusion
  333.4 2.1 fusion.1
  338.8 8.6 %qkv_outer.3 = (bf16[2,256,384]{2,1,0:T(8,128)(2,1)}, bf16[2,256,384]{2,1,0:T(8,128)(2,1)}, f32[8,384]{1,0:T(8,128)}) custom-call(s32[2]{0:T(128)} %pad_add_fusion.2.place, bf16[2,1024,832]{2,1,0:T(8,128)(2,1)} %bitcast.97, bf16[1664,128]{1,0:T(8,128)(2,1)} %bitcast.116, bf16[1664,128]{1,0:T(8,128)(2,1)} %bitcast.117, bf16[1664,128]{1,0:T(8,128)(2,1)} %bitcast.118, ...), custom_call_target="tpu_custom_call" | custom-call | flops 1 | bytes 1 | tf_op jit(solution)/shard_map/qkv_outer/pallas_call | solution.py:437
  347.4 8.2 %d_mod.2 = (bf16[1,832,1024]{2,1,0:T(8,128)(2,1)}, bf16[1,832,1024]{2,1,0:T(8,128)(2,1)}) custom-call(s32[1]{0:T(128)} %bitcast.core.flag, bf16[1,1664,384]{2,1,0:T(8,128)(2,1)} %get-tuple-element.198.refs_0_, bf16[1,1664,128]{2,1,0:T(8,128)(2,1)} %get-tuple-element.234.refs_1_, bf16[1,1664,384]{2,1,0:T(8,128)(2,1)} %get-tuple-element.204.refs_2_, ...), custom_call_target="tpu_custom_call" | custom-call | flops 1 | bytes 1 | tf_op jit(solution)/shard_map/d_mod/pallas_call | solution.py:482
  355.7 10.9 %d_mod.3 = (bf16[1,832,1024]{2,1,0:T(8,128)(2,1)}, bf16[1,832,1024]{2,1,0:T(8,128)(2,1)}) custom-call(s32[1]{0:T(128)} %bitcast.core.flag, bf16[1,1664,384]{2,1,0:T(8,128)(2,1)} %get-tuple-element.200.refs_0_, bf16[1,1664,128]{2,1,0:T(8,128)(2,1)} %get-tuple-element.238.refs_1_, bf16[1,1664,384]{2,1,0:T(8,128)(2,1)} %get-tuple-element.201.refs_2_, ...), custom_call_target="tpu_custom_call" | custom-call | flops 1 | bytes 1 | tf_op jit(solution)/shard_map/d_mod/pallas_call | solution.py:482
  368.7 2.0 add_convert_fusion.2
  377.4 2.4 collective-permute-start.14
  381.3 17.9 %in_outer.1 = (bf16[1,2,256,768]{3,2,1,0:T(8,128)(2,1)}, bf16[1,2,256,768]{3,2,1,0:T(8,128)(2,1)}, f32[1,8,1024]{2,1,0:T(8,128)}, bf16[1,832,1024]{2,1,0:T(8,128)(2,1)}) custom-call(s32[2]{0:T(128)} %pad_add_fusion.2.place, f32[1,832,1024]{2,1,0:T(8,128)} %get-tuple-element.178.dres_ref.refs_1_, f32[1,6,1024]{2,1,0:T(8,128)} %reshape.1287.emb_ref.refs_2_, ...), custom_call_target="tpu_custom_call" | custom-call | flops 1 | bytes 1 | tf_op jit(solution)/shard_map/in_outer/pallas_call | solution.py:546
  404.4 7.6 %collective-permute-done.18 = bf16[160,1024]{1,0:T(8,128)(2,1)S(1)} collective-permute-done((bf16[160,1024]{1,0:T(8,128)(2,1)S(1)}, bf16[160,1024]{1,0:T(8,128)(2,1)S(1)}, u32[]{:S(2)}, u32[]{:S(2)}) %collective-permute-start.18) | collective-permute-done | bytes 327712 | tf_op jit(solution)/shard_map/ppermute | solution.py:50
  421.7 5.7 %collective-permute-start.24 = (bf16[320,1024]{1,0:T(8,128)(2,1)S(1)}, bf16[320,1024]{1,0:T(8,128)(2,1)S(1)}, u32[]{:S(2)}, u32[]{:S(2)}) collective-permute-start(bf16[320,1024]{1,0:T(8,128)(2,1)S(1)} %pad_maximum_fusion.3), channel_id=1, source_target_pairs={{0,8},{8,0},{16,24},{24,16},{1,9},{9,1},{17,25},{25,17},{2,10},{10... | collective-permute-start | bytes 1966088 | tf_op jit(solution)/shard_map/ppermute | solution.py:50
  432.0 2.4 collective-permute-start.25
  436.5 7.4 %ada.3 = f32[1,1024]{1,0:T(1,128)} custom-call(bf16[1,6144]{1,0:T(2,128)(2,1)} %convert_element_type.347.t_ref, bf16[1024,6144]{1,0:T(8,128)(2,1)} %w_ref.3), custom_call_target="tpu_custom_call" | custom-call | flops 1 | bytes 1 | tf_op jit(solution)/shard_map/ada/pallas_call | solution.py:201
  448.1 2.3 collective-permute-start.26
  451.1 2.3 collective-permute-done.27
  453.5 6.7 %collective-permute-done.26 = bf16[256,768]{1,0:T(8,128)(2,1)S(1)} collective-permute-done((bf16[256,768]{1,0:T(8,128)(2,1)S(1)}, bf16[256,768]{1,0:T(8,128)(2,1)S(1)}, u32[]{:S(2)}, u32[]{:S(2)}) %collective-permute-start.26) | collective-permute-done | bytes 393248 | tf_op jit(solution)/shard_map/ppermute | solution.py:50
  460.2 4.4 collective-permute-done.28
  466.7 2.3 collective-permute-start.29
  470.9 11.0 %d_in.1 = (f32[1,832,100]{2,1,0:T(8,128)}, f32[1,832,100]{2,1,0:T(8,128)}, f32[1,832,512]{2,1,0:T(8,128)}) custom-call(bf16[1,832,768]{2,1,0:T(8,128)(2,1)} %copy-done, f32[1,832,1024]{2,1,0:T(8,128)} %get-tuple-element.178.dres_ref.refs_1_, f32[1,6,1024]{2,1,0:T(8,128)} %reshape.1287.emb_ref.refs_2_, f32[1,832,2]{2,1,0:T(8,128)} %copy.63.refs_3_, ...), custom_call_target="tpu_custom_call" | custom-call | flops 1 | bytes 1 | tf_op jit(solution)/shard_map/d_in/pallas_call | solution.py:593
  490.1 3.7 fusion.11
  501.5 2.0 concatenate.154
  (285 shorter events, 97.2 us)
Async XLA Ops:
  7.2 267.1 %reduce-scatter.2.cloned.1.call-start = ((), (), s32[]{:S(2)}) async-start(), calls=%async_computation.1 | async-start | bytes 13107200 | tf_op jit(solution)/shard_map/reduce_scatter | solution.py:964
  14.0 19.0 %collective-permute-start = (bf16[1,832,768]{2,1,0:T(8,128)(2,1)S(1)}, bf16[1,832,768]{2,1,0:T(8,128)(2,1)}, u32[]{:S(2)}, u32[]{:S(2)}) collective-permute-start(bf16[1,832,768]{2,1,0:T(8,128)(2,1)S(1)} %maximum_maximum_fusion.x0_ref.x_ref.refs_0_), channel_id=1, source_target_pairs={{0,1},{1,0},{2,3},{3,2},{4,5},{5,4},{6,7},{7,6},{8,9},{9,8},{10,11... | collective-permute-start | bytes 3833864 | tf_op jit(solution)/shard_map/ppermute | solution.py:40
  14.5 32.9 %collective-permute-start.1 = (bf16[1,832,768]{2,1,0:T(8,128)(2,1)S(1)}, bf16[1,832,768]{2,1,0:T(8,128)(2,1)S(1)}, u32[]{:S(2)}, u32[]{:S(2)}) collective-permute-start(bf16[1,832,768]{2,1,0:T(8,128)(2,1)S(1)} %maximum_maximum_fusion.x0_ref.x_ref.refs_0_), channel_id=1, source_target_pairs={{0,2},{2,0},{1,3},{3,1},{4,6},{6,4},{5,7},{7,5},{8,10},{10,8},{9,1... | collective-permute-start | bytes 3833864 | tf_op jit(solution)/shard_map/ppermute | solution.py:35
  121.1 5.6 %collective-permute-start.3 = (bf16[1,832,512]{2,1,0:T(8,128)(2,1)}, bf16[1,832,512]{2,1,0:T(8,128)(2,1)S(1)}, u32[]{:S(2)}, u32[]{:S(2)}) collective-permute-start(bf16[1,832,512]{2,1,0:T(8,128)(2,1)} %get-tuple-element.210.refs_3_), channel_id=1, source_target_pairs={{0,1},{1,0},{2,3},{3,2},{4,5},{5,4},{6,7},{7,6},{8,9},{9,8},{10,11... | collective-permute-start | bytes 2555912 | tf_op jit(solution)/shard_map/ppermute | solution.py:40
  293.3 35.6 %collective-permute-start.6 = (bf16[640,1024]{1,0:T(8,128)(2,1)}, bf16[640,1024]{1,0:T(8,128)(2,1)S(1)}, u32[]{:S(2)}, u32[]{:S(2)}) collective-permute-start(bf16[640,1024]{1,0:T(8,128)(2,1)} %constant_dynamic-slice_fusion.5), channel_id=1, source_target_pairs={{0,4},{4,0},{1,5},{5,1},{2,6},{6,2},{3,7},{7,3},{8,12},{12,8},{9,1... | collective-permute-start | bytes 3932168 | tf_op jit(solution)/shard_map/ppermute | solution.py:40
  297.3 31.5 %collective-permute-start.7 = (bf16[512,1152]{1,0:T(8,128)(2,1)}, bf16[512,1152]{1,0:T(8,128)(2,1)}, u32[]{:S(2)}, u32[]{:S(2)}) collective-permute-start(bf16[512,1152]{1,0:T(8,128)(2,1)} %pad_maximum_fusion.2), channel_id=1, source_target_pairs={{0,2},{2,0},{1,3},{3,1},{4,6},{6,4},{5,7},{7,5},{8,10},{10,8},{9,1... | collective-permute-start | bytes 3538952 | tf_op jit(solution)/shard_map/ppermute | solution.py:35
  335.5 31.1 %collective-permute-start.8 = (bf16[320,1024]{1,0:T(8,128)(2,1)S(1)}, bf16[320,1024]{1,0:T(8,128)(2,1)S(1)}, u32[]{:S(2)}, u32[]{:S(2)}) collective-permute-start(bf16[320,1024]{1,0:T(8,128)(2,1)S(1)} %constant_dynamic-slice_fusion.4), channel_id=1, source_target_pairs={{0,8},{8,0},{16,24},{24,16},{1,9},{9,1},{17,25},{25,17},{2,10},{10... | collective-permute-start | bytes 1966088 | tf_op jit(solution)/shard_map/ppermute | solution.py:50
  337.2 29.4 %collective-permute-start.9 = (bf16[256,1152]{1,0:T(8,128)(2,1)}, bf16[256,1152]{1,0:T(8,128)(2,1)}, u32[]{:S(2)}, u32[]{:S(2)}) collective-permute-start(bf16[256,1152]{1,0:T(8,128)(2,1)} %fusion.1), channel_id=1, source_target_pairs={{0,4},{4,0},{1,5},{5,1},{2,6},{6,2},{3,7},{7,3},{8,12},{12,8},{9,1... | collective-permute-start | bytes 1769480 | tf_op jit(solution)/shard_map/ppermute | solution.py:40
  367.4 7.6 %collective-permute-start.10 = (bf16[1,832,1024]{2,1,0:T(8,128)(2,1)}, bf16[1,832,1024]{2,1,0:T(8,128)(2,1)S(1)}, u32[]{:S(2)}, u32[]{:S(2)}) collective-permute-start(bf16[1,832,1024]{2,1,0:T(8,128)(2,1)} %get-tuple-element.248), channel_id=1, source_target_pairs={{0,1},{1,0},{2,3},{3,2},{4,5},{5,4},{6,7},{7,6},{8,9},{9,8},{10,11... | collective-permute-start | bytes 5111816 | tf_op jit(solution)/shard_map/ppermute | solution.py:40
  367.4 7.6 %collective-permute-start.11 = (bf16[1,832,1024]{2,1,0:T(8,128)(2,1)}, bf16[1,832,1024]{2,1,0:T(8,128)(2,1)S(1)}, u32[]{:S(2)}, u32[]{:S(2)}) collective-permute-start(bf16[1,832,1024]{2,1,0:T(8,128)(2,1)} %get-tuple-element.249), channel_id=1, source_target_pairs={{0,1},{1,0},{2,3},{3,2},{4,5},{5,4},{6,7},{7,6},{8,9},{9,8},{10,11... | collective-permute-start | bytes 5111816 | tf_op jit(solution)/shard_map/ppermute | solution.py:40
  368.7 5.6 %collective-permute-start.12 = (bf16[2,256,384]{2,1,0:T(8,128)(2,1)}, bf16[2,256,384]{2,1,0:T(8,128)(2,1)S(1)}, u32[]{:S(2)}, u32[]{:S(2)}) collective-permute-start(bf16[2,256,384]{2,1,0:T(8,128)(2,1)} %get-tuple-element.252), channel_id=1, source_target_pairs={{0,1},{1,0},{2,3},{3,2},{4,5},{5,4},{6,7},{7,6},{8,9},{9,8},{10,11... | collective-permute-start | bytes 1179656 | tf_op jit(solution)/shard_map/ppermute | solution.py:40
  375.1 24.2 %collective-permute-start.13 = (bf16[256,768]{1,0:T(8,128)(2,1)S(1)}, bf16[256,768]{1,0:T(8,128)(2,1)}, u32[]{:S(2)}, u32[]{:S(2)}) collective-permute-start(bf16[256,768]{1,0:T(8,128)(2,1)S(1)} %pad_maximum_fusion.9), channel_id=1, source_target_pairs={{0,2},{2,0},{1,3},{3,1},{4,6},{6,4},{5,7},{7,5},{8,10},{10,8},{9,1... | collective-permute-start | bytes 1179656 | tf_op jit(solution)/shard_map/ppermute | solution.py:35
  377.4 21.8 %collective-permute-start.14 = (bf16[160,1024]{1,0:T(8,128)(2,1)}, bf16[160,1024]{1,0:T(8,128)(2,1)S(1)}, u32[]{:S(2)}, u32[]{:S(2)}) collective-permute-start(bf16[160,1024]{1,0:T(8,128)(2,1)} %constant_dynamic-slice_fusion.3), channel_id=1, source_target_pairs={{0,24},{8,16},{16,8},{24,0},{1,25},{9,17},{17,9},{25,1},{2,26},{10... | collective-permute-start | bytes 983048 | tf_op jit(solution)/shard_map/ppermute | solution.py:50
  379.9 19.4 %collective-permute-start.15 = (bf16[128,1152]{1,0:T(8,128)(2,1)}, bf16[128,1152]{1,0:T(8,128)(2,1)}, u32[]{:S(2)}, u32[]{:S(2)}) collective-permute-start(bf16[128,1152]{1,0:T(8,128)(2,1)} %constant_dynamic-slice_fusion.2), channel_id=1, source_target_pairs={{0,8},{8,0},{16,24},{24,16},{1,9},{9,1},{17,25},{25,17},{2,10},{10... | collective-permute-start | bytes 884744 | tf_op jit(solution)/shard_map/ppermute | solution.py:50
  400.9 11.1 %collective-permute-start.18 = (bf16[160,1024]{1,0:T(8,128)(2,1)S(1)}, bf16[160,1024]{1,0:T(8,128)(2,1)S(1)}, u32[]{:S(2)}, u32[]{:S(2)}) collective-permute-start(bf16[160,1024]{1,0:T(8,128)(2,1)S(1)} %add_convert_fusion.6), channel_id=1, source_target_pairs={{0,24},{8,16},{16,8},{24,0},{1,25},{9,17},{17,9},{25,1},{2,26},{10... | collective-permute-start | bytes 983048 | tf_op jit(solution)/shard_map/ppermute | solution.py:50
  401.9 10.0 %collective-permute-start.16 = (bf16[2,256,768]{2,1,0:T(8,128)(2,1)}, bf16[2,256,768]{2,1,0:T(8,128)(2,1)S(1)}, u32[]{:S(2)}, u32[]{:S(2)}) collective-permute-start(bf16[2,256,768]{2,1,0:T(8,128)(2,1)} %bitcast.146), channel_id=1, source_target_pairs={{0,1},{1,0},{2,3},{3,2},{4,5},{5,4},{6,7},{7,6},{8,9},{9,8},{10,11... | collective-permute-start | bytes 2359304 | tf_op jit(solution)/shard_map/ppermute | solution.py:40
  414.6 14.1 %collective-permute-start.19 = (bf16[256,768]{1,0:T(8,128)(2,1)}, bf16[256,768]{1,0:T(8,128)(2,1)}, u32[]{:S(2)}, u32[]{:S(2)}) collective-permute-start(bf16[256,768]{1,0:T(8,128)(2,1)} %fusion.2), channel_id=1, source_target_pairs={{0,2},{2,0},{1,3},{3,1},{4,6},{6,4},{5,7},{7,5},{8,10},{10,8},{9,1... | collective-permute-start | bytes 1179656 | tf_op jit(solution)/shard_map/ppermute | solution.py:35
  416.7 12.0 %collective-permute-start.21 = (bf16[64,1152]{1,0:T(8,128)(2,1)}, bf16[64,1152]{1,0:T(8,128)(2,1)}, u32[]{:S(2)}, u32[]{:S(2)}) collective-permute-start(bf16[64,1152]{1,0:T(8,128)(2,1)} %constant_dynamic-slice_fusion.1), channel_id=1, source_target_pairs={{0,24},{8,16},{16,8},{24,0},{1,25},{9,17},{17,9},{25,1},{2,26},{10... | collective-permute-start | bytes 442376 | tf_op jit(solution)/shard_map/ppermute | solution.py:50
  419.6 9.1 %collective-permute-start.20 = (f32[14336]{0:T(1024)S(1)}, f32[14336]{0:T(1024)S(1)}, u32[]{:S(2)}, u32[]{:S(2)}) collective-permute-start(f32[14336]{0:T(1024)S(1)} %add.305), channel_id=1, source_target_pairs={{0,2},{2,0},{1,3},{3,1},{4,6},{6,4},{5,7},{7,5},{8,10},{10,8},{9,1... | collective-permute-start | bytes 172040 | tf_op jit(solution)/shard_map/ppermute | solution.py:40
  421.7 24.1 %collective-permute-start.24 = (bf16[320,1024]{1,0:T(8,128)(2,1)S(1)}, bf16[320,1024]{1,0:T(8,128)(2,1)S(1)}, u32[]{:S(2)}, u32[]{:S(2)}) collective-permute-start(bf16[320,1024]{1,0:T(8,128)(2,1)S(1)} %pad_maximum_fusion.3), channel_id=1, source_target_pairs={{0,8},{8,0},{16,24},{24,16},{1,9},{9,1},{17,25},{25,17},{2,10},{10... | collective-permute-start | bytes 1966088 | tf_op jit(solution)/shard_map/ppermute | solution.py:50
  427.3 43.6 %collective-permute-start.31 = (bf16[1,832,1024]{2,1,0:T(8,128)(2,1)}, bf16[1,832,1024]{2,1,0:T(8,128)(2,1)}, u32[]{:S(2)}, u32[]{:S(2)}) collective-permute-start(bf16[1,832,1024]{2,1,0:T(8,128)(2,1)} %get-tuple-element.298), channel_id=1, source_target_pairs={{0,2},{2,0},{1,3},{3,1},{4,6},{6,4},{5,7},{7,5},{8,10},{10,8},{9,1... | collective-permute-start | bytes 5111816 | tf_op jit(solution)/shard_map/ppermute | solution.py:35
  432.0 13.7 %collective-permute-start.25 = (bf16[64,1152]{1,0:T(8,128)(2,1)S(1)}, bf16[64,1152]{1,0:T(8,128)(2,1)S(1)}, u32[]{:S(2)}, u32[]{:S(2)}) collective-permute-start(bf16[64,1152]{1,0:T(8,128)(2,1)S(1)} %add_convert_fusion.10), channel_id=1, source_target_pairs={{0,24},{8,16},{16,8},{24,0},{1,25},{9,17},{17,9},{25,1},{2,26},{10... | collective-permute-start | bytes 442376 | tf_op jit(solution)/shard_map/ppermute | solution.py:50
  434.4 11.3 %collective-permute-start.23 = (bf16[256,768]{1,0:T(8,128)(2,1)S(1)}, bf16[256,768]{1,0:T(8,128)(2,1)S(1)}, u32[]{:S(2)}, u32[]{:S(2)}) collective-permute-start(bf16[256,768]{1,0:T(8,128)(2,1)S(1)} %pad_maximum_fusion.10), channel_id=1, source_target_pairs={{0,4},{4,0},{1,5},{5,1},{2,6},{6,2},{3,7},{7,3},{8,12},{12,8},{9,1... | collective-permute-start | bytes 1179656 | tf_op jit(solution)/shard_map/ppermute | solution.py:40
  435.0 8.9 %collective-permute-start.22 = (f32[1,8448]{1,0:T(1,128)S(1)}, f32[1,8448]{1,0:T(1,128)S(1)}, u32[]{:S(2)}, u32[]{:S(2)}) collective-permute-start(f32[1,8448]{1,0:T(1,128)S(1)} %pad_maximum_fusion.17), channel_id=1, source_target_pairs={{0,4},{4,0},{1,5},{5,1},{2,6},{6,2},{3,7},{7,3},{8,12},{12,8},{9,1... | collective-permute-start | bytes 101384 | tf_op jit(solution)/shard_map/ppermute | solution.py:40
  446.1 47.7 %collective-permute-start.34 = (bf16[640,1024]{1,0:T(8,128)(2,1)S(1)}, bf16[640,1024]{1,0:T(8,128)(2,1)}, u32[]{:S(2)}, u32[]{:S(2)}) collective-permute-start(bf16[640,1024]{1,0:T(8,128)(2,1)S(1)} %pad_maximum_fusion.1), channel_id=1, source_target_pairs={{0,4},{4,0},{1,5},{5,1},{2,6},{6,2},{3,7},{7,3},{8,12},{12,8},{9,1... | collective-permute-start | bytes 3932168 | tf_op jit(solution)/shard_map/ppermute | solution.py:40
  446.5 6.9 %collective-permute-start.27 = (f32[2,8448]{1,0:T(2,128)S(1)}, f32[2,8448]{1,0:T(2,128)S(1)}, u32[]{:S(2)}, u32[]{:S(2)}) collective-permute-start(f32[2,8448]{1,0:T(2,128)S(1)} %pad_maximum_fusion.16), channel_id=1, source_target_pairs={{0,24},{8,16},{16,8},{24,0},{1,25},{9,17},{17,9},{25,1},{2,26},{10... | collective-permute-start | bytes 202760 | tf_op jit(solution)/shard_map/ppermute | solution.py:50
  448.1 12.0 %collective-permute-start.26 = (bf16[256,768]{1,0:T(8,128)(2,1)S(1)}, bf16[256,768]{1,0:T(8,128)(2,1)S(1)}, u32[]{:S(2)}, u32[]{:S(2)}) collective-permute-start(bf16[256,768]{1,0:T(8,128)(2,1)S(1)} %add_convert_fusion.5), channel_id=1, source_target_pairs={{0,8},{8,0},{16,24},{24,16},{1,9},{9,1},{17,25},{25,17},{2,10},{10... | collective-permute-start | bytes 1179656 | tf_op jit(solution)/shard_map/ppermute | solution.py:50
  450.4 14.2 %collective-permute-start.28 = (bf16[128,1152]{1,0:T(8,128)(2,1)S(1)}, bf16[128,1152]{1,0:T(8,128)(2,1)S(1)}, u32[]{:S(2)}, u32[]{:S(2)}) collective-permute-start(bf16[128,1152]{1,0:T(8,128)(2,1)S(1)} %pad_maximum_fusion.12), channel_id=1, source_target_pairs={{0,8},{8,0},{16,24},{24,16},{1,9},{9,1},{17,25},{25,17},{2,10},{10... | collective-permute-start | bytes 884744 | tf_op jit(solution)/shard_map/ppermute | solution.py:50
  464.6 6.2 %collective-permute-start.30 = (f32[4,8448]{1,0:T(4,128)S(1)}, f32[4,8448]{1,0:T(4,128)S(1)}, u32[]{:S(2)}, u32[]{:S(2)}) collective-permute-start(f32[4,8448]{1,0:T(4,128)S(1)} %pad_maximum_fusion.15), channel_id=1, source_target_pairs={{0,8},{8,0},{16,24},{24,16},{1,9},{9,1},{17,25},{25,17},{2,10},{10... | collective-permute-start | bytes 405512 | tf_op jit(solution)/shard_map/ppermute | solution.py:50
  465.0 34.5 %collective-permute-start.33 = (bf16[256,1152]{1,0:T(8,128)(2,1)S(1)}, bf16[256,1152]{1,0:T(8,128)(2,1)}, u32[]{:S(2)}, u32[]{:S(2)}) collective-permute-start(bf16[256,1152]{1,0:T(8,128)(2,1)S(1)} %pad_maximum_fusion.4), channel_id=1, source_target_pairs={{0,4},{4,0},{1,5},{5,1},{2,6},{6,2},{3,7},{7,3},{8,12},{12,8},{9,1... | collective-permute-start | bytes 1769480 | tf_op jit(solution)/shard_map/ppermute | solution.py:40
  466.7 15.3 %collective-permute-start.29 = (bf16[256,768]{1,0:T(8,128)(2,1)S(1)}, bf16[256,768]{1,0:T(8,128)(2,1)S(1)}, u32[]{:S(2)}, u32[]{:S(2)}) collective-permute-start(bf16[256,768]{1,0:T(8,128)(2,1)S(1)} %add_convert_fusion.4), channel_id=1, source_target_pairs={{0,24},{8,16},{16,8},{24,0},{1,25},{9,17},{17,9},{25,1},{2,26},{10... | collective-permute-start | bytes 1179656 | tf_op jit(solution)/shard_map/ppermute | solution.py:50
  483.3 16.3 %collective-permute-start.32 = (bf16[256,768]{1,0:T(8,128)(2,1)S(1)}, bf16[256,768]{1,0:T(8,128)(2,1)S(1)}, u32[]{:S(2)}, u32[]{:S(2)}) collective-permute-start(bf16[256,768]{1,0:T(8,128)(2,1)S(1)} %add_convert_fusion.3), channel_id=1, source_target_pairs={{0,4},{4,0},{1,5},{5,1},{2,6},{6,2},{3,7},{7,3},{8,12},{12,8},{9,1... | collective-permute-start | bytes 1179656 | tf_op jit(solution)/shard_map/ppermute | solution.py:40
  (37 other events, 412.9 us)
Sparse Core Ops, SparseCore 0:
  184.4 85.6 reduce-scatter.1

commit v4 on v3

--- a/solution.py
+++ b/solution.py
@@ -215,12 +215,25 @@
 
 def mid_kernel(
     core, x_ref, om_ref, oo_ref, g_ref, valid_ref, emb_ref,
-    win_ref, bin_ref, wom_ref, woo_ref, bout_ref, wup_ref, bup_ref, wdn_ref, bdn_ref,
-    out_ref, dres_ref, dom_ref, doo_ref, mod_ref, act_ref, dhid_ref, dff_ref, dbr_ref,
-    sums_ref, bupg_ref, slope_ref,
+    win_ref, bin_ref, wom_ref, woo_ref, bout_ref, wup_hbm, bup_ref, wdn_hbm, bdn_ref,
+    dres_ref, dom_ref, doo_ref, dbr_ref, sums_ref, bupg_ref,
+    out_hbm, mod_hbm, act_hbm, dhid_hbm, dff_hbm,
+    slope_ref, wup_ref, wdn_ref, out_ref, mod_ref, act_ref, dhid_ref, dff_ref, come, go,
 ):
     hidden_width = wup_ref.shape[1]
     step = 512
+    row = pl.program_id(0)
+    fetch_up = pltpu.make_async_copy(wup_hbm, wup_ref, come.at[0])
+    fetch_down = pltpu.make_async_copy(wdn_hbm, wdn_ref, come.at[1])
+    fetch_up.start()
+    fetch_down.start()
+    gone = []
+
+    def leave(ref, hbm):
+        copy = pltpu.make_async_copy(ref, hbm.at[row], go.at[len(gone)])
+        copy.start()
+        gone.append(copy)
+
     gate_one, shift_two = emb_ref[2:3, :], emb_ref[3:4, :]
     scale_two, gate_two = emb_ref[4:5, :], emb_ref[5:6, :]
     total = lambda v: jnp.sum(v, axis=0, keepdims=True)
@@ -234,6 +247,9 @@
     normed = center * inv
     mod = (normed * (1.0 + scale_two) + shift_two).astype(BF)
     mod_ref[...] = mod
+    leave(mod_ref, mod_hbm)
+    fetch_up.wait()
+    fetch_down.wait()
     ff = None
     for j in range(0, hidden_width, step):
         h = dot_nn(mod, wup_ref[:, j : j + step]) + bup_ref[:, j : j + step]
@@ -246,12 +262,15 @@
         slope_ref[:, j : j + step] = slope.astype(BF)
         part = dot_nn(act, wdn_ref[j : j + step, :])
         ff = part if ff is None else ff + part
+    leave(act_ref, act_hbm)
     ff = ff + bdn_ref[...]
     out_ref[...] = (resid + gate_two * ff).astype(BF)
+    leave(out_ref, out_hbm)
     g = g_ref[...].astype(F32)
     sums_ref[0:1, :] = total(g * ff)
     d_ff = (g * gate_two).astype(BF)
     dff_ref[...] = d_ff
+    leave(dff_ref, dff_hbm)
     sums_ref[1:2, :] = total(d_ff.astype(F32))
     d_mod = None
     for j in range(0, hidden_width, step):
@@ -261,6 +280,7 @@
         bupg_ref[:, j : j + step] = total(d_hid.astype(F32))
         part = dot_nt(d_hid, wup_ref[:, j : j + step])
         d_mod = part if d_mod is None else d_mod + part
+    leave(dhid_ref, dhid_hbm)
     sums_ref[2:3, :] = total(d_mod)
     sums_ref[3:4, :] = total(d_mod * normed)
     u = d_mod * (1.0 + scale_two)
@@ -272,6 +292,8 @@
     sums_ref[5:6, :] = total(d_branch.astype(F32))
     dom_ref[...] = dot_nt(d_branch, wom_ref[...]).astype(BF)
     doo_ref[...] = dot_nt(d_branch, woo_ref[...]).astype(BF)
+    for copy in gone:
+        copy.wait()
 
 
 def mid(core, x, o_mine, o_other, g, valid, emb, w_in, b_in, w_out, b_out, w_up, b_up, w_down, b_down):
@@ -285,6 +307,7 @@
     out_half = lambda f: pl.BlockSpec(
         (half, model), lambda r, c: (f(c[0]), 0), pipeline_mode=pl.Buffered(buffer_count=1)
     )
+    anywhere = pl.BlockSpec(memory_space=pl.ANY)
     shape = lambda w, t: jax.ShapeDtypeStruct((rows, span, w), t)
     return pl.pallas_call(
         mid_kernel,
@@ -296,21 +319,32 @@
                 pl.BlockSpec((None, 6, model), lambda r, c: (r, 0, 0)),
                 whole(*w_in.shape), whole(1, model),
                 out_half(lambda c: c), out_half(lambda c: 1 - c), whole(1, model),
-                whole(model, hidden), whole(1, hidden), whole(hidden, model), whole(1, model),
+                anywhere, whole(1, hidden), anywhere, whole(1, model),
             ],
             out_specs=[
-                frame(model), frame(model), frame(half), frame(half), frame(model),
-                frame(hidden), frame(hidden), frame(model), frame(model),
+                frame(model), frame(half), frame(half), frame(model),
                 pl.BlockSpec((None, 8, model), lambda r, c: (r, 0, 0)),
                 pl.BlockSpec((None, 1, hidden), lambda r, c: (r, 0, 0)),
+            ] + [anywhere] * 5,
+            scratch_shapes=[
+                pltpu.VMEM((span, hidden), BF),
+                pltpu.VMEM((model, hidden), BF),
+                pltpu.VMEM((hidden, model), BF),
+                pltpu.VMEM((span, model), BF),
+                pltpu.VMEM((span, model), BF),
+                pltpu.VMEM((span, hidden), BF),
+                pltpu.VMEM((span, hidden), BF),
+                pltpu.VMEM((span, model), BF),
+                pltpu.SemaphoreType.DMA((2,)),
+                pltpu.SemaphoreType.DMA((5,)),
             ],
-            scratch_shapes=[pltpu.VMEM((span, hidden), BF)],
         ),
         out_shape=[
-            shape(model, BF), shape(model, F32), shape(half, BF), shape(half, BF), shape(model, BF),
-            shape(hidden, BF), shape(hidden, BF), shape(model, BF), shape(model, BF),
+            shape(model, F32), shape(half, BF), shape(half, BF), shape(model, BF),
             jax.ShapeDtypeStruct((rows, 8, model), F32),
             jax.ShapeDtypeStruct((rows, 1, hidden), F32),
+            shape(model, BF), shape(model, BF), shape(hidden, BF), shape(hidden, BF),
+            shape(model, BF),
         ],
         compiler_params=pltpu.CompilerParams(vmem_limit_bytes=60 * MIB),
         cost_estimate=QUICK,
@@ -318,66 +352,66 @@
     )(core, x, o_mine, o_other, g, valid, emb, w_in, b_in, w_out, w_out, b_out, w_up, b_up, w_down, b_down)
 
 
-def outer_kernel(core, mod_ref, act_ref, om_ref, oo_ref, dhid_ref, dff_ref, dbr_ref, out_ref):
+def outer_kernel(core, mod_ref, act_ref, om_ref, oo_ref, dhid_ref, dff_ref, dbr_ref, out_ref, left):
     step = pl.program_id(0)
-    seq, model = out_ref.shape[0], out_ref.shape[2]
-    r = model // seq
-
-    def put(left, right, size, first, at):
-        product = dot_nn(left.T, right).astype(BF)
-        for n in range(model // size):
-            out_ref[first + n, at : at + size, :] = product[n * size : (n + 1) * size]
-
-    @pl.when(step < 2)
+    seq, r, model = out_ref.shape
+
+    def put(rows, right):
+        product = dot_nn(rows, right).astype(BF)
+        for n in range(seq):
+            out_ref[n] = product[n * r : (n + 1) * r]
+
+    @pl.when(step == 0)
     def _():
-        product = dot_nn(mod_ref[...].T, dhid_ref[...]).astype(BF)
-        for j in range(2):
-            @pl.when(step == j)
-            def _():
-                for n in range(seq):
-                    out_ref[n, j * r : (j + 1) * r, :] = product[n * r : (n + 1) * r]
-
-    @pl.when((step >= 2) & (step < 4))
+        left[:model, :] = mod_ref[...].T
+
+    @pl.when(step == 2)
     def _():
-        product = dot_nn(act_ref[...].T, dff_ref[...]).astype(BF)
-        for j in range(2):
-            @pl.when(step == 2 + j)
-            def _():
-                for n in range(seq // 2):
-                    out_ref[j * (seq // 2) + n, 2 * r : 4 * r, :] = product[
-                        n * 2 * r : (n + 1) * 2 * r
-                    ]
+        left[...] = act_ref[...].T
 
     @pl.when(step == 4)
     def _():
         mine, other = om_ref[...], oo_ref[...]
         low = core[0] == 0
-        mixed = jnp.concatenate([jnp.where(low, mine, other), jnp.where(low, other, mine)], axis=1)
-        product = dot_nn(mixed.T, dbr_ref[...]).astype(BF)
-        for n in range(seq):
-            out_ref[n, 4 * r :, :] = product[n * r : (n + 1) * r]
+        half = model // 2
+        left[:half, :] = jnp.where(low, mine, other).T
+        left[half:model, :] = jnp.where(low, other, mine).T
+
+    @pl.when(step < 2)
+    def _():
+        put(left[:model, :], dhid_ref[...])
+
+    for j in range(2):
+
+        @pl.when(step == 2 + j)
+        def _():
+            at = [(2 * n + j) * r for n in range(seq)]
+            put(jnp.concatenate([left[a : a + r, :] for a in at], axis=0), dff_ref[...])
+
+    @pl.when(step == 4)
+    def _():
+        put(left[:model, :], dbr_ref[...])
 
 
 def outer(core, mod, act, o_mine, o_other, d_hid, d_ff, d_br):
     n, model = mod.shape
     seq = lax.axis_size("sx") * 2
-    low = lambda i: jnp.minimum(i, 1)
-    high = lambda i: jnp.clip(i - 2, 0, 1)
+    rows = model // seq
     once = lambda w: pl.BlockSpec((n, w), lambda i, c: (0, 0))
-    shape = (seq, 5 * model // seq, model)
     return pl.pallas_call(
         outer_kernel,
         grid_spec=pltpu.PrefetchScalarGridSpec(
             num_scalar_prefetch=1,
             grid=(5,),
             in_specs=[
-                once(model), pl.BlockSpec((n, model), lambda i, c: (0, high(i))),
-                once(model // 2), once(model // 2),
-                pl.BlockSpec((n, model), lambda i, c: (0, low(i))), once(model), once(model),
+                once(model), once(act.shape[1]), once(model // 2), once(model // 2),
+                pl.BlockSpec((n, model), lambda i, c: (0, jnp.minimum(i, 1))),
+                once(model), once(model),
             ],
-            out_specs=pl.BlockSpec(shape, lambda i, c: (0, 0, 0)),
+            out_specs=pl.BlockSpec((seq, rows, model), lambda i, c: (0, i, 0)),
+            scratch_shapes=[pltpu.VMEM((act.shape[1], n), BF)],
         ),
-        out_shape=jax.ShapeDtypeStruct(shape, BF),
+        out_shape=jax.ShapeDtypeStruct((seq, 5 * rows, model), BF),
         compiler_params=pltpu.CompilerParams(vmem_limit_bytes=60 * MIB),
         cost_estimate=QUICK,
         name="outer",
@@ -506,15 +540,27 @@
     return center * inv, inv
 
 
-def in_outer_kernel(place, dres_ref, emb_ref, win_ref, bin_ref, *refs, blocks):
+def in_outer_kernel(place, dres_hbm, emb_ref, win_ref, bin_ref, *refs, blocks):
     ins, refs = [refs[3 * n : 3 * n + 3] for n in range(blocks)], refs[3 * blocks :]
     keep_out, give_out, sums_ref = refs[:3]
-    far_out, turned, joined = refs[3:-2], refs[-2], refs[-1]
-    span = dres_ref.shape[0]
+    far_out, refs = refs[3 : 2 + blocks], refs[2 + blocks :]
+    turned, joined, sems, dres_ref, *later = refs
+    row = pl.program_id(0)
+    come = [pltpu.make_async_copy(dres_hbm.at[row], dres_ref, sems.at[0])]
+    far_hbm = [ref for block in ins[1:] for ref in block]
+    for n, (src, dst) in enumerate(zip(far_hbm, later)):
+        come.append(pltpu.make_async_copy(src.at[row], dst, sems.at[n + 1]))
+    for copy in come:
+        copy.start()
+    ins = [ins[0]] + [later[3 * n : 3 * n + 3] for n in range(blocks - 1)]
+    span = ins[0][0].shape[0]
     total = lambda v: jnp.sum(v, axis=0, keepdims=True)
     sums_ref[...] = jnp.zeros(sums_ref.shape, F32)
     for n, (x_ref, mine_ref, recv_ref) in enumerate(ins):
         cut = slice(n * span, (n + 1) * span)
+        if n:
+            for copy in come[3 * n - 2 : 3 * n + 1]:
+                copy.wait()
         normed, inv = first_norm(x_ref, win_ref, bin_ref)
         d = mine_ref[...].astype(F32) + recv_ref[...].astype(F32)
         if n:
@@ -522,6 +568,8 @@
         sums_ref[0:1, :] += total(d)
         sums_ref[1:2, :] += total(d * normed)
         d = norm_back(normed, inv, d * (1.0 + emb_ref[1:2, :]))
+        if n == 0:
+            come[0].wait()
         d = (d if n else d + dres_ref[...]).astype(BF)
         sums_ref[2:3, :] += total(d.astype(F32))
         turned[:, cut] = d.T
@@ -543,21 +591,24 @@
     frame = lambda w: pl.BlockSpec((None, span, w), lambda r, c: (r, 0, 0))
     whole = lambda a, b: pl.BlockSpec((a, b), lambda r, c: (0, 0))
     out = pl.BlockSpec((None, chips, block, width), lambda r, c: (r, 0, 0, 0))
+    anywhere = pl.BlockSpec(memory_space=pl.ANY)
     return pl.pallas_call(
         functools.partial(in_outer_kernel, blocks=len(blocks)),
         grid_spec=pltpu.PrefetchScalarGridSpec(
             num_scalar_prefetch=1,
             grid=(rows,),
             in_specs=[
-                frame(model), pl.BlockSpec((None, 6, model), lambda r, c: (r, 0, 0)),
-                whole(*w_in.shape), whole(1, model),
-            ] + [frame(width), frame(model), frame(model)] * len(blocks),
+                anywhere, pl.BlockSpec((None, 6, model), lambda r, c: (r, 0, 0)),
+                whole(*w_in.shape), whole(1, model), frame(width), frame(model), frame(model),
+            ] + [anywhere] * (3 * len(blocks) - 3),
             out_specs=[out, out, pl.BlockSpec((None, 8, model), lambda r, c: (r, 0, 0))]
             + [frame(model)] * (len(blocks) - 1),
             scratch_shapes=[
                 pltpu.VMEM((model, len(blocks) * span), BF),
                 pltpu.VMEM((len(blocks) * span, width), BF),
-            ],
+                pltpu.SemaphoreType.DMA((3 * len(blocks) - 2,)),
+                pltpu.VMEM((span, model), F32),
+            ] + [pltpu.VMEM((span, w), BF) for w in (width, model, model)] * (len(blocks) - 1),
         ),
         out_shape=[
             jax.ShapeDtypeStruct((rows, chips, block, width), BF),
@@ -916,7 +967,7 @@
 
     time_float = time_embed.astype(F32)
     time_act = jax.nn.silu(time_float).astype(BF)
-    embedding = (ada(time_act, ada_w, False) + ada_b.astype(F32)).reshape(rows, 6, model)
+    embedding = (dot_nn(time_act, ada_w) + ada_b.astype(F32)).reshape(rows, 6, model)
 
     def tables(frame_ids):
         inside, offsets = frame_table(seg_lengths, frame_ids)
@@ -952,7 +1003,7 @@
     )
 
     o_other = flip(o_give, "core", 1)
-    result, d_resid, d_o_mine, d_o_give, mod_two, act, d_hid, d_ff, d_br, sums, up_sums = mid(
+    d_resid, d_o_mine, d_o_give, d_br, sums, up_sums, result, mod_two, act, d_hid, d_ff = mid(
         core_arg, inputs, o_mine, o_other, cotangent, frame_valid, embedding, w_in, bi,
         w_out, as_row(b_out), w_up, as_row(b_up), w_down, as_row(b_down),
     )
@@ -961,6 +1012,7 @@
     early = outer(
         core_arg, *[flat(a) for a in (mod_two, act, o_mine, o_other, d_hid, d_ff, d_br)]
     )
+    early, d_o_other = lax.optimization_barrier((early, d_o_other))
     early = lax.psum_scatter(early, ("sx", "core"), scatter_dimension=0, tiled=False)
 
     pairs = half // 128
@@ -1031,24 +1083,28 @@
     far_parts = far_part([(j, [m[2 * j - 1] for m in (first_made, last_made)]) for j in (1, 2)])
     near_grads = [(0, [m[0] for m in (first_made, last_made)])]
     near_grads += [(j, [m[2 * j] for m in (first_made, last_made)]) for j in (1, 2)]
-    near_mine, near_give = d_mod(core_arg, near_grads, w_qkv, span)
-    far_parts, near_mine, near_give, last_given, early_got, first_recv = tie(
-        far_parts, near_mine, near_give, last_given, early_got, first_recv
-    )
-    near_recv = flip(near_give, "core", 1)
-    far_parts = [(mine, flip(give, "core", 1)) for mine, give in far_parts]
-    last_given = flip(last_given, "core", 1)
+    far_parts, early_got = tie(far_parts, early_got)
     early = keep_half(early, early_got, "rz", zbits[0])
     for bit in zbits[1:-1]:
         early = keep_half(early, near_flip(give_half(early, "rz", bit), "rz", bit), "rz", bit)
     early_give = give_half(early, "rz", zbits[-1])
+    near_arrays, early_give = tie([g for _, g in near_grads], early_give)
+    early_got = near_flip(early_give, "rz", zbits[-1])
+    near_mine, near_give = d_mod(core_arg, list(enumerate(near_arrays)), w_qkv, span)
+    far_parts, near_mine, near_give, last_given, first_recv, early_got = tie(
+        far_parts, near_mine, near_give, last_given, first_recv, early_got
+    )
+    near_recv = flip(near_give, "core", 1)
+    far_parts = [(mine, flip(give, "core", 1)) for mine, give in far_parts]
+    last_given = flip(last_given, "core", 1)
     first_late = total([first_half(y), first_recv])
     first_give = give_half(first_late, "rz", zbits[0])
     last_blocks = [jnp.concatenate([last_kept[t], last_given[t]], axis=1) for t in range(1, chips)]
-    far_parts, near_recv, early_give, last_blocks, first_give = tie(
-        far_parts, near_recv, early_give, last_blocks, first_give
-    )
-    early_got = near_flip(early_give, "rz", zbits[-1])
+    early = keep_half(early, early_got, "rz", zbits[-1])
+    far_parts, near_recv, early, last_blocks, first_give = tie(
+        far_parts, near_recv, early, last_blocks, first_give
+    )
+    early_got = near_flip(early, "rz", zbits[-1])
     first_recv = near_flip(first_give, "rz", zbits[0])
     last_got = send(last_blocks)
     d_blocks = [(inputs, near_mine, near_recv)]
@@ -1085,20 +1141,16 @@
     for bit in zbits[1:-1]:
         first_give = give_half(first_late, "rz", bit)
         first_late = keep_half(first_late, near_flip(first_give, "rz", bit), "rz", bit)
-    early = keep_half(early, early_got, "rz", zbits[-1])
-    early_got = near_flip(early, "rz", zbits[-1])
-    in_given, other, first_late, early_got = tie(in_given, other, first_late, early_got)
-    in_blocks = [total([in_kept[t], in_given[t]]) for t in range(1, chips)]
-    vector = vector + other
     early = join_halves(early, early_got, "rz", zbits[-1])
     for bit in zbits[-2:0:-1]:
         early = join_halves(early, near_flip(early, "rz", bit), "rz", bit)
-    in_blocks, vector, far_sums, first_late, early = tie(
-        in_blocks, vector, far_sums, first_late, early
-    )
+    early_got = near_flip(early, "rz", zbits[0])
+    in_given, other, first_late = tie(in_given, other, first_late)
+    in_blocks = [total([in_kept[t], in_given[t]]) for t in range(1, chips)]
+    vector = vector + other
+    in_blocks, vector, far_sums, first_late = tie(in_blocks, vector, far_sums, first_late)
     in_got = send(in_blocks)
     vector = sum_small(vector, "sx")
-    early_got = near_flip(early, "rz", zbits[0])
     first_got = near_flip(give_half(first_late, "rz", zbits[-1]), "rz", zbits[-1])
     in_got, vector, first_got = tie(in_got, vector, first_got)
     far_got = [shift(p, "sx", t + 1) for t, p in enumerate(far_sums)]

time: 516 us -> 506 us (0.981)
  Pallas kernels: 344 us -> 330 us
  matrix products: 5.43 us -> 11.8 us
    pallas_call x2 -> x1, Pallas kernels: 15.1 us -> 7.42 us  [ada(): pl.pallas_call(functools.partial(ada_kernel, turned=turned), grid=(n // s...]
    ppermute x12, waiting for transfers between devices: 24.6 us -> 17.2 us  [near_flip(): lax.ppermute(v, axis, [(i, place[gray(i) ^ bit]) for i in range(size)])]
    ppermute x18, waiting for transfers between devices: 2.54 us -> 9.52 us  [flip(): return lax.ppermute(v, axis, [(i, i ^ bit) for i in range(size)])]
    dot_general x0 -> x1, matrix products: none -> 6.33 us  [dot_nn(): return jnp.dot(a, b, preferred_element_type=F32)]
    unnamed x92 -> x96, local copies, waits for them, and re-layouts: 14.9 us -> 16.9 us
  transfers between devices with their start and end apart: 36 -> 36, of which waited for: 8 -> 9; matrix products, arithmetic and copies ran while one was open for 11% -> 12% of each run, Pallas kernels for 39% -> 43%
where the time goes in v4:
time: 506 us; the launch traced here: 500 us
  Pallas kernels  330 us (65%)
  other arithmetic  44.3 us (9%)
  starting transfers between devices  39.4 us (8%)
  local copies, waits for them, and re-layouts  31.3 us (6%)
  waiting for transfers between devices  27.6 us (5%)
  between operations  15.4 us (3%)
  matrix products  11.8 us (2%)
    pallas_call x2, Pallas kernels, attend_back(): pl.pallas_call(functools.partial(attend_back_kernel, blocks=len(blocks),...  115 us
    pallas_call x1, Pallas kernels, attend(): pl.pallas_call(attend_kernel, grid_spec=pltpu.PrefetchScalarGridSpec(num_...  57.5 us
    pallas_call x1, Pallas kernels, mid(): pl.pallas_call(mid_kernel, grid_spec=pltpu.PrefetchScalarGridSpec(num_sca...  31.6 us
    pallas_call x2, Pallas kernels, front(): pl.pallas_call(functools.partial(front_kernel, parts=parts), grid_spec=pl...  26.4 us
    pallas_call x2, Pallas kernels, qkv_outer(): pl.pallas_call(functools.partial(qkv_outer_kernel, far=len(far)), grid_sp...  24.7 us
    pallas_call x1, Pallas kernels, outer(): pl.pallas_call(outer_kernel, grid_spec=pltpu.PrefetchScalarGridSpec(num_s...  20.2 us
    ppermute x12, starting transfers between devices, near_flip(): lax.ppermute(v, axis, [(i, place[gray(i) ^ bit]) for i in range(size)])  19.3 us
    pallas_call x2, Pallas kernels, d_mod(): pl.pallas_call(functools.partial(d_mod_kernel, parts=tuple((len(g) for _,...  19.1 us
  transfers between devices with their start and end apart: 36, of which 9 were waited for; matrix products, arithmetic and copies ran while one was open for 12% of the time, Pallas kernels for 43%

profile of v4, /device:TPU:0, one launch (start us, length us, event | category | flops | bytes accessed | tf_op | source)
XLA Modules:
  0.0 499.9 jit_solution(4685776789815897891)
XLA Ops:
  14.5 2.6 collective-permute-start.1
  18.8 6.3 %fusion.22 = f32[1,6144]{1,0:T(1,128)S(1)} fusion(bf16[1024,6144]{1,0:T(8,128)(2,1)} %w_ref.1, bf16[1,1024]{1,0:T(2,128)(2,1)S(1)} %copy-done.20), kind=kOutput, calls=%fused_computation.168 | convolution fusion | flops 12589056 | bytes 12609536 | tf_op jit(solution)/shard_map/dot_general | solution.py:22
  30.3 14.6 %front.2 = (bf16[1,2,1024,832]{3,2,1,0:T(8,128)(2,1)}, bf16[1,1664,512]{2,1,0:T(8,128)(2,1)}, bf16[1,1664,512]{2,1,0:T(8,128)(2,1)}, bf16[1,1664,512]{2,1,0:T(8,128)(2,1)}) custom-call(s32[1]{0:T(128)} %bitcast.core.flag, bf16[1,832,768]{2,1,0:T(8,128)(2,1)} %copy-done, bf16[1,832,768]{2,1,0:T(8,128)(2,1)} %collective-permute-done.x1_ref, ...), custom_call_target="tpu_custom_call" | custom-call | flops 1 | bytes 1 | tf_op jit(solution)/shard_map/front/pallas_call | solution.py:172
  49.9 11.8 %front.3 = (bf16[1,2,1024,832]{3,2,1,0:T(8,128)(2,1)}, bf16[1,1664,512]{2,1,0:T(8,128)(2,1)}, bf16[1,1664,512]{2,1,0:T(8,128)(2,1)}) custom-call(s32[1]{0:T(128)} %bitcast.core.flag, bf16[1,832,768]{2,1,0:T(8,128)(2,1)} %copy-done.2, bf16[1,832,768]{2,1,0:T(8,128)(2,1)} %copy-done.12, bf16[712,1024]{1,0:T(8,128)(2,1)} %refs_4_.3, f32[1,1024]{1,0:T(1,128)} %bitcast.129, ...), custom_call_target="tpu_custom_call" | custom-call | flops 1 | bytes 1 | tf_op jit(solution)/shard_map/front/pallas_call | solution.py:172
  61.7 57.5 %attend.1 = (bf16[1,832,512]{2,1,0:T(8,128)(2,1)}, bf16[1,832,512]{2,1,0:T(8,128)(2,1)}, f32[1,1664,512]{2,1,0:T(8,128)}) custom-call(s32[1]{0:T(128)} %bitcast.core.flag, bf16[1,1664,512]{2,1,0:T(8,128)(2,1)} %get-tuple-element.219.q_ref.refs_0_, bf16[1,1664,128]{2,1,0:T(8,128)(2,1)} %get-tuple-element.220.qx_ref.refs_1_, ...), custom_call_target="tpu_custom_call" | custom-call | flops 1 | bytes 1 | tf_op jit(solution)/shard_map/attend/pallas_call | solution.py:727
  122.8 2.2 convert_subtract_fusion.valid_ref
  125.9 31.6 %mid.1 = (f32[1,832,1024]{2,1,0:T(8,128)}, bf16[1,832,512]{2,1,0:T(8,128)(2,1)}, bf16[1,832,512]{2,1,0:T(8,128)(2,1)}, bf16[1,832,1024]{2,1,0:T(8,128)(2,1)}, f3...) custom-call(s32[1]{0:T(128)} %bitcast.core.flag, ...), custom_call_target="tpu_custom_call" | custom-call | flops 1 | bytes 1 | tf_op jit(solution)/shard_map/mid/pallas_call | solution.py:312
  157.7 20.2 %outer.1 = bf16[4,1280,1024]{2,1,0:T(8,128)(2,1)} custom-call(s32[1]{0:T(128)} %bitcast.core.flag, bf16[832,1024]{1,0:T(8,128)(2,1)} %bitcast.116, bf16[832,2048]{1,0:T(8,128)(2,1)} %bitcast.110, bf16[832,512]{1,0:T(8,128)(2,1)} %bitcast.104, bf16[832,512]{1,0:T(8,128)(2,1)} %bitcast.112, bf16[832,2048]{1,0:T(8,128)(2,1)} %bitcast.111, ...), custom_call_target="tpu_custom_call" | custom-call | flops 1 | bytes 1 | tf_op jit(solution)/shard_map/outer/pallas_call | solution.py:401
  182.6 84.3 %attend_back.2 = (bf16[1,1664,384]{2,1,0:T(8,128)(2,1)}, bf16[1,1664,384]{2,1,0:T(8,128)(2,1)}, bf16[1,1664,384]{2,1,0:T(8,128)(2,1)}, bf16[1,1664,384]{2,1,0:T(8,128)(2,1)}, bf16[1,1664,384]{2,1,0:T(8,128)(2,1)}) custom-call(s32[1]{0:T(128)} %bitcast.core.flag, bf16[1,1664,512]{2,1,0:T(8,128)(2,1)} %get-tuple-element.219.q_ref.refs_0_, ...), custom_call_target="tpu_custom_call" | custom-call | flops 1 | bytes 1 | tf_op jit(solution)/shard_map/attend_back/pallas_call | solution.py:881
  268.4 16.1 %qkv_outer.2 = (bf16[2,256,1152]{2,1,0:T(8,128)(2,1)}, bf16[2,256,1152]{2,1,0:T(8,128)(2,1)}, f32[8,1152]{1,0:T(8,128)}) custom-call(s32[2]{0:T(128)} %pad_add_fusion.2.place, bf16[2,1024,832]{2,1,0:T(8,128)(2,1)} %bitcast.100, bf16[1664,384]{1,0:T(8,128)(2,1)} %bitcast.107, bf16[1664,384]{1,0:T(8,128)(2,1)} %bitcast.108, bf16[1664,384]{1,0:T(8,128)(2,1)} %bitcast.109, ...), custom_call_target="tpu_custom_call" | custom-call | flops 1 | bytes 1 | tf_op jit(solution)/shard_map/qkv_outer/pallas_call | solution.py:471
  291.7 31.0 %attend_back.3 = (bf16[1,1664,128]{2,1,0:T(8,128)(2,1)}, bf16[1,1664,128]{2,1,0:T(8,128)(2,1)}, bf16[1,1664,128]{2,1,0:T(8,128)(2,1)}, bf16[1,1664,128]{2,1,0:T(8,128)(2,1)}, bf16[1,1664,128]{2,1,0:T(8,128)(2,1)}) custom-call(s32[1]{0:T(128)} %bitcast.core.flag, bf16[1,1664,512]{2,1,0:T(8,128)(2,1)} %get-tuple-element.219.q_ref.refs_0_, ...), custom_call_target="tpu_custom_call" | custom-call | flops 1 | bytes 1 | tf_op jit(solution)/shard_map/attend_back/pallas_call | solution.py:881
  323.7 2.3 add_convert_fusion
  327.3 2.1 fusion.1
  332.6 8.6 %qkv_outer.3 = (bf16[2,256,384]{2,1,0:T(8,128)(2,1)}, bf16[2,256,384]{2,1,0:T(8,128)(2,1)}, f32[8,384]{1,0:T(8,128)}) custom-call(s32[2]{0:T(128)} %pad_add_fusion.2.place, bf16[2,1024,832]{2,1,0:T(8,128)(2,1)} %bitcast.101, bf16[1664,128]{1,0:T(8,128)(2,1)} %bitcast.120, bf16[1664,128]{1,0:T(8,128)(2,1)} %bitcast.121, bf16[1664,128]{1,0:T(8,128)(2,1)} %bitcast.122, ...), custom_call_target="tpu_custom_call" | custom-call | flops 1 | bytes 1 | tf_op jit(solution)/shard_map/qkv_outer/pallas_call | solution.py:471
  342.7 8.2 %d_mod.2 = (bf16[1,832,1024]{2,1,0:T(8,128)(2,1)}, bf16[1,832,1024]{2,1,0:T(8,128)(2,1)}) custom-call(s32[1]{0:T(128)} %bitcast.core.flag, bf16[1,1664,384]{2,1,0:T(8,128)(2,1)} %get-tuple-element.210.refs_0_, bf16[1,1664,128]{2,1,0:T(8,128)(2,1)} %get-tuple-element.246.refs_1_, bf16[1,1664,384]{2,1,0:T(8,128)(2,1)} %get-tuple-element.216.refs_2_, ...), custom_call_target="tpu_custom_call" | custom-call | flops 1 | bytes 1 | tf_op jit(solution)/shard_map/d_mod/pallas_call | solution.py:516
  352.3 2.6 collective-permute-start.10
  355.5 10.9 %d_mod.3 = (bf16[1,832,1024]{2,1,0:T(8,128)(2,1)}, bf16[1,832,1024]{2,1,0:T(8,128)(2,1)}) custom-call(s32[1]{0:T(128)} %bitcast.core.flag, bf16[1,1664,384]{2,1,0:T(8,128)(2,1)} %get-tuple-element.257.refs_0_, bf16[1,1664,128]{2,1,0:T(8,128)(2,1)} %get-tuple-element.258.refs_1_, bf16[1,1664,384]{2,1,0:T(8,128)(2,1)} %get-tuple-element.259.refs_2_, ...), custom_call_target="tpu_custom_call" | custom-call | flops 1 | bytes 1 | tf_op jit(solution)/shard_map/d_mod/pallas_call | solution.py:516
  371.8 2.2 collective-permute-done.13
  378.0 4.0 collective-permute-start.16
  382.9 16.9 %in_outer.1 = (bf16[1,2,256,768]{3,2,1,0:T(8,128)(2,1)}, bf16[1,2,256,768]{3,2,1,0:T(8,128)(2,1)}, f32[1,8,1024]{2,1,0:T(8,128)}, bf16[1,832,1024]{2,1,0:T(8,128)(2,1)}) custom-call(s32[2]{0:T(128)} %pad_add_fusion.2.place, f32[1,832,1024]{2,1,0:T(8,128)} %get-tuple-element.188.dres_hbm.refs_1_, f32[1,6,1024]{2,1,0:T(8,128)} %reshape.1294.emb_ref.refs_2_, ...), custom_call_target="tpu_custom_call" | custom-call | flops 1 | bytes 1 | tf_op jit(solution)/shard_map/in_outer/pallas_call | solution.py:595
  411.5 7.0 %collective-permute-done.20 = f32[14336]{0:T(1024)S(1)} collective-permute-done((f32[14336]{0:T(1024)S(1)}, f32[14336]{0:T(1024)S(1)}, u32[]{:S(2)}, u32[]{:S(2)}) %collective-permute-start.20) | collective-permute-done | bytes 57376 | tf_op jit(solution)/shard_map/ppermute | solution.py:40
  423.2 7.4 %ada.1 = f32[1,1024]{1,0:T(1,128)} custom-call(bf16[1,6144]{1,0:T(2,128)(2,1)} %convert_element_type.350.t_ref, bf16[1024,6144]{1,0:T(8,128)(2,1)} %w_ref.1), custom_call_target="tpu_custom_call" | custom-call | flops 1 | bytes 1 | tf_op jit(solution)/shard_map/ada/pallas_call | solution.py:201
  432.6 2.2 collective-permute-start.27
  434.8 2.0 collective-permute-start.28
  439.5 7.9 %collective-permute-done.26 = bf16[256,768]{1,0:T(8,128)(2,1)S(1)} collective-permute-done((bf16[256,768]{1,0:T(8,128)(2,1)S(1)}, bf16[256,768]{1,0:T(8,128)(2,1)S(1)}, u32[]{:S(2)}, u32[]{:S(2)}) %collective-permute-start.26) | collective-permute-done | bytes 393248 | tf_op jit(solution)/shard_map/ppermute | solution.py:50
  447.5 3.4 collective-permute-done.28
  452.9 2.6 collective-permute-start.29
  455.6 3.3 collective-permute-done.30
  458.9 11.0 %d_in.1 = (f32[1,832,100]{2,1,0:T(8,128)}, f32[1,832,100]{2,1,0:T(8,128)}, f32[1,832,512]{2,1,0:T(8,128)}) custom-call(bf16[1,832,768]{2,1,0:T(8,128)(2,1)} %copy-done, f32[1,832,1024]{2,1,0:T(8,128)} %get-tuple-element.188.dres_hbm.refs_1_, f32[1,6,1024]{2,1,0:T(8,128)} %reshape.1294.emb_ref.refs_2_, f32[1,832,2]{2,1,0:T(8,128)} %copy.63.refs_3_, ...), custom_call_target="tpu_custom_call" | custom-call | flops 1 | bytes 1 | tf_op jit(solution)/shard_map/d_in/pallas_call | solution.py:644
  474.8 2.1 copy.65
  478.2 3.7 fusion.11
  489.6 2.0 concatenate.154
  (288 shorter events, 93.6 us)
Async XLA Ops:
  7.2 259.8 %reduce-scatter.2.cloned.1.call-start = ((), (), s32[]{:S(2)}) async-start(), calls=%async_computation.1 | async-start | bytes 13107200 | tf_op jit(solution)/shard_map/reduce_scatter | solution.py:1016
  14.0 16.2 %collective-permute-start = (bf16[1,832,768]{2,1,0:T(8,128)(2,1)S(1)}, bf16[1,832,768]{2,1,0:T(8,128)(2,1)}, u32[]{:S(2)}, u32[]{:S(2)}) collective-permute-start(bf16[1,832,768]{2,1,0:T(8,128)(2,1)S(1)} %maximum_maximum_fusion.x0_ref.x_ref.refs_0_), channel_id=1, source_target_pairs={{0,1},{1,0},{2,3},{3,2},{4,5},{5,4},{6,7},{7,6},{8,9},{9,8},{10,11... | collective-permute-start | bytes 3833864 | tf_op jit(solution)/shard_map/ppermute | solution.py:40
  14.5 31.2 %collective-permute-start.1 = (bf16[1,832,768]{2,1,0:T(8,128)(2,1)S(1)}, bf16[1,832,768]{2,1,0:T(8,128)(2,1)S(1)}, u32[]{:S(2)}, u32[]{:S(2)}) collective-permute-start(bf16[1,832,768]{2,1,0:T(8,128)(2,1)S(1)} %maximum_maximum_fusion.x0_ref.x_ref.refs_0_), channel_id=1, source_target_pairs={{0,2},{2,0},{1,3},{3,1},{4,6},{6,4},{5,7},{7,5},{8,10},{10,8},{9,1... | collective-permute-start | bytes 3833864 | tf_op jit(solution)/shard_map/ppermute | solution.py:35
  119.2 5.8 %collective-permute-start.3 = (bf16[1,832,512]{2,1,0:T(8,128)(2,1)}, bf16[1,832,512]{2,1,0:T(8,128)(2,1)S(1)}, u32[]{:S(2)}, u32[]{:S(2)}) collective-permute-start(bf16[1,832,512]{2,1,0:T(8,128)(2,1)} %get-tuple-element.222.refs_3_), channel_id=1, source_target_pairs={{0,1},{1,0},{2,3},{3,2},{4,5},{5,4},{6,7},{7,6},{8,9},{9,8},{10,11... | collective-permute-start | bytes 2555912 | tf_op jit(solution)/shard_map/ppermute | solution.py:40
  157.6 20.2 %collective-permute-start.4 = (bf16[1,832,512]{2,1,0:T(8,128)(2,1)}, bf16[1,832,512]{2,1,0:T(8,128)(2,1)S(1)}, u32[]{:S(2)}, u32[]{:S(2)}) collective-permute-start(bf16[1,832,512]{2,1,0:T(8,128)(2,1)} %get-tuple-element.195), channel_id=1, source_target_pairs={{0,1},{1,0},{2,3},{3,2},{4,5},{5,4},{6,7},{7,6},{8,9},{9,8},{10,11... | collective-permute-start | bytes 2555912 | tf_op jit(solution)/shard_map/ppermute | solution.py:40
  285.0 37.6 %collective-permute-start.6 = (bf16[640,1024]{1,0:T(8,128)(2,1)S(1)}, bf16[640,1024]{1,0:T(8,128)(2,1)S(1)}, u32[]{:S(2)}, u32[]{:S(2)}) collective-permute-start(bf16[640,1024]{1,0:T(8,128)(2,1)S(1)} %constant_dynamic-slice_fusion.5), channel_id=1, source_target_pairs={{0,4},{4,0},{1,5},{5,1},{2,6},{6,2},{3,7},{7,3},{8,12},{12,8},{9,1... | collective-permute-start | bytes 3932168 | tf_op jit(solution)/shard_map/ppermute | solution.py:40
  290.1 32.5 %collective-permute-start.7 = (bf16[512,1152]{1,0:T(8,128)(2,1)}, bf16[512,1152]{1,0:T(8,128)(2,1)}, u32[]{:S(2)}, u32[]{:S(2)}) collective-permute-start(bf16[512,1152]{1,0:T(8,128)(2,1)} %pad_maximum_fusion.2), channel_id=1, source_target_pairs={{0,2},{2,0},{1,3},{3,1},{4,6},{6,4},{5,7},{7,5},{8,10},{10,8},{9,1... | collective-permute-start | bytes 3538952 | tf_op jit(solution)/shard_map/ppermute | solution.py:35
  329.4 21.6 %collective-permute-start.8 = (bf16[320,1024]{1,0:T(8,128)(2,1)S(1)}, bf16[320,1024]{1,0:T(8,128)(2,1)}, u32[]{:S(2)}, u32[]{:S(2)}) collective-permute-start(bf16[320,1024]{1,0:T(8,128)(2,1)S(1)} %constant_dynamic-slice_fusion.4), channel_id=1, source_target_pairs={{0,8},{8,0},{16,24},{24,16},{1,9},{9,1},{17,25},{25,17},{2,10},{10... | collective-permute-start | bytes 1966088 | tf_op jit(solution)/shard_map/ppermute | solution.py:50
  341.2 25.2 %collective-permute-start.9 = (bf16[256,1152]{1,0:T(8,128)(2,1)}, bf16[256,1152]{1,0:T(8,128)(2,1)}, u32[]{:S(2)}, u32[]{:S(2)}) collective-permute-start(bf16[256,1152]{1,0:T(8,128)(2,1)} %fusion.1), channel_id=1, source_target_pairs={{0,4},{4,0},{1,5},{5,1},{2,6},{6,2},{3,7},{7,3},{8,12},{12,8},{9,1... | collective-permute-start | bytes 1769480 | tf_op jit(solution)/shard_map/ppermute | solution.py:40
  352.3 14.1 %collective-permute-start.10 = (bf16[160,1024]{1,0:T(8,128)(2,1)S(1)}, bf16[160,1024]{1,0:T(8,128)(2,1)S(1)}, u32[]{:S(2)}, u32[]{:S(2)}) collective-permute-start(bf16[160,1024]{1,0:T(8,128)(2,1)S(1)} %constant_dynamic-slice_fusion.3), channel_id=1, source_target_pairs={{0,24},{8,16},{16,8},{24,0},{1,25},{9,17},{17,9},{25,1},{2,26},{10... | collective-permute-start | bytes 983048 | tf_op jit(solution)/shard_map/ppermute | solution.py:50
  367.2 6.9 %collective-permute-start.11 = (bf16[1,832,1024]{2,1,0:T(8,128)(2,1)}, bf16[1,832,1024]{2,1,0:T(8,128)(2,1)S(1)}, u32[]{:S(2)}, u32[]{:S(2)}) collective-permute-start(bf16[1,832,1024]{2,1,0:T(8,128)(2,1)} %get-tuple-element.270), channel_id=1, source_target_pairs={{0,1},{1,0},{2,3},{3,2},{4,5},{5,4},{6,7},{7,6},{8,9},{9,8},{10,11... | collective-permute-start | bytes 5111816 | tf_op jit(solution)/shard_map/ppermute | solution.py:40
  367.2 6.9 %collective-permute-start.12 = (bf16[1,832,1024]{2,1,0:T(8,128)(2,1)}, bf16[1,832,1024]{2,1,0:T(8,128)(2,1)S(1)}, u32[]{:S(2)}, u32[]{:S(2)}) collective-permute-start(bf16[1,832,1024]{2,1,0:T(8,128)(2,1)} %get-tuple-element.271), channel_id=1, source_target_pairs={{0,1},{1,0},{2,3},{3,2},{4,5},{5,4},{6,7},{7,6},{8,9},{9,8},{10,11... | collective-permute-start | bytes 5111816 | tf_op jit(solution)/shard_map/ppermute | solution.py:40
  369.0 4.9 collective-permute-start.13
  375.3 24.5 %collective-permute-start.14 = (bf16[256,768]{1,0:T(8,128)(2,1)S(1)}, bf16[256,768]{1,0:T(8,128)(2,1)}, u32[]{:S(2)}, u32[]{:S(2)}) collective-permute-start(bf16[256,768]{1,0:T(8,128)(2,1)S(1)} %pad_maximum_fusion.9), channel_id=1, source_target_pairs={{0,2},{2,0},{1,3},{3,1},{4,6},{6,4},{5,7},{7,5},{8,10},{10,8},{9,1... | collective-permute-start | bytes 1179656 | tf_op jit(solution)/shard_map/ppermute | solution.py:35
  376.6 23.1 %collective-permute-start.15 = (bf16[160,1024]{1,0:T(8,128)(2,1)S(1)}, bf16[160,1024]{1,0:T(8,128)(2,1)S(1)}, u32[]{:S(2)}, u32[]{:S(2)}) collective-permute-start(bf16[160,1024]{1,0:T(8,128)(2,1)S(1)} %add_convert_fusion.6), channel_id=1, source_target_pairs={{0,24},{8,16},{16,8},{24,0},{1,25},{9,17},{17,9},{25,1},{2,26},{10... | collective-permute-start | bytes 983048 | tf_op jit(solution)/shard_map/ppermute | solution.py:50
  378.0 21.7 %collective-permute-start.16 = (bf16[128,1152]{1,0:T(8,128)(2,1)}, bf16[128,1152]{1,0:T(8,128)(2,1)}, u32[]{:S(2)}, u32[]{:S(2)}) collective-permute-start(bf16[128,1152]{1,0:T(8,128)(2,1)} %constant_dynamic-slice_fusion.2), channel_id=1, source_target_pairs={{0,8},{8,0},{16,24},{24,16},{1,9},{9,1},{17,25},{25,17},{2,10},{10... | collective-permute-start | bytes 884744 | tf_op jit(solution)/shard_map/ppermute | solution.py:50
  405.2 13.3 %collective-permute-start.19 = (bf16[256,768]{1,0:T(8,128)(2,1)S(1)}, bf16[256,768]{1,0:T(8,128)(2,1)S(1)}, u32[]{:S(2)}, u32[]{:S(2)}) collective-permute-start(bf16[256,768]{1,0:T(8,128)(2,1)S(1)} %fusion.2), channel_id=1, source_target_pairs={{0,2},{2,0},{1,3},{3,1},{4,6},{6,4},{5,7},{7,5},{8,10},{10,8},{9,1... | collective-permute-start | bytes 1179656 | tf_op jit(solution)/shard_map/ppermute | solution.py:35
  406.8 11.7 %collective-permute-start.21 = (bf16[64,1152]{1,0:T(8,128)(2,1)S(1)}, bf16[64,1152]{1,0:T(8,128)(2,1)S(1)}, u32[]{:S(2)}, u32[]{:S(2)}) collective-permute-start(bf16[64,1152]{1,0:T(8,128)(2,1)S(1)} %constant_dynamic-slice_fusion.1), channel_id=1, source_target_pairs={{0,24},{8,16},{16,8},{24,0},{1,25},{9,17},{17,9},{25,1},{2,26},{10... | collective-permute-start | bytes 442376 | tf_op jit(solution)/shard_map/ppermute | solution.py:50
  408.1 23.5 %collective-permute-start.24 = (bf16[320,1024]{1,0:T(8,128)(2,1)S(1)}, bf16[320,1024]{1,0:T(8,128)(2,1)S(1)}, u32[]{:S(2)}, u32[]{:S(2)}) collective-permute-start(bf16[320,1024]{1,0:T(8,128)(2,1)S(1)} %pad_maximum_fusion.3), channel_id=1, source_target_pairs={{0,8},{8,0},{16,24},{24,16},{1,9},{9,1},{17,25},{25,17},{2,10},{10... | collective-permute-start | bytes 1966088 | tf_op jit(solution)/shard_map/ppermute | solution.py:50
  408.2 10.3 %collective-permute-start.20 = (f32[14336]{0:T(1024)S(1)}, f32[14336]{0:T(1024)S(1)}, u32[]{:S(2)}, u32[]{:S(2)}) collective-permute-start(f32[14336]{0:T(1024)S(1)} %add.306), channel_id=1, source_target_pairs={{0,2},{2,0},{1,3},{3,1},{4,6},{6,4},{5,7},{7,5},{8,10},{10,8},{9,1... | collective-permute-start | bytes 172040 | tf_op jit(solution)/shard_map/ppermute | solution.py:40
  410.0 49.0 %collective-permute-start.31 = (bf16[1,832,1024]{2,1,0:T(8,128)(2,1)}, bf16[1,832,1024]{2,1,0:T(8,128)(2,1)}, u32[]{:S(2)}, u32[]{:S(2)}) collective-permute-start(bf16[1,832,1024]{2,1,0:T(8,128)(2,1)} %get-tuple-element.318), channel_id=1, source_target_pairs={{0,2},{2,0},{1,3},{3,1},{4,6},{6,4},{5,7},{7,5},{8,10},{10,8},{9,1... | collective-permute-start | bytes 5111816 | tf_op jit(solution)/shard_map/ppermute | solution.py:35
  419.9 11.6 %collective-permute-start.25 = (bf16[64,1152]{1,0:T(8,128)(2,1)S(1)}, bf16[64,1152]{1,0:T(8,128)(2,1)S(1)}, u32[]{:S(2)}, u32[]{:S(2)}) collective-permute-start(bf16[64,1152]{1,0:T(8,128)(2,1)S(1)} %add_convert_fusion.10), channel_id=1, source_target_pairs={{0,24},{8,16},{16,8},{24,0},{1,25},{9,17},{17,9},{25,1},{2,26},{10... | collective-permute-start | bytes 442376 | tf_op jit(solution)/shard_map/ppermute | solution.py:50
  421.1 10.4 %collective-permute-start.23 = (bf16[256,768]{1,0:T(8,128)(2,1)S(1)}, bf16[256,768]{1,0:T(8,128)(2,1)S(1)}, u32[]{:S(2)}, u32[]{:S(2)}) collective-permute-start(bf16[256,768]{1,0:T(8,128)(2,1)S(1)} %pad_maximum_fusion.10), channel_id=1, source_target_pairs={{0,4},{4,0},{1,5},{5,1},{2,6},{6,2},{3,7},{7,3},{8,12},{12,8},{9,1... | collective-permute-start | bytes 1179656 | tf_op jit(solution)/shard_map/ppermute | solution.py:40
  421.6 9.2 %collective-permute-start.22 = (f32[1,8448]{1,0:T(1,128)S(1)}, f32[1,8448]{1,0:T(1,128)S(1)}, u32[]{:S(2)}, u32[]{:S(2)}) collective-permute-start(f32[1,8448]{1,0:T(1,128)S(1)} %pad_maximum_fusion.17), channel_id=1, source_target_pairs={{0,4},{4,0},{1,5},{5,1},{2,6},{6,2},{3,7},{7,3},{8,12},{12,8},{9,1... | collective-permute-start | bytes 101384 | tf_op jit(solution)/shard_map/ppermute | solution.py:40
  432.1 49.8 %collective-permute-start.34 = (bf16[640,1024]{1,0:T(8,128)(2,1)S(1)}, bf16[640,1024]{1,0:T(8,128)(2,1)}, u32[]{:S(2)}, u32[]{:S(2)}) collective-permute-start(bf16[640,1024]{1,0:T(8,128)(2,1)S(1)} %pad_maximum_fusion.1), channel_id=1, source_target_pairs={{0,4},{4,0},{1,5},{5,1},{2,6},{6,2},{3,7},{7,3},{8,12},{12,8},{9,1... | collective-permute-start | bytes 3932168 | tf_op jit(solution)/shard_map/ppermute | solution.py:40
  432.6 6.9 %collective-permute-start.27 = (f32[2,8448]{1,0:T(2,128)S(1)}, f32[2,8448]{1,0:T(2,128)S(1)}, u32[]{:S(2)}, u32[]{:S(2)}) collective-permute-start(f32[2,8448]{1,0:T(2,128)S(1)} %pad_maximum_fusion.16), channel_id=1, source_target_pairs={{0,24},{8,16},{16,8},{24,0},{1,25},{9,17},{17,9},{25,1},{2,26},{10... | collective-permute-start | bytes 202760 | tf_op jit(solution)/shard_map/ppermute | solution.py:50
  434.8 12.6 %collective-permute-start.26 = (bf16[256,768]{1,0:T(8,128)(2,1)S(1)}, bf16[256,768]{1,0:T(8,128)(2,1)S(1)}, u32[]{:S(2)}, u32[]{:S(2)}) collective-permute-start(bf16[256,768]{1,0:T(8,128)(2,1)S(1)} %add_convert_fusion.5), channel_id=1, source_target_pairs={{0,8},{8,0},{16,24},{24,16},{1,9},{9,1},{17,25},{25,17},{2,10},{10... | collective-permute-start | bytes 1179656 | tf_op jit(solution)/shard_map/ppermute | solution.py:50
  434.8 16.1 %collective-permute-start.28 = (bf16[128,1152]{1,0:T(8,128)(2,1)S(1)}, bf16[128,1152]{1,0:T(8,128)(2,1)S(1)}, u32[]{:S(2)}, u32[]{:S(2)}) collective-permute-start(bf16[128,1152]{1,0:T(8,128)(2,1)S(1)} %pad_maximum_fusion.12), channel_id=1, source_target_pairs={{0,8},{8,0},{16,24},{24,16},{1,9},{9,1},{17,25},{25,17},{2,10},{10... | collective-permute-start | bytes 884744 | tf_op jit(solution)/shard_map/ppermute | solution.py:50
  450.9 7.9 %collective-permute-start.30 = (f32[4,8448]{1,0:T(4,128)S(1)}, f32[4,8448]{1,0:T(4,128)S(1)}, u32[]{:S(2)}, u32[]{:S(2)}) collective-permute-start(f32[4,8448]{1,0:T(4,128)S(1)} %pad_maximum_fusion.15), channel_id=1, source_target_pairs={{0,8},{8,0},{16,24},{24,16},{1,9},{9,1},{17,25},{25,17},{2,10},{10... | collective-permute-start | bytes 405512 | tf_op jit(solution)/shard_map/ppermute | solution.py:50
  451.3 36.3 %collective-permute-start.33 = (bf16[256,1152]{1,0:T(8,128)(2,1)S(1)}, bf16[256,1152]{1,0:T(8,128)(2,1)}, u32[]{:S(2)}, u32[]{:S(2)}) collective-permute-start(bf16[256,1152]{1,0:T(8,128)(2,1)S(1)} %pad_maximum_fusion.4), channel_id=1, source_target_pairs={{0,4},{4,0},{1,5},{5,1},{2,6},{6,2},{3,7},{7,3},{8,12},{12,8},{9,1... | collective-permute-start | bytes 1769480 | tf_op jit(solution)/shard_map/ppermute | solution.py:40
  452.9 17.1 %collective-permute-start.29 = (bf16[256,768]{1,0:T(8,128)(2,1)S(1)}, bf16[256,768]{1,0:T(8,128)(2,1)S(1)}, u32[]{:S(2)}, u32[]{:S(2)}) collective-permute-start(bf16[256,768]{1,0:T(8,128)(2,1)S(1)} %add_convert_fusion.4), channel_id=1, source_target_pairs={{0,24},{8,16},{16,8},{24,0},{1,25},{9,17},{17,9},{25,1},{2,26},{10... | collective-permute-start | bytes 1179656 | tf_op jit(solution)/shard_map/ppermute | solution.py:50
  471.3 16.4 %collective-permute-start.32 = (bf16[256,768]{1,0:T(8,128)(2,1)S(1)}, bf16[256,768]{1,0:T(8,128)(2,1)S(1)}, u32[]{:S(2)}, u32[]{:S(2)}) collective-permute-start(bf16[256,768]{1,0:T(8,128)(2,1)S(1)} %add_convert_fusion.3), channel_id=1, source_target_pairs={{0,4},{4,0},{1,5},{5,1},{2,6},{6,2},{3,7},{7,3},{8,12},{12,8},{9,1... | collective-permute-start | bytes 1179656 | tf_op jit(solution)/shard_map/ppermute | solution.py:40
  (39 other events, 406.1 us)
Sparse Core Ops, SparseCore 0:
  178.0 86.9 reduce-scatter.1

commit v5 on v4

--- a/solution.py
+++ b/solution.py
@@ -136,7 +136,10 @@
     angle_ref, mod_ref = rest[2 * len(parts) : 2 * len(parts) + 2]
     outs = rest[2 * len(parts) + 2 :]
     x = jnp.where(pl.program_id(1) == 0, x0_ref[...], x1_ref[...])[:, : win_ref.shape[0]]
-    cos, sin = wide_tables(angle_ref)
+    angles = angle_ref[...]
+    span = x0_ref.shape[0]
+    angles = jnp.where(pl.program_id(1) == 0, angles[:, :, :span], angles[:, :, span:])
+    cos, sin = wide_tables(angles)
     resid = dot_nn(x, win_ref[...]) + bin_ref[...]
     center = resid - jnp.mean(resid, axis=1, keepdims=True)
     inv = lax.rsqrt(jnp.mean(center * center, axis=1, keepdims=True) + EPS)
@@ -177,7 +180,7 @@
             in_specs=[one, one, whole(*w_in.shape), whole(1, model)]
             + [pl.BlockSpec((None, 6, model), lambda r, i, c: (r, 0, 0))]
             + w_specs
-            + [pl.BlockSpec((None, None, 2, 32, span), lambda r, i, c: (r, i, 0, 0, 0))],
+            + [pl.BlockSpec((None, 2, 32, n), lambda r, i, c: (r, 0, 0, 0))],
             out_specs=[pl.BlockSpec((None, None, model, span), lambda r, i, c: (r, i, 0, 0))]
             + [frame(half)] * len(parts),
         ),
@@ -910,7 +913,9 @@
 
 
 def frame_table(seg_lengths, frames):
-    ends = jnp.cumsum(seg_lengths, axis=1)
+    place = jnp.arange(seg_lengths.shape[1])
+    upto = place[None, :] <= place[:, None]
+    ends = jnp.sum(jnp.where(upto, seg_lengths[:, None, :], 0), axis=2)
     starts = ends - seg_lengths
     at = frames[None, :, None]
     inside = (at >= starts[:, None, :]) & (at < ends[:, None, :])
@@ -948,8 +953,8 @@
         return jnp.concatenate([(chip * 2 + core) * span + ramp, (chip * 2 + 1 - core) * span + ramp])
 
     member, _ = frame_table(seg_lengths, seq_index * span + ramp)
-    keep_audio = 1.0 - jnp.einsum("rcs,rs->rc", member, audio_drop.astype(F32))
-    keep_text = 1.0 - jnp.einsum("rcs,rs->rc", member, text_drop.astype(F32))
+    keep_audio = 1.0 - jnp.sum(member * audio_drop.astype(F32)[:, None, :], axis=2)
+    keep_text = 1.0 - jnp.sum(member * text_drop.astype(F32)[:, None, :], axis=2)
     keep = jnp.stack([keep_audio, keep_text], axis=2)
     frame_valid = 1.0 - member[:, :, -1:]
     width = w_in.shape[0]
@@ -975,15 +980,12 @@
         angles = rotary_angles(offsets, head_dim)
         return jnp.concatenate([inside, pad], axis=2), angles
 
-    def two_blocks(angles):
-        return jnp.moveaxis(angles.reshape(rows, 2, 32, 2, span), 3, 1)
-
     inside_near, ang_near = tables(chip_frames(sx))
     qx = jnp.where(jnp.arange(128) < seg_lengths.shape[1], 1.0 - inside_near, 0.0).astype(BF)
     kx_near = (MASKED * inside_near).astype(BF)
     bq, bi = as_row(b_qkv), as_row(b_in)
     mod_near, q, k_near, v_near = front(
-        core_arg, inputs, inputs_other, w_in, bi, embedding, w_qkv, bq, two_blocks(ang_near),
+        core_arg, inputs, inputs_other, w_in, bi, embedding, w_qkv, bq, ang_near,
         ("q", "k", "v"),
     )
     q, far_blocks = lax.optimization_barrier((q, far_blocks))
@@ -993,7 +995,7 @@
         inside, angles = tables(chip_frames((sx + t) % chips))
         made = front(
             core_arg, block, flip(block, "core", 1), w_in, bi, embedding, w_qkv, bq,
-            two_blocks(angles), ("k", "v"),
+            angles, ("k", "v"),
         )
         far.append((*made, (MASKED * inside).astype(BF), angles))
     join = lambda n, axis: far[0][n] if chips == 2 else jnp.concatenate([f[n] for f in far], axis=axis)

time: 506 us -> 502 us (level)
    unnamed x96 -> x94, local copies, waits for them, and re-layouts: 16.9 us -> 16.8 us
  transfers between devices with their start and end apart: 36 -> 36, of which waited for: 9 -> 10; matrix products, arithmetic and copies ran while one was open for 12% -> 11% of each run, Pallas kernels for 43% -> 43%
where the time goes in v5:
time: 502 us; the launch traced here: 496 us
  Pallas kernels  330 us (66%)
  other arithmetic  42.5 us (8%)
  starting transfers between devices  37.5 us (7%)
  waiting for transfers between devices  30.7 us (6%)
  local copies, waits for them, and re-layouts  29.7 us (6%)
  between operations  15.4 us (3%)
  matrix products  10 us (2%)
    pallas_call x2, Pallas kernels, attend_back(): pl.pallas_call(functools.partial(attend_back_kernel, blocks=len(blocks),...  115 us
    pallas_call x1, Pallas kernels, attend(): pl.pallas_call(attend_kernel, grid_spec=pltpu.PrefetchScalarGridSpec(num_...  57.5 us
    pallas_call x1, Pallas kernels, mid(): pl.pallas_call(mid_kernel, grid_spec=pltpu.PrefetchScalarGridSpec(num_sca...  31.6 us
    pallas_call x2, Pallas kernels, front(): pl.pallas_call(functools.partial(front_kernel, parts=parts), grid_spec=pl...  26.6 us
    pallas_call x2, Pallas kernels, qkv_outer(): pl.pallas_call(functools.partial(qkv_outer_kernel, far=len(far)), grid_sp...  24.7 us
    pallas_call x1, Pallas kernels, outer(): pl.pallas_call(outer_kernel, grid_spec=pltpu.PrefetchScalarGridSpec(num_s...  20.2 us
    pallas_call x2, Pallas kernels, d_mod(): pl.pallas_call(functools.partial(d_mod_kernel, parts=tuple((len(g) for _,...  19.1 us
    ppermute x12, starting transfers between devices, near_flip(): lax.ppermute(v, axis, [(i, place[gray(i) ^ bit]) for i in range(size)])  19 us
  transfers between devices with their start and end apart: 36, of which 10 were waited for; matrix products, arithmetic and copies ran while one was open for 11% of the time, Pallas kernels for 43%

profile of v5, /device:TPU:0, one launch (start us, length us, event | category | flops | bytes accessed | tf_op | source)
XLA Modules:
  0.0 495.7 jit_solution(13790953691459183355)
XLA Ops:
  15.6 2.6 collective-permute-start.1
  19.3 6.3 %fusion.16 = f32[1,6144]{1,0:T(1,128)S(1)} fusion(bf16[1024,6144]{1,0:T(8,128)(2,1)} %w_ref.1, bf16[1,1024]{1,0:T(2,128)(2,1)S(1)} %copy-done.19), kind=kOutput, calls=%fused_computation.152 | convolution fusion | flops 12589056 | bytes 12609536 | tf_op jit(solution)/shard_map/dot_general | solution.py:22
  30.0 14.7 %front.2 = (bf16[1,2,1024,832]{3,2,1,0:T(8,128)(2,1)}, bf16[1,1664,512]{2,1,0:T(8,128)(2,1)}, bf16[1,1664,512]{2,1,0:T(8,128)(2,1)}, bf16[1,1664,512]{2,1,0:T(8,128)(2,1)}) custom-call(s32[1]{0:T(128)} %bitcast.core.flag, bf16[1,832,768]{2,1,0:T(8,128)(2,1)} %copy-done, bf16[1,832,768]{2,1,0:T(8,128)(2,1)} %collective-permute-done.x1_ref, ...), custom_call_target="tpu_custom_call" | custom-call | flops 1 | bytes 1 | tf_op jit(solution)/shard_map/front/pallas_call | solution.py:175
  44.7 2.1 collective-permute-done.1.x0_ref.refs_3_
  51.7 11.9 %front.3 = (bf16[1,2,1024,832]{3,2,1,0:T(8,128)(2,1)}, bf16[1,1664,512]{2,1,0:T(8,128)(2,1)}, bf16[1,1664,512]{2,1,0:T(8,128)(2,1)}) custom-call(s32[1]{0:T(128)} %bitcast.core.flag, bf16[1,832,768]{2,1,0:T(8,128)(2,1)} %copy-done.2, bf16[1,832,768]{2,1,0:T(8,128)(2,1)} %copy-done.12, bf16[712,1024]{1,0:T(8,128)(2,1)} %refs_4_.3, f32[1,1024]{1,0:T(1,128)} %bitcast.121, ...), custom_call_target="tpu_custom_call" | custom-call | flops 1 | bytes 1 | tf_op jit(solution)/shard_map/front/pallas_call | solution.py:175
  63.7 57.5 %attend.1 = (bf16[1,832,512]{2,1,0:T(8,128)(2,1)}, bf16[1,832,512]{2,1,0:T(8,128)(2,1)}, f32[1,1664,512]{2,1,0:T(8,128)}) custom-call(s32[1]{0:T(128)} %bitcast.core.flag, bf16[1,1664,512]{2,1,0:T(8,128)(2,1)} %get-tuple-element.219.q_ref.refs_0_, bf16[1,1664,128]{2,1,0:T(8,128)(2,1)} %get-tuple-element.220.qx_ref.refs_1_, ...), custom_call_target="tpu_custom_call" | custom-call | flops 1 | bytes 1 | tf_op jit(solution)/shard_map/attend/pallas_call | solution.py:730
  125.6 31.6 %mid.1 = (f32[1,832,1024]{2,1,0:T(8,128)}, bf16[1,832,512]{2,1,0:T(8,128)(2,1)}, bf16[1,832,512]{2,1,0:T(8,128)(2,1)}, bf16[1,832,1024]{2,1,0:T(8,128)(2,1)}, f3...) custom-call(s32[1]{0:T(128)} %bitcast.core.flag, ...), custom_call_target="tpu_custom_call" | custom-call | flops 1 | bytes 1 | tf_op jit(solution)/shard_map/mid/pallas_call | solution.py:315
  157.3 20.2 %outer.1 = bf16[4,1280,1024]{2,1,0:T(8,128)(2,1)} custom-call(s32[1]{0:T(128)} %bitcast.core.flag, bf16[832,1024]{1,0:T(8,128)(2,1)} %bitcast.108, bf16[832,2048]{1,0:T(8,128)(2,1)} %bitcast.102, bf16[832,512]{1,0:T(8,128)(2,1)} %bitcast.96, bf16[832,512]{1,0:T(8,128)(2,1)} %bitcast.104, bf16[832,2048]{1,0:T(8,128)(2,1)} %bitcast.103, ...), custom_call_target="tpu_custom_call" | custom-call | flops 1 | bytes 1 | tf_op jit(solution)/shard_map/outer/pallas_call | solution.py:404
  179.0 84.0 %attend_back.2 = (bf16[1,1664,384]{2,1,0:T(8,128)(2,1)}, bf16[1,1664,384]{2,1,0:T(8,128)(2,1)}, bf16[1,1664,384]{2,1,0:T(8,128)(2,1)}, bf16[1,1664,384]{2,1,0:T(8,128)(2,1)}, bf16[1,1664,384]{2,1,0:T(8,128)(2,1)}) custom-call(s32[1]{0:T(128)} %bitcast.core.flag, bf16[1,1664,512]{2,1,0:T(8,128)(2,1)} %get-tuple-element.219.q_ref.refs_0_, ...), custom_call_target="tpu_custom_call" | custom-call | flops 1 | bytes 1 | tf_op jit(solution)/shard_map/attend_back/pallas_call | solution.py:884
  266.0 16.0 %qkv_outer.2 = (bf16[2,256,1152]{2,1,0:T(8,128)(2,1)}, bf16[2,256,1152]{2,1,0:T(8,128)(2,1)}, f32[8,1152]{1,0:T(8,128)}) custom-call(s32[2]{0:T(128)} %pad_add_fusion.2.place, bf16[2,1024,832]{2,1,0:T(8,128)(2,1)} %bitcast.92, bf16[1664,384]{1,0:T(8,128)(2,1)} %bitcast.99, bf16[1664,384]{1,0:T(8,128)(2,1)} %bitcast.100, bf16[1664,384]{1,0:T(8,128)(2,1)} %bitcast.101, ...), custom_call_target="tpu_custom_call" | custom-call | flops 1 | bytes 1 | tf_op jit(solution)/shard_map/qkv_outer/pallas_call | solution.py:474
  287.6 30.9 %attend_back.3 = (bf16[1,1664,128]{2,1,0:T(8,128)(2,1)}, bf16[1,1664,128]{2,1,0:T(8,128)(2,1)}, bf16[1,1664,128]{2,1,0:T(8,128)(2,1)}, bf16[1,1664,128]{2,1,0:T(8,128)(2,1)}, bf16[1,1664,128]{2,1,0:T(8,128)(2,1)}) custom-call(s32[1]{0:T(128)} %bitcast.core.flag, bf16[1,1664,512]{2,1,0:T(8,128)(2,1)} %get-tuple-element.219.q_ref.refs_0_, ...), custom_call_target="tpu_custom_call" | custom-call | flops 1 | bytes 1 | tf_op jit(solution)/shard_map/attend_back/pallas_call | solution.py:884
  319.6 2.3 add_convert_fusion
  323.2 2.1 fusion.1
  328.6 8.6 %qkv_outer.3 = (bf16[2,256,384]{2,1,0:T(8,128)(2,1)}, bf16[2,256,384]{2,1,0:T(8,128)(2,1)}, f32[8,384]{1,0:T(8,128)}) custom-call(s32[2]{0:T(128)} %pad_add_fusion.2.place, bf16[2,1024,832]{2,1,0:T(8,128)(2,1)} %bitcast.93, bf16[1664,128]{1,0:T(8,128)(2,1)} %bitcast.112, bf16[1664,128]{1,0:T(8,128)(2,1)} %bitcast.113, bf16[1664,128]{1,0:T(8,128)(2,1)} %bitcast.114, ...), custom_call_target="tpu_custom_call" | custom-call | flops 1 | bytes 1 | tf_op jit(solution)/shard_map/qkv_outer/pallas_call | solution.py:474
  338.7 8.2 %d_mod.2 = (bf16[1,832,1024]{2,1,0:T(8,128)(2,1)}, bf16[1,832,1024]{2,1,0:T(8,128)(2,1)}) custom-call(s32[1]{0:T(128)} %bitcast.core.flag, bf16[1,1664,384]{2,1,0:T(8,128)(2,1)} %get-tuple-element.210.refs_0_, bf16[1,1664,128]{2,1,0:T(8,128)(2,1)} %get-tuple-element.246.refs_1_, bf16[1,1664,384]{2,1,0:T(8,128)(2,1)} %get-tuple-element.216.refs_2_, ...), custom_call_target="tpu_custom_call" | custom-call | flops 1 | bytes 1 | tf_op jit(solution)/shard_map/d_mod/pallas_call | solution.py:519
  348.3 2.4 collective-permute-start.10
  351.4 10.9 %d_mod.3 = (bf16[1,832,1024]{2,1,0:T(8,128)(2,1)}, bf16[1,832,1024]{2,1,0:T(8,128)(2,1)}) custom-call(s32[1]{0:T(128)} %bitcast.core.flag, bf16[1,1664,384]{2,1,0:T(8,128)(2,1)} %get-tuple-element.257.refs_0_, bf16[1,1664,128]{2,1,0:T(8,128)(2,1)} %get-tuple-element.258.refs_1_, bf16[1,1664,384]{2,1,0:T(8,128)(2,1)} %get-tuple-element.259.refs_2_, ...), custom_call_target="tpu_custom_call" | custom-call | flops 1 | bytes 1 | tf_op jit(solution)/shard_map/d_mod/pallas_call | solution.py:519
  367.6 2.2 collective-permute-done.13
  374.9 3.5 collective-permute-start.16
  379.3 16.9 %in_outer.1 = (bf16[1,2,256,768]{3,2,1,0:T(8,128)(2,1)}, bf16[1,2,256,768]{3,2,1,0:T(8,128)(2,1)}, f32[1,8,1024]{2,1,0:T(8,128)}, bf16[1,832,1024]{2,1,0:T(8,128)(2,1)}) custom-call(s32[2]{0:T(128)} %pad_add_fusion.2.place, f32[1,832,1024]{2,1,0:T(8,128)} %get-tuple-element.188.dres_hbm.refs_1_, f32[1,6,1024]{2,1,0:T(8,128)} %reshape.1310.emb_ref.refs_2_, ...), custom_call_target="tpu_custom_call" | custom-call | flops 1 | bytes 1 | tf_op jit(solution)/shard_map/in_outer/pallas_call | solution.py:598
  407.3 7.6 %collective-permute-done.20 = f32[14336]{0:T(1024)S(1)} collective-permute-done((f32[14336]{0:T(1024)S(1)}, f32[14336]{0:T(1024)S(1)}, u32[]{:S(2)}, u32[]{:S(2)}) %collective-permute-start.20) | collective-permute-done | bytes 57376 | tf_op jit(solution)/shard_map/ppermute | solution.py:40
  419.6 7.4 %ada.1 = f32[1,1024]{1,0:T(1,128)} custom-call(bf16[1,6144]{1,0:T(2,128)(2,1)} %convert_element_type.346.t_ref, bf16[1024,6144]{1,0:T(8,128)(2,1)} %w_ref.1), custom_call_target="tpu_custom_call" | custom-call | flops 1 | bytes 1 | tf_op jit(solution)/shard_map/ada/pallas_call | solution.py:204
  428.7 2.6 collective-permute-start.27
  431.3 2.0 collective-permute-start.28
  435.6 8.0 %collective-permute-done.26 = bf16[256,768]{1,0:T(8,128)(2,1)S(1)} collective-permute-done((bf16[256,768]{1,0:T(8,128)(2,1)S(1)}, bf16[256,768]{1,0:T(8,128)(2,1)S(1)}, u32[]{:S(2)}, u32[]{:S(2)}) %collective-permute-start.26) | collective-permute-done | bytes 393248 | tf_op jit(solution)/shard_map/ppermute | solution.py:50
  443.7 3.5 collective-permute-done.28
  449.0 2.3 collective-permute-start.29
  451.3 3.3 collective-permute-done.30
  454.8 11.0 %d_in.1 = (f32[1,832,100]{2,1,0:T(8,128)}, f32[1,832,100]{2,1,0:T(8,128)}, f32[1,832,512]{2,1,0:T(8,128)}) custom-call(bf16[1,832,768]{2,1,0:T(8,128)(2,1)} %copy-done, f32[1,832,1024]{2,1,0:T(8,128)} %get-tuple-element.188.dres_hbm.refs_1_, f32[1,6,1024]{2,1,0:T(8,128)} %reshape.1310.emb_ref.refs_2_, f32[1,832,2]{2,1,0:T(8,128)} %copy.68.refs_3_, ...), custom_call_target="tpu_custom_call" | custom-call | flops 1 | bytes 1 | tf_op jit(solution)/shard_map/d_in/pallas_call | solution.py:647
  470.5 2.1 copy.70
  474.0 3.7 fusion.11
  485.4 2.0 concatenate.140
  (273 shorter events, 89.6 us)
Async XLA Ops:
  7.2 257.4 %reduce-scatter.2.cloned.1.call-start = ((), (), s32[]{:S(2)}) async-start(), calls=%async_computation.1 | async-start | bytes 13107200 | tf_op jit(solution)/shard_map/reduce_scatter | solution.py:1018
  15.1 14.9 %collective-permute-start = (bf16[1,832,768]{2,1,0:T(8,128)(2,1)S(1)}, bf16[1,832,768]{2,1,0:T(8,128)(2,1)}, u32[]{:S(2)}, u32[]{:S(2)}) collective-permute-start(bf16[1,832,768]{2,1,0:T(8,128)(2,1)S(1)} %maximum_maximum_fusion.x0_ref.x_ref.refs_0_), channel_id=1, source_target_pairs={{0,1},{1,0},{2,3},{3,2},{4,5},{5,4},{6,7},{7,6},{8,9},{9,8},{10,11... | collective-permute-start | bytes 3833864 | tf_op jit(solution)/shard_map/ppermute | solution.py:40
  15.6 31.2 %collective-permute-start.1 = (bf16[1,832,768]{2,1,0:T(8,128)(2,1)S(1)}, bf16[1,832,768]{2,1,0:T(8,128)(2,1)S(1)}, u32[]{:S(2)}, u32[]{:S(2)}) collective-permute-start(bf16[1,832,768]{2,1,0:T(8,128)(2,1)S(1)} %maximum_maximum_fusion.x0_ref.x_ref.refs_0_), channel_id=1, source_target_pairs={{0,2},{2,0},{1,3},{3,1},{4,6},{6,4},{5,7},{7,5},{8,10},{10,8},{9,1... | collective-permute-start | bytes 3833864 | tf_op jit(solution)/shard_map/ppermute | solution.py:35
  46.8 3.8 collective-permute-start.2
  157.2 20.3 %collective-permute-start.4 = (bf16[1,832,512]{2,1,0:T(8,128)(2,1)}, bf16[1,832,512]{2,1,0:T(8,128)(2,1)S(1)}, u32[]{:S(2)}, u32[]{:S(2)}) collective-permute-start(bf16[1,832,512]{2,1,0:T(8,128)(2,1)} %get-tuple-element.195), channel_id=1, source_target_pairs={{0,1},{1,0},{2,3},{3,2},{4,5},{5,4},{6,7},{7,6},{8,9},{9,8},{10,11... | collective-permute-start | bytes 2555912 | tf_op jit(solution)/shard_map/ppermute | solution.py:40
  282.0 36.5 %collective-permute-start.6 = (bf16[640,1024]{1,0:T(8,128)(2,1)S(1)}, bf16[640,1024]{1,0:T(8,128)(2,1)S(1)}, u32[]{:S(2)}, u32[]{:S(2)}) collective-permute-start(bf16[640,1024]{1,0:T(8,128)(2,1)S(1)} %constant_dynamic-slice_fusion.5), channel_id=1, source_target_pairs={{0,4},{4,0},{1,5},{5,1},{2,6},{6,2},{3,7},{7,3},{8,12},{12,8},{9,1... | collective-permute-start | bytes 3932168 | tf_op jit(solution)/shard_map/ppermute | solution.py:40
  287.3 31.3 %collective-permute-start.7 = (bf16[512,1152]{1,0:T(8,128)(2,1)}, bf16[512,1152]{1,0:T(8,128)(2,1)}, u32[]{:S(2)}, u32[]{:S(2)}) collective-permute-start(bf16[512,1152]{1,0:T(8,128)(2,1)} %pad_maximum_fusion.2), channel_id=1, source_target_pairs={{0,2},{2,0},{1,3},{3,1},{4,6},{6,4},{5,7},{7,5},{8,10},{10,8},{9,1... | collective-permute-start | bytes 3538952 | tf_op jit(solution)/shard_map/ppermute | solution.py:35
  325.3 21.7 %collective-permute-start.8 = (bf16[320,1024]{1,0:T(8,128)(2,1)S(1)}, bf16[320,1024]{1,0:T(8,128)(2,1)}, u32[]{:S(2)}, u32[]{:S(2)}) collective-permute-start(bf16[320,1024]{1,0:T(8,128)(2,1)S(1)} %constant_dynamic-slice_fusion.4), channel_id=1, source_target_pairs={{0,8},{8,0},{16,24},{24,16},{1,9},{9,1},{17,25},{25,17},{2,10},{10... | collective-permute-start | bytes 1966088 | tf_op jit(solution)/shard_map/ppermute | solution.py:50
  337.3 25.0 %collective-permute-start.9 = (bf16[256,1152]{1,0:T(8,128)(2,1)}, bf16[256,1152]{1,0:T(8,128)(2,1)}, u32[]{:S(2)}, u32[]{:S(2)}) collective-permute-start(bf16[256,1152]{1,0:T(8,128)(2,1)} %fusion.1), channel_id=1, source_target_pairs={{0,4},{4,0},{1,5},{5,1},{2,6},{6,2},{3,7},{7,3},{8,12},{12,8},{9,1... | collective-permute-start | bytes 1769480 | tf_op jit(solution)/shard_map/ppermute | solution.py:40
  348.3 13.9 %collective-permute-start.10 = (bf16[160,1024]{1,0:T(8,128)(2,1)S(1)}, bf16[160,1024]{1,0:T(8,128)(2,1)S(1)}, u32[]{:S(2)}, u32[]{:S(2)}) collective-permute-start(bf16[160,1024]{1,0:T(8,128)(2,1)S(1)} %constant_dynamic-slice_fusion.3), channel_id=1, source_target_pairs={{0,24},{8,16},{16,8},{24,0},{1,25},{9,17},{17,9},{25,1},{2,26},{10... | collective-permute-start | bytes 983048 | tf_op jit(solution)/shard_map/ppermute | solution.py:50
  363.0 6.9 %collective-permute-start.11 = (bf16[1,832,1024]{2,1,0:T(8,128)(2,1)}, bf16[1,832,1024]{2,1,0:T(8,128)(2,1)S(1)}, u32[]{:S(2)}, u32[]{:S(2)}) collective-permute-start(bf16[1,832,1024]{2,1,0:T(8,128)(2,1)} %get-tuple-element.270), channel_id=1, source_target_pairs={{0,1},{1,0},{2,3},{3,2},{4,5},{5,4},{6,7},{7,6},{8,9},{9,8},{10,11... | collective-permute-start | bytes 5111816 | tf_op jit(solution)/shard_map/ppermute | solution.py:40
  363.0 6.9 %collective-permute-start.12 = (bf16[1,832,1024]{2,1,0:T(8,128)(2,1)}, bf16[1,832,1024]{2,1,0:T(8,128)(2,1)S(1)}, u32[]{:S(2)}, u32[]{:S(2)}) collective-permute-start(bf16[1,832,1024]{2,1,0:T(8,128)(2,1)} %get-tuple-element.271), channel_id=1, source_target_pairs={{0,1},{1,0},{2,3},{3,2},{4,5},{5,4},{6,7},{7,6},{8,9},{9,8},{10,11... | collective-permute-start | bytes 5111816 | tf_op jit(solution)/shard_map/ppermute | solution.py:40
  364.9 5.0 collective-permute-start.13
  371.1 25.1 %collective-permute-start.14 = (bf16[256,768]{1,0:T(8,128)(2,1)S(1)}, bf16[256,768]{1,0:T(8,128)(2,1)}, u32[]{:S(2)}, u32[]{:S(2)}) collective-permute-start(bf16[256,768]{1,0:T(8,128)(2,1)S(1)} %pad_maximum_fusion.9), channel_id=1, source_target_pairs={{0,2},{2,0},{1,3},{3,1},{4,6},{6,4},{5,7},{7,5},{8,10},{10,8},{9,1... | collective-permute-start | bytes 1179656 | tf_op jit(solution)/shard_map/ppermute | solution.py:35
  373.4 22.8 %collective-permute-start.15 = (bf16[160,1024]{1,0:T(8,128)(2,1)S(1)}, bf16[160,1024]{1,0:T(8,128)(2,1)S(1)}, u32[]{:S(2)}, u32[]{:S(2)}) collective-permute-start(bf16[160,1024]{1,0:T(8,128)(2,1)S(1)} %add_convert_fusion.6), channel_id=1, source_target_pairs={{0,24},{8,16},{16,8},{24,0},{1,25},{9,17},{17,9},{25,1},{2,26},{10... | collective-permute-start | bytes 983048 | tf_op jit(solution)/shard_map/ppermute | solution.py:50
  374.9 21.3 %collective-permute-start.16 = (bf16[128,1152]{1,0:T(8,128)(2,1)}, bf16[128,1152]{1,0:T(8,128)(2,1)}, u32[]{:S(2)}, u32[]{:S(2)}) collective-permute-start(bf16[128,1152]{1,0:T(8,128)(2,1)} %constant_dynamic-slice_fusion.2), channel_id=1, source_target_pairs={{0,8},{8,0},{16,24},{24,16},{1,9},{9,1},{17,25},{25,17},{2,10},{10... | collective-permute-start | bytes 884744 | tf_op jit(solution)/shard_map/ppermute | solution.py:50
  401.6 13.3 %collective-permute-start.19 = (bf16[256,768]{1,0:T(8,128)(2,1)S(1)}, bf16[256,768]{1,0:T(8,128)(2,1)S(1)}, u32[]{:S(2)}, u32[]{:S(2)}) collective-permute-start(bf16[256,768]{1,0:T(8,128)(2,1)S(1)} %fusion.2), channel_id=1, source_target_pairs={{0,2},{2,0},{1,3},{3,1},{4,6},{6,4},{5,7},{7,5},{8,10},{10,8},{9,1... | collective-permute-start | bytes 1179656 | tf_op jit(solution)/shard_map/ppermute | solution.py:35
  402.5 12.4 %collective-permute-start.21 = (bf16[64,1152]{1,0:T(8,128)(2,1)S(1)}, bf16[64,1152]{1,0:T(8,128)(2,1)S(1)}, u32[]{:S(2)}, u32[]{:S(2)}) collective-permute-start(bf16[64,1152]{1,0:T(8,128)(2,1)S(1)} %constant_dynamic-slice_fusion.1), channel_id=1, source_target_pairs={{0,24},{8,16},{16,8},{24,0},{1,25},{9,17},{17,9},{25,1},{2,26},{10... | collective-permute-start | bytes 442376 | tf_op jit(solution)/shard_map/ppermute | solution.py:50
  403.9 23.5 %collective-permute-start.24 = (bf16[320,1024]{1,0:T(8,128)(2,1)S(1)}, bf16[320,1024]{1,0:T(8,128)(2,1)S(1)}, u32[]{:S(2)}, u32[]{:S(2)}) collective-permute-start(bf16[320,1024]{1,0:T(8,128)(2,1)S(1)} %pad_maximum_fusion.3), channel_id=1, source_target_pairs={{0,8},{8,0},{16,24},{24,16},{1,9},{9,1},{17,25},{25,17},{2,10},{10... | collective-permute-start | bytes 1966088 | tf_op jit(solution)/shard_map/ppermute | solution.py:50
  404.0 10.9 %collective-permute-start.20 = (f32[14336]{0:T(1024)S(1)}, f32[14336]{0:T(1024)S(1)}, u32[]{:S(2)}, u32[]{:S(2)}) collective-permute-start(f32[14336]{0:T(1024)S(1)} %add.270), channel_id=1, source_target_pairs={{0,2},{2,0},{1,3},{3,1},{4,6},{6,4},{5,7},{7,5},{8,10},{10,8},{9,1... | collective-permute-start | bytes 172040 | tf_op jit(solution)/shard_map/ppermute | solution.py:40
  406.4 48.4 %collective-permute-start.31 = (bf16[1,832,1024]{2,1,0:T(8,128)(2,1)}, bf16[1,832,1024]{2,1,0:T(8,128)(2,1)}, u32[]{:S(2)}, u32[]{:S(2)}) collective-permute-start(bf16[1,832,1024]{2,1,0:T(8,128)(2,1)} %get-tuple-element.318), channel_id=1, source_target_pairs={{0,2},{2,0},{1,3},{3,1},{4,6},{6,4},{5,7},{7,5},{8,10},{10,8},{9,1... | collective-permute-start | bytes 5111816 | tf_op jit(solution)/shard_map/ppermute | solution.py:35
  416.3 11.1 %collective-permute-start.25 = (bf16[64,1152]{1,0:T(8,128)(2,1)S(1)}, bf16[64,1152]{1,0:T(8,128)(2,1)S(1)}, u32[]{:S(2)}, u32[]{:S(2)}) collective-permute-start(bf16[64,1152]{1,0:T(8,128)(2,1)S(1)} %add_convert_fusion.10), channel_id=1, source_target_pairs={{0,24},{8,16},{16,8},{24,0},{1,25},{9,17},{17,9},{25,1},{2,26},{10... | collective-permute-start | bytes 442376 | tf_op jit(solution)/shard_map/ppermute | solution.py:50
  417.5 9.9 %collective-permute-start.23 = (bf16[256,768]{1,0:T(8,128)(2,1)S(1)}, bf16[256,768]{1,0:T(8,128)(2,1)S(1)}, u32[]{:S(2)}, u32[]{:S(2)}) collective-permute-start(bf16[256,768]{1,0:T(8,128)(2,1)S(1)} %pad_maximum_fusion.10), channel_id=1, source_target_pairs={{0,4},{4,0},{1,5},{5,1},{2,6},{6,2},{3,7},{7,3},{8,12},{12,8},{9,1... | collective-permute-start | bytes 1179656 | tf_op jit(solution)/shard_map/ppermute | solution.py:40
  418.1 9.2 %collective-permute-start.22 = (f32[1,8448]{1,0:T(1,128)S(1)}, f32[1,8448]{1,0:T(1,128)S(1)}, u32[]{:S(2)}, u32[]{:S(2)}) collective-permute-start(f32[1,8448]{1,0:T(1,128)S(1)} %pad_maximum_fusion.17), channel_id=1, source_target_pairs={{0,4},{4,0},{1,5},{5,1},{2,6},{6,2},{3,7},{7,3},{8,12},{12,8},{9,1... | collective-permute-start | bytes 101384 | tf_op jit(solution)/shard_map/ppermute | solution.py:40
  428.0 49.7 %collective-permute-start.34 = (bf16[640,1024]{1,0:T(8,128)(2,1)S(1)}, bf16[640,1024]{1,0:T(8,128)(2,1)}, u32[]{:S(2)}, u32[]{:S(2)}) collective-permute-start(bf16[640,1024]{1,0:T(8,128)(2,1)S(1)} %pad_maximum_fusion.1), channel_id=1, source_target_pairs={{0,4},{4,0},{1,5},{5,1},{2,6},{6,2},{3,7},{7,3},{8,12},{12,8},{9,1... | collective-permute-start | bytes 3932168 | tf_op jit(solution)/shard_map/ppermute | solution.py:40
  428.7 6.9 %collective-permute-start.27 = (f32[2,8448]{1,0:T(2,128)S(1)}, f32[2,8448]{1,0:T(2,128)S(1)}, u32[]{:S(2)}, u32[]{:S(2)}) collective-permute-start(f32[2,8448]{1,0:T(2,128)S(1)} %pad_maximum_fusion.16), channel_id=1, source_target_pairs={{0,24},{8,16},{16,8},{24,0},{1,25},{9,17},{17,9},{25,1},{2,26},{10... | collective-permute-start | bytes 202760 | tf_op jit(solution)/shard_map/ppermute | solution.py:50
  431.3 12.3 %collective-permute-start.26 = (bf16[256,768]{1,0:T(8,128)(2,1)S(1)}, bf16[256,768]{1,0:T(8,128)(2,1)S(1)}, u32[]{:S(2)}, u32[]{:S(2)}) collective-permute-start(bf16[256,768]{1,0:T(8,128)(2,1)S(1)} %add_convert_fusion.5), channel_id=1, source_target_pairs={{0,8},{8,0},{16,24},{24,16},{1,9},{9,1},{17,25},{25,17},{2,10},{10... | collective-permute-start | bytes 1179656 | tf_op jit(solution)/shard_map/ppermute | solution.py:50
  431.3 15.8 %collective-permute-start.28 = (bf16[128,1152]{1,0:T(8,128)(2,1)S(1)}, bf16[128,1152]{1,0:T(8,128)(2,1)S(1)}, u32[]{:S(2)}, u32[]{:S(2)}) collective-permute-start(bf16[128,1152]{1,0:T(8,128)(2,1)S(1)} %pad_maximum_fusion.12), channel_id=1, source_target_pairs={{0,8},{8,0},{16,24},{24,16},{1,9},{9,1},{17,25},{25,17},{2,10},{10... | collective-permute-start | bytes 884744 | tf_op jit(solution)/shard_map/ppermute | solution.py:50
  447.1 7.6 %collective-permute-start.30 = (f32[4,8448]{1,0:T(4,128)S(1)}, f32[4,8448]{1,0:T(4,128)S(1)}, u32[]{:S(2)}, u32[]{:S(2)}) collective-permute-start(f32[4,8448]{1,0:T(4,128)S(1)} %pad_maximum_fusion.15), channel_id=1, source_target_pairs={{0,8},{8,0},{16,24},{24,16},{1,9},{9,1},{17,25},{25,17},{2,10},{10... | collective-permute-start | bytes 405512 | tf_op jit(solution)/shard_map/ppermute | solution.py:50
  447.5 36.0 %collective-permute-start.33 = (bf16[256,1152]{1,0:T(8,128)(2,1)S(1)}, bf16[256,1152]{1,0:T(8,128)(2,1)}, u32[]{:S(2)}, u32[]{:S(2)}) collective-permute-start(bf16[256,1152]{1,0:T(8,128)(2,1)S(1)} %pad_maximum_fusion.4), channel_id=1, source_target_pairs={{0,4},{4,0},{1,5},{5,1},{2,6},{6,2},{3,7},{7,3},{8,12},{12,8},{9,1... | collective-permute-start | bytes 1769480 | tf_op jit(solution)/shard_map/ppermute | solution.py:40
  449.0 16.8 %collective-permute-start.29 = (bf16[256,768]{1,0:T(8,128)(2,1)S(1)}, bf16[256,768]{1,0:T(8,128)(2,1)S(1)}, u32[]{:S(2)}, u32[]{:S(2)}) collective-permute-start(bf16[256,768]{1,0:T(8,128)(2,1)S(1)} %add_convert_fusion.4), channel_id=1, source_target_pairs={{0,24},{8,16},{16,8},{24,0},{1,25},{9,17},{17,9},{25,1},{2,26},{10... | collective-permute-start | bytes 1179656 | tf_op jit(solution)/shard_map/ppermute | solution.py:50
  467.1 16.4 %collective-permute-start.32 = (bf16[256,768]{1,0:T(8,128)(2,1)S(1)}, bf16[256,768]{1,0:T(8,128)(2,1)S(1)}, u32[]{:S(2)}, u32[]{:S(2)}) collective-permute-start(bf16[256,768]{1,0:T(8,128)(2,1)S(1)} %add_convert_fusion.3), channel_id=1, source_target_pairs={{0,4},{4,0},{1,5},{5,1},{2,6},{6,2},{3,7},{7,3},{8,12},{12,8},{9,1... | collective-permute-start | bytes 1179656 | tf_op jit(solution)/shard_map/ppermute | solution.py:40
  (38 other events, 399.1 us)
Sparse Core Ops, SparseCore 0:
  177.6 86.9 reduce-scatter.1

commit v6 on v5

--- a/solution.py
+++ b/solution.py
@@ -217,19 +217,22 @@
 
 
 def mid_kernel(
-    core, x_ref, om_ref, oo_ref, g_ref, valid_ref, emb_ref,
+    core, x_ref, om_ref, oo_ref, g_hbm, valid_ref, emb_ref,
     win_ref, bin_ref, wom_ref, woo_ref, bout_ref, wup_hbm, bup_ref, wdn_hbm, bdn_ref,
-    dres_ref, dom_ref, doo_ref, dbr_ref, sums_ref, bupg_ref,
-    out_hbm, mod_hbm, act_hbm, dhid_hbm, dff_hbm,
-    slope_ref, wup_ref, wdn_ref, out_ref, mod_ref, act_ref, dhid_ref, dff_ref, come, go,
+    dom_ref, doo_ref, sums_ref, bupg_ref,
+    out_hbm, mod_hbm, act_hbm, dhid_hbm, dff_hbm, dres_hbm, dbr_hbm,
+    slope_ref, wup_ref, wdn_ref, out_ref, mod_ref, act_ref, dhid_ref, dff_ref, dres_ref, dbr_ref,
+    g_ref, come, go,
 ):
     hidden_width = wup_ref.shape[1]
     step = 512
     row = pl.program_id(0)
     fetch_up = pltpu.make_async_copy(wup_hbm, wup_ref, come.at[0])
     fetch_down = pltpu.make_async_copy(wdn_hbm, wdn_ref, come.at[1])
+    fetch_g = pltpu.make_async_copy(g_hbm.at[row], g_ref, come.at[2])
     fetch_up.start()
     fetch_down.start()
+    fetch_g.start()
     gone = []
 
     def leave(ref, hbm):
@@ -269,6 +272,7 @@
     ff = ff + bdn_ref[...]
     out_ref[...] = (resid + gate_two * ff).astype(BF)
     leave(out_ref, out_hbm)
+    fetch_g.wait()
     g = g_ref[...].astype(F32)
     sums_ref[0:1, :] = total(g * ff)
     d_ff = (g * gate_two).astype(BF)
@@ -289,9 +293,11 @@
     u = d_mod * (1.0 + scale_two)
     d_res = g + inv * (u - mean(u) - normed * mean(u * normed))
     dres_ref[...] = d_res
+    leave(dres_ref, dres_hbm)
     sums_ref[4:5, :] = total(d_res * branch)
     d_branch = (d_res * gate_one * valid_ref[...]).astype(BF)
     dbr_ref[...] = d_branch
+    leave(dbr_ref, dbr_hbm)
     sums_ref[5:6, :] = total(d_branch.astype(F32))
     dom_ref[...] = dot_nt(d_branch, wom_ref[...]).astype(BF)
     doo_ref[...] = dot_nt(d_branch, woo_ref[...]).astype(BF)
@@ -318,17 +324,17 @@
             num_scalar_prefetch=1,
             grid=(rows,),
             in_specs=[
-                frame(width), frame(half), frame(half), frame(model), frame(1),
+                frame(width), frame(half), frame(half), anywhere, frame(1),
                 pl.BlockSpec((None, 6, model), lambda r, c: (r, 0, 0)),
                 whole(*w_in.shape), whole(1, model),
                 out_half(lambda c: c), out_half(lambda c: 1 - c), whole(1, model),
                 anywhere, whole(1, hidden), anywhere, whole(1, model),
             ],
             out_specs=[
-                frame(model), frame(half), frame(half), frame(model),
+                frame(half), frame(half),
                 pl.BlockSpec((None, 8, model), lambda r, c: (r, 0, 0)),
                 pl.BlockSpec((None, 1, hidden), lambda r, c: (r, 0, 0)),
-            ] + [anywhere] * 5,
+            ] + [anywhere] * 7,
             scratch_shapes=[
                 pltpu.VMEM((span, hidden), BF),
                 pltpu.VMEM((model, hidden), BF),
@@ -338,16 +344,19 @@
                 pltpu.VMEM((span, hidden), BF),
                 pltpu.VMEM((span, hidden), BF),
                 pltpu.VMEM((span, model), BF),
-                pltpu.SemaphoreType.DMA((2,)),
-                pltpu.SemaphoreType.DMA((5,)),
+                pltpu.VMEM((span, model), F32),
+                pltpu.VMEM((span, model), BF),
+                pltpu.VMEM((span, model), BF),
+                pltpu.SemaphoreType.DMA((3,)),
+                pltpu.SemaphoreType.DMA((7,)),
             ],
         ),
         out_shape=[
-            shape(model, F32), shape(half, BF), shape(half, BF), shape(model, BF),
+            shape(half, BF), shape(half, BF),
             jax.ShapeDtypeStruct((rows, 8, model), F32),
             jax.ShapeDtypeStruct((rows, 1, hidden), F32),
             shape(model, BF), shape(model, BF), shape(hidden, BF), shape(hidden, BF),
-            shape(model, BF),
+            shape(model, BF), shape(model, F32), shape(model, BF),
         ],
         compiler_params=pltpu.CompilerParams(vmem_limit_bytes=60 * MIB),
         cost_estimate=QUICK,
@@ -1005,7 +1014,7 @@
     )
 
     o_other = flip(o_give, "core", 1)
-    d_resid, d_o_mine, d_o_give, d_br, sums, up_sums, result, mod_two, act, d_hid, d_ff = mid(
+    d_o_mine, d_o_give, sums, up_sums, result, mod_two, act, d_hid, d_ff, d_resid, d_br = mid(
         core_arg, inputs, o_mine, o_other, cotangent, frame_valid, embedding, w_in, bi,
         w_out, as_row(b_out), w_up, as_row(b_up), w_down, as_row(b_down),
     )

time: 502 us -> 500 us (level)
  no operation moved by 1% of the time
where the time goes in v6:
time: 500 us; the launch traced here: 494 us
  Pallas kernels  329 us (66%)
  other arithmetic  42.5 us (8%)
  starting transfers between devices  37.4 us (7%)
  waiting for transfers between devices  30.8 us (6%)
  local copies, waits for them, and re-layouts  29.7 us (6%)
  between operations  15.4 us (3%)
  matrix products  10 us (2%)
    pallas_call x2, Pallas kernels, attend_back(): pl.pallas_call(functools.partial(attend_back_kernel, blocks=len(blocks),...  115 us
    pallas_call x1, Pallas kernels, attend(): pl.pallas_call(attend_kernel, grid_spec=pltpu.PrefetchScalarGridSpec(num_...  57.5 us
    pallas_call x1, Pallas kernels, mid(): pl.pallas_call(mid_kernel, grid_spec=pltpu.PrefetchScalarGridSpec(num_sca...  30.2 us
    pallas_call x2, Pallas kernels, front(): pl.pallas_call(functools.partial(front_kernel, parts=parts), grid_spec=pl...  26.6 us
    pallas_call x2, Pallas kernels, qkv_outer(): pl.pallas_call(functools.partial(qkv_outer_kernel, far=len(far)), grid_sp...  24.7 us
    pallas_call x1, Pallas kernels, outer(): pl.pallas_call(outer_kernel, grid_spec=pltpu.PrefetchScalarGridSpec(num_s...  20.2 us
    pallas_call x2, Pallas kernels, d_mod(): pl.pallas_call(functools.partial(d_mod_kernel, parts=tuple((len(g) for _,...  19.1 us
    ppermute x12, starting transfers between devices, near_flip(): lax.ppermute(v, axis, [(i, place[gray(i) ^ bit]) for i in range(size)])  19 us
  transfers between devices with their start and end apart: 36, of which 10 were waited for; matrix products, arithmetic and copies ran while one was open for 11% of the time, Pallas kernels for 43%

profile of v6, /device:TPU:0, one launch (start us, length us, event | category | flops | bytes accessed | tf_op | source)
XLA Modules:
  0.0 494.3 jit_solution(13885652751025002958)
XLA Ops:
  15.6 2.6 collective-permute-start.1
  19.3 6.3 %fusion.16 = f32[1,6144]{1,0:T(1,128)S(1)} fusion(bf16[1024,6144]{1,0:T(8,128)(2,1)} %w_ref.1, bf16[1,1024]{1,0:T(2,128)(2,1)S(1)} %copy-done.19), kind=kOutput, calls=%fused_computation.152 | convolution fusion | flops 12589056 | bytes 12609536 | tf_op jit(solution)/shard_map/dot_general | solution.py:22
  30.0 14.7 %front.2 = (bf16[1,2,1024,832]{3,2,1,0:T(8,128)(2,1)}, bf16[1,1664,512]{2,1,0:T(8,128)(2,1)}, bf16[1,1664,512]{2,1,0:T(8,128)(2,1)}, bf16[1,1664,512]{2,1,0:T(8,128)(2,1)}) custom-call(s32[1]{0:T(128)} %bitcast.core.flag, bf16[1,832,768]{2,1,0:T(8,128)(2,1)} %copy-done, bf16[1,832,768]{2,1,0:T(8,128)(2,1)} %collective-permute-done.x1_ref, ...), custom_call_target="tpu_custom_call" | custom-call | flops 1 | bytes 1 | tf_op jit(solution)/shard_map/front/pallas_call | solution.py:175
  44.7 2.1 collective-permute-done.1.x0_ref.refs_3_
  51.7 11.9 %front.3 = (bf16[1,2,1024,832]{3,2,1,0:T(8,128)(2,1)}, bf16[1,1664,512]{2,1,0:T(8,128)(2,1)}, bf16[1,1664,512]{2,1,0:T(8,128)(2,1)}) custom-call(s32[1]{0:T(128)} %bitcast.core.flag, bf16[1,832,768]{2,1,0:T(8,128)(2,1)} %copy-done.2, bf16[1,832,768]{2,1,0:T(8,128)(2,1)} %copy-done.12, bf16[712,1024]{1,0:T(8,128)(2,1)} %refs_4_.3, f32[1,1024]{1,0:T(1,128)} %bitcast.121, ...), custom_call_target="tpu_custom_call" | custom-call | flops 1 | bytes 1 | tf_op jit(solution)/shard_map/front/pallas_call | solution.py:175
  63.7 57.5 %attend.1 = (bf16[1,832,512]{2,1,0:T(8,128)(2,1)}, bf16[1,832,512]{2,1,0:T(8,128)(2,1)}, f32[1,1664,512]{2,1,0:T(8,128)}) custom-call(s32[1]{0:T(128)} %bitcast.core.flag, bf16[1,1664,512]{2,1,0:T(8,128)(2,1)} %get-tuple-element.219.q_ref.refs_0_, bf16[1,1664,128]{2,1,0:T(8,128)(2,1)} %get-tuple-element.220.qx_ref.refs_1_, ...), custom_call_target="tpu_custom_call" | custom-call | flops 1 | bytes 1 | tf_op jit(solution)/shard_map/attend/pallas_call | solution.py:739
  125.6 30.2 %mid.1 = (bf16[1,832,512]{2,1,0:T(8,128)(2,1)}, bf16[1,832,512]{2,1,0:T(8,128)(2,1)}, f32[1,8,1024]{2,1,0:T(8,128)}, f32[1,1,2048]{2,1,0:T(1,128)}, bf16[1,832,1...) custom-call(s32[1]{0:T(128)} %bitcast.core.flag, ...), custom_call_target="tpu_custom_call" | custom-call | flops 1 | bytes 1 | tf_op jit(solution)/shard_map/mid/pallas_call | solution.py:321
  155.9 20.2 %outer.1 = bf16[4,1280,1024]{2,1,0:T(8,128)(2,1)} custom-call(s32[1]{0:T(128)} %bitcast.core.flag, bf16[832,1024]{1,0:T(8,128)(2,1)} %bitcast.107, bf16[832,2048]{1,0:T(8,128)(2,1)} %bitcast.102, bf16[832,512]{1,0:T(8,128)(2,1)} %bitcast.96, bf16[832,512]{1,0:T(8,128)(2,1)} %bitcast.104, bf16[832,2048]{1,0:T(8,128)(2,1)} %bitcast.103, ...), custom_call_target="tpu_custom_call" | custom-call | flops 1 | bytes 1 | tf_op jit(solution)/shard_map/outer/pallas_call | solution.py:413
  177.6 84.0 %attend_back.2 = (bf16[1,1664,384]{2,1,0:T(8,128)(2,1)}, bf16[1,1664,384]{2,1,0:T(8,128)(2,1)}, bf16[1,1664,384]{2,1,0:T(8,128)(2,1)}, bf16[1,1664,384]{2,1,0:T(8,128)(2,1)}, bf16[1,1664,384]{2,1,0:T(8,128)(2,1)}) custom-call(s32[1]{0:T(128)} %bitcast.core.flag, bf16[1,1664,512]{2,1,0:T(8,128)(2,1)} %get-tuple-element.219.q_ref.refs_0_, ...), custom_call_target="tpu_custom_call" | custom-call | flops 1 | bytes 1 | tf_op jit(solution)/shard_map/attend_back/pallas_call | solution.py:893
  264.6 16.0 %qkv_outer.2 = (bf16[2,256,1152]{2,1,0:T(8,128)(2,1)}, bf16[2,256,1152]{2,1,0:T(8,128)(2,1)}, f32[8,1152]{1,0:T(8,128)}) custom-call(s32[2]{0:T(128)} %pad_add_fusion.2.place, bf16[2,1024,832]{2,1,0:T(8,128)(2,1)} %bitcast.92, bf16[1664,384]{1,0:T(8,128)(2,1)} %bitcast.99, bf16[1664,384]{1,0:T(8,128)(2,1)} %bitcast.100, bf16[1664,384]{1,0:T(8,128)(2,1)} %bitcast.101, ...), custom_call_target="tpu_custom_call" | custom-call | flops 1 | bytes 1 | tf_op jit(solution)/shard_map/qkv_outer/pallas_call | solution.py:483
  286.2 30.9 %attend_back.3 = (bf16[1,1664,128]{2,1,0:T(8,128)(2,1)}, bf16[1,1664,128]{2,1,0:T(8,128)(2,1)}, bf16[1,1664,128]{2,1,0:T(8,128)(2,1)}, bf16[1,1664,128]{2,1,0:T(8,128)(2,1)}, bf16[1,1664,128]{2,1,0:T(8,128)(2,1)}) custom-call(s32[1]{0:T(128)} %bitcast.core.flag, bf16[1,1664,512]{2,1,0:T(8,128)(2,1)} %get-tuple-element.219.q_ref.refs_0_, ...), custom_call_target="tpu_custom_call" | custom-call | flops 1 | bytes 1 | tf_op jit(solution)/shard_map/attend_back/pallas_call | solution.py:893
  318.2 2.3 add_convert_fusion
  321.8 2.1 fusion.1
  327.3 8.6 %qkv_outer.3 = (bf16[2,256,384]{2,1,0:T(8,128)(2,1)}, bf16[2,256,384]{2,1,0:T(8,128)(2,1)}, f32[8,384]{1,0:T(8,128)}) custom-call(s32[2]{0:T(128)} %pad_add_fusion.2.place, bf16[2,1024,832]{2,1,0:T(8,128)(2,1)} %bitcast.93, bf16[1664,128]{1,0:T(8,128)(2,1)} %bitcast.112, bf16[1664,128]{1,0:T(8,128)(2,1)} %bitcast.113, bf16[1664,128]{1,0:T(8,128)(2,1)} %bitcast.114, ...), custom_call_target="tpu_custom_call" | custom-call | flops 1 | bytes 1 | tf_op jit(solution)/shard_map/qkv_outer/pallas_call | solution.py:483
  337.4 8.2 %d_mod.2 = (bf16[1,832,1024]{2,1,0:T(8,128)(2,1)}, bf16[1,832,1024]{2,1,0:T(8,128)(2,1)}) custom-call(s32[1]{0:T(128)} %bitcast.core.flag, bf16[1,1664,384]{2,1,0:T(8,128)(2,1)} %get-tuple-element.210.refs_0_, bf16[1,1664,128]{2,1,0:T(8,128)(2,1)} %get-tuple-element.246.refs_1_, bf16[1,1664,384]{2,1,0:T(8,128)(2,1)} %get-tuple-element.216.refs_2_, ...), custom_call_target="tpu_custom_call" | custom-call | flops 1 | bytes 1 | tf_op jit(solution)/shard_map/d_mod/pallas_call | solution.py:528
  347.0 2.4 collective-permute-start.10
  350.0 10.9 %d_mod.3 = (bf16[1,832,1024]{2,1,0:T(8,128)(2,1)}, bf16[1,832,1024]{2,1,0:T(8,128)(2,1)}) custom-call(s32[1]{0:T(128)} %bitcast.core.flag, bf16[1,1664,384]{2,1,0:T(8,128)(2,1)} %get-tuple-element.257.refs_0_, bf16[1,1664,128]{2,1,0:T(8,128)(2,1)} %get-tuple-element.258.refs_1_, bf16[1,1664,384]{2,1,0:T(8,128)(2,1)} %get-tuple-element.259.refs_2_, ...), custom_call_target="tpu_custom_call" | custom-call | flops 1 | bytes 1 | tf_op jit(solution)/shard_map/d_mod/pallas_call | solution.py:528
  366.2 2.2 collective-permute-done.13
  373.6 3.6 collective-permute-start.16
  378.0 16.9 %in_outer.1 = (bf16[1,2,256,768]{3,2,1,0:T(8,128)(2,1)}, bf16[1,2,256,768]{3,2,1,0:T(8,128)(2,1)}, f32[1,8,1024]{2,1,0:T(8,128)}, bf16[1,832,1024]{2,1,0:T(8,128)(2,1)}) custom-call(s32[2]{0:T(128)} %pad_add_fusion.2.place, f32[1,832,1024]{2,1,0:T(8,128)} %get-tuple-element.188.dres_hbm.refs_1_, f32[1,6,1024]{2,1,0:T(8,128)} %reshape.1310.emb_ref.refs_2_, ...), custom_call_target="tpu_custom_call" | custom-call | flops 1 | bytes 1 | tf_op jit(solution)/shard_map/in_outer/pallas_call | solution.py:607
  405.9 7.6 %collective-permute-done.20 = f32[14336]{0:T(1024)S(1)} collective-permute-done((f32[14336]{0:T(1024)S(1)}, f32[14336]{0:T(1024)S(1)}, u32[]{:S(2)}, u32[]{:S(2)}) %collective-permute-start.20) | collective-permute-done | bytes 57376 | tf_op jit(solution)/shard_map/ppermute | solution.py:40
  418.2 7.4 %ada.1 = f32[1,1024]{1,0:T(1,128)} custom-call(bf16[1,6144]{1,0:T(2,128)(2,1)} %convert_element_type.346.t_ref, bf16[1024,6144]{1,0:T(8,128)(2,1)} %w_ref.1), custom_call_target="tpu_custom_call" | custom-call | flops 1 | bytes 1 | tf_op jit(solution)/shard_map/ada/pallas_call | solution.py:204
  427.3 2.6 collective-permute-start.27
  429.9 2.0 collective-permute-start.28
  434.2 8.0 %collective-permute-done.26 = bf16[256,768]{1,0:T(8,128)(2,1)S(1)} collective-permute-done((bf16[256,768]{1,0:T(8,128)(2,1)S(1)}, bf16[256,768]{1,0:T(8,128)(2,1)S(1)}, u32[]{:S(2)}, u32[]{:S(2)}) %collective-permute-start.26) | collective-permute-done | bytes 393248 | tf_op jit(solution)/shard_map/ppermute | solution.py:50
  442.3 3.5 collective-permute-done.28
  447.7 2.3 collective-permute-start.29
  450.0 3.3 collective-permute-done.30
  453.4 11.0 %d_in.1 = (f32[1,832,100]{2,1,0:T(8,128)}, f32[1,832,100]{2,1,0:T(8,128)}, f32[1,832,512]{2,1,0:T(8,128)}) custom-call(bf16[1,832,768]{2,1,0:T(8,128)(2,1)} %copy-done, f32[1,832,1024]{2,1,0:T(8,128)} %get-tuple-element.188.dres_hbm.refs_1_, f32[1,6,1024]{2,1,0:T(8,128)} %reshape.1310.emb_ref.refs_2_, f32[1,832,2]{2,1,0:T(8,128)} %copy.68.refs_3_, ...), custom_call_target="tpu_custom_call" | custom-call | flops 1 | bytes 1 | tf_op jit(solution)/shard_map/d_in/pallas_call | solution.py:656
  469.2 2.1 copy.70
  472.6 3.7 fusion.11
  484.0 2.0 concatenate.140
  (273 shorter events, 89.6 us)
Async XLA Ops:
  7.2 256.0 %reduce-scatter.2.cloned.1.call-start = ((), (), s32[]{:S(2)}) async-start(), calls=%async_computation.1 | async-start | bytes 13107200 | tf_op jit(solution)/shard_map/reduce_scatter | solution.py:1027
  15.1 14.9 %collective-permute-start = (bf16[1,832,768]{2,1,0:T(8,128)(2,1)S(1)}, bf16[1,832,768]{2,1,0:T(8,128)(2,1)}, u32[]{:S(2)}, u32[]{:S(2)}) collective-permute-start(bf16[1,832,768]{2,1,0:T(8,128)(2,1)S(1)} %maximum_maximum_fusion.x0_ref.x_ref.refs_0_), channel_id=1, source_target_pairs={{0,1},{1,0},{2,3},{3,2},{4,5},{5,4},{6,7},{7,6},{8,9},{9,8},{10,11... | collective-permute-start | bytes 3833864 | tf_op jit(solution)/shard_map/ppermute | solution.py:40
  15.6 31.2 %collective-permute-start.1 = (bf16[1,832,768]{2,1,0:T(8,128)(2,1)S(1)}, bf16[1,832,768]{2,1,0:T(8,128)(2,1)S(1)}, u32[]{:S(2)}, u32[]{:S(2)}) collective-permute-start(bf16[1,832,768]{2,1,0:T(8,128)(2,1)S(1)} %maximum_maximum_fusion.x0_ref.x_ref.refs_0_), channel_id=1, source_target_pairs={{0,2},{2,0},{1,3},{3,1},{4,6},{6,4},{5,7},{7,5},{8,10},{10,8},{9,1... | collective-permute-start | bytes 3833864 | tf_op jit(solution)/shard_map/ppermute | solution.py:35
  46.8 3.8 collective-permute-start.2
  155.8 20.3 %collective-permute-start.4 = (bf16[1,832,512]{2,1,0:T(8,128)(2,1)}, bf16[1,832,512]{2,1,0:T(8,128)(2,1)S(1)}, u32[]{:S(2)}, u32[]{:S(2)}) collective-permute-start(bf16[1,832,512]{2,1,0:T(8,128)(2,1)} %get-tuple-element.195), channel_id=1, source_target_pairs={{0,1},{1,0},{2,3},{3,2},{4,5},{5,4},{6,7},{7,6},{8,9},{9,8},{10,11... | collective-permute-start | bytes 2555912 | tf_op jit(solution)/shard_map/ppermute | solution.py:40
  280.7 36.5 %collective-permute-start.6 = (bf16[640,1024]{1,0:T(8,128)(2,1)S(1)}, bf16[640,1024]{1,0:T(8,128)(2,1)S(1)}, u32[]{:S(2)}, u32[]{:S(2)}) collective-permute-start(bf16[640,1024]{1,0:T(8,128)(2,1)S(1)} %constant_dynamic-slice_fusion.5), channel_id=1, source_target_pairs={{0,4},{4,0},{1,5},{5,1},{2,6},{6,2},{3,7},{7,3},{8,12},{12,8},{9,1... | collective-permute-start | bytes 3932168 | tf_op jit(solution)/shard_map/ppermute | solution.py:40
  285.9 31.3 %collective-permute-start.7 = (bf16[512,1152]{1,0:T(8,128)(2,1)}, bf16[512,1152]{1,0:T(8,128)(2,1)}, u32[]{:S(2)}, u32[]{:S(2)}) collective-permute-start(bf16[512,1152]{1,0:T(8,128)(2,1)} %pad_maximum_fusion.2), channel_id=1, source_target_pairs={{0,2},{2,0},{1,3},{3,1},{4,6},{6,4},{5,7},{7,5},{8,10},{10,8},{9,1... | collective-permute-start | bytes 3538952 | tf_op jit(solution)/shard_map/ppermute | solution.py:35
  323.9 21.7 %collective-permute-start.8 = (bf16[320,1024]{1,0:T(8,128)(2,1)S(1)}, bf16[320,1024]{1,0:T(8,128)(2,1)}, u32[]{:S(2)}, u32[]{:S(2)}) collective-permute-start(bf16[320,1024]{1,0:T(8,128)(2,1)S(1)} %constant_dynamic-slice_fusion.4), channel_id=1, source_target_pairs={{0,8},{8,0},{16,24},{24,16},{1,9},{9,1},{17,25},{25,17},{2,10},{10... | collective-permute-start | bytes 1966088 | tf_op jit(solution)/shard_map/ppermute | solution.py:50
  335.9 25.0 %collective-permute-start.9 = (bf16[256,1152]{1,0:T(8,128)(2,1)}, bf16[256,1152]{1,0:T(8,128)(2,1)}, u32[]{:S(2)}, u32[]{:S(2)}) collective-permute-start(bf16[256,1152]{1,0:T(8,128)(2,1)} %fusion.1), channel_id=1, source_target_pairs={{0,4},{4,0},{1,5},{5,1},{2,6},{6,2},{3,7},{7,3},{8,12},{12,8},{9,1... | collective-permute-start | bytes 1769480 | tf_op jit(solution)/shard_map/ppermute | solution.py:40
  347.0 13.9 %collective-permute-start.10 = (bf16[160,1024]{1,0:T(8,128)(2,1)S(1)}, bf16[160,1024]{1,0:T(8,128)(2,1)S(1)}, u32[]{:S(2)}, u32[]{:S(2)}) collective-permute-start(bf16[160,1024]{1,0:T(8,128)(2,1)S(1)} %constant_dynamic-slice_fusion.3), channel_id=1, source_target_pairs={{0,24},{8,16},{16,8},{24,0},{1,25},{9,17},{17,9},{25,1},{2,26},{10... | collective-permute-start | bytes 983048 | tf_op jit(solution)/shard_map/ppermute | solution.py:50
  361.7 6.9 %collective-permute-start.11 = (bf16[1,832,1024]{2,1,0:T(8,128)(2,1)}, bf16[1,832,1024]{2,1,0:T(8,128)(2,1)S(1)}, u32[]{:S(2)}, u32[]{:S(2)}) collective-permute-start(bf16[1,832,1024]{2,1,0:T(8,128)(2,1)} %get-tuple-element.270), channel_id=1, source_target_pairs={{0,1},{1,0},{2,3},{3,2},{4,5},{5,4},{6,7},{7,6},{8,9},{9,8},{10,11... | collective-permute-start | bytes 5111816 | tf_op jit(solution)/shard_map/ppermute | solution.py:40
  361.7 6.9 %collective-permute-start.12 = (bf16[1,832,1024]{2,1,0:T(8,128)(2,1)}, bf16[1,832,1024]{2,1,0:T(8,128)(2,1)S(1)}, u32[]{:S(2)}, u32[]{:S(2)}) collective-permute-start(bf16[1,832,1024]{2,1,0:T(8,128)(2,1)} %get-tuple-element.271), channel_id=1, source_target_pairs={{0,1},{1,0},{2,3},{3,2},{4,5},{5,4},{6,7},{7,6},{8,9},{9,8},{10,11... | collective-permute-start | bytes 5111816 | tf_op jit(solution)/shard_map/ppermute | solution.py:40
  363.5 5.0 %collective-permute-start.13 = (bf16[2,256,384]{2,1,0:T(8,128)(2,1)}, bf16[2,256,384]{2,1,0:T(8,128)(2,1)S(1)}, u32[]{:S(2)}, u32[]{:S(2)}) collective-permute-start(bf16[2,256,384]{2,1,0:T(8,128)(2,1)} %get-tuple-element.274), channel_id=1, source_target_pairs={{0,1},{1,0},{2,3},{3,2},{4,5},{5,4},{6,7},{7,6},{8,9},{9,8},{10,11... | collective-permute-start | bytes 1179656 | tf_op jit(solution)/shard_map/ppermute | solution.py:40
  369.8 25.1 %collective-permute-start.14 = (bf16[256,768]{1,0:T(8,128)(2,1)S(1)}, bf16[256,768]{1,0:T(8,128)(2,1)}, u32[]{:S(2)}, u32[]{:S(2)}) collective-permute-start(bf16[256,768]{1,0:T(8,128)(2,1)S(1)} %pad_maximum_fusion.9), channel_id=1, source_target_pairs={{0,2},{2,0},{1,3},{3,1},{4,6},{6,4},{5,7},{7,5},{8,10},{10,8},{9,1... | collective-permute-start | bytes 1179656 | tf_op jit(solution)/shard_map/ppermute | solution.py:35
  372.1 22.8 %collective-permute-start.15 = (bf16[160,1024]{1,0:T(8,128)(2,1)S(1)}, bf16[160,1024]{1,0:T(8,128)(2,1)S(1)}, u32[]{:S(2)}, u32[]{:S(2)}) collective-permute-start(bf16[160,1024]{1,0:T(8,128)(2,1)S(1)} %add_convert_fusion.6), channel_id=1, source_target_pairs={{0,24},{8,16},{16,8},{24,0},{1,25},{9,17},{17,9},{25,1},{2,26},{10... | collective-permute-start | bytes 983048 | tf_op jit(solution)/shard_map/ppermute | solution.py:50
  373.6 21.3 %collective-permute-start.16 = (bf16[128,1152]{1,0:T(8,128)(2,1)}, bf16[128,1152]{1,0:T(8,128)(2,1)}, u32[]{:S(2)}, u32[]{:S(2)}) collective-permute-start(bf16[128,1152]{1,0:T(8,128)(2,1)} %constant_dynamic-slice_fusion.2), channel_id=1, source_target_pairs={{0,8},{8,0},{16,24},{24,16},{1,9},{9,1},{17,25},{25,17},{2,10},{10... | collective-permute-start | bytes 884744 | tf_op jit(solution)/shard_map/ppermute | solution.py:50
  400.3 13.3 %collective-permute-start.19 = (bf16[256,768]{1,0:T(8,128)(2,1)S(1)}, bf16[256,768]{1,0:T(8,128)(2,1)S(1)}, u32[]{:S(2)}, u32[]{:S(2)}) collective-permute-start(bf16[256,768]{1,0:T(8,128)(2,1)S(1)} %fusion.2), channel_id=1, source_target_pairs={{0,2},{2,0},{1,3},{3,1},{4,6},{6,4},{5,7},{7,5},{8,10},{10,8},{9,1... | collective-permute-start | bytes 1179656 | tf_op jit(solution)/shard_map/ppermute | solution.py:35
  401.2 12.4 %collective-permute-start.21 = (bf16[64,1152]{1,0:T(8,128)(2,1)S(1)}, bf16[64,1152]{1,0:T(8,128)(2,1)S(1)}, u32[]{:S(2)}, u32[]{:S(2)}) collective-permute-start(bf16[64,1152]{1,0:T(8,128)(2,1)S(1)} %constant_dynamic-slice_fusion.1), channel_id=1, source_target_pairs={{0,24},{8,16},{16,8},{24,0},{1,25},{9,17},{17,9},{25,1},{2,26},{10... | collective-permute-start | bytes 442376 | tf_op jit(solution)/shard_map/ppermute | solution.py:50
  402.5 23.6 %collective-permute-start.24 = (bf16[320,1024]{1,0:T(8,128)(2,1)S(1)}, bf16[320,1024]{1,0:T(8,128)(2,1)S(1)}, u32[]{:S(2)}, u32[]{:S(2)}) collective-permute-start(bf16[320,1024]{1,0:T(8,128)(2,1)S(1)} %pad_maximum_fusion.3), channel_id=1, source_target_pairs={{0,8},{8,0},{16,24},{24,16},{1,9},{9,1},{17,25},{25,17},{2,10},{10... | collective-permute-start | bytes 1966088 | tf_op jit(solution)/shard_map/ppermute | solution.py:50
  402.6 11.0 %collective-permute-start.20 = (f32[14336]{0:T(1024)S(1)}, f32[14336]{0:T(1024)S(1)}, u32[]{:S(2)}, u32[]{:S(2)}) collective-permute-start(f32[14336]{0:T(1024)S(1)} %add.270), channel_id=1, source_target_pairs={{0,2},{2,0},{1,3},{3,1},{4,6},{6,4},{5,7},{7,5},{8,10},{10,8},{9,1... | collective-permute-start | bytes 172040 | tf_op jit(solution)/shard_map/ppermute | solution.py:40
  405.0 48.3 %collective-permute-start.31 = (bf16[1,832,1024]{2,1,0:T(8,128)(2,1)}, bf16[1,832,1024]{2,1,0:T(8,128)(2,1)}, u32[]{:S(2)}, u32[]{:S(2)}) collective-permute-start(bf16[1,832,1024]{2,1,0:T(8,128)(2,1)} %get-tuple-element.318), channel_id=1, source_target_pairs={{0,2},{2,0},{1,3},{3,1},{4,6},{6,4},{5,7},{7,5},{8,10},{10,8},{9,1... | collective-permute-start | bytes 5111816 | tf_op jit(solution)/shard_map/ppermute | solution.py:35
  414.9 11.1 %collective-permute-start.25 = (bf16[64,1152]{1,0:T(8,128)(2,1)S(1)}, bf16[64,1152]{1,0:T(8,128)(2,1)S(1)}, u32[]{:S(2)}, u32[]{:S(2)}) collective-permute-start(bf16[64,1152]{1,0:T(8,128)(2,1)S(1)} %add_convert_fusion.10), channel_id=1, source_target_pairs={{0,24},{8,16},{16,8},{24,0},{1,25},{9,17},{17,9},{25,1},{2,26},{10... | collective-permute-start | bytes 442376 | tf_op jit(solution)/shard_map/ppermute | solution.py:50
  416.2 9.9 %collective-permute-start.23 = (bf16[256,768]{1,0:T(8,128)(2,1)S(1)}, bf16[256,768]{1,0:T(8,128)(2,1)S(1)}, u32[]{:S(2)}, u32[]{:S(2)}) collective-permute-start(bf16[256,768]{1,0:T(8,128)(2,1)S(1)} %pad_maximum_fusion.10), channel_id=1, source_target_pairs={{0,4},{4,0},{1,5},{5,1},{2,6},{6,2},{3,7},{7,3},{8,12},{12,8},{9,1... | collective-permute-start | bytes 1179656 | tf_op jit(solution)/shard_map/ppermute | solution.py:40
  416.8 9.2 %collective-permute-start.22 = (f32[1,8448]{1,0:T(1,128)S(1)}, f32[1,8448]{1,0:T(1,128)S(1)}, u32[]{:S(2)}, u32[]{:S(2)}) collective-permute-start(f32[1,8448]{1,0:T(1,128)S(1)} %pad_maximum_fusion.17), channel_id=1, source_target_pairs={{0,4},{4,0},{1,5},{5,1},{2,6},{6,2},{3,7},{7,3},{8,12},{12,8},{9,1... | collective-permute-start | bytes 101384 | tf_op jit(solution)/shard_map/ppermute | solution.py:40
  426.7 49.7 %collective-permute-start.34 = (bf16[640,1024]{1,0:T(8,128)(2,1)S(1)}, bf16[640,1024]{1,0:T(8,128)(2,1)}, u32[]{:S(2)}, u32[]{:S(2)}) collective-permute-start(bf16[640,1024]{1,0:T(8,128)(2,1)S(1)} %pad_maximum_fusion.1), channel_id=1, source_target_pairs={{0,4},{4,0},{1,5},{5,1},{2,6},{6,2},{3,7},{7,3},{8,12},{12,8},{9,1... | collective-permute-start | bytes 3932168 | tf_op jit(solution)/shard_map/ppermute | solution.py:40
  427.3 6.9 %collective-permute-start.27 = (f32[2,8448]{1,0:T(2,128)S(1)}, f32[2,8448]{1,0:T(2,128)S(1)}, u32[]{:S(2)}, u32[]{:S(2)}) collective-permute-start(f32[2,8448]{1,0:T(2,128)S(1)} %pad_maximum_fusion.16), channel_id=1, source_target_pairs={{0,24},{8,16},{16,8},{24,0},{1,25},{9,17},{17,9},{25,1},{2,26},{10... | collective-permute-start | bytes 202760 | tf_op jit(solution)/shard_map/ppermute | solution.py:50
  429.9 12.3 %collective-permute-start.26 = (bf16[256,768]{1,0:T(8,128)(2,1)S(1)}, bf16[256,768]{1,0:T(8,128)(2,1)S(1)}, u32[]{:S(2)}, u32[]{:S(2)}) collective-permute-start(bf16[256,768]{1,0:T(8,128)(2,1)S(1)} %add_convert_fusion.5), channel_id=1, source_target_pairs={{0,8},{8,0},{16,24},{24,16},{1,9},{9,1},{17,25},{25,17},{2,10},{10... | collective-permute-start | bytes 1179656 | tf_op jit(solution)/shard_map/ppermute | solution.py:50
  429.9 15.8 %collective-permute-start.28 = (bf16[128,1152]{1,0:T(8,128)(2,1)S(1)}, bf16[128,1152]{1,0:T(8,128)(2,1)S(1)}, u32[]{:S(2)}, u32[]{:S(2)}) collective-permute-start(bf16[128,1152]{1,0:T(8,128)(2,1)S(1)} %pad_maximum_fusion.12), channel_id=1, source_target_pairs={{0,8},{8,0},{16,24},{24,16},{1,9},{9,1},{17,25},{25,17},{2,10},{10... | collective-permute-start | bytes 884744 | tf_op jit(solution)/shard_map/ppermute | solution.py:50
  445.8 7.5 %collective-permute-start.30 = (f32[4,8448]{1,0:T(4,128)S(1)}, f32[4,8448]{1,0:T(4,128)S(1)}, u32[]{:S(2)}, u32[]{:S(2)}) collective-permute-start(f32[4,8448]{1,0:T(4,128)S(1)} %pad_maximum_fusion.15), channel_id=1, source_target_pairs={{0,8},{8,0},{16,24},{24,16},{1,9},{9,1},{17,25},{25,17},{2,10},{10... | collective-permute-start | bytes 405512 | tf_op jit(solution)/shard_map/ppermute | solution.py:50
  446.2 35.9 %collective-permute-start.33 = (bf16[256,1152]{1,0:T(8,128)(2,1)S(1)}, bf16[256,1152]{1,0:T(8,128)(2,1)}, u32[]{:S(2)}, u32[]{:S(2)}) collective-permute-start(bf16[256,1152]{1,0:T(8,128)(2,1)S(1)} %pad_maximum_fusion.4), channel_id=1, source_target_pairs={{0,4},{4,0},{1,5},{5,1},{2,6},{6,2},{3,7},{7,3},{8,12},{12,8},{9,1... | collective-permute-start | bytes 1769480 | tf_op jit(solution)/shard_map/ppermute | solution.py:40
  447.7 16.7 %collective-permute-start.29 = (bf16[256,768]{1,0:T(8,128)(2,1)S(1)}, bf16[256,768]{1,0:T(8,128)(2,1)S(1)}, u32[]{:S(2)}, u32[]{:S(2)}) collective-permute-start(bf16[256,768]{1,0:T(8,128)(2,1)S(1)} %add_convert_fusion.4), channel_id=1, source_target_pairs={{0,24},{8,16},{16,8},{24,0},{1,25},{9,17},{17,9},{25,1},{2,26},{10... | collective-permute-start | bytes 1179656 | tf_op jit(solution)/shard_map/ppermute | solution.py:50
  465.8 16.4 %collective-permute-start.32 = (bf16[256,768]{1,0:T(8,128)(2,1)S(1)}, bf16[256,768]{1,0:T(8,128)(2,1)S(1)}, u32[]{:S(2)}, u32[]{:S(2)}) collective-permute-start(bf16[256,768]{1,0:T(8,128)(2,1)S(1)} %add_convert_fusion.3), channel_id=1, source_target_pairs={{0,4},{4,0},{1,5},{5,1},{2,6},{6,2},{3,7},{7,3},{8,12},{12,8},{9,1... | collective-permute-start | bytes 1179656 | tf_op jit(solution)/shard_map/ppermute | solution.py:40
  (38 other events, 399.1 us)
Sparse Core Ops, SparseCore 0:
  176.3 86.9 reduce-scatter.1
